TPU v7x, 32 devices: a whole 2x2x4 slice. The times are simulated.
32 devices in a mesh: dp: 8 (over z, x), tensor: 4 (over y, core).
Axes of the slice: x: 2, y: 2, z: 4, core: 2. Of those that a mesh axis runs over, the one named last changes fastest.
Arguments:
- hidden_in: bfloat16 [8192, 2048], P(('dp', 'tensor')), may hold values from -6 to 6
- cotangent: bfloat16 [8192, 2048], P(('dp', 'tensor')), may hold values from -6 to 6
- seq_lengths: int32 [8], P('dp'), may hold values from 769 to 1024, as said below
- expert_ids: int32 [8192, 8], P(('dp', 'tensor')), may hold values from 0 to 63, all different within a row; in each aligned block of 256 rows (0 to 255, 256 to 511, ...) at most 32 rows name the same one
- attn_gain: bfloat16 [2048], replicated, may hold values from 0.099609375 to 1.8984375
- w_query: bfloat16 [2048, 2048], P(None, 'tensor'), may hold values from -0.125 to 0.125
- w_key: bfloat16 [2048, 2048], P(None, 'tensor'), may hold values from -0.125 to 0.125
- w_value: bfloat16 [2048, 2048], P(None, 'tensor'), may hold values from -0.125 to 0.125
- query_gain: bfloat16 [2048], P('tensor'), may hold values from 0.099609375 to 1.8984375
- key_gain: bfloat16 [2048], P('tensor'), may hold values from 0.099609375 to 1.8984375
- w_out: bfloat16 [2048, 2048], P('tensor'), may hold values from -1 to 1
- ffn_gain: bfloat16 [2048], replicated, may hold values from 0.099609375 to 1.8984375
- w_router: bfloat16 [2048, 64], replicated, may hold values from -0.0625 to 0.0625
- w_gate: bfloat16 [64, 2048, 1024], P('dp', None, 'tensor'), may hold values from -0.125 to 0.125
- w_up: bfloat16 [64, 2048, 1024], P('dp', None, 'tensor'), may hold values from -0.125 to 0.125
- w_down: bfloat16 [64, 1024, 2048], P('dp', 'tensor'), may hold values from -4 to 4
Outputs:
- output: bfloat16 [8192, 2048], P(('dp', 'tensor'))
- grad_input: bfloat16 [8192, 2048], P(('dp', 'tensor'))
- grad_w_query: float32 [2048, 2048], P(None, 'tensor')
- grad_w_key: float32 [2048, 2048], P(None, 'tensor')
- grad_w_value: float32 [2048, 2048], P(None, 'tensor')
- grad_query_gain: float32 [2048], P('tensor')
- grad_key_gain: float32 [2048], P('tensor')
- grad_w_out: float32 [2048, 2048], P('tensor')
- grad_attn_gain: float32 [2048], replicated
- grad_ffn_gain: float32 [2048], replicated
- grad_w_router: float32 [2048, 64], replicated
- grad_w_gate: float32 [64, 2048, 1024], P('dp', None, 'tensor')
- grad_w_up: float32 [64, 2048, 1024], P('dp', None, 'tensor')
- grad_w_down: float32 [64, 1024, 2048], P('dp', 'tensor')
Inputs may be any that keep to these rules, and one draw needn't show every extreme that they name: `expert_ids`: among the 256 rows of one device (aligned blocks), every expert is named by exactly 32 rows; a row names 8 different experts. Sequence g is live at positions below seq_lengths[g]; some sequence is live in full.
All inputs are finite; a program needn't handle non-finite values.
Results may differ from a plain program's by a relative error of at most 0.023.
Values may be sent and summed in bfloat16 or wider, within the bound.
No kernel may reach another device: no remote copies, remote signals or barrier semaphores. Data moves between devices by JAX's collectives and lax.ppermute only.
A program may use at most 640 MiB of HBM per device.

v0:
```python
import math

import jax
import jax.numpy as jnp
from jax import lax
from jax.sharding import PartitionSpec as P

HDIM = 128


EPS = 1e-05
ROPE_BASE = 10000.0


def rms_scale(values):
    return lax.rsqrt(jnp.mean(values * values, axis=-1, keepdims=True) + EPS)


def rope_tables(count, head_width):
    half_width = head_width // 2
    frequency = jnp.exp(
        -(jnp.arange(half_width, dtype=jnp.float32) * 2.0 / head_width) * math.log(ROPE_BASE)
    )
    angles = jnp.arange(count, dtype=jnp.float32)[:, None] * frequency[None, :]
    return (jnp.cos(angles)[:, None, :], jnp.sin(angles)[:, None, :])


def rotate(values_in, cosine, sine_table):
    half_width = values_in.shape[-1] // 2
    front_half = values_in[..., :half_width]
    back_half = values_in[..., half_width:]
    return jnp.concatenate(
        [
            front_half * cosine - back_half * sine_table,
            back_half * cosine + front_half * sine_table,
        ],
        axis=-1,
    )


def unrotate(grads_in, cosine, sine_table):
    half_width = grads_in.shape[-1] // 2
    front_half = grads_in[..., :half_width]
    back_half = grads_in[..., half_width:]
    return jnp.concatenate(
        [
            front_half * cosine + back_half * sine_table,
            back_half * cosine - front_half * sine_table,
        ],
        axis=-1,
    )


def contract_rows(left, right):
    return lax.dot_general(
        left, right, (((0,), (0,)), ((), ())), preferred_element_type=jnp.float32
    )


def times_transpose(left, right):
    return lax.dot_general(
        left, right, (((1,), (1,)), ((), ())), preferred_element_type=jnp.float32
    )


def local(
    hidden_in,
    cotangent,
    seq_lengths,
    expert_ids,
    attn_gain,
    w_query,
    w_key,
    w_value,
    query_gain,
    key_gain,
    w_out,
    ffn_gain,
    w_router,
    w_gate,
    w_up,
    w_down,
):
    tensor_count = lax.axis_size("tensor")
    group_count = lax.axis_size("dp")
    device_total = tensor_count * group_count
    tok_rows, model_width = hidden_in.shape
    topk_count = expert_ids.shape[1]
    local_experts = w_gate.shape[0]
    expert_total = w_router.shape[1]
    slot_count = tok_rows * topk_count // expert_total
    per_group = local_experts * slot_count
    seq_len = tok_rows * tensor_count
    local_width = w_query.shape[1]
    head_width = HDIM
    local_heads = local_width // head_width
    block_rows = min(512, seq_len)
    block_count = seq_len // block_rows
    score_scale = head_width ** (-0.5)
    live_length = seq_lengths[0]
    cosine, sine_table = rope_tables(seq_len, head_width)
    key_pos = jnp.arange(seq_len)
    key_live = key_pos < live_length

    def send_out(rows_low):
        grouped_rows = rows_low.reshape(group_count, 1, per_group, model_width)
        copies = jnp.broadcast_to(
            grouped_rows, (group_count, tensor_count, per_group, model_width)
        ).reshape(device_total, per_group, model_width)
        arrived = lax.all_to_all(copies, ("dp", "tensor"), split_axis=0, concat_axis=0, tiled=True)
        return arrived.reshape(device_total, local_experts, slot_count, model_width)

    def send_back(parts_low):
        returned = lax.all_to_all(
            parts_low.reshape(device_total, per_group, model_width),
            ("dp", "tensor"),
            split_axis=0,
            concat_axis=0,
            tiled=True,
        )
        return jnp.sum(
            returned.reshape(group_count, tensor_count, per_group, model_width).astype(jnp.float32),
            axis=1,
        ).reshape(-1, model_width)

    resid = hidden_in.astype(jnp.float32)
    scale_one = rms_scale(resid)
    normed = resid * scale_one
    attn_in = (normed * attn_gain.astype(jnp.float32)).astype(jnp.bfloat16)
    gathered = lax.all_gather(attn_in, "tensor", axis=0, tiled=True)
    q_raw = jnp.dot(gathered, w_query, preferred_element_type=jnp.float32)
    k_raw = jnp.dot(gathered, w_key, preferred_element_type=jnp.float32)
    v_raw = jnp.dot(gathered, w_value, preferred_element_type=jnp.float32)
    q_square, k_square = lax.psum(
        (jnp.sum(q_raw * q_raw, axis=1), jnp.sum(k_raw * k_raw, axis=1)), "tensor"
    )
    q_rscale = lax.rsqrt(q_square / model_width + EPS)[:, None]
    k_rscale = lax.rsqrt(k_square / model_width + EPS)[:, None]
    query_hat = q_raw * q_rscale
    key_hat = k_raw * k_rscale
    q_gain = query_gain.astype(jnp.float32)
    k_gain = key_gain.astype(jnp.float32)
    q_rot = rotate(
        (query_hat * q_gain).reshape(seq_len, local_heads, head_width), cosine, sine_table
    ).astype(jnp.bfloat16)
    k_rot = rotate(
        (key_hat * k_gain).reshape(seq_len, local_heads, head_width), cosine, sine_table
    ).astype(jnp.bfloat16)
    v_low = v_raw.astype(jnp.bfloat16).reshape(seq_len, local_heads, head_width)
    starts = jnp.arange(block_count) * block_rows
    q_blocks = q_rot.reshape(block_count, block_rows, local_heads, head_width)

    def allowed_mask(row_start):
        q_pos = row_start + jnp.arange(block_rows)
        return ((key_pos[None, :] <= q_pos[:, None]) & key_live[None, :])[None]

    def attend(inputs):
        q_block, row_start = inputs
        scores = (
            jnp.einsum("qhd,khd->hqk", q_block, k_rot, preferred_element_type=jnp.float32)
            * score_scale
        )
        scores = jnp.where(allowed_mask(row_start), scores, -1e30)
        row_max = jnp.max(scores, axis=-1, keepdims=True)
        exp_scores = jnp.exp(scores - row_max)
        row_total = jnp.sum(exp_scores, axis=-1, keepdims=True)
        soft_low = (exp_scores / row_total).astype(jnp.bfloat16)
        attended = jnp.einsum("hqk,khd->qhd", soft_low, v_low, preferred_element_type=jnp.float32)
        return (attended, (row_max + jnp.log(row_total))[..., 0])

    o_blocks, lse_blocks = lax.map(attend, (q_blocks, starts))
    o_low = o_blocks.reshape(seq_len, local_width).astype(jnp.bfloat16)
    attn_rows = lax.psum_scatter(
        jnp.dot(o_low, w_out, preferred_element_type=jnp.float32),
        "tensor",
        scatter_dimension=0,
        tiled=True,
    )
    mixed = resid + attn_rows
    scale_two = rms_scale(mixed)
    mixed_norm = mixed * scale_two
    ffn_in = (mixed_norm * ffn_gain.astype(jnp.float32)).astype(jnp.bfloat16)
    logits = jnp.dot(ffn_in, w_router, preferred_element_type=jnp.float32)
    router_probs = jax.nn.softmax(logits, axis=-1)
    expert_hot = (expert_ids[:, :, None] == jnp.arange(expert_total)[None, None, :]).astype(
        jnp.float32
    )
    gate_values = jnp.einsum("tke,te->tk", expert_hot, router_probs)
    flat_ids = expert_ids.reshape(-1)
    sort_order = jnp.argsort(flat_ids, stable=True)
    inverse = jnp.argsort(sort_order)
    expert_in = send_out(ffn_in[sort_order // topk_count])
    gate_pre = jnp.einsum("secd,edf->secf", expert_in, w_gate, preferred_element_type=jnp.float32)
    up_pre = jnp.einsum("secd,edf->secf", expert_in, w_up, preferred_element_type=jnp.float32)
    silu_gate = jax.nn.silu(gate_pre)
    acts = (silu_gate * up_pre).astype(jnp.bfloat16)
    partial_value = jnp.einsum(
        "secf,efd->secd", acts, w_down, preferred_element_type=jnp.float32
    ).astype(jnp.bfloat16)
    out_sorted = send_back(partial_value)
    out_assign = out_sorted[inverse].reshape(tok_rows, topk_count, model_width)
    expert_mix = jnp.einsum("tk,tkd->td", gate_values, out_assign)
    result = mixed + expert_mix
    d_result = cotangent.astype(jnp.float32)
    d_gates = jnp.einsum("tkd,td->tk", out_assign, d_result)
    d_out = (
        (gate_values[:, :, None] * d_result[:, None, :])
        .astype(jnp.bfloat16)
        .reshape(-1, model_width)[sort_order]
    )
    d_arrived = send_out(d_out)
    d_acts = jnp.einsum("secd,efd->secf", d_arrived, w_down, preferred_element_type=jnp.float32)
    sigmoid_gate = jax.nn.sigmoid(gate_pre)
    d_gate_pre = (d_acts * up_pre * sigmoid_gate * (1.0 + gate_pre * (1.0 - sigmoid_gate))).astype(
        jnp.bfloat16
    )
    d_up_pre = (d_acts * silu_gate).astype(jnp.bfloat16)
    grad_w_down = jnp.einsum("secf,secd->efd", acts, d_arrived, preferred_element_type=jnp.float32)
    grad_w_gate = jnp.einsum(
        "secd,secf->edf", expert_in, d_gate_pre, preferred_element_type=jnp.float32
    )
    grad_w_up = jnp.einsum(
        "secd,secf->edf", expert_in, d_up_pre, preferred_element_type=jnp.float32
    )
    d_rows = (
        jnp.einsum("secf,edf->secd", d_gate_pre, w_gate, preferred_element_type=jnp.float32)
        + jnp.einsum("secf,edf->secd", d_up_pre, w_up, preferred_element_type=jnp.float32)
    ).astype(jnp.bfloat16)
    d_sorted = send_back(d_rows)
    d_ffn = jnp.sum(d_sorted[inverse].reshape(tok_rows, topk_count, model_width), axis=1)
    d_probs = jnp.einsum("tk,tke->te", d_gates, expert_hot)
    d_logits = (
        router_probs * (d_probs - jnp.sum(router_probs * d_probs, axis=-1, keepdims=True))
    ).astype(jnp.bfloat16)
    router_part = contract_rows(ffn_in, d_logits)
    d_ffn = d_ffn + times_transpose(d_logits, w_router)
    ffn_gain_part = jnp.sum(d_ffn * mixed_norm, axis=0)
    d_norm_two = d_ffn * ffn_gain.astype(jnp.float32)
    d_mixed = d_result + scale_two * (
        d_norm_two - mixed_norm * jnp.mean(d_norm_two * mixed_norm, axis=-1, keepdims=True)
    )
    d_attn = d_mixed.astype(jnp.bfloat16)
    d_attn_all = lax.all_gather(d_attn, "tensor", axis=0, tiled=True)
    grad_w_out = contract_rows(o_low, d_attn_all)
    d_attended = (
        times_transpose(d_attn_all, w_out)
        .astype(jnp.bfloat16)
        .reshape(block_count, block_rows, local_heads, head_width)
    )

    def attend_back(carry, inputs):
        dk_total, dv_total = carry
        q_block, do_block, lse_block, row_start = inputs
        scores = (
            jnp.einsum("qhd,khd->hqk", q_block, k_rot, preferred_element_type=jnp.float32)
            * score_scale
        )
        allowed = allowed_mask(row_start)
        scores = jnp.where(allowed, scores, -1e30)
        soft = jnp.where(allowed, jnp.exp(scores - lse_block[..., None]), 0.0)
        d_weights = jnp.einsum("qhd,khd->hqk", do_block, v_low, preferred_element_type=jnp.float32)
        d_scores = (soft * (d_weights - jnp.sum(soft * d_weights, axis=-1, keepdims=True))).astype(
            jnp.bfloat16
        )
        dq_block = (
            jnp.einsum("hqk,khd->qhd", d_scores, k_rot, preferred_element_type=jnp.float32)
            * score_scale
        )
        dk_total = (
            dk_total
            + jnp.einsum("hqk,qhd->khd", d_scores, q_block, preferred_element_type=jnp.float32)
            * score_scale
        )
        dv_total = dv_total + jnp.einsum(
            "hqk,qhd->khd", soft.astype(jnp.bfloat16), do_block, preferred_element_type=jnp.float32
        )
        return ((dk_total, dv_total), dq_block)

    zero_field = jnp.zeros((seq_len, local_heads, head_width), jnp.float32)
    (dk_rot, dv_full), dq_blocks = lax.scan(
        attend_back, (zero_field, zero_field), (q_blocks, d_attended, lse_blocks, starts)
    )
    dq_gain = unrotate(
        dq_blocks.reshape(seq_len, local_heads, head_width), cosine, sine_table
    ).reshape(seq_len, local_width)
    dk_gain = unrotate(dk_rot, cosine, sine_table).reshape(seq_len, local_width)
    query_gain_part = jnp.sum(dq_gain * query_hat, axis=0)
    key_gain_part = jnp.sum(dk_gain * key_hat, axis=0)
    dq_hat = dq_gain * q_gain
    dk_hat = dk_gain * k_gain
    q_inner, k_inner = lax.psum(
        (jnp.sum(dq_hat * query_hat, axis=1), jnp.sum(dk_hat * key_hat, axis=1)), "tensor"
    )
    dq_raw = (q_rscale * (dq_hat - query_hat * (q_inner / model_width)[:, None])).astype(
        jnp.bfloat16
    )
    dk_raw = (k_rscale * (dk_hat - key_hat * (k_inner / model_width)[:, None])).astype(jnp.bfloat16)
    dv_raw = dv_full.reshape(seq_len, local_width).astype(jnp.bfloat16)
    grad_query = contract_rows(gathered, dq_raw)
    grad_key = contract_rows(gathered, dk_raw)
    grad_value = contract_rows(gathered, dv_raw)
    total_term = times_transpose(dq_raw, w_query)
    total_term = total_term + times_transpose(dk_raw, w_key)
    d_attn_in = lax.psum_scatter(
        (total_term + times_transpose(dv_raw, w_value)).astype(jnp.bfloat16),
        "tensor",
        scatter_dimension=0,
        tiled=True,
    ).astype(jnp.float32)
    attn_gain_part = jnp.sum(d_attn_in * normed, axis=0)
    d_norm_one = d_attn_in * attn_gain.astype(jnp.float32)
    d_input = d_mixed + scale_one * (
        d_norm_one - normed * jnp.mean(d_norm_one * normed, axis=-1, keepdims=True)
    )
    dp_sums = (
        lax.psum(grad_query.astype(jnp.bfloat16), "dp").astype(jnp.float32),
        lax.psum(grad_key.astype(jnp.bfloat16), "dp").astype(jnp.float32),
        lax.psum(grad_value.astype(jnp.bfloat16), "dp").astype(jnp.float32),
        lax.psum(query_gain_part.astype(jnp.bfloat16), "dp").astype(jnp.float32),
        lax.psum(key_gain_part.astype(jnp.bfloat16), "dp").astype(jnp.float32),
        lax.psum(grad_w_out.astype(jnp.bfloat16), "dp").astype(jnp.float32),
    )
    shared = lax.psum((attn_gain_part, ffn_gain_part, router_part), ("dp", "tensor"))
    return (
        result.astype(jnp.bfloat16),
        d_input.astype(jnp.bfloat16),
        dp_sums[0],
        dp_sums[1],
        dp_sums[2],
        dp_sums[3],
        dp_sums[4],
        dp_sums[5],
        shared[0],
        shared[1],
        shared[2],
        grad_w_gate,
        grad_w_up,
        grad_w_down,
    )


def solution(mesh):
    return jax.shard_map(
        local,
        mesh=mesh,
        in_specs=(
            P(("dp", "tensor"), None),
            P(("dp", "tensor"), None),
            P("dp"),
            P(("dp", "tensor"), None),
            P(),
            P(None, "tensor"),
            P(None, "tensor"),
            P(None, "tensor"),
            P("tensor"),
            P("tensor"),
            P("tensor", None),
            P(),
            P(),
            P("dp", None, "tensor"),
            P("dp", None, "tensor"),
            P("dp", "tensor", None),
        ),
        out_specs=(
            P(("dp", "tensor"), None),
            P(("dp", "tensor"), None),
            P(None, "tensor"),
            P(None, "tensor"),
            P(None, "tensor"),
            P("tensor"),
            P("tensor"),
            P("tensor", None),
            P(),
            P(),
            P(),
            P("dp", None, "tensor"),
            P("dp", None, "tensor"),
            P("dp", "tensor", None),
        ),
        check_vma=False,
    )
```

profile of v0, /device:TPU:0, one launch (start us, length us, event | category | flops | bytes accessed | tf_op | source)
XLA Modules:
  0.0 4005.9 jit_solution(13693268854694066916)
XLA Ops:
  15.7 34.4 all-gather.3.cloned.1.call-done
  50.1 6.2 convolution_convert_fusion.5
  57.9 6.7 multiply_reduce_fusion.6
  64.6 3.8 multiply_reduce_fusion.7
  68.4 6.4 all-reduce.2
  94.1 4.9 subtract_convert_fusion
  102.2 24.3 while.28
  110.1 3.3 fusion.192
  122.3 3.3 fusion.192
  130.0 5.7 fusion.96
  136.7 5.0 sort.34
  141.8 67.0 %reduce-scatter.3.cloned.1.call-done = f32[256,2048]{1,0:T(8,128)} async-done(((f32[1024,2048]{1,0:T(8,128)}), f32[256,2048]{1,0:T(8,128)}) %reduce-scatter.3.cloned.1.call-update) | async-done | bytes 2097168 | tf_op jit(solution)/shard_map/reduce_scatter | solution.py:173
  212.3 10.9 gather_fusion
  223.2 13.5 broadcast_in_dim.62
  236.6 4.9 all-to-all-start
  246.3 5.9 fusion.43
  252.2 20.8 gather_fusion.2
  273.0 696.3 %all-to-all-done = bf16[32,256,2048]{2,1,0:T(8,128)(2,1)} async-done(((bf16[32,256,2048]{2,1,0:T(8,128)(2,1)}), bf16[32,256,2048]{2,1,0:T(8,128)(2,1)}, u32[]{:S(2)}, u32[]{:S(2)}) %all-to-all-start) | async-done | bytes 33554464 | tf_op jit(solution)/shard_map/all_to_all | solution.py:110
  969.3 13.5 broadcast_in_dim.72
  982.8 32.3 all-to-all-start.2
  1015.1 20.6 fusion.39
  1035.7 20.5 fusion.41
  1056.2 686.7 %all-to-all-done.2 = bf16[32,256,2048]{2,1,0:T(8,128)(2,1)} async-done(((bf16[32,256,2048]{2,1,0:T(8,128)(2,1)}), bf16[32,256,2048]{2,1,0:T(8,128)(2,1)}, u32[]{:S(2)}, u32[]{:S(2)}) %all-to-all-start.2) | async-done | bytes 33554464 | tf_op jit(solution)/shard_map/all_to_all | solution.py:110
  1742.9 25.7 fusion.56
  1768.7 18.4 convert_bitcast_fusion
  1787.1 23.0 copy.60
  1810.1 32.2 all-to-all-start.1
  1842.3 27.6 fusion.50
  1869.9 36.7 fusion.34
  1906.6 22.9 copy.62
  1929.6 640.6 %all-to-all-done.1 = bf16[32,256,2048]{2,1,0:T(8,128)(2,1)} async-done(((bf16[32,256,2048]{2,1,0:T(8,128)(2,1)}), bf16[32,256,2048]{2,1,0:T(8,128)(2,1)}, u32[]{:S(2)}, u32[]{:S(2)}) %all-to-all-start.1) | async-done | bytes 33554464 | tf_op jit(solution)/shard_map/all_to_all | solution.py:114
  2570.1 32.0 all-to-all-start.3
  2602.2 5.0 sort.35
  2607.3 18.3 convert_reduce_fusion.1
  2625.6 20.9 gather_fusion.1
  2646.6 8.5 fusion.92
  2655.3 674.7 %all-to-all-done.3 = bf16[32,256,2048]{2,1,0:T(8,128)(2,1)} async-done(((bf16[32,256,2048]{2,1,0:T(8,128)(2,1)}), bf16[32,256,2048]{2,1,0:T(8,128)(2,1)}, u32[]{:S(2)}, u32[]{:S(2)}) %all-to-all-start.3) | async-done | bytes 33554464 | tf_op jit(solution)/shard_map/all_to_all | solution.py:114
  3330.0 20.3 convert_reduce_fusion
  3350.3 22.0 gather_fusion.3
  3372.3 8.2 bitcast_reduce_fusion
  3385.1 62.0 %all-gather.5.cloned.1.call-done = bf16[1024,2048]{1,0:T(8,128)(2,1)} async-done(((bf16[256,2048]{1,0:T(8,128)(2,1)}), bf16[1024,2048]{1,0:T(8,128)(2,1)}) %all-gather.5.cloned.1.call-update) | async-done | bytes 4194320 | tf_op jit(solution)/shard_map/all_gather | solution.py:243
  3447.0 6.2 convolution_convert_fusion.4
  3455.6 35.4 while.29
  3460.7 4.4 multiply_reduce_fusion.9
  3478.4 4.4 multiply_reduce_fusion.9
  3496.7 6.7 multiply_add_fusion
  3508.2 3.5 fusion.81
  3516.6 3.4 fusion.82
  3519.9 6.2 all-reduce.1
  3534.9 6.4 add_convert_fusion.1
  3541.4 22.1 convolution_bitcast_fusion
  3563.6 6.1 convolution_convert_fusion
  3569.7 3.9 convolution_convert_fusion.1
  3573.6 3.8 convolution_convert_fusion.2
  3577.3 3.8 convolution_convert_fusion.3
  3581.2 20.6 fusion.64
  3601.9 21.2 convolution_bitcast_fusion.1
  3624.2 7.2 fusion.46
  3631.4 22.5 all-reduce.3
  3657.4 5.9 fusion.76
  3663.2 201.2 %all-reduce.10.cloned.1.call-done = (bf16[2048,512]{1,0:T(8,128)(2,1)}, bf16[2048,512]{1,0:T(8,128)(2,1)}, bf16[2048,512]{1,0:T(8,128)(2,1)}, bf16[512,2048]{1,0:T(8,128)(2,1)}) async-done(((bf16[2048,512]{1,0:T(8,128)(2,1)}, bf16[2048,512]{1,0:T(8,128)(2,1)}, bf16[2048,512]{1,0:T(8,128)(2,1)}, bf16[512,2048]{1,0:T(8,128)(2,1)}), (bf16[2048,512]{1,0:T(8,128)(2,1)}, bf16[2048,512]{1,0:T(8,128)(2,1)}, ...) | async-done | bytes 8388624 | tf_op jit(solution)/shard_map/psum | solution.py:316
  3864.5 4.3 convert_element_type.189
  3876.6 39.2 all-reduce
  3915.8 81.2 %all-reduce.8.cloned.1.call-done = f32[2048,64]{0,1:T(8,128)} async-done(((f32[2048,64]{0,1:T(8,128)}), f32[2048,64]{0,1:T(8,128)}) %all-reduce.8.cloned.1.call-update) | async-done | bytes 524304 | tf_op jit(solution)/shard_map/psum | solution.py:323
  (320 shorter events, 134.3 us)
Async XLA Ops:
  7.2 57.4 %copy-start = (bf16[2048,512]{1,0:T(8,128)(2,1)S(1)}, bf16[2048,512]{1,0:T(8,128)(2,1)}, u32[]{:S(2)}) copy-start(bf16[2048,512]{1,0:T(8,128)(2,1)} %param.25) | copy-start | bytes 6291460
  7.2 5.6 copy-start.81
  7.2 5.6 copy-start.82
  7.2 42.9 %all-gather.3.cloned.1.call-start = ((), (), s32[]{:S(2)}) async-start(), calls=%async_computation.6 | async-start | bytes 5242880 | tf_op jit(solution)/shard_map/all_gather | solution.py:130
  12.7 196.0 %reduce-scatter.3.cloned.1.call-start = ((), (), s32[]{:S(2)}) async-start(), calls=%async_computation.7 | async-start | bytes 10485760 | tf_op jit(solution)/shard_map/reduce_scatter | solution.py:173
  12.8 71.7 %copy-start.61 = (f32[512]{0:T(512)}, f32[512]{0:T(512)S(1)}, u32[]{:S(2)}) copy-start(f32[512]{0:T(512)S(1)} %convert_element_type.157) | copy-start | bytes 6148
  12.9 62.0 %copy-start.59 = (f32[512]{0:T(512)}, f32[512]{0:T(512)S(1)}, u32[]{:S(2)}) copy-start(f32[512]{0:T(512)S(1)} %convert_element_type.158) | copy-start | bytes 6148
  57.9 6.7 copy-start.83
  74.9 9.6 copy-start.57
  126.5 9.2 copy-start.10
  126.5 9.2 copy-start.53
  126.5 9.2 copy-start.87
  126.6 3.5 copy-start.85
  135.8 73.0 %copy-start.14 = (bf16[256,2048]{1,0:T(8,128)(2,1)S(1)}, bf16[256,2048]{1,0:T(8,128)(2,1)}, u32[]{:S(2)}) copy-start(bf16[256,2048]{1,0:T(8,128)(2,1)} %param.20) | copy-start | bytes 3145732
  136.5 74.3 %copy-start.48 = (f32[2048]{0:T(1024)}, f32[2048]{0:T(1024)S(1)}, u32[]{:S(2)}) copy-start(f32[2048]{0:T(1024)S(1)} %convert_element_type.162) | copy-start | bytes 24580
  136.6 109.1 %copy-start.42 = (s32[256,8]{1,0:T(8,128)}, s32[256,8]{1,0:T(8,128)S(1)}, u32[]{:S(2)}) copy-start(s32[256,8]{1,0:T(8,128)S(1)} %copy.56) | copy-start | bytes 24580
  141.8 68.9 %copy-start.64 = (s32[2048]{0:T(1024)}, s32[2048]{0:T(1024)S(1)}, u32[]{:S(2)}) copy-start(s32[2048]{0:T(1024)S(1)} %get-tuple-element.129) | copy-start | bytes 24580
  212.3 32.1 copy-start.1
  236.6 732.7 %all-to-all-start = ((bf16[32,256,2048]{2,1,0:T(8,128)(2,1)}), bf16[32,256,2048]{2,1,0:T(8,128)(2,1)}, u32[]{:S(2)}, u32[]{:S(2)}) async-start(bf16[32,256,2048]{2,1,0:T(8,128)(2,1)} %bitcast.300), calls=%async_computation.1 | async-start | bytes 67108864 | tf_op jit(solution)/shard_map/all_to_all | solution.py:110
  244.9 7.3 copy-start.66
  245.5 6.7 copy-start.71
  246.2 6.0 copy-start.44
  982.8 760.1 %all-to-all-start.2 = ((bf16[32,256,2048]{2,1,0:T(8,128)(2,1)}), bf16[32,256,2048]{2,1,0:T(8,128)(2,1)}, u32[]{:S(2)}, u32[]{:S(2)}) async-start(bf16[32,256,2048]{2,1,0:T(8,128)(2,1)} %bitcast.301), calls=%async_computation.3 | async-start | bytes 67108864 | tf_op jit(solution)/shard_map/all_to_all | solution.py:110
  1810.1 760.1 %all-to-all-start.1 = ((bf16[32,256,2048]{2,1,0:T(8,128)(2,1)}), bf16[32,256,2048]{2,1,0:T(8,128)(2,1)}, u32[]{:S(2)}, u32[]{:S(2)}) async-start(bf16[32,256,2048]{2,1,0:T(8,128)(2,1)} %bitcast.303), calls=%async_computation.2 | async-start | bytes 67108864 | tf_op jit(solution)/shard_map/all_to_all | solution.py:114
  2570.1 32.1 copy-start.65
  2570.1 759.8 %all-to-all-start.3 = ((bf16[32,256,2048]{2,1,0:T(8,128)(2,1)}), bf16[32,256,2048]{2,1,0:T(8,128)(2,1)}, u32[]{:S(2)}, u32[]{:S(2)}) async-start(bf16[32,256,2048]{2,1,0:T(8,128)(2,1)} %bitcast.302), calls=%async_computation.4 | async-start | bytes 67108864 | tf_op jit(solution)/shard_map/all_to_all | solution.py:114
  2602.2 844.9 %all-gather.5.cloned.1.call-start = ((), (), s32[]{:S(2)}) async-start(), calls=%async_computation.8 | async-start | bytes 5242880 | tf_op jit(solution)/shard_map/all_gather | solution.py:243
  2625.6 20.9 copy-start.19
  2625.6 20.9 copy-start.43
  2646.5 8.6 copy-start.31
  2646.5 8.6 copy-start.67
  2646.6 8.6 copy-start.72
  2655.3 725.3 %copy-start.46 = (bf16[256,64]{0,1:T(8,128)(2,1)}, bf16[256,64]{0,1:T(8,128)(2,1)S(1)}, u32[]{:S(2)}) copy-start(bf16[256,64]{0,1:T(8,128)(2,1)S(1)} %fusion.108) | copy-start | bytes 98308
  3372.3 8.2 copy-start.8
  3372.3 8.2 copy-start.41
  3372.3 8.3 copy-start.49
  3372.3 8.3 copy-start.69
  3385.0 270.1 %reduce-scatter.5.cloned.1.call-start = ((), (), s32[]{:S(2)}) async-start(), calls=%async_computation.9 | async-start | bytes 5242880 | tf_op jit(solution)/shard_map/reduce_scatter | solution.py:304
  3493.7 3.0 copy-start.24
  3493.7 3.0 copy-start.25
  3505.3 2.9 copy-start.60
  3508.2 3.5 copy-start.22
  3508.2 3.5 copy-start.23
  3513.7 2.9 copy-start.62
  3526.2 3.5 copy-start.18
  3541.4 22.2 copy-start.37
  3541.4 323.1 %all-reduce.10.cloned.1.call-start = ((), (), s32[]{:S(2)}) async-start(), calls=%async_computation.11 | async-start | bytes 16777216 | tf_op jit(solution)/shard_map/psum | solution.py:316
  3563.5 6.2 copy-start.26
  3563.5 6.1 copy-start.84
  3569.7 3.9 copy-start.35
  3573.6 3.8 copy-start.33
  3581.2 415.8 %all-reduce.8.cloned.1.call-start = ((), (), s32[]{:S(2)}) async-start(), calls=%async_computation.10 | async-start | bytes 1048576 | tf_op jit(solution)/shard_map/psum | solution.py:323
  3601.9 21.2 copy-start.2
  3601.9 21.2 copy-start.47
  3601.9 22.3 copy-start.45
  3624.1 7.2 copy-start.78
  3624.1 7.2 copy-start.79
  3624.1 30.9 copy-start.15
  3624.1 30.9 copy-start.52
  3624.1 30.9 copy-start.74
  3631.3 26.0 copy-start.50
  3631.3 26.0 copy-start.70
  3631.3 26.0 copy-start.76
  3864.5 4.4 copy-start.29
  (45 other events, 78.0 us)
Sparse Core Ops, SparseCore 0:
  12.9 37.1 all-gather.2
  135.9 72.7 reduce-scatter.2
  3385.1 61.8 all-gather.4
  3541.5 45.5 reduce-scatter.4
  3591.5 272.8 all-reduce.9
  3870.2 126.7 all-reduce.7
where the time goes:
time: 4010 us
  waiting for transfers between devices  3140 us (78%)
  matrix products  322 us (8%)
  local copies, waits for them, and re-layouts  202 us (5%)
  other arithmetic  146 us (4%)
  starting transfers between devices  102 us (3%)
  blocking collectives  74.4 us (2%)
    all_to_all x2, waiting for transfers between devices, send_out(): lax.all_to_all(copies, ('dp', 'tensor'), split_axis=0, concat_axis=0, til...  1380 us
    all_to_all x2, waiting for transfers between devices, send_back(): lax.all_to_all(parts_low.reshape(device_total, per_group, model_width), (...  1320 us
    psum x1, waiting for transfers between devices, local(): lax.psum(grad_query.astype(jnp.bfloat16), 'dp').astype(jnp.float32)  201 us
    psum x1, waiting for transfers between devices, local(): lax.psum((attn_gain_part, ffn_gain_part, router_part), ('dp', 'tensor'))  81.2 us
  transfers between devices with their start and end apart: 10, of which 9 were waited for; matrix products, arithmetic and copies ran while one was open for 8% of the time, Pallas kernels for 0%

commit v1 on v0

v1 whole, which is shorter than its diff:
```python
import functools
import math

import jax
import jax.numpy as jnp
from jax import lax
from jax.experimental import pallas as pl
from jax.experimental.pallas import tpu as pltpu
from jax.sharding import PartitionSpec as P

HDIM = 128
EPS = 1e-05
ROPE_BASE = 10000.0
BOTH = ("dp", "tensor")
F32 = jnp.float32
BF16 = jnp.bfloat16
fence = lax.optimization_barrier


def rms_scale(values):
    return lax.rsqrt(jnp.mean(values * values, axis=-1, keepdims=True) + EPS)


def rope_tables(count, head_width):
    half_width = head_width // 2
    frequency = jnp.exp(
        -(jnp.arange(half_width, dtype=F32) * 2.0 / head_width) * math.log(ROPE_BASE)
    )
    angles = jnp.arange(count, dtype=F32)[:, None] * frequency[None, :]
    return (jnp.cos(angles), jnp.sin(angles))


def rotate(values_in, cosine, sine_table):
    half_width = values_in.shape[-1] // 2
    front_half = values_in[..., :half_width]
    back_half = values_in[..., half_width:]
    return jnp.concatenate(
        [
            front_half * cosine - back_half * sine_table,
            back_half * cosine + front_half * sine_table,
        ],
        axis=-1,
    )


def unrotate(grads_in, cosine, sine_table):
    return rotate(grads_in, cosine, -sine_table)


def contract_rows(left, right):
    return lax.dot_general(left, right, (((0,), (0,)), ((), ())), preferred_element_type=F32)


def times_transpose(left, right):
    return lax.dot_general(left, right, (((1,), (1,)), ((), ())), preferred_element_type=F32)


def add_low(*terms):
    total = terms[0].astype(F32)
    for term in terms[1:]:
        total = total + term.astype(F32)
    return total.astype(BF16)


def add_wide(*terms):
    total = terms[0].astype(F32)
    for term in terms[1:]:
        total = total + term.astype(F32)
    return total


def swap_tensor(value, bit):
    count = lax.axis_size("tensor")
    return lax.ppermute(value, "tensor", [(s, s ^ bit) for s in range(count)])


def tensor_gather(block):
    across = swap_tensor(block, 2)
    mate = swap_tensor(block, 1)
    return [block, mate, across, swap_tensor(across, 1)]


def tensor_scatter(blocks):
    across = add_low(blocks[2], swap_tensor(blocks[3], 1))
    here = add_wide(blocks[0], swap_tensor(blocks[1], 1))
    return here + swap_tensor(across, 2).astype(F32)


CHUNKS = (
    ((0, 0, 0, 0), (1, 0, 0, 0), (0, 1, 0, 0), (0, 0, 1, 0), (0, 0, 0, 1), (0, 1, 0, 1), (0, 0, 1, 1), (2, 0, 0, 0)),
    ((1, 1, 0, 0), (1, 0, 1, 0), (1, 0, 0, 1), (1, 1, 0, 1), (1, 0, 1, 1), (3, 0, 0, 0), (2, 1, 0, 0), (2, 0, 1, 0)),
    ((2, 0, 0, 1), (2, 1, 0, 1), (2, 0, 1, 1), (3, 1, 0, 0), (3, 0, 1, 0), (3, 0, 0, 1), (3, 1, 0, 1), (3, 0, 1, 1)),
    ((0, 1, 1, 0), (2, 1, 1, 0), (0, 1, 1, 1), (2, 1, 1, 1), (1, 1, 1, 0), (3, 1, 1, 0), (1, 1, 1, 1), (3, 1, 1, 1)),
)
PLACES = tuple(place for chunk in CHUNKS for place in chunk)
RING = 4


def device_pairs(move):
    pairs = []
    for z in range(RING):
        for x in range(2):
            for y in range(2):
                for c in range(2):
                    tz, tx, ty, tc = move(z, x, y, c)
                    pairs.append(((z * 2 + x) * 4 + y * 2 + c, (tz * 2 + tx) * 4 + ty * 2 + tc))
    return pairs


def send_x(value):
    return lax.ppermute(value, BOTH, device_pairs(lambda z, x, y, c: (z, x ^ 1, y, c)))


def send_y(value):
    return lax.ppermute(value, BOTH, device_pairs(lambda z, x, y, c: (z, x, y ^ 1, c)))


def send_c(value):
    return lax.ppermute(value, BOTH, device_pairs(lambda z, x, y, c: (z, x, y, c ^ 1)))


def send_z(value):
    return lax.ppermute(value, BOTH, device_pairs(lambda z, x, y, c: ((z - 1) % RING, x, y, c)))


def gather_everywhere(block):
    out = {(0, 0, 0, 0): block}

    def cross(*places):
        for k, dx, dy in places:
            out[k, dx, dy, 1] = send_c(out[k, dx, dy, 0])

    col_1, x_0, y_0 = fence((send_z(block), send_x(block), send_y(block)))
    out[1, 0, 0, 0], out[0, 1, 0, 0], out[0, 0, 1, 0] = col_1, x_0, y_0
    cross((0, 0, 0), (0, 1, 0), (0, 0, 1))
    col_2, x_1, y_1 = fence((send_z(col_1), send_x(col_1), send_y(col_1)))
    out[2, 0, 0, 0], out[1, 1, 0, 0], out[1, 0, 1, 0] = col_2, x_1, y_1
    cross((1, 0, 0), (1, 1, 0), (1, 0, 1))
    col_3, x_2, y_2 = fence((send_z(col_2), send_x(col_2), send_y(col_2)))
    out[3, 0, 0, 0], out[2, 1, 0, 0], out[2, 0, 1, 0] = col_3, x_2, y_2
    cross((2, 0, 0), (2, 1, 0), (2, 0, 1))
    x_3, y_3, x_0, y_2 = fence((send_x(col_3), send_y(col_3), x_0, y_2))
    out[3, 1, 0, 0], out[3, 0, 1, 0] = x_3, y_3
    cross((3, 0, 0), (3, 1, 0), (3, 0, 1))
    d_0, d_2, x_1, y_3 = fence((send_y(x_0), send_x(y_2), x_1, y_3))
    out[0, 1, 1, 0], out[2, 1, 1, 0] = d_0, d_2
    cross((0, 1, 1), (2, 1, 1))
    out[1, 1, 1, 0], out[3, 1, 1, 0] = send_y(x_1), send_x(y_3)
    cross((1, 1, 1), (3, 1, 1))
    return out


def scatter_everywhere(parts):
    held = {}
    for dx, dy in ((1, 1), (0, 1), (1, 0), (0, 0)):
        for k in (1, 2, 3, 0):
            held[k, dx, dy] = add_low(parts[k, dx, dy, 0], send_c(parts[k, dx, dy, 1]))
    by_x, by_y = fence((send_x(held[1, 1, 1]), send_y(held[2, 1, 1])))
    held[1, 0, 1] = add_low(held[1, 0, 1], by_x)
    held[2, 1, 0] = add_low(held[2, 1, 0], by_y)
    third, zeroth, _ = fence((held[3, 1, 1], held[0, 1, 1], by_x))
    by_x, by_y = fence((send_x(third), send_y(zeroth)))
    held[3, 0, 1] = add_low(held[3, 0, 1], by_x)
    held[0, 1, 0] = add_low(held[0, 1, 0], by_y)
    last, total = by_x, None
    for k in (1, 2, 3, 0):
        for_x, for_y, _ = fence((held[k, 1, 0], held[k, 0, 1], last))
        if total is None:
            by_x, by_y = fence((send_x(for_x), send_y(for_y)))
            total = add_low(held[k, 0, 0], by_x, by_y)
        else:
            by_x, by_y, by_z = fence((send_x(for_x), send_y(for_y), send_z(total)))
            total = (add_low if k else add_wide)(held[k, 0, 0], by_x, by_y, by_z)
        last = by_x
    return total


def place_indices():
    group, member = lax.axis_index("dp"), lax.axis_index("tensor")
    z, x, y, c = group // 2, group % 2, member // 2, member % 2
    absolute = jnp.stack(
        [(((z + k) % RING) * 2 + (x ^ dx)) * 4 + (y ^ dy) * 2 + (c ^ dc) for k, dx, dy, dc in PLACES]
    )
    table = [0] * len(PLACES)
    for position, (k, dx, dy, dc) in enumerate(PLACES):
        table[((k * 2 + dx) * 2 + dy) * 2 + dc] = position
    numbers = jnp.arange(len(PLACES))
    other_z, other_x = numbers // 8, (numbers // 4) % 2
    other_y, other_c = (numbers // 2) % 2, numbers % 2
    offset = ((((other_z - z) % RING) * 2 + (other_x ^ x)) * 2 + (other_y ^ y)) * 2 + (other_c ^ c)
    return absolute, jnp.asarray(table, jnp.int32)[offset]


def nn(left, right):
    return lax.dot_general(left, right, (((1,), (0,)), ((), ())), preferred_element_type=F32)


def nt(left, right):
    return lax.dot_general(left, right, (((1,), (1,)), ((), ())), preferred_element_type=F32)


def pick_rows(picks_ref, blocks, rows_ref, slot_count, width):
    experts = rows_ref.shape[0]
    for b, block in enumerate(blocks):
        for low in range(0, block.shape[1], width):
            columns = pl.ds(low, width)
            picked = nn(picks_ref[b], block[:, columns]).astype(BF16)
            for e in range(experts):
                rows_ref[e, pl.ds(b * slot_count, slot_count), columns] = picked[
                    e * slot_count : (e + 1) * slot_count
                ]


def give_rows(gives_ref, rows_ref, blocks, slot_count, width):
    experts = rows_ref.shape[0]
    for b, block in enumerate(blocks):
        for low in range(0, block.shape[1], width):
            columns = pl.ds(low, width)
            slots = jnp.concatenate(
                [rows_ref[e, pl.ds(b * slot_count, slot_count), columns] for e in range(experts)], axis=0
            )
            block[:, columns] = nn(gives_ref[b], slots).astype(BF16)


def cot_kernel(count, slot_count, picks_ref, down_ref, *refs):
    blocks, (rows_out, acts_out, rows_ref) = refs[:count], refs[count:]
    e = pl.program_id(0)

    @pl.when(e == 0)
    def _():
        pick_rows(picks_ref, blocks, rows_ref, slot_count, 512)

    rows = rows_ref[e]
    rows_out[0] = rows
    acts_out[0] = nt(rows, down_ref[0])


def main_kernel(count, slot_count, picks_ref, gives_ref, acts_ref, gates_ref, gate_ref, up_ref, *refs):
    blocks = refs[:count]
    rows_out, scaled_out, d_gate_out, d_up_out, inner_out = refs[count : count + 5]
    results = refs[count + 5 : 2 * count + 5]
    rows_ref = refs[2 * count + 5]
    e = pl.program_id(0)

    @pl.when(e == 0)
    def _():
        pick_rows(picks_ref, blocks, rows_ref, slot_count, 512)

    rows = rows_ref[e]
    rows_out[0] = rows
    pre, up = nn(rows, gate_ref[0]), nn(rows, up_ref[0])
    cot_acts = acts_ref[0]
    gate = jnp.concatenate([gates_ref[0]] * (pre.shape[1] // gates_ref.shape[2]), axis=1)
    sig = jax.nn.sigmoid(pre)
    silu = pre * sig
    acts = silu * up
    scaled_out[0] = (gate * acts).astype(BF16)
    inner = acts.astype(BF16).astype(F32) * cot_acts
    half = inner.shape[1] // 2
    inner_out[0] = inner[:, :half] + inner[:, half:]
    d_acts = gate * cot_acts
    d_pre = (d_acts * up * sig * (1.0 + pre * (1.0 - sig))).astype(BF16)
    d_up = (d_acts * silu).astype(BF16)
    d_gate_out[0] = d_pre
    d_up_out[0] = d_up
    rows_ref[e] = (nt(d_pre, gate_ref[0]) + nt(d_up, up_ref[0])).astype(BF16)

    @pl.when(e == pl.num_programs(0) - 1)
    def _():
        give_rows(gives_ref, rows_ref, results, slot_count, 512)


def out_kernel(count, slot_count, gives_ref, scaled_ref, down_ref, *refs):
    results, rows_ref = refs[:count], refs[count]
    e = pl.program_id(0)
    rows_ref[e] = nn(scaled_ref[0], down_ref[0]).astype(BF16)

    @pl.when(e == pl.num_programs(0) - 1)
    def _():
        give_rows(gives_ref, rows_ref, results, slot_count, 512)


def per_expert(*shape):
    return pl.BlockSpec((1,) + shape, lambda e: (e,) + (0,) * len(shape))


def resident(*shape):
    return pl.BlockSpec(shape, lambda e: (0,) * len(shape), pipeline_mode=pl.Buffered(1))


def cot_chunk(picks, w_down, blocks, slot_count):
    experts, hidden, width = w_down.shape
    count, tokens = len(blocks), blocks[0].shape[0]
    rows = count * slot_count
    return pl.pallas_call(
        functools.partial(cot_kernel, count, slot_count),
        grid=(experts,),
        in_specs=[resident(*picks.shape), per_expert(hidden, width)] + [resident(tokens, width)] * count,
        out_specs=[per_expert(rows, width), per_expert(rows, hidden)],
        out_shape=[
            jax.ShapeDtypeStruct((experts, rows, width), BF16),
            jax.ShapeDtypeStruct((experts, rows, hidden), F32),
        ],
        scratch_shapes=[pltpu.VMEM((experts, rows, width), BF16)],
        compiler_params=pltpu.CompilerParams(vmem_limit_bytes=40 << 20),
        cost_estimate=pl.CostEstimate(
            flops=2 * experts * rows * width * (hidden + tokens),
            bytes_accessed=2 * (count * tokens * width + experts * (rows + hidden) * width),
            transcendentals=0,
        ),
    )(picks, w_down, *blocks)


def main_chunk(picks, gives, cot_acts, gates, w_gate, w_up, blocks, slot_count):
    experts, width, hidden = w_gate.shape
    count, tokens = len(blocks), blocks[0].shape[0]
    rows = count * slot_count
    lanes = gates.shape[-1]
    outs = pl.pallas_call(
        functools.partial(main_kernel, count, slot_count),
        grid=(experts,),
        in_specs=[
            resident(*picks.shape),
            resident(*gives.shape),
            per_expert(rows, hidden),
            per_expert(rows, lanes),
            per_expert(width, hidden),
            per_expert(width, hidden),
        ]
        + [resident(tokens, width)] * count,
        out_specs=[
            per_expert(rows, width),
            per_expert(rows, hidden),
            per_expert(rows, hidden),
            per_expert(rows, hidden),
            per_expert(rows, hidden // 2),
        ]
        + [resident(tokens, width)] * count,
        out_shape=[
            jax.ShapeDtypeStruct((experts, rows, width), BF16),
            jax.ShapeDtypeStruct((experts, rows, hidden), BF16),
            jax.ShapeDtypeStruct((experts, rows, hidden), BF16),
            jax.ShapeDtypeStruct((experts, rows, hidden), BF16),
            jax.ShapeDtypeStruct((experts, rows, hidden // 2), F32),
        ]
        + [jax.ShapeDtypeStruct((tokens, width), BF16)] * count,
        scratch_shapes=[pltpu.VMEM((experts, rows, width), BF16)],
        compiler_params=pltpu.CompilerParams(vmem_limit_bytes=50 << 20),
        cost_estimate=pl.CostEstimate(
            flops=2 * experts * rows * width * (4 * hidden + 2 * tokens),
            bytes_accessed=2 * (2 * count * tokens * width + experts * (rows + 2 * hidden) * width),
            transcendentals=experts * rows * hidden,
        ),
    )(picks, gives, cot_acts, gates, w_gate, w_up, *blocks)
    return outs[:5], outs[5:]


def out_chunk(gives, scaled, w_down, slot_count):
    experts, hidden, width = w_down.shape
    count, tokens = gives.shape[:2]
    rows = count * slot_count
    return pl.pallas_call(
        functools.partial(out_kernel, count, slot_count),
        grid=(experts,),
        in_specs=[resident(*gives.shape), per_expert(rows, hidden), per_expert(hidden, width)],
        out_specs=[resident(tokens, width)] * count,
        out_shape=[jax.ShapeDtypeStruct((tokens, width), BF16)] * count,
        scratch_shapes=[pltpu.VMEM((experts, rows, width), BF16)],
        compiler_params=pltpu.CompilerParams(vmem_limit_bytes=40 << 20),
        cost_estimate=pl.CostEstimate(
            flops=2 * experts * rows * width * (hidden + tokens),
            bytes_accessed=2 * (count * tokens * width + experts * (rows + hidden) * width),
            transcendentals=0,
        ),
    )(gives, scaled, w_down)


def grad_kernel(count, *refs):
    rows, cots, scaled, d_gate, d_up = (refs[i * count : (i + 1) * count] for i in range(5))
    gate_out, up_out, down_out = refs[5 * count :]

    def total(lefts, rights):
        value = None
        for left, right in zip(lefts, rights):
            term = contract_rows(left[0], right[0])
            value = term if value is None else value + term
        return value

    gate_out[0] = total(rows, d_gate)
    up_out[0] = total(rows, d_up)
    down_out[0] = total(scaled, cots)


def expert_grads(rows, cots, scaled, d_gate, d_up):
    count = len(rows)
    experts, slots, width = rows[0].shape
    hidden = scaled[0].shape[2]
    tile = 512

    def wide(e, n):
        return (e, 0, n)

    def narrow(e, n):
        return (e, 0, 0)

    wide_spec = pl.BlockSpec((1, slots, tile), wide)
    narrow_spec = pl.BlockSpec((1, slots, hidden), narrow)
    return pl.pallas_call(
        functools.partial(grad_kernel, count),
        grid=(experts, width // tile),
        in_specs=[wide_spec] * (2 * count) + [narrow_spec] * (3 * count),
        out_specs=[
            pl.BlockSpec((1, tile, hidden), lambda e, n: (e, n, 0)),
            pl.BlockSpec((1, tile, hidden), lambda e, n: (e, n, 0)),
            pl.BlockSpec((1, hidden, tile), lambda e, n: (e, 0, n)),
        ],
        out_shape=[
            jax.ShapeDtypeStruct((experts, width, hidden), F32),
            jax.ShapeDtypeStruct((experts, width, hidden), F32),
            jax.ShapeDtypeStruct((experts, hidden, width), F32),
        ],
        compiler_params=pltpu.CompilerParams(vmem_limit_bytes=40 << 20),
        cost_estimate=pl.CostEstimate(
            flops=6 * experts * count * slots * width * hidden,
            bytes_accessed=4 * experts * count * slots * width + 12 * experts * width * hidden,
            transcendentals=0,
        ),
    )(*rows, *cots, *scaled, *d_gate, *d_up)


class GatheredExperts:
    def __init__(self, expert_ids, cotangent, w_gate, w_up, w_down, expert_total):
        tok_rows, self.topk = expert_ids.shape
        self.tok_rows = tok_rows
        self.w_gate, self.w_up, self.w_down = w_gate, w_up, w_down
        self.experts = w_gate.shape[0]
        self.slot_count = tok_rows * self.topk // expert_total
        self.absolute, self.position = place_indices()
        devices = len(PLACES)
        ids = lax.all_gather(expert_ids.T, BOTH, axis=0, tiled=False)[self.absolute]
        first = lax.axis_index("dp") * self.experts
        wanted = first + jnp.arange(self.experts)
        self.match = ids[:, None, :, :] == wanted[None, :, None, None]
        hot = jnp.any(self.match, axis=2)
        earlier = jnp.triu(jnp.ones((tok_rows, tok_rows), F32), 1).astype(BF16)
        rank = jnp.einsum("pet,tu->peu", hot.astype(BF16), earlier, preferred_element_type=F32)
        slot_of = jnp.where(hot, rank, -1.0)
        slots = jnp.arange(self.slot_count, dtype=F32)
        picks = (slot_of[:, :, None, :] == slots[None, None, :, None]).astype(BF16)
        self.picks = picks.reshape(devices, self.experts * self.slot_count, tok_rows)
        slot_turned = slot_of.transpose(0, 2, 1)
        gives = (slot_turned[:, :, :, None] == slots[None, None, None, :]).astype(BF16)
        self.gives = gives.reshape(devices, tok_rows, self.experts * self.slot_count)
        cot_blocks = gather_everywhere(cotangent)
        self.cots = [
            cot_chunk(self.part(self.picks, i), w_down, [cot_blocks[p] for p in chunk], self.slot_count)
            for i, chunk in enumerate(CHUNKS)
        ]

    def part(self, array, i):
        size = len(CHUNKS[i])
        return array[i * size : (i + 1) * size]

    def run(self, ffn_in, gate_values):
        devices, slots = len(PLACES), self.slot_count
        gates = lax.all_gather(gate_values.T, BOTH, axis=0, tiled=False)[self.absolute]
        token_gates = jnp.sum(jnp.where(self.match, gates[:, None, :, :], 0.0), axis=2)
        picks = self.picks.reshape(devices, self.experts, slots, self.tok_rows)
        slot_gates = jnp.sum(picks.astype(F32) * token_gates[:, :, None, :], axis=3)
        slot_gates = slot_gates.transpose(1, 0, 2).reshape(self.experts, devices * slots, 1)
        slot_gates = jnp.broadcast_to(slot_gates, (self.experts, devices * slots, 128))
        blocks = gather_everywhere(ffn_in)
        kept, d_parts = [], {}
        for i, chunk in enumerate(CHUNKS):
            size = len(chunk) * slots
            saved, results = main_chunk(
                self.part(self.picks, i),
                self.part(self.gives, i),
                self.cots[i][1],
                slot_gates[:, i * size : (i + 1) * size],
                self.w_gate,
                self.w_up,
                [blocks[p] for p in chunk],
                slots,
            )
            kept.append(saved)
            d_parts.update(zip(chunk, results))
        d_ffn = scatter_everywhere(d_parts)
        inner = jnp.concatenate([jnp.sum(saved[4], axis=-1) for saved in kept], axis=1)
        inner = inner.reshape(self.experts, devices, slots).transpose(1, 0, 2)
        d_probs = jnp.sum(picks.astype(F32) * inner[:, :, :, None], axis=2)
        d_probs = d_probs[self.position]
        arrived = lax.all_to_all(d_probs, BOTH, split_axis=0, concat_axis=0, tiled=True)
        tensor_count = lax.axis_size("tensor")
        d_probs = jnp.sum(
            arrived.reshape(-1, tensor_count, self.experts, self.tok_rows), axis=1
        ).reshape(-1, self.tok_rows).T
        self.kept = kept
        return d_ffn, d_probs

    def output(self, after):
        parts = {}
        for i, chunk in enumerate(CHUNKS):
            results = out_chunk(self.part(self.gives, i), self.kept[i][1], self.w_down, self.slot_count)
            parts.update(zip(chunk, results))
        held, _ = fence((parts, after))
        return scatter_everywhere(held)

    def grads(self):
        rows, scaled, d_gate, d_up, _ = zip(*self.kept)
        return expert_grads(rows, [cot[0] for cot in self.cots], scaled, d_gate, d_up)


class SentExperts:
    def __init__(self, expert_ids, cotangent, w_gate, w_up, w_down, expert_total):
        self.ids, self.cotangent = expert_ids, cotangent
        self.w_gate, self.w_up, self.w_down = w_gate, w_up, w_down
        self.expert_total = expert_total
        self.groups, self.members = lax.axis_size("dp"), lax.axis_size("tensor")
        self.experts = w_gate.shape[0]
        self.slot_count = expert_ids.size // expert_total

    def send_out(self, rows):
        width = rows.shape[1]
        per_group = self.experts * self.slot_count
        copies = jnp.broadcast_to(
            rows.reshape(self.groups, 1, per_group, width), (self.groups, self.members, per_group, width)
        ).reshape(-1, per_group, width)
        arrived = lax.all_to_all(copies, BOTH, split_axis=0, concat_axis=0, tiled=True)
        return arrived.reshape(-1, self.experts, self.slot_count, width)

    def send_back(self, parts):
        width = parts.shape[-1]
        per_group = self.experts * self.slot_count
        returned = lax.all_to_all(
            parts.reshape(-1, per_group, width), BOTH, split_axis=0, concat_axis=0, tiled=True
        )
        returned = returned.reshape(self.groups, self.members, per_group, width)
        return jnp.sum(returned.astype(F32), axis=1).reshape(-1, width)

    def run(self, ffn_in, gate_values):
        tok_rows, topk = self.ids.shape
        width = ffn_in.shape[1]
        order = jnp.argsort(self.ids.reshape(-1), stable=True)
        inverse = jnp.argsort(order)
        wide = dict(preferred_element_type=F32)
        rows = self.send_out(ffn_in[order // topk])
        pre = jnp.einsum("secd,edf->secf", rows, self.w_gate, **wide)
        up = jnp.einsum("secd,edf->secf", rows, self.w_up, **wide)
        sig = jax.nn.sigmoid(pre)
        silu = pre * sig
        acts = (silu * up).astype(BF16)
        part = jnp.einsum("secf,efd->secd", acts, self.w_down, **wide).astype(BF16)
        choice_out = self.send_back(part)[inverse].reshape(tok_rows, topk, width)
        self.mix = jnp.sum(gate_values[:, :, None] * choice_out, axis=1)
        d_result = self.cotangent.astype(F32)
        d_gates = jnp.sum(choice_out * d_result[:, None, :], axis=2)
        d_out = (gate_values[:, :, None] * d_result[:, None, :]).astype(BF16)
        d_out = self.send_out(d_out.reshape(-1, width)[order])
        d_acts = jnp.einsum("secd,efd->secf", d_out, self.w_down, **wide)
        d_pre = (d_acts * up * sig * (1.0 + pre * (1.0 - sig))).astype(BF16)
        d_up = (d_acts * silu).astype(BF16)
        self.weight_grads = (
            jnp.einsum("secd,secf->edf", rows, d_pre, **wide),
            jnp.einsum("secd,secf->edf", rows, d_up, **wide),
            jnp.einsum("secf,secd->efd", acts, d_out, **wide),
        )
        d_rows = jnp.einsum("secf,edf->secd", d_pre, self.w_gate, **wide) + jnp.einsum(
            "secf,edf->secd", d_up, self.w_up, **wide
        )
        d_sorted = self.send_back(d_rows.astype(BF16))
        d_ffn = jnp.sum(d_sorted[inverse].reshape(tok_rows, topk, width), axis=1)
        hot = self.ids[:, :, None] == jnp.arange(self.expert_total)[None, None, :]
        d_probs = jnp.sum(jnp.where(hot, d_gates[:, :, None], 0.0), axis=1)
        return d_ffn, d_probs

    def output(self, after):
        return self.mix

    def grads(self):
        return self.weight_grads


def local(
    hidden_in,
    cotangent,
    seq_lengths,
    expert_ids,
    attn_gain,
    w_query,
    w_key,
    w_value,
    query_gain,
    key_gain,
    w_out,
    ffn_gain,
    w_router,
    w_gate,
    w_up,
    w_down,
):
    tensor_count = lax.axis_size("tensor")
    group_count = lax.axis_size("dp")
    tok_rows, model_width = hidden_in.shape
    expert_total = w_router.shape[1]
    seq_len = tok_rows * tensor_count
    local_width = w_query.shape[1]
    head_width = HDIM
    local_heads = local_width // head_width
    block_rows = min(512, seq_len)
    block_count = seq_len // block_rows
    score_scale = head_width ** (-0.5)
    live_length = seq_lengths[0]
    gathered_plan = (group_count, tensor_count) == (2 * RING, 4)
    experts_kind = GatheredExperts if gathered_plan else SentExperts

    member = lax.axis_index("tensor")
    blocks_at = member ^ jnp.arange(tensor_count)
    cosine, sine_table = rope_tables(seq_len, head_width)
    half_width = head_width // 2
    cosine = cosine.reshape(tensor_count, tok_rows, half_width)[blocks_at].reshape(seq_len, 1, half_width)
    sine_table = sine_table.reshape(tensor_count, tok_rows, half_width)[blocks_at].reshape(
        seq_len, 1, half_width
    )
    positions = (blocks_at[:, None] * tok_rows + jnp.arange(tok_rows)[None, :]).reshape(-1)
    key_live = positions < live_length

    resid = hidden_in.astype(F32)
    scale_one = rms_scale(resid)
    normed = resid * scale_one
    attn_in = (normed * attn_gain.astype(F32)).astype(BF16)
    gathered = jnp.concatenate(tensor_gather(attn_in), axis=0)
    q_raw = jnp.dot(gathered, w_query, preferred_element_type=F32)
    k_raw = jnp.dot(gathered, w_key, preferred_element_type=F32)
    v_raw = jnp.dot(gathered, w_value, preferred_element_type=F32)
    experts = experts_kind(expert_ids, cotangent, w_gate, w_up, w_down, expert_total)

    def token_sums(*values):
        stacked = jnp.stack([jnp.sum(value, axis=1).reshape(tensor_count, tok_rows) for value in values])
        summed = lax.psum(stacked[:, blocks_at], "tensor")
        return summed[:, blocks_at].reshape(len(values), seq_len)

    q_square, k_square = token_sums(q_raw * q_raw, k_raw * k_raw)
    q_rscale = lax.rsqrt(q_square / model_width + EPS)[:, None]
    k_rscale = lax.rsqrt(k_square / model_width + EPS)[:, None]
    query_hat = q_raw * q_rscale
    key_hat = k_raw * k_rscale
    q_gain = query_gain.astype(F32)
    k_gain = key_gain.astype(F32)
    q_rot = rotate(
        (query_hat * q_gain).reshape(seq_len, local_heads, head_width), cosine, sine_table
    ).astype(BF16)
    k_rot = rotate(
        (key_hat * k_gain).reshape(seq_len, local_heads, head_width), cosine, sine_table
    ).astype(BF16)
    v_low = v_raw.astype(BF16).reshape(seq_len, local_heads, head_width)
    q_blocks = q_rot.reshape(block_count, block_rows, local_heads, head_width)
    q_positions = positions.reshape(block_count, block_rows)

    def allowed_mask(q_pos):
        return ((positions[None, :] <= q_pos[:, None]) & key_live[None, :])[None]

    def attend(inputs):
        q_block, q_pos = inputs
        scores = jnp.einsum("qhd,khd->hqk", q_block, k_rot, preferred_element_type=F32) * score_scale
        scores = jnp.where(allowed_mask(q_pos), scores, -1e30)
        row_max = jnp.max(scores, axis=-1, keepdims=True)
        exp_scores = jnp.exp(scores - row_max)
        row_total = jnp.sum(exp_scores, axis=-1, keepdims=True)
        soft_low = (exp_scores / row_total).astype(BF16)
        attended = jnp.einsum("hqk,khd->qhd", soft_low, v_low, preferred_element_type=F32)
        return (attended, (row_max + jnp.log(row_total))[..., 0])

    o_blocks, lse_blocks = lax.map(attend, (q_blocks, q_positions))
    o_low = o_blocks.reshape(seq_len, local_width).astype(BF16)
    projected = jnp.dot(o_low, w_out, preferred_element_type=F32).astype(BF16)
    attn_rows = tensor_scatter(jnp.split(projected, tensor_count, axis=0))
    mixed = resid + attn_rows
    scale_two = rms_scale(mixed)
    mixed_norm = mixed * scale_two
    ffn_in = (mixed_norm * ffn_gain.astype(F32)).astype(BF16)
    logits = jnp.dot(ffn_in, w_router, preferred_element_type=F32)
    router_probs = jax.nn.softmax(logits, axis=-1)
    gate_values = jnp.take_along_axis(router_probs, expert_ids, axis=1)
    d_ffn, d_probs = experts.run(ffn_in, gate_values)
    d_result = cotangent.astype(F32)
    d_logits = (
        router_probs * (d_probs - jnp.sum(router_probs * d_probs, axis=-1, keepdims=True))
    ).astype(BF16)
    router_part = contract_rows(ffn_in, d_logits)
    d_ffn = d_ffn + times_transpose(d_logits, w_router)
    ffn_gain_part = jnp.sum(d_ffn * mixed_norm, axis=0)
    d_norm_two = d_ffn * ffn_gain.astype(F32)
    d_mixed = d_result + scale_two * (
        d_norm_two - mixed_norm * jnp.mean(d_norm_two * mixed_norm, axis=-1, keepdims=True)
    )
    d_attn = d_mixed.astype(BF16)
    d_attn_all = jnp.concatenate(tensor_gather(d_attn), axis=0)
    result = mixed + experts.output(d_attn_all)
    grad_w_out = contract_rows(o_low, d_attn_all)
    d_attended = (
        times_transpose(d_attn_all, w_out)
        .astype(BF16)
        .reshape(block_count, block_rows, local_heads, head_width)
    )

    def attend_back(carry, inputs):
        dk_total, dv_total = carry
        q_block, do_block, lse_block, q_pos = inputs
        scores = jnp.einsum("qhd,khd->hqk", q_block, k_rot, preferred_element_type=F32) * score_scale
        allowed = allowed_mask(q_pos)
        scores = jnp.where(allowed, scores, -1e30)
        soft = jnp.where(allowed, jnp.exp(scores - lse_block[..., None]), 0.0)
        d_weights = jnp.einsum("qhd,khd->hqk", do_block, v_low, preferred_element_type=F32)
        d_scores = (soft * (d_weights - jnp.sum(soft * d_weights, axis=-1, keepdims=True))).astype(BF16)
        dq_block = jnp.einsum("hqk,khd->qhd", d_scores, k_rot, preferred_element_type=F32) * score_scale
        dk_total = (
            dk_total
            + jnp.einsum("hqk,qhd->khd", d_scores, q_block, preferred_element_type=F32) * score_scale
        )
        dv_total = dv_total + jnp.einsum(
            "hqk,qhd->khd", soft.astype(BF16), do_block, preferred_element_type=F32
        )
        return ((dk_total, dv_total), dq_block)

    zero_field = jnp.zeros((seq_len, local_heads, head_width), F32)
    (dk_rot, dv_full), dq_blocks = lax.scan(
        attend_back, (zero_field, zero_field), (q_blocks, d_attended, lse_blocks, q_positions)
    )
    dq_gain = unrotate(
        dq_blocks.reshape(seq_len, local_heads, head_width), cosine, sine_table
    ).reshape(seq_len, local_width)
    dk_gain = unrotate(dk_rot, cosine, sine_table).reshape(seq_len, local_width)
    query_gain_part = jnp.sum(dq_gain * query_hat, axis=0)
    key_gain_part = jnp.sum(dk_gain * key_hat, axis=0)
    dq_hat = dq_gain * q_gain
    dk_hat = dk_gain * k_gain
    q_inner, k_inner = token_sums(dq_hat * query_hat, dk_hat * key_hat)
    dq_raw = (q_rscale * (dq_hat - query_hat * (q_inner / model_width)[:, None])).astype(BF16)
    dk_raw = (k_rscale * (dk_hat - key_hat * (k_inner / model_width)[:, None])).astype(BF16)
    dv_raw = dv_full.reshape(seq_len, local_width).astype(BF16)
    grad_query = contract_rows(gathered, dq_raw)
    grad_key = contract_rows(gathered, dk_raw)
    grad_value = contract_rows(gathered, dv_raw)
    total_term = times_transpose(dq_raw, w_query)
    total_term = total_term + times_transpose(dk_raw, w_key)
    total_term = (total_term + times_transpose(dv_raw, w_value)).astype(BF16)
    d_attn_in = tensor_scatter(jnp.split(total_term, tensor_count, axis=0))
    attn_gain_part = jnp.sum(d_attn_in * normed, axis=0)
    d_norm_one = d_attn_in * attn_gain.astype(F32)
    d_input = d_mixed + scale_one * (
        d_norm_one - normed * jnp.mean(d_norm_one * normed, axis=-1, keepdims=True)
    )
    grad_w_gate, grad_w_up, grad_w_down = experts.grads()

    def dp_sum(value):
        return lax.psum(value.astype(BF16), "dp").astype(F32)

    return (
        result.astype(BF16),
        d_input.astype(BF16),
        dp_sum(grad_query),
        dp_sum(grad_key),
        dp_sum(grad_value),
        dp_sum(query_gain_part),
        dp_sum(key_gain_part),
        dp_sum(grad_w_out),
        lax.psum(attn_gain_part, BOTH),
        lax.psum(ffn_gain_part, BOTH),
        lax.psum(router_part, BOTH),
        grad_w_gate,
        grad_w_up,
        grad_w_down,
    )


def solution(mesh):
    rows, columns = P(BOTH, None), P(None, "tensor")
    return jax.shard_map(
        local,
        mesh=mesh,
        in_specs=(
            rows,
            rows,
            P("dp"),
            rows,
            P(),
            columns,
            columns,
            columns,
            P("tensor"),
            P("tensor"),
            P("tensor", None),
            P(),
            P(),
            P("dp", None, "tensor"),
            P("dp", None, "tensor"),
            P("dp", "tensor", None),
        ),
        out_specs=(
            rows,
            rows,
            columns,
            columns,
            columns,
            P("tensor"),
            P("tensor"),
            P("tensor", None),
            P(),
            P(),
            P(),
            P("dp", None, "tensor"),
            P("dp", None, "tensor"),
            P("dp", "tensor", None),
        ),
        check_vma=False,
    )
```

time: 4010 us -> 1630 us (0.41)
  waiting for transfers between devices: 3140 us -> 618 us
  Pallas kernels: 0 us -> 261 us
  matrix products: 322 us -> 126 us
  blocking collectives: 74.4 us -> 187 us
    all_to_all x4 -> x1, waiting for transfers between devices: 2700 us -> 0.01 us  [run(): lax.all_to_all(d_probs, BOTH, split_axis=0, concat_axis=0, tiled=True)]
    ppermute x0 -> x136, waiting for transfers between devices: none -> 438 us  [the longest x24 176 us: send_x(): lax.ppermute(value, BOTH, device_pairs(lambda z, x, y, c: (z, x ^ 1, y, c)))]
    pallas_call x0 -> x13, Pallas kernels: none -> 261 us  [the longest x4 110 us: main_chunk(): pl.pallas_call(functools.partial(main_kernel, count, slot_count), grid=(e...]
    dot_general x31 -> x20, matrix products: 284 us -> 76 us  [the longest x2 14.9 us: attend_back(): jnp.einsum('qhd,khd->hqk', q_block, k_rot, preferred_element_type=F32)]
    all_gather x0 -> x2, blocking collectives: none -> 113 us  [the longest x1 72.5 us: __init__(): ids = lax.all_gather(expert_ids.T, BOTH, axis=0, tiled=False)[self.absolute]]
    psum x2, waiting for transfers between devices: 282 us -> 180 us  [the longest x1 121 us: local(): lax.psum(router_part, BOTH)]
    all_to_all x4 -> x1, starting transfers between devices: 101 us -> 2.58 us  [run(): lax.all_to_all(d_probs, BOTH, split_axis=0, concat_axis=0, tiled=True)]
    all_gather x2 -> x0, waiting for transfers between devices: 96.3 us -> none  [the longest x1 62 us: local(): d_attn_all = lax.all_gather(d_attn, 'tensor', axis=0, tiled=True)]
  transfers between devices with their start and end apart: 10 -> 139, of which waited for: 9 -> 37; matrix products, arithmetic and copies ran while one was open for 8% -> 22% of each run, Pallas kernels for 0% -> 16%
where the time goes in v1:
time: 1630 us; the launch traced here: 1620 us
  waiting for transfers between devices  618 us (38%)
  Pallas kernels  261 us (16%)
  blocking collectives  187 us (11%)
  local copies, waits for them, and re-layouts  173 us (11%)
  other arithmetic  141 us (9%)
  matrix products  126 us (8%)
  starting transfers between devices  95.5 us (6%)
  between operations  17.2 us (1%)
    ppermute x24, waiting for transfers between devices, send_x(): lax.ppermute(value, BOTH, device_pairs(lambda z, x, y, c: (z, x ^ 1, y, c)))  176 us
    ppermute x12, waiting for transfers between devices, send_z(): lax.ppermute(value, BOTH, device_pairs(lambda z, x, y, c: ((z - 1) % RING...  124 us
    psum x1, waiting for transfers between devices, local(): lax.psum(router_part, BOTH)  121 us
    pallas_call x4, Pallas kernels, main_chunk(): pl.pallas_call(functools.partial(main_kernel, count, slot_count), grid=(e...  110 us
    ppermute x24, waiting for transfers between devices, send_y(): lax.ppermute(value, BOTH, device_pairs(lambda z, x, y, c: (z, x, y ^ 1, c)))  79.8 us
    unnamed x498, local copies, waits for them, and re-layouts  72.6 us
    all_gather x1, blocking collectives, __init__(): ids = lax.all_gather(expert_ids.T, BOTH, axis=0, tiled=False)[self.absolute]  72.5 us
    psum x1, waiting for transfers between devices, dp_sum(): return lax.psum(value.astype(BF16), 'dp').astype(F32)  59.9 us
  transfers between devices with their start and end apart: 139, of which 37 were waited for; matrix products, arithmetic and copies ran while one was open for 22% of the time, Pallas kernels for 16%

profile of v1, /device:TPU:0, one launch (start us, length us, event | category | flops | bytes accessed | tf_op | source)
XLA Modules:
  0.0 1619.6 jit_solution(12612278244851361995)
XLA Ops:
  20.7 18.6 %collective-permute-done.1 = bf16[256,2048]{1,0:T(8,128)(2,1)} collective-permute-done((bf16[256,2048]{1,0:T(8,128)(2,1)}, bf16[256,2048]{1,0:T(8,128)(2,1)}, u32[]{:S(2)}, u32[]{:S(2)}) %collective-permute-start.1) | collective-permute-done | bytes 1048608 | tf_op jit(solution)/shard_map/ppermute | solution.py:74
  48.8 6.6 multiply_reduce_fusion.6
  55.3 5.9 multiply_reduce_fusion.7
  61.8 8.1 psum.77
  89.8 6.2 subtract_convert_fusion
  97.7 5.6 convolution_convert_fusion.6
  109.0 22.4 %while.31 = (s32[]{:T(128)}, bf16[2,512,4,128]{3,1,2,0:T(8,128)(2,1)}, f32[2,4,512]{2,1,0:T(4,128)S(1)}, s32[2,512]{1,0:T(2,128)S(1)}, bf16[2,512,4,128]{3,1,2,0...) while((s32[]{:T(128)}, ...), condition=%wide.region_7.8_spmd.clone.clone, body=%wide.region_4.7_spmd.clone.clone.sunk | while | flops 1099957248 | bytes 43608308 | solution.py:674
  144.1 19.4 %collective-permute-done.12.refs_7_ = bf16[256,2048]{1,0:T(8,128)(2,1)S(1)} collective-permute-done((bf16[256,2048]{1,0:T(8,128)(2,1)}, bf16[256,2048]{1,0:T(8,128)(2,1)S(1)}, u32[]{:S(2)}, u32[]{:S(2)}) %collective-permute-start.12) | collective-permute-done | bytes 1048608 | tf_op jit(solution)/shard_map/ppermute | solution.py:123
  169.7 20.6 %collective-permute-done.5 = bf16[256,2048]{1,0:T(8,128)(2,1)S(1)} collective-permute-done((bf16[256,2048]{1,0:T(8,128)(2,1)S(1)}, bf16[256,2048]{1,0:T(8,128)(2,1)S(1)}, u32[]{:S(2)}, u32[]{:S(2)}) %collective-permute-start.5) | collective-permute-done | bytes 1048608 | tf_op jit(solution)/shard_map/ppermute | solution.py:74
  192.9 19.8 %collective-permute-done.26.refs_7_ = bf16[256,2048]{1,0:T(8,128)(2,1)S(1)} collective-permute-done((bf16[256,2048]{1,0:T(8,128)(2,1)S(1)}, bf16[256,2048]{1,0:T(8,128)(2,1)S(1)}, u32[]{:S(2)}, u32[]{:S(2)}) %collective-permute-start.26) | collective-permute-done | bytes 1048608 | tf_op jit(solution)/shard_map/ppermute | solution.py:115
  216.2 18.0 %collective-permute-done.17.refs_3_ = bf16[256,2048]{1,0:T(8,128)(2,1)} collective-permute-done((bf16[256,2048]{1,0:T(8,128)(2,1)S(1)}, bf16[256,2048]{1,0:T(8,128)(2,1)}, u32[]{:S(2)}, u32[]{:S(2)}) %collective-permute-start.17) | collective-permute-done | bytes 1048608 | tf_op jit(solution)/shard_map/ppermute | solution.py:115
  241.2 72.5 %all-gather = s32[256,256]{1,0:T(8,128)} all-gather(s32[8,256]{1,0:T(8,128)S(1)} %bitcast.292), channel_id=2, replica_groups=mesh['dp'=8,'tensor'=4] {'dp','tensor'}, dimensions={0}, use_global_device_ids=true | all-gather | bytes 270336 | tf_op jit(solution)/shard_map/all_gather | solution.py:440
  340.7 9.0 collective-permute-done.29.refs_0_
  351.9 20.9 %collective-permute-done.38.refs_6_ = bf16[256,2048]{1,0:T(8,128)(2,1)} collective-permute-done((bf16[256,2048]{1,0:T(8,128)(2,1)}, bf16[256,2048]{1,0:T(8,128)(2,1)}, u32[]{:S(2)}, u32[]{:S(2)}) %collective-permute-start.38) | collective-permute-done | bytes 1048608 | tf_op jit(solution)/shard_map/ppermute | solution.py:111
  375.2 14.0 shard_map.272
  396.8 16.8 %gather_fusion.10 = f32[2048]{0:T(1024)S(1)} fusion(f32[256,64]{0,1:T(8,128)S(1)} %fusion.66, s32[2048]{0:T(1024)S(1)} %reshape.1938), kind=kCustom, calls=%fused_computation.10 | custom fusion | bytes 32768 | tf_op jit(solution)/shard_map/jit(take_along_axis)/gather | solution.py:684
  416.0 40.7 %all-gather.1 = f32[256,256]{1,0:T(8,128)} all-gather(f32[8,256]{1,0:T(8,128)S(1)} %select_bitcast_fusion), channel_id=3, replica_groups=mesh['dp'=8,'tensor'=4] {'dp','tensor'}, dimensions={0}, use_global_device_ids=true | all-gather | bytes 270336 | tf_op jit(solution)/shard_map/all_gather | solution.py:466
  466.8 27.8 %shard_map.273 = (bf16[8,256,2048]{2,1,0:T(8,128)(2,1)}, bf16[8,256,256]{2,1,0:T(8,128)(2,1)S(1)}, bf16[8,256,256]{2,1,0:T(8,128)(2,1)S(1)}, bf16[8,256,256]{2,1...) custom-call(bf16[8,256,256]{2,1,0:T(8,128)(2,1)} %bitcast.261, ...), custom_call_target="tpu_custom_call" | custom-call | flops 12884901888 | bytes 41943040 | tf_op jit(solution)/shard_map/pallas_call | solution.py:319
  500.5 14.0 shard_map.278
  515.9 13.5 shard_map.281
  534.8 10.9 shard_map.274
  555.2 27.2 %shard_map.279 = (bf16[8,256,2048]{2,1,0:T(8,128)(2,1)}, bf16[8,256,256]{2,1,0:T(8,128)(2,1)S(1)}, bf16[8,256,256]{2,1,0:T(8,128)(2,1)S(1)}, bf16[8,256,256]{2,1...) custom-call(bf16[8,256,256]{2,1,0:T(8,128)(2,1)} %bitcast.258, ...), custom_call_target="tpu_custom_call" | custom-call | flops 12884901888 | bytes 41943040 | tf_op jit(solution)/shard_map/pallas_call | solution.py:319
  582.5 10.9 shard_map.280
  606.3 27.3 %shard_map.282 = (bf16[8,256,2048]{2,1,0:T(8,128)(2,1)}, bf16[8,256,256]{2,1,0:T(8,128)(2,1)S(1)}, bf16[8,256,256]{2,1,0:T(8,128)(2,1)S(1)}, bf16[8,256,256]{2,1...) custom-call(bf16[8,256,256]{2,1,0:T(8,128)(2,1)} %bitcast.256, ...), custom_call_target="tpu_custom_call" | custom-call | flops 12884901888 | bytes 41943040 | tf_op jit(solution)/shard_map/pallas_call | solution.py:319
  633.8 14.2 shard_map.275
  659.0 11.8 shard_map.283
  680.3 27.3 %shard_map.276 = (bf16[8,256,2048]{2,1,0:T(8,128)(2,1)}, bf16[8,256,256]{2,1,0:T(8,128)(2,1)S(1)}, bf16[8,256,256]{2,1,0:T(8,128)(2,1)S(1)}, bf16[8,256,256]{2,1...) custom-call(bf16[8,256,256]{2,1,0:T(8,128)(2,1)} %bitcast.254, ...), custom_call_target="tpu_custom_call" | custom-call | flops 12884901888 | bytes 41943040 | tf_op jit(solution)/shard_map/pallas_call | solution.py:319
  726.1 9.9 shard_map.277
  755.9 17.0 %collective-permute-done.73 = bf16[256,2048]{1,0:T(8,128)(2,1)S(1)} collective-permute-done((bf16[256,2048]{1,0:T(8,128)(2,1)S(1)}, bf16[256,2048]{1,0:T(8,128)(2,1)S(1)}, u32[]{:S(2)}, u32[]{:S(2)}) %collective-permute-start.73) | collective-permute-done | bytes 1048608 | tf_op jit(solution)/shard_map/ppermute | solution.py:111
  780.5 19.7 %collective-permute-done.76 = bf16[256,2048]{1,0:T(8,128)(2,1)S(1)} collective-permute-done((bf16[256,2048]{1,0:T(8,128)(2,1)S(1)}, bf16[256,2048]{1,0:T(8,128)(2,1)S(1)}, u32[]{:S(2)}, u32[]{:S(2)}) %collective-permute-start.76) | collective-permute-done | bytes 1048608 | tf_op jit(solution)/shard_map/ppermute | solution.py:111
  804.5 21.2 %collective-permute-done.85 = bf16[256,2048]{1,0:T(8,128)(2,1)S(1)} collective-permute-done((bf16[256,2048]{1,0:T(8,128)(2,1)S(1)}, bf16[256,2048]{1,0:T(8,128)(2,1)S(1)}, u32[]{:S(2)}, u32[]{:S(2)}) %collective-permute-start.85) | collective-permute-done | bytes 1048608 | tf_op jit(solution)/shard_map/ppermute | solution.py:111
  834.4 16.9 %collective-permute-done.87 = bf16[256,2048]{1,0:T(8,128)(2,1)S(1)} collective-permute-done((bf16[256,2048]{1,0:T(8,128)(2,1)S(1)}, bf16[256,2048]{1,0:T(8,128)(2,1)S(1)}, u32[]{:S(2)}, u32[]{:S(2)}) %collective-permute-start.87) | collective-permute-done | bytes 1048608 | tf_op jit(solution)/shard_map/ppermute | solution.py:111
  862.7 15.6 collective-permute-done.91
  886.5 19.3 %collective-permute-done.107 = bf16[256,2048]{1,0:T(8,128)(2,1)S(1)} collective-permute-done((bf16[256,2048]{1,0:T(8,128)(2,1)S(1)}, bf16[256,2048]{1,0:T(8,128)(2,1)S(1)}, u32[]{:S(2)}, u32[]{:S(2)}) %collective-permute-start.107) | collective-permute-done | bytes 1048608 | tf_op jit(solution)/shard_map/ppermute | solution.py:111
  912.7 13.6 collective-permute-done.95
  926.3 4.7 collective-permute-done.96
  938.2 18.4 %collective-permute-done.110 = bf16[256,2048]{1,0:T(8,128)(2,1)S(1)} collective-permute-done((bf16[256,2048]{1,0:T(8,128)(2,1)S(1)}, bf16[256,2048]{1,0:T(8,128)(2,1)S(1)}, u32[]{:S(2)}, u32[]{:S(2)}) %collective-permute-start.110) | collective-permute-done | bytes 1048608 | tf_op jit(solution)/shard_map/ppermute | solution.py:111
  962.1 18.6 %collective-permute-done.100 = bf16[256,2048]{1,0:T(8,128)(2,1)S(1)} collective-permute-done((bf16[256,2048]{1,0:T(8,128)(2,1)S(1)}, bf16[256,2048]{1,0:T(8,128)(2,1)S(1)}, u32[]{:S(2)}, u32[]{:S(2)}) %collective-permute-start.100) | collective-permute-done | bytes 1048608 | tf_op jit(solution)/shard_map/ppermute | solution.py:74
  982.8 18.9 %collective-permute-done.120 = bf16[256,2048]{1,0:T(8,128)(2,1)S(1)} collective-permute-done((bf16[256,2048]{1,0:T(8,128)(2,1)S(1)}, bf16[256,2048]{1,0:T(8,128)(2,1)S(1)}, u32[]{:S(2)}, u32[]{:S(2)}) %collective-permute-start.120) | collective-permute-done | bytes 1048608 | tf_op jit(solution)/shard_map/ppermute | solution.py:115
  1007.1 5.7 convolution_convert_fusion.5
  1013.9 69.2 %while.32 = (s32[]{:T(128)}, f32[1024,4,128]{0,2,1:T(8,128)}, f32[1024,4,128]{0,2,1:T(8,128)}, f32[2,512,4,128]{3,1,0,2:T(8,128)}, bf16[2,512,4,128]{3,1,2,0:T(8...) while((s32[]{:T(128)}, f32[1024,4,128]{0,2,1:T(8,128)}, ...), condition=%wide.region_24.25_spmd.clone.clone.clone, body=%wide.region_22.24_spmd.clone.clone.clone.sunk | while | flops 2709259264 | bytes 226560512 | solution.py:727
  1015.2 5.9 fusion.167
  1022.3 7.4 multiply_reduce_fusion.9
  1035.6 4.8 bitcast_add_fusion.4
  1049.5 5.9 fusion.167
  1056.6 7.4 multiply_reduce_fusion.9
  1069.9 5.5 bitcast_add_fusion.4
  1086.3 4.9 multiply_subtract_fusion
  1105.0 6.0 psum.78
  1121.3 5.9 convolution_convert_fusion.4
  1127.2 6.0 convolution_convert_fusion.3
  1133.4 6.3 convolution_convert_fusion.2
  1148.5 57.8 %collective-permute-done.124 = bf16[256,2048]{1,0:T(8,128)(2,1)S(1)} collective-permute-done((bf16[256,2048]{1,0:T(8,128)(2,1)}, bf16[256,2048]{1,0:T(8,128)(2,1)S(1)}, u32[]{:S(2)}, u32[]{:S(2)}) %collective-permute-start.124) | collective-permute-done | bytes 1048608 | tf_op jit(solution)/shard_map/ppermute | solution.py:123
  1210.3 5.8 fusion.104
  1216.1 5.8 fusion.105
  1221.9 8.3 add_convert_fusion
  1236.1 39.8 %collective-permute-done.128 = bf16[256,2048]{1,0:T(8,128)(2,1)} collective-permute-done((bf16[256,2048]{1,0:T(8,128)(2,1)}, bf16[256,2048]{1,0:T(8,128)(2,1)}, u32[]{:S(2)}, u32[]{:S(2)}) %collective-permute-start.128) | collective-permute-done | bytes 1048608 | tf_op jit(solution)/shard_map/ppermute | solution.py:123
  1285.2 7.1 collective-permute-done.129
  1293.8 52.5 %shard_map.284 = (f32[8,2048,256]{2,1,0:T(8,128)}, f32[8,2048,256]{2,1,0:T(8,128)}, f32[8,256,2048]{2,1,0:T(8,128)}) custom-call(bf16[8,256,2048]{2,1,0:T(8,128)(2,1)} %get-tuple-element.534.refs_0_, bf16[8,256,2048]{2,1,0:T(8,128)(2,1)} %get-tuple-element.535.refs_1_, bf16[8,256,2048]{2,1,0:T(8,128)(2,1)} %get-tuple-element.536.refs_2_, ...), custom_call_target="tpu_custom_call" | custom-call | flops 25769803776 | bytes 117440512 | tf_op jit(solution)/shard_map/pallas_call | solution.py:408
  1347.4 18.7 %all-reduce.1 = (bf16[512]{0:T(512)(128)(2,1)S(1)}, bf16[512]{0:T(512)(128)(2,1)S(1)}) all-reduce(bf16[512]{0:T(512)(128)(2,1)S(1)} %get-tuple-element.861, bf16[512]{0:T(512)(128)(2,1)S(1)} %get-tuple-element.859), channel_id=1, replica_groups=mesh['dp'=8,'tensor'=4] {'dp'}, use_global_device_ids=true, to_apply=%region_33.34 | all-reduce | flops 1024 | bytes 4096 | tf_op jit(solution)/shard_map/psum | solution.py:757
  1370.8 6.4 fusion.50
  1377.2 40.7 %all-reduce = (f32[2048]{0:T(1024)}, f32[2048]{0:T(1024)}) all-reduce(f32[2048]{0:T(1024)S(1)} %get-tuple-element.857, f32[2048]{0:T(1024)S(1)} %copy-done.215), channel_id=1, replica_groups=mesh['dp'=8,'tensor'=4] {'dp','tensor'}, use_global_device_ids=true, to_apply=%region_38.39 | all-reduce | flops 4096 | bytes 32768 | tf_op jit(solution)/shard_map/psum | solution.py:768
  1418.0 59.9 %all-reduce.8.cloned.1.call-done = (bf16[2048,512]{1,0:T(8,128)(2,1)}, bf16[2048,512]{1,0:T(8,128)(2,1)}, bf16[2048,512]{1,0:T(8,128)(2,1)}, bf16[512,2048]{1,0:T(8,128)(2,1)}) async-done(((bf16[2048,512]{1,0:T(8,128)(2,1)}, bf16[2048,512]{1,0:T(8,128)(2,1)}, bf16[2048,512]{1,0:T(8,128)(2,1)}, bf16[512,2048]{1,0:T(8,128)(2,1)}), (bf16[2048,512]{1,0:T(8,128)(2,1)}, bf16[2048,512]{1,0:T(8,128)(2,1)}, ...) | async-done | bytes 8388624 | tf_op jit(solution)/shard_map/psum | solution.py:757
  1490.0 120.5 %all-reduce.6.cloned.1.call-done = f32[2048,64]{0,1:T(8,128)} async-done(((f32[2048,64]{0,1:T(8,128)}), f32[2048,64]{0,1:T(8,128)}) %all-reduce.6.cloned.1.call-update) | async-done | bytes 524304 | tf_op jit(solution)/shard_map/psum | solution.py:770
  (1007 shorter events, 425.5 us)
Async XLA Ops:
  15.1 121.3 %collective-permute-start.6 = (bf16[256,2048]{1,0:T(8,128)(2,1)S(1)}, bf16[256,2048]{1,0:T(8,128)(2,1)}, u32[]{:S(2)}, u32[]{:S(2)}) collective-permute-start(bf16[256,2048]{1,0:T(8,128)(2,1)S(1)} %copy-done.1), channel_id=1, source_target_pairs={{0,24},{1,25},{2,26},{3,27},{4,28},{5,29},{6,30},{7,31},{8,0},{9,1... | collective-permute-start | bytes 3145736 | tf_op jit(solution)/shard_map/ppermute | solution.py:123
  18.7 117.7 %collective-permute-start.7 = (bf16[256,2048]{1,0:T(8,128)(2,1)S(1)}, bf16[256,2048]{1,0:T(8,128)(2,1)}, u32[]{:S(2)}, u32[]{:S(2)}) collective-permute-start(bf16[256,2048]{1,0:T(8,128)(2,1)S(1)} %copy-done.1), channel_id=1, source_target_pairs={{0,4},{1,5},{2,6},{3,7},{4,0},{5,1},{6,2},{7,3},{8,12},{9,13},{10,... | collective-permute-start | bytes 3145736 | tf_op jit(solution)/shard_map/ppermute | solution.py:111
  20.2 116.2 %collective-permute-start.8 = (bf16[256,2048]{1,0:T(8,128)(2,1)S(1)}, bf16[256,2048]{1,0:T(8,128)(2,1)}, u32[]{:S(2)}, u32[]{:S(2)}) collective-permute-start(bf16[256,2048]{1,0:T(8,128)(2,1)S(1)} %copy-done.1), channel_id=1, source_target_pairs={{0,2},{1,3},{2,0},{3,1},{4,6},{5,7},{6,4},{7,5},{8,10},{9,11},{10,... | collective-permute-start | bytes 3145736 | tf_op jit(solution)/shard_map/ppermute | solution.py:115
  142.5 47.8 %collective-permute-start.5 = (bf16[256,2048]{1,0:T(8,128)(2,1)S(1)}, bf16[256,2048]{1,0:T(8,128)(2,1)S(1)}, u32[]{:S(2)}, u32[]{:S(2)}) collective-permute-start(bf16[256,2048]{1,0:T(8,128)(2,1)S(1)} %add_convert_fusion.49), channel_id=1, source_target_pairs={{0,2},{1,3},{2,0},{3,1},{4,6},{5,7},{6,4},{7,5},{8,10},{9,11},{10,... | collective-permute-start | bytes 3145736 | tf_op jit(solution)/shard_map/ppermute | solution.py:74
  169.2 43.6 %collective-permute-start.26 = (bf16[256,2048]{1,0:T(8,128)(2,1)S(1)}, bf16[256,2048]{1,0:T(8,128)(2,1)S(1)}, u32[]{:S(2)}, u32[]{:S(2)}) collective-permute-start(bf16[256,2048]{1,0:T(8,128)(2,1)S(1)} %collective-permute-done.12.refs_7_), channel_id=1, source_target_pairs={{0,2},{1,3},{2,0},{3,1},{4,6},{5,7},{6,4},{7,5},{8,10},{9,11},{10,... | collective-permute-start | bytes 3145736 | tf_op jit(solution)/shard_map/ppermute | solution.py:115
  192.4 41.9 %collective-permute-start.17 = (bf16[256,2048]{1,0:T(8,128)(2,1)S(1)}, bf16[256,2048]{1,0:T(8,128)(2,1)}, u32[]{:S(2)}, u32[]{:S(2)}) collective-permute-start(bf16[256,2048]{1,0:T(8,128)(2,1)S(1)} %multiply_convert_fusion.3.refs_0_), channel_id=1, source_target_pairs={{0,2},{1,3},{2,0},{3,1},{4,6},{5,7},{6,4},{7,5},{8,10},{9,11},{10,... | collective-permute-start | bytes 3145736 | tf_op jit(solution)/shard_map/ppermute | solution.py:115
  192.9 41.9 %collective-permute-start.9 = (bf16[256,2048]{1,0:T(8,128)(2,1)S(1)}, bf16[256,2048]{1,0:T(8,128)(2,1)S(1)}, u32[]{:S(2)}, u32[]{:S(2)}) collective-permute-start(bf16[256,2048]{1,0:T(8,128)(2,1)S(1)} %copy-done.1), channel_id=1, source_target_pairs={{0,1},{1,0},{2,3},{3,2},{4,5},{5,4},{6,7},{7,6},{8,9},{9,8},{10,11... | collective-permute-start | bytes 3145736 | tf_op jit(solution)/shard_map/ppermute | solution.py:119
  214.9 100.4 %collective-permute-start.27 = (bf16[256,2048]{1,0:T(8,128)(2,1)}, bf16[256,2048]{1,0:T(8,128)(2,1)}, u32[]{:S(2)}, u32[]{:S(2)}) collective-permute-start(bf16[256,2048]{1,0:T(8,128)(2,1)} %collective-permute-done.24.refs_5_), channel_id=1, source_target_pairs={{0,4},{1,5},{2,6},{3,7},{4,0},{5,1},{6,2},{7,3},{8,12},{9,13},{10,... | collective-permute-start | bytes 3145736 | tf_op jit(solution)/shard_map/ppermute | solution.py:111
  234.3 81.4 %collective-permute-start.28 = (bf16[256,2048]{1,0:T(8,128)(2,1)}, bf16[256,2048]{1,0:T(8,128)(2,1)}, u32[]{:S(2)}, u32[]{:S(2)}) collective-permute-start(bf16[256,2048]{1,0:T(8,128)(2,1)} %collective-permute-done.24.refs_5_), channel_id=1, source_target_pairs={{0,2},{1,3},{2,0},{3,1},{4,6},{5,7},{6,4},{7,5},{8,10},{9,11},{10,... | collective-permute-start | bytes 3145736 | tf_op jit(solution)/shard_map/ppermute | solution.py:115
  235.8 80.0 %collective-permute-start.21 = (bf16[256,2048]{1,0:T(8,128)(2,1)}, bf16[256,2048]{1,0:T(8,128)(2,1)}, u32[]{:S(2)}, u32[]{:S(2)}) collective-permute-start(bf16[256,2048]{1,0:T(8,128)(2,1)} %collective-permute-done.15.refs_1_), channel_id=1, source_target_pairs={{0,24},{1,25},{2,26},{3,27},{4,28},{5,29},{6,30},{7,31},{8,0},{9,1... | collective-permute-start | bytes 3145736 | tf_op jit(solution)/shard_map/ppermute | solution.py:123
  237.2 79.0 %collective-permute-start.22 = (bf16[256,2048]{1,0:T(8,128)(2,1)}, bf16[256,2048]{1,0:T(8,128)(2,1)}, u32[]{:S(2)}, u32[]{:S(2)}) collective-permute-start(bf16[256,2048]{1,0:T(8,128)(2,1)} %collective-permute-done.15.refs_1_), channel_id=1, source_target_pairs={{0,4},{1,5},{2,6},{3,7},{4,0},{5,1},{6,2},{7,3},{8,12},{9,13},{10,... | collective-permute-start | bytes 3145736 | tf_op jit(solution)/shard_map/ppermute | solution.py:111
  238.8 77.6 %collective-permute-start.23 = (bf16[256,2048]{1,0:T(8,128)(2,1)}, bf16[256,2048]{1,0:T(8,128)(2,1)}, u32[]{:S(2)}, u32[]{:S(2)}) collective-permute-start(bf16[256,2048]{1,0:T(8,128)(2,1)} %collective-permute-done.15.refs_1_), channel_id=1, source_target_pairs={{0,2},{1,3},{2,0},{3,1},{4,6},{5,7},{6,4},{7,5},{8,10},{9,11},{10,... | collective-permute-start | bytes 3145736 | tf_op jit(solution)/shard_map/ppermute | solution.py:115
  326.2 46.6 %collective-permute-start.38 = (bf16[256,2048]{1,0:T(8,128)(2,1)}, bf16[256,2048]{1,0:T(8,128)(2,1)}, u32[]{:S(2)}, u32[]{:S(2)}) collective-permute-start(bf16[256,2048]{1,0:T(8,128)(2,1)} %collective-permute-done.21.refs_7_), channel_id=1, source_target_pairs={{0,4},{1,5},{2,6},{3,7},{4,0},{5,1},{6,2},{7,3},{8,12},{9,13},{10,... | collective-permute-start | bytes 3145736 | tf_op jit(solution)/shard_map/ppermute | solution.py:111
  327.2 45.6 %collective-permute-start.39 = (bf16[256,2048]{1,0:T(8,128)(2,1)}, bf16[256,2048]{1,0:T(8,128)(2,1)}, u32[]{:S(2)}, u32[]{:S(2)}) collective-permute-start(bf16[256,2048]{1,0:T(8,128)(2,1)} %collective-permute-done.21.refs_7_), channel_id=1, source_target_pairs={{0,2},{1,3},{2,0},{3,1},{4,6},{5,7},{6,4},{7,5},{8,10},{9,11},{10,... | collective-permute-start | bytes 3145736 | tf_op jit(solution)/shard_map/ppermute | solution.py:115
  349.7 41.3 %collective-permute-start.58 = (bf16[256,2048]{1,0:T(8,128)(2,1)S(1)}, bf16[256,2048]{1,0:T(8,128)(2,1)S(1)}, u32[]{:S(2)}, u32[]{:S(2)}) collective-permute-start(bf16[256,2048]{1,0:T(8,128)(2,1)S(1)} %copy-done.14), channel_id=1, source_target_pairs={{0,1},{1,0},{2,3},{3,2},{4,5},{5,4},{6,7},{7,6},{8,9},{9,8},{10,11... | collective-permute-start | bytes 3145736 | tf_op jit(solution)/shard_map/ppermute | solution.py:119
  351.4 40.6 %collective-permute-start.59 = (bf16[256,2048]{1,0:T(8,128)(2,1)}, bf16[256,2048]{1,0:T(8,128)(2,1)S(1)}, u32[]{:S(2)}, u32[]{:S(2)}) collective-permute-start(bf16[256,2048]{1,0:T(8,128)(2,1)} %collective-permute-done.24.refs_5_), channel_id=1, source_target_pairs={{0,1},{1,0},{2,3},{3,2},{4,5},{5,4},{6,7},{7,6},{8,9},{9,8},{10,11... | collective-permute-start | bytes 3145736 | tf_op jit(solution)/shard_map/ppermute | solution.py:119
  351.4 44.3 %collective-permute-start.18 = (bf16[256,2048]{1,0:T(8,128)(2,1)S(1)}, bf16[256,2048]{1,0:T(8,128)(2,1)S(1)}, u32[]{:S(2)}, u32[]{:S(2)}) collective-permute-start(bf16[256,2048]{1,0:T(8,128)(2,1)S(1)} %copy-done.145), channel_id=1, source_target_pairs={{0,1},{1,0},{2,3},{3,2},{4,5},{5,4},{6,7},{7,6},{8,9},{9,8},{10,11... | collective-permute-start | bytes 3145736 | tf_op jit(solution)/shard_map/ppermute | solution.py:119
  392.0 71.7 %collective-permute-start.31 = (bf16[256,2048]{1,0:T(8,128)(2,1)}, bf16[256,2048]{1,0:T(8,128)(2,1)}, u32[]{:S(2)}, u32[]{:S(2)}) collective-permute-start(bf16[256,2048]{1,0:T(8,128)(2,1)} %collective-permute-done.29.refs_0_), channel_id=1, source_target_pairs={{0,1},{1,0},{2,3},{3,2},{4,5},{5,4},{6,7},{7,6},{8,9},{9,8},{10,11... | collective-permute-start | bytes 3145736 | tf_op jit(solution)/shard_map/ppermute | solution.py:119
  392.9 71.2 %collective-permute-start.19 = (bf16[256,2048]{1,0:T(8,128)(2,1)}, bf16[256,2048]{1,0:T(8,128)(2,1)}, u32[]{:S(2)}, u32[]{:S(2)}) collective-permute-start(bf16[256,2048]{1,0:T(8,128)(2,1)} %collective-permute-done.16.refs_2_), channel_id=1, source_target_pairs={{0,1},{1,0},{2,3},{3,2},{4,5},{5,4},{6,7},{7,6},{8,9},{9,8},{10,11... | collective-permute-start | bytes 3145736 | tf_op jit(solution)/shard_map/ppermute | solution.py:119
  394.4 69.9 %collective-permute-start.20 = (bf16[256,2048]{1,0:T(8,128)(2,1)}, bf16[256,2048]{1,0:T(8,128)(2,1)}, u32[]{:S(2)}, u32[]{:S(2)}) collective-permute-start(bf16[256,2048]{1,0:T(8,128)(2,1)} %collective-permute-done.17.refs_3_), channel_id=1, source_target_pairs={{0,1},{1,0},{2,3},{3,2},{4,5},{5,4},{6,7},{7,6},{8,9},{9,8},{10,11... | collective-permute-start | bytes 3145736 | tf_op jit(solution)/shard_map/ppermute | solution.py:119
  395.4 69.8 %collective-permute-start.40 = (bf16[256,2048]{1,0:T(8,128)(2,1)}, bf16[256,2048]{1,0:T(8,128)(2,1)}, u32[]{:S(2)}, u32[]{:S(2)}) collective-permute-start(bf16[256,2048]{1,0:T(8,128)(2,1)} %collective-permute-done.37.refs_5_), channel_id=1, source_target_pairs={{0,4},{1,5},{2,6},{3,7},{4,0},{5,1},{6,2},{7,3},{8,12},{9,13},{10,... | collective-permute-start | bytes 3145736 | tf_op jit(solution)/shard_map/ppermute | solution.py:111
  395.7 69.5 %collective-permute-start.41 = (bf16[256,2048]{1,0:T(8,128)(2,1)}, bf16[256,2048]{1,0:T(8,128)(2,1)}, u32[]{:S(2)}, u32[]{:S(2)}) collective-permute-start(bf16[256,2048]{1,0:T(8,128)(2,1)} %collective-permute-done.37.refs_5_), channel_id=1, source_target_pairs={{0,2},{1,3},{2,0},{3,1},{4,6},{5,7},{6,4},{7,5},{8,10},{9,11},{10,... | collective-permute-start | bytes 3145736 | tf_op jit(solution)/shard_map/ppermute | solution.py:115
  496.5 56.2 %collective-permute-start.54 = (bf16[256,2048]{1,0:T(8,128)(2,1)}, bf16[256,2048]{1,0:T(8,128)(2,1)}, u32[]{:S(2)}, u32[]{:S(2)}) collective-permute-start(bf16[256,2048]{1,0:T(8,128)(2,1)} %collective-permute-done.22.refs_0_), channel_id=1, source_target_pairs={{0,1},{1,0},{2,3},{3,2},{4,5},{5,4},{6,7},{7,6},{8,9},{9,8},{10,11... | collective-permute-start | bytes 3145736 | tf_op jit(solution)/shard_map/ppermute | solution.py:119
  497.0 55.8 %collective-permute-start.55 = (bf16[256,2048]{1,0:T(8,128)(2,1)}, bf16[256,2048]{1,0:T(8,128)(2,1)}, u32[]{:S(2)}, u32[]{:S(2)}) collective-permute-start(bf16[256,2048]{1,0:T(8,128)(2,1)} %collective-permute-done.23.refs_1_), channel_id=1, source_target_pairs={{0,1},{1,0},{2,3},{3,2},{4,5},{5,4},{6,7},{7,6},{8,9},{9,8},{10,11... | collective-permute-start | bytes 3145736 | tf_op jit(solution)/shard_map/ppermute | solution.py:119
  497.0 56.2 %collective-permute-start.78 = (bf16[256,2048]{1,0:T(8,128)(2,1)}, bf16[256,2048]{1,0:T(8,128)(2,1)}, u32[]{:S(2)}, u32[]{:S(2)}) collective-permute-start(bf16[256,2048]{1,0:T(8,128)(2,1)} %get-tuple-element.429), channel_id=1, source_target_pairs={{0,1},{1,0},{2,3},{3,2},{4,5},{5,4},{6,7},{7,6},{8,9},{9,8},{10,11... | collective-permute-start | bytes 3145736 | tf_op jit(solution)/shard_map/ppermute | solution.py:119
  497.5 55.8 %collective-permute-start.42 = (bf16[256,2048]{1,0:T(8,128)(2,1)}, bf16[256,2048]{1,0:T(8,128)(2,1)}, u32[]{:S(2)}, u32[]{:S(2)}) collective-permute-start(bf16[256,2048]{1,0:T(8,128)(2,1)} %collective-permute-done.16.refs_2_), channel_id=1, source_target_pairs={{0,2},{1,3},{2,0},{3,1},{4,6},{5,7},{6,4},{7,5},{8,10},{9,11},{10,... | collective-permute-start | bytes 3145736 | tf_op jit(solution)/shard_map/ppermute | solution.py:115
  498.5 55.2 %collective-permute-start.43 = (bf16[256,2048]{1,0:T(8,128)(2,1)}, bf16[256,2048]{1,0:T(8,128)(2,1)}, u32[]{:S(2)}, u32[]{:S(2)}) collective-permute-start(bf16[256,2048]{1,0:T(8,128)(2,1)} %collective-permute-done.39.refs_7_), channel_id=1, source_target_pairs={{0,4},{1,5},{2,6},{3,7},{4,0},{5,1},{6,2},{7,3},{8,12},{9,13},{10,... | collective-permute-start | bytes 3145736 | tf_op jit(solution)/shard_map/ppermute | solution.py:111
  552.7 49.7 %collective-permute-start.64 = (bf16[256,2048]{1,0:T(8,128)(2,1)}, bf16[256,2048]{1,0:T(8,128)(2,1)S(1)}, u32[]{:S(2)}, u32[]{:S(2)}) collective-permute-start(bf16[256,2048]{1,0:T(8,128)(2,1)} %collective-permute-done.39.refs_7_), channel_id=1, source_target_pairs={{0,1},{1,0},{2,3},{3,2},{4,5},{5,4},{6,7},{7,6},{8,9},{9,8},{10,11... | collective-permute-start | bytes 3145736 | tf_op jit(solution)/shard_map/ppermute | solution.py:119
  552.7 49.9 %collective-permute-start.65 = (bf16[256,2048]{1,0:T(8,128)(2,1)}, bf16[256,2048]{1,0:T(8,128)(2,1)S(1)}, u32[]{:S(2)}, u32[]{:S(2)}) collective-permute-start(bf16[256,2048]{1,0:T(8,128)(2,1)} %collective-permute-done.37.refs_5_), channel_id=1, source_target_pairs={{0,1},{1,0},{2,3},{3,2},{4,5},{5,4},{6,7},{7,6},{8,9},{9,8},{10,11... | collective-permute-start | bytes 3145736 | tf_op jit(solution)/shard_map/ppermute | solution.py:119
  553.2 48.7 %collective-permute-start.63 = (bf16[256,2048]{1,0:T(8,128)(2,1)}, bf16[256,2048]{1,0:T(8,128)(2,1)S(1)}, u32[]{:S(2)}, u32[]{:S(2)}) collective-permute-start(bf16[256,2048]{1,0:T(8,128)(2,1)} %collective-permute-done.38.refs_6_), channel_id=1, source_target_pairs={{0,1},{1,0},{2,3},{3,2},{4,5},{5,4},{6,7},{7,6},{8,9},{9,8},{10,11... | collective-permute-start | bytes 3145736 | tf_op jit(solution)/shard_map/ppermute | solution.py:119
  553.3 49.7 %collective-permute-start.66 = (bf16[256,2048]{1,0:T(8,128)(2,1)}, bf16[256,2048]{1,0:T(8,128)(2,1)S(1)}, u32[]{:S(2)}, u32[]{:S(2)}) collective-permute-start(bf16[256,2048]{1,0:T(8,128)(2,1)} %collective-permute-done.40.refs_3_), channel_id=1, source_target_pairs={{0,1},{1,0},{2,3},{3,2},{4,5},{5,4},{6,7},{7,6},{8,9},{9,8},{10,11... | collective-permute-start | bytes 3145736 | tf_op jit(solution)/shard_map/ppermute | solution.py:119
  553.7 50.3 %collective-permute-start.67 = (bf16[256,2048]{1,0:T(8,128)(2,1)}, bf16[256,2048]{1,0:T(8,128)(2,1)S(1)}, u32[]{:S(2)}, u32[]{:S(2)}) collective-permute-start(bf16[256,2048]{1,0:T(8,128)(2,1)} %collective-permute-done.41.refs_4_), channel_id=1, source_target_pairs={{0,1},{1,0},{2,3},{3,2},{4,5},{5,4},{6,7},{7,6},{8,9},{9,8},{10,11... | collective-permute-start | bytes 3145736 | tf_op jit(solution)/shard_map/ppermute | solution.py:119
  602.6 48.4 %collective-permute-start.83 = (bf16[256,2048]{1,0:T(8,128)(2,1)}, bf16[256,2048]{1,0:T(8,128)(2,1)}, u32[]{:S(2)}, u32[]{:S(2)}) collective-permute-start(bf16[256,2048]{1,0:T(8,128)(2,1)} %get-tuple-element.441), channel_id=1, source_target_pairs={{0,1},{1,0},{2,3},{3,2},{4,5},{5,4},{6,7},{7,6},{8,9},{9,8},{10,11... | collective-permute-start | bytes 3145736 | tf_op jit(solution)/shard_map/ppermute | solution.py:119
  603.0 48.4 %collective-permute-start.46 = (bf16[256,2048]{1,0:T(8,128)(2,1)}, bf16[256,2048]{1,0:T(8,128)(2,1)}, u32[]{:S(2)}, u32[]{:S(2)}) collective-permute-start(bf16[256,2048]{1,0:T(8,128)(2,1)} %collective-permute-done.22.refs_0_), channel_id=1, source_target_pairs={{0,2},{1,3},{2,0},{3,1},{4,6},{5,7},{6,4},{7,5},{8,10},{9,11},{10,... | collective-permute-start | bytes 3145736 | tf_op jit(solution)/shard_map/ppermute | solution.py:115
  604.0 47.5 %collective-permute-start.47 = (bf16[256,2048]{1,0:T(8,128)(2,1)}, bf16[256,2048]{1,0:T(8,128)(2,1)}, u32[]{:S(2)}, u32[]{:S(2)}) collective-permute-start(bf16[256,2048]{1,0:T(8,128)(2,1)} %collective-permute-done.41.refs_4_), channel_id=1, source_target_pairs={{0,4},{1,5},{2,6},{3,7},{4,0},{5,1},{6,2},{7,3},{8,12},{9,13},{10,... | collective-permute-start | bytes 3145736 | tf_op jit(solution)/shard_map/ppermute | solution.py:111
  633.7 42.1 %collective-permute-start.79 = (bf16[256,2048]{1,0:T(8,128)(2,1)}, bf16[256,2048]{1,0:T(8,128)(2,1)}, u32[]{:S(2)}, u32[]{:S(2)}) collective-permute-start(bf16[256,2048]{1,0:T(8,128)(2,1)} %get-tuple-element.431), channel_id=1, source_target_pairs={{0,1},{1,0},{2,3},{3,2},{4,5},{5,4},{6,7},{7,6},{8,9},{9,8},{10,11... | collective-permute-start | bytes 3145736 | tf_op jit(solution)/shard_map/ppermute | solution.py:119
  675.8 102.6 %collective-permute-start.84 = (bf16[256,2048]{1,0:T(8,128)(2,1)}, bf16[256,2048]{1,0:T(8,128)(2,1)}, u32[]{:S(2)}, u32[]{:S(2)}) collective-permute-start(bf16[256,2048]{1,0:T(8,128)(2,1)} %get-tuple-element.443), channel_id=1, source_target_pairs={{0,1},{1,0},{2,3},{3,2},{4,5},{5,4},{6,7},{7,6},{8,9},{9,8},{10,11... | collective-permute-start | bytes 3145736 | tf_op jit(solution)/shard_map/ppermute | solution.py:119
  678.5 43.4 %collective-permute-start.82 = (bf16[256,2048]{1,0:T(8,128)(2,1)}, bf16[256,2048]{1,0:T(8,128)(2,1)}, u32[]{:S(2)}, u32[]{:S(2)}) collective-permute-start(bf16[256,2048]{1,0:T(8,128)(2,1)} %get-tuple-element.439), channel_id=1, source_target_pairs={{0,1},{1,0},{2,3},{3,2},{4,5},{5,4},{6,7},{7,6},{8,9},{9,8},{10,11... | collective-permute-start | bytes 3145736 | tf_op jit(solution)/shard_map/ppermute | solution.py:119
  721.9 755.9 %all-reduce.8.cloned.1.call-start = ((), (), s32[]{:S(2)}) async-start(), calls=%async_computation.2 | async-start | bytes 16777216 | tf_op jit(solution)/shard_map/psum | solution.py:757
  754.0 73.5 %collective-permute-start.89 = (bf16[256,2048]{1,0:T(8,128)(2,1)S(1)}, bf16[256,2048]{1,0:T(8,128)(2,1)S(1)}, u32[]{:S(2)}, u32[]{:S(2)}) collective-permute-start(bf16[256,2048]{1,0:T(8,128)(2,1)S(1)} %copy-done.239), channel_id=1, source_target_pairs={{0,1},{1,0},{2,3},{3,2},{4,5},{5,4},{6,7},{7,6},{8,9},{9,8},{10,11... | collective-permute-start | bytes 3145736 | tf_op jit(solution)/shard_map/ppermute | solution.py:119
  883.0 49.1 %collective-permute-start.68 = (bf16[256,2048]{1,0:T(8,128)(2,1)S(1)}, bf16[256,2048]{1,0:T(8,128)(2,1)S(1)}, u32[]{:S(2)}, u32[]{:S(2)}) collective-permute-start(bf16[256,2048]{1,0:T(8,128)(2,1)S(1)} %copy-done.236), channel_id=1, source_target_pairs={{0,1},{1,0},{2,3},{3,2},{4,5},{5,4},{6,7},{7,6},{8,9},{9,8},{10,11... | collective-permute-start | bytes 3145736 | tf_op jit(solution)/shard_map/ppermute | solution.py:119
  885.5 40.8 %collective-permute-start.95 = (bf16[256,2048]{1,0:T(8,128)(2,1)S(1)}, bf16[256,2048]{1,0:T(8,128)(2,1)S(1)}, u32[]{:S(2)}, u32[]{:S(2)}) collective-permute-start(bf16[256,2048]{1,0:T(8,128)(2,1)S(1)} %add_convert_fusion.42), channel_id=1, source_target_pairs={{0,4},{1,5},{2,6},{3,7},{4,0},{5,1},{6,2},{7,3},{8,12},{9,13},{10,... | collective-permute-start | bytes 3145736 | tf_op jit(solution)/shard_map/ppermute | solution.py:111
  886.0 45.1 %collective-permute-start.96 = (bf16[256,2048]{1,0:T(8,128)(2,1)S(1)}, bf16[256,2048]{1,0:T(8,128)(2,1)S(1)}, u32[]{:S(2)}, u32[]{:S(2)}) collective-permute-start(bf16[256,2048]{1,0:T(8,128)(2,1)S(1)} %copy-done.160), channel_id=1, source_target_pairs={{0,2},{1,3},{2,0},{3,1},{4,6},{5,7},{6,4},{7,5},{8,10},{9,11},{10,... | collective-permute-start | bytes 3145736 | tf_op jit(solution)/shard_map/ppermute | solution.py:115
  912.7 49.4 %collective-permute-start.115 = (bf16[256,2048]{1,0:T(8,128)(2,1)S(1)}, bf16[256,2048]{1,0:T(8,128)(2,1)S(1)}, u32[]{:S(2)}, u32[]{:S(2)}) collective-permute-start(bf16[256,2048]{1,0:T(8,128)(2,1)S(1)} %copy-done.87), channel_id=1, source_target_pairs={{0,1},{1,0},{2,3},{3,2},{4,5},{5,4},{6,7},{7,6},{8,9},{9,8},{10,11... | collective-permute-start | bytes 3145736 | tf_op jit(solution)/shard_map/ppermute | solution.py:119
  936.4 44.2 %collective-permute-start.100 = (bf16[256,2048]{1,0:T(8,128)(2,1)S(1)}, bf16[256,2048]{1,0:T(8,128)(2,1)S(1)}, u32[]{:S(2)}, u32[]{:S(2)}) collective-permute-start(bf16[256,2048]{1,0:T(8,128)(2,1)S(1)} %fusion.92), channel_id=1, source_target_pairs={{0,2},{1,3},{2,0},{3,1},{4,6},{5,7},{6,4},{7,5},{8,10},{9,11},{10,... | collective-permute-start | bytes 3145736 | tf_op jit(solution)/shard_map/ppermute | solution.py:74
  956.6 45.0 %collective-permute-start.123 = (bf16[256,2048]{1,0:T(8,128)(2,1)S(1)}, bf16[256,2048]{1,0:T(8,128)(2,1)S(1)}, u32[]{:S(2)}, u32[]{:S(2)}) collective-permute-start(bf16[256,2048]{1,0:T(8,128)(2,1)S(1)} %copy-done.79), channel_id=1, source_target_pairs={{0,1},{1,0},{2,3},{3,2},{4,5},{5,4},{6,7},{7,6},{8,9},{9,8},{10,11... | collective-permute-start | bytes 3145736 | tf_op jit(solution)/shard_map/ppermute | solution.py:119
  959.2 42.5 %collective-permute-start.120 = (bf16[256,2048]{1,0:T(8,128)(2,1)S(1)}, bf16[256,2048]{1,0:T(8,128)(2,1)S(1)}, u32[]{:S(2)}, u32[]{:S(2)}) collective-permute-start(bf16[256,2048]{1,0:T(8,128)(2,1)S(1)} %add_convert_fusion.9), channel_id=1, source_target_pairs={{0,2},{1,3},{2,0},{3,1},{4,6},{5,7},{6,4},{7,5},{8,10},{9,11},{10,... | collective-permute-start | bytes 3145736 | tf_op jit(solution)/shard_map/ppermute | solution.py:115
  962.1 41.8 %collective-permute-start.99 = (bf16[256,2048]{1,0:T(8,128)(2,1)S(1)}, bf16[256,2048]{1,0:T(8,128)(2,1)S(1)}, u32[]{:S(2)}, u32[]{:S(2)}) collective-permute-start(bf16[256,2048]{1,0:T(8,128)(2,1)S(1)} %fusion.92), channel_id=1, source_target_pairs={{0,1},{1,0},{2,3},{3,2},{4,5},{5,4},{6,7},{7,6},{8,9},{9,8},{10,11... | collective-permute-start | bytes 3145736 | tf_op jit(solution)/shard_map/ppermute | solution.py:74
  982.2 157.6 %collective-permute-start.113 = (bf16[256,2048]{1,0:T(8,128)(2,1)}, bf16[256,2048]{1,0:T(8,128)(2,1)}, u32[]{:S(2)}, u32[]{:S(2)}) collective-permute-start(bf16[256,2048]{1,0:T(8,128)(2,1)} %get-tuple-element.492), channel_id=1, source_target_pairs={{0,1},{1,0},{2,3},{3,2},{4,5},{5,4},{6,7},{7,6},{8,9},{9,8},{10,11... | collective-permute-start | bytes 3145736 | tf_op jit(solution)/shard_map/ppermute | solution.py:119
  1001.6 144.2 %collective-permute-start.114 = (bf16[256,2048]{1,0:T(8,128)(2,1)}, bf16[256,2048]{1,0:T(8,128)(2,1)}, u32[]{:S(2)}, u32[]{:S(2)}) collective-permute-start(bf16[256,2048]{1,0:T(8,128)(2,1)} %get-tuple-element.494), channel_id=1, source_target_pairs={{0,1},{1,0},{2,3},{3,2},{4,5},{5,4},{6,7},{7,6},{8,9},{9,8},{10,11... | collective-permute-start | bytes 3145736 | tf_op jit(solution)/shard_map/ppermute | solution.py:119
  1001.6 204.7 %collective-permute-start.127 = (bf16[256,2048]{1,0:T(8,128)(2,1)}, bf16[256,2048]{1,0:T(8,128)(2,1)}, u32[]{:S(2)}, u32[]{:S(2)}) collective-permute-start(bf16[256,2048]{1,0:T(8,128)(2,1)} %get-tuple-element.517), channel_id=1, source_target_pairs={{0,1},{1,0},{2,3},{3,2},{4,5},{5,4},{6,7},{7,6},{8,9},{9,8},{10,11... | collective-permute-start | bytes 3145736 | tf_op jit(solution)/shard_map/ppermute | solution.py:119
  1003.9 144.1 %collective-permute-start.121 = (bf16[256,2048]{1,0:T(8,128)(2,1)}, bf16[256,2048]{1,0:T(8,128)(2,1)}, u32[]{:S(2)}, u32[]{:S(2)}) collective-permute-start(bf16[256,2048]{1,0:T(8,128)(2,1)} %add_convert_fusion.13), channel_id=1, source_target_pairs={{0,4},{1,5},{2,6},{3,7},{4,0},{5,1},{6,2},{7,3},{8,12},{9,13},{10,... | collective-permute-start | bytes 3145736 | tf_op jit(solution)/shard_map/ppermute | solution.py:111
  1005.5 143.0 %collective-permute-start.122 = (bf16[256,2048]{1,0:T(8,128)(2,1)}, bf16[256,2048]{1,0:T(8,128)(2,1)}, u32[]{:S(2)}, u32[]{:S(2)}) collective-permute-start(bf16[256,2048]{1,0:T(8,128)(2,1)} %add_convert_fusion.12), channel_id=1, source_target_pairs={{0,2},{1,3},{2,0},{3,1},{4,6},{5,7},{6,4},{7,5},{8,10},{9,11},{10,... | collective-permute-start | bytes 3145736 | tf_op jit(solution)/shard_map/ppermute | solution.py:115
  1139.7 470.7 %all-reduce.6.cloned.1.call-start = ((), (), s32[]{:S(2)}) async-start(), calls=%async_computation.1 | async-start | bytes 1048576 | tf_op jit(solution)/shard_map/psum | solution.py:770
  1139.8 66.5 %collective-permute-start.124 = (bf16[256,2048]{1,0:T(8,128)(2,1)}, bf16[256,2048]{1,0:T(8,128)(2,1)S(1)}, u32[]{:S(2)}, u32[]{:S(2)}) collective-permute-start(bf16[256,2048]{1,0:T(8,128)(2,1)} %add_convert_fusion.7), channel_id=1, source_target_pairs={{0,24},{1,25},{2,26},{3,27},{4,28},{5,29},{6,30},{7,31},{8,0},{9,1... | collective-permute-start | bytes 3145736 | tf_op jit(solution)/shard_map/ppermute | solution.py:123
  1145.8 85.7 %collective-permute-start.103 = (bf16[256,2048]{1,0:T(8,128)(2,1)S(1)}, bf16[256,2048]{1,0:T(8,128)(2,1)S(1)}, u32[]{:S(2)}, u32[]{:S(2)}) collective-permute-start(bf16[256,2048]{1,0:T(8,128)(2,1)S(1)} %copy-done.75), channel_id=1, source_target_pairs={{0,1},{1,0},{2,3},{3,2},{4,5},{5,4},{6,7},{7,6},{8,9},{9,8},{10,11... | collective-permute-start | bytes 3145736 | tf_op jit(solution)/shard_map/ppermute | solution.py:119
  1148.0 132.4 %collective-permute-start.131 = (bf16[256,2048]{1,0:T(8,128)(2,1)S(1)}, bf16[256,2048]{1,0:T(8,128)(2,1)S(1)}, u32[]{:S(2)}, u32[]{:S(2)}) collective-permute-start(bf16[256,2048]{1,0:T(8,128)(2,1)S(1)} %copy-done.77), channel_id=1, source_target_pairs={{0,1},{1,0},{2,3},{3,2},{4,5},{5,4},{6,7},{7,6},{8,9},{9,8},{10,11... | collective-permute-start | bytes 3145736 | tf_op jit(solution)/shard_map/ppermute | solution.py:119
  1210.1 65.8 %collective-permute-start.128 = (bf16[256,2048]{1,0:T(8,128)(2,1)}, bf16[256,2048]{1,0:T(8,128)(2,1)}, u32[]{:S(2)}, u32[]{:S(2)}) collective-permute-start(bf16[256,2048]{1,0:T(8,128)(2,1)} %add_convert_fusion.5), channel_id=1, source_target_pairs={{0,24},{1,25},{2,26},{3,27},{4,28},{5,29},{6,30},{7,31},{8,0},{9,1... | collective-permute-start | bytes 3145736 | tf_op jit(solution)/shard_map/ppermute | solution.py:123
  1231.5 52.2 %collective-permute-start.134 = (bf16[256,2048]{1,0:T(8,128)(2,1)S(1)}, bf16[256,2048]{1,0:T(8,128)(2,1)S(1)}, u32[]{:S(2)}, u32[]{:S(2)}) collective-permute-start(bf16[256,2048]{1,0:T(8,128)(2,1)S(1)} %get-tuple-element.927), channel_id=1, source_target_pairs={{0,1},{1,0},{2,3},{3,2},{4,5},{5,4},{6,7},{7,6},{8,9},{9,8},{10,11... | collective-permute-start | bytes 3145736 | tf_op jit(solution)/shard_map/ppermute | solution.py:74
  1236.1 134.5 %collective-permute-start.102 = (bf16[256,2048]{1,0:T(8,128)(2,1)}, bf16[256,2048]{1,0:T(8,128)(2,1)}, u32[]{:S(2)}, u32[]{:S(2)}) collective-permute-start(bf16[256,2048]{1,0:T(8,128)(2,1)} %get-tuple-element.474), channel_id=1, source_target_pairs={{0,1},{1,0},{2,3},{3,2},{4,5},{5,4},{6,7},{7,6},{8,9},{9,8},{10,11... | collective-permute-start | bytes 3145736 | tf_op jit(solution)/shard_map/ppermute | solution.py:119
  1279.5 67.9 %collective-permute-start.130 = (bf16[256,2048]{1,0:T(8,128)(2,1)}, bf16[256,2048]{1,0:T(8,128)(2,1)}, u32[]{:S(2)}, u32[]{:S(2)}) collective-permute-start(bf16[256,2048]{1,0:T(8,128)(2,1)} %add_convert_fusion.18), channel_id=1, source_target_pairs={{0,2},{1,3},{2,0},{3,1},{4,6},{5,7},{6,4},{7,5},{8,10},{9,11},{10,... | collective-permute-start | bytes 3145736 | tf_op jit(solution)/shard_map/ppermute | solution.py:115
  1283.7 63.7 %collective-permute-start.132 = (bf16[256,2048]{1,0:T(8,128)(2,1)}, bf16[256,2048]{1,0:T(8,128)(2,1)}, u32[]{:S(2)}, u32[]{:S(2)}) collective-permute-start(bf16[256,2048]{1,0:T(8,128)(2,1)} %add_convert_fusion.3), channel_id=1, source_target_pairs={{0,24},{1,25},{2,26},{3,27},{4,28},{5,29},{6,30},{7,31},{8,0},{9,1... | collective-permute-start | bytes 3145736 | tf_op jit(solution)/shard_map/ppermute | solution.py:123
  1283.7 83.6 %collective-permute-start.133 = (bf16[256,2048]{1,0:T(8,128)(2,1)}, bf16[256,2048]{1,0:T(8,128)(2,1)}, u32[]{:S(2)}, u32[]{:S(2)}) collective-permute-start(bf16[256,2048]{1,0:T(8,128)(2,1)} %get-tuple-element.926), channel_id=1, source_target_pairs={{0,1},{1,0},{2,3},{3,2},{4,5},{5,4},{6,7},{7,6},{8,9},{9,8},{10,11... | collective-permute-start | bytes 3145736 | tf_op jit(solution)/shard_map/ppermute | solution.py:74
  1292.2 75.1 %collective-permute-start.135 = (bf16[256,2048]{1,0:T(8,128)(2,1)}, bf16[256,2048]{1,0:T(8,128)(2,1)}, u32[]{:S(2)}, u32[]{:S(2)}) collective-permute-start(bf16[256,2048]{1,0:T(8,128)(2,1)} %add_convert_fusion.1), channel_id=1, source_target_pairs={{0,2},{1,3},{2,0},{3,1},{4,6},{5,7},{6,4},{7,5},{8,10},{9,11},{10,... | collective-permute-start | bytes 3145736 | tf_op jit(solution)/shard_map/ppermute | solution.py:74
  (345 other events, 5374.0 us)
Sparse Core Ops, SparseCore 0:
  1139.9 337.9 all-reduce.7
  1483.7 126.7 all-reduce.5

commit v2 on v0

v2 whole, which is shorter than its diff:
```python
import functools
import math

import jax
import jax.numpy as jnp
from jax import lax
from jax.experimental import pallas as pl
from jax.experimental.pallas import tpu as pltpu
from jax.sharding import PartitionSpec as P

HDIM = 128
EPS = 1e-05
ROPE_BASE = 10000.0
BOTH = ("dp", "tensor")
F32 = jnp.float32
BF16 = jnp.bfloat16
VMEM_GRANT = 60 << 20
fence = lax.optimization_barrier


def rms_scale(values):
    return lax.rsqrt(jnp.mean(values * values, axis=-1, keepdims=True) + EPS)


def rope_tables(count, head_width):
    half_width = head_width // 2
    frequency = jnp.exp(
        -(jnp.arange(half_width, dtype=F32) * 2.0 / head_width) * math.log(ROPE_BASE)
    )
    angles = jnp.arange(count, dtype=F32)[:, None] * frequency[None, :]
    return (jnp.cos(angles), jnp.sin(angles))


def rotate(values_in, cosine, sine_table):
    half_width = values_in.shape[-1] // 2
    front_half = values_in[..., :half_width]
    back_half = values_in[..., half_width:]
    return jnp.concatenate(
        [
            front_half * cosine - back_half * sine_table,
            back_half * cosine + front_half * sine_table,
        ],
        axis=-1,
    )


def unrotate(grads_in, cosine, sine_table):
    return rotate(grads_in, cosine, -sine_table)


def contract_rows(left, right):
    return lax.dot_general(left, right, (((0,), (0,)), ((), ())), preferred_element_type=F32)


def times_transpose(left, right):
    return lax.dot_general(left, right, (((1,), (1,)), ((), ())), preferred_element_type=F32)


def add_low(*terms):
    total = terms[0].astype(F32)
    for term in terms[1:]:
        total = total + term.astype(F32)
    return total.astype(BF16)


def add_wide(*terms):
    total = terms[0].astype(F32)
    for term in terms[1:]:
        total = total + term.astype(F32)
    return total


RING = 4
COLUMNS = (
    ((0, 0, 0), (1, 0, 0), (0, 1, 0), (0, 0, 1)),
    ((2, 0, 0), (1, 1, 0), (1, 0, 1), (2, 1, 0)),
    ((3, 0, 0), (3, 1, 0), (2, 0, 1), (3, 0, 1)),
    ((1, 1, 1), (2, 1, 1)),
    ((0, 1, 1), (3, 1, 1)),
)
CHUNKS = tuple(tuple(chip + (dc,) for dc in (0, 1) for chip in chips) for chips in COLUMNS)
STARTS = tuple(sum(len(chunk) for chunk in CHUNKS[:i]) for i in range(len(CHUNKS)))
PLACES = tuple(place for chunk in CHUNKS for place in chunk)
MOVES = {
    "x": lambda z, x, y, c: (z, x ^ 1, y, c),
    "y": lambda z, x, y, c: (z, x, y ^ 1, c),
    "c": lambda z, x, y, c: (z, x, y, c ^ 1),
    "z": lambda z, x, y, c: ((z - 1) % RING, x, y, c),
    "u1": lambda z, x, y, c: ((z + 1) % RING, x, y, c),
    "u2": lambda z, x, y, c: ((z + 2) % RING, x, y, c),
    "u3": lambda z, x, y, c: ((z + 3) % RING, x, y, c),
    "z1": lambda z, x, y, c: (z ^ 1, x, y, c),
    "z2": lambda z, x, y, c: (z ^ 2, x, y, c),
}


def device_pairs(move):
    pairs = []
    for z in range(RING):
        for x in range(2):
            for y in range(2):
                for c in range(2):
                    tz, tx, ty, tc = move(z, x, y, c)
                    pairs.append(((z * 2 + x) * 4 + y * 2 + c, (tz * 2 + tx) * 4 + ty * 2 + tc))
    return pairs


def send(value, axis):
    return lax.ppermute(value, BOTH, device_pairs(MOVES[axis]))


def small_sum(value, axes):
    for axis in axes:
        value = value + send(value, axis)
    return value


def hop(axis, k, dx, dy):
    return {"z": ((k + 1) % RING, dx, dy), "x": (k, dx ^ 1, dy), "y": (k, dx, dy ^ 1)}[axis]


class Stages:
    def __init__(self, token):
        self.token = token

    def run(self, sends, works=()):
        values, args, _ = fence(([s[0] for s in sends], [w[1] for w in works], self.token))
        got, crossed = [], []
        for value, (_, axis) in zip(values, sends):
            if axis == "c" and len(crossed) >= 2:
                value, _ = fence((value, crossed[-2]))
            got.append(send(value, axis))
            if axis == "c":
                crossed.append(got[-1])
        made = [work(*arg) for (work, _), arg in zip(works, args)]
        got, made = fence((got, made))
        self.token = jax.tree.leaves((got, made))[0]
        return got, made


class Gather:
    def __init__(self, block):
        self.held = {(0, 0, 0, 0): block}

    def sends(self, hops):
        return [(self.held[chip + (0,)], axis) for axis, chip in hops]

    def take(self, hops, got):
        for (axis, chip), value in zip(hops, got):
            self.held[chip + (1,) if axis == "c" else hop(axis, *chip) + (0,)] = value

    def chunk(self, i):
        chunk = CHUNKS[i]
        late = [place for place in chunk if place not in self.held]
        values = [self.held[place] for place in chunk if place in self.held]
        return values, [self.held[place[:3] + (0,)] for place in late], late

    @staticmethod
    def complete(i, values, crossing, late):
        blocks = dict(zip([place for place in CHUNKS[i] if place not in late], values))
        done = []
        for place, value in zip(late, crossing):
            if len(done) >= 2:
                value, _ = fence((value, done[-2]))
            done.append(send(value, "c"))
            blocks[place] = done[-1]
        return [blocks[place] for place in CHUNKS[i]]


class Scatter:
    def __init__(self):
        self.held = {}

    def put(self, i, sums):
        for chip, value in zip(COLUMNS[i], sums):
            self.held.setdefault(chip, []).append(value)

    def sends(self, hops):
        return [(add_low(*self.held[chip]), axis) for axis, chip in hops]

    def take(self, hops, got):
        for (axis, chip), value in zip(hops, got):
            self.held.setdefault(hop(axis, *chip), []).append(value)

    def total(self):
        return add_wide(*self.held[0, 0, 0])


class DpSum:
    def __init__(self, value):
        group = lax.axis_index("dp")
        self.z, self.x = group // 2, group % 2
        self.value = value
        self.half, self.piece = value.shape[0] // 2, value.shape[0] // (2 * RING)

    def split_x(self):
        return [(lax.dynamic_slice_in_dim(self.value, (1 - self.x) * self.half, self.half), "x")]

    def add_x(self, got):
        self.sum = add_low(lax.dynamic_slice_in_dim(self.value, self.x * self.half, self.half), got[0])

    def split_z(self):
        return [
            (lax.dynamic_slice_in_dim(self.sum, ((self.z + d) % RING) * self.piece, self.piece), f"u{d}")
            for d in (1, 2, 3)
        ]

    def add_z(self, got):
        self.part = add_low(lax.dynamic_slice_in_dim(self.sum, self.z * self.piece, self.piece), *got)

    def join_z(self):
        return [(self.part, f"u{d}") for d in (1, 2, 3)]

    def took_z(self, got):
        stack = jnp.stack([self.part] + list(got))
        order = (self.z - jnp.arange(RING)) % RING
        self.whole_half = stack[order].reshape(self.half, -1)

    def join_x(self):
        return [(self.whole_half, "x")]

    def took_x(self, got):
        mine, other = self.whole_half, got[0]
        first = jnp.where(self.x == 0, mine, other)
        second = jnp.where(self.x == 0, other, mine)
        self.result = jnp.concatenate([first, second], axis=0).astype(F32)


def core_sum(near, far):
    return pair_sum(near, send(far, "c"))


def place_indices():
    group, member = lax.axis_index("dp"), lax.axis_index("tensor")
    z, x, y, c = group // 2, group % 2, member // 2, member % 2
    absolute = jnp.stack(
        [(((z + k) % RING) * 2 + (x ^ dx)) * 4 + (y ^ dy) * 2 + (c ^ dc) for k, dx, dy, dc in PLACES]
    )
    table = [0] * len(PLACES)
    for position, (k, dx, dy, dc) in enumerate(PLACES):
        table[((k * 2 + dx) * 2 + dy) * 2 + dc] = position
    numbers = jnp.arange(len(PLACES))
    other_z, other_x = numbers // 8, (numbers // 4) % 2
    other_y, other_c = (numbers // 2) % 2, numbers % 2
    offset = ((((other_z - z) % RING) * 2 + (other_x ^ x)) * 2 + (other_y ^ y)) * 2 + (other_c ^ c)
    return absolute, jnp.asarray(table, jnp.int32)[offset]


def nn(left, right):
    return lax.dot_general(left, right, (((1,), (0,)), ((), ())), preferred_element_type=F32)


def nt(left, right):
    return lax.dot_general(left, right, (((1,), (1,)), ((), ())), preferred_element_type=F32)


def pick_rows(picks_ref, blocks, rows_ref, slot_count, width):
    experts = rows_ref.shape[0]
    for b, block in enumerate(blocks):
        for low in range(0, block.shape[1], width):
            columns = pl.ds(low, width)
            picked = nn(picks_ref[b], block[:, columns]).astype(BF16)
            for e in range(experts):
                rows_ref[e, pl.ds(b * slot_count, slot_count), columns] = picked[
                    e * slot_count : (e + 1) * slot_count
                ]


def give_rows(picks_ref, rows_ref, blocks, slot_count, width):
    experts = rows_ref.shape[0]
    for b, block in enumerate(blocks):
        for low in range(0, block.shape[1], width):
            columns = pl.ds(low, width)
            slots = jnp.concatenate(
                [rows_ref[e, pl.ds(b * slot_count, slot_count), columns] for e in range(experts)], axis=0
            )
            block[:, columns] = contract_rows(picks_ref[b], slots).astype(BF16)


def cot_kernel(count, slot_count, picks_ref, down_ref, *refs):
    blocks, (rows_out, acts_out, rows_ref) = refs[:count], refs[count:]
    e = pl.program_id(0)

    @pl.when(e == 0)
    def _():
        pick_rows(picks_ref, blocks, rows_ref, slot_count, 512)

    rows = rows_ref[e]
    rows_out[0] = rows
    acts_out[0] = nt(rows, down_ref[0])


def main_kernel(count, slot_count, picks_ref, gates_ref, acts_ref, gate_ref, up_ref, *refs):
    blocks = refs[:count]
    rows_out, scaled_out, d_gate_out, d_up_out, d_probs_out = refs[count : count + 5]
    near_out, far_out, rows_ref = refs[count + 5 :]
    results = [out.at[b] for out in (near_out, far_out) for b in range(count // 2)]
    e = pl.program_id(0)

    @pl.when(e == 0)
    def _():
        pick_rows(picks_ref, blocks, rows_ref, slot_count, 512)

    rows = rows_ref[e]
    rows_out[0] = rows
    pre, up = nn(rows, gate_ref[0]), nn(rows, up_ref[0])
    cot_acts = acts_ref[0]
    own_slots = pl.ds(pl.multiple_of(e * slot_count, slot_count), slot_count)
    own_picks = [picks_ref[b, own_slots, :].astype(F32) for b in range(count)]
    gate = jnp.concatenate(
        [
            jnp.sum(pick * gates_ref[b, pl.ds(e, 1), :], axis=1, keepdims=True)
            for b, pick in enumerate(own_picks)
        ],
        axis=0,
    )
    sig = jax.nn.sigmoid(pre)
    silu = pre * sig
    acts = silu * up
    scaled_out[0] = (gate * acts).astype(BF16)
    inner = jnp.sum(acts.astype(BF16).astype(F32) * cot_acts, axis=1, keepdims=True)
    for b, pick in enumerate(own_picks):
        here = inner[b * slot_count : (b + 1) * slot_count]
        d_probs_out[b, pl.ds(e, 1), :] = jnp.sum(pick * here, axis=0, keepdims=True)
    d_acts = gate * cot_acts
    d_pre = (d_acts * up * sig * (1.0 + pre * (1.0 - sig))).astype(BF16)
    d_up = (d_acts * silu).astype(BF16)
    d_gate_out[0] = d_pre
    d_up_out[0] = d_up
    rows_ref[e] = (nt(d_pre, gate_ref[0]) + nt(d_up, up_ref[0])).astype(BF16)

    @pl.when(e == pl.num_programs(0) - 1)
    def _():
        give_rows(picks_ref, rows_ref, results, slot_count, 512)


def out_kernel(count, slot_count, picks_ref, scaled_ref, down_ref, *refs):
    near_out, far_out, rows_ref = refs
    results = [out.at[b] for out in (near_out, far_out) for b in range(count // 2)]
    e = pl.program_id(0)
    rows_ref[e] = nn(scaled_ref[0], down_ref[0]).astype(BF16)

    @pl.when(e == pl.num_programs(0) - 1)
    def _():
        give_rows(picks_ref, rows_ref, results, slot_count, 512)


def per_expert(*shape):
    return pl.BlockSpec((1,) + shape, lambda e: (e,) + (0,) * len(shape))


def resident(*shape):
    return pl.BlockSpec(shape, lambda e: (0,) * len(shape), pipeline_mode=pl.Buffered(1))


def cot_chunk(picks, w_down, blocks, slot_count):
    experts, hidden, width = w_down.shape
    count, tokens = len(blocks), blocks[0].shape[0]
    rows = count * slot_count
    return pl.pallas_call(
        functools.partial(cot_kernel, count, slot_count),
        grid=(experts,),
        in_specs=[resident(*picks.shape), per_expert(hidden, width)] + [resident(tokens, width)] * count,
        out_specs=[per_expert(rows, width), per_expert(rows, hidden)],
        out_shape=[
            jax.ShapeDtypeStruct((experts, rows, width), BF16),
            jax.ShapeDtypeStruct((experts, rows, hidden), F32),
        ],
        scratch_shapes=[pltpu.VMEM((experts, rows, width), BF16)],
        compiler_params=pltpu.CompilerParams(vmem_limit_bytes=VMEM_GRANT),
        cost_estimate=pl.CostEstimate(
            flops=2 * experts * rows * width * (hidden + tokens),
            bytes_accessed=2 * (count * tokens * width + experts * (rows + hidden) * width),
            transcendentals=0,
        ),
    )(picks, w_down, *blocks)


def main_chunk(picks, gates, cot_acts, w_gate, w_up, blocks, slot_count):
    experts, width, hidden = w_gate.shape
    count, tokens = len(blocks), blocks[0].shape[0]
    rows = count * slot_count
    outs = pl.pallas_call(
        functools.partial(main_kernel, count, slot_count),
        grid=(experts,),
        in_specs=[
            resident(*picks.shape),
            resident(*gates.shape),
            per_expert(rows, hidden),
            per_expert(width, hidden),
            per_expert(width, hidden),
        ]
        + [resident(tokens, width)] * count,
        out_specs=[
            per_expert(rows, width),
            per_expert(rows, hidden),
            per_expert(rows, hidden),
            per_expert(rows, hidden),
            resident(*gates.shape),
        ]
        + [resident(count // 2, tokens, width)] * 2,
        out_shape=[
            jax.ShapeDtypeStruct((experts, rows, width), BF16),
            jax.ShapeDtypeStruct((experts, rows, hidden), BF16),
            jax.ShapeDtypeStruct((experts, rows, hidden), BF16),
            jax.ShapeDtypeStruct((experts, rows, hidden), BF16),
            jax.ShapeDtypeStruct(gates.shape, F32),
        ]
        + [jax.ShapeDtypeStruct((count // 2, tokens, width), BF16)] * 2,
        scratch_shapes=[pltpu.VMEM((experts, rows, width), BF16)],
        compiler_params=pltpu.CompilerParams(vmem_limit_bytes=VMEM_GRANT),
        cost_estimate=pl.CostEstimate(
            flops=2 * experts * rows * width * (4 * hidden + 2 * tokens),
            bytes_accessed=2 * (2 * count * tokens * width + experts * (rows + 2 * hidden) * width),
            transcendentals=experts * rows * hidden,
        ),
    )(picks, gates, cot_acts, w_gate, w_up, *blocks)
    return outs[:5], outs[5:]


def out_chunk(picks, scaled, w_down, slot_count):
    experts, hidden, width = w_down.shape
    count, _, tokens = picks.shape
    rows = count * slot_count
    return pl.pallas_call(
        functools.partial(out_kernel, count, slot_count),
        grid=(experts,),
        in_specs=[resident(*picks.shape), per_expert(rows, hidden), per_expert(hidden, width)],
        out_specs=[resident(count // 2, tokens, width)] * 2,
        out_shape=[jax.ShapeDtypeStruct((count // 2, tokens, width), BF16)] * 2,
        scratch_shapes=[pltpu.VMEM((experts, rows, width), BF16)],
        compiler_params=pltpu.CompilerParams(vmem_limit_bytes=VMEM_GRANT),
        cost_estimate=pl.CostEstimate(
            flops=2 * experts * rows * width * (hidden + tokens),
            bytes_accessed=2 * (count * tokens * width + experts * (rows + hidden) * width),
            transcendentals=0,
        ),
    )(picks, scaled, w_down)


def grad_kernel(count, *refs):
    rows, cots, scaled, d_gate, d_up = (refs[i * count : (i + 1) * count] for i in range(5))
    gate_out, up_out, down_out = refs[-3:]

    def total(lefts, rights):
        value = None
        for left, right in zip(lefts, rights):
            term = contract_rows(left[0], right[0])
            value = term if value is None else value + term
        return value

    gate_out[0] = total(rows, d_gate)
    up_out[0] = total(rows, d_up)
    down_out[0] = total(scaled, cots)


def expert_grads(rows, cots, scaled, d_gate, d_up, first, last, earlier=None, tile=512):
    count, experts, width = len(rows), rows[0].shape[0], rows[0].shape[2]
    hidden = scaled[0].shape[2]
    slots = sum(part.shape[1] for part in rows)
    wide = [pl.BlockSpec((1, part.shape[1], tile), lambda e, n: (first + e, 0, n)) for part in rows]
    narrow = [pl.BlockSpec((1, part.shape[1], hidden), lambda e, n: (first + e, 0, 0)) for part in rows]
    tall = pl.BlockSpec((1, tile, hidden), lambda e, n: (first + e, n, 0))
    given = [] if earlier is None else list(earlier)
    return pl.pallas_call(
        functools.partial(grad_kernel, count),
        grid=(last - first, width // tile),
        in_specs=wide * 2 + narrow * 3 + [pl.BlockSpec(memory_space=pl.ANY)] * len(given),
        out_specs=[tall, tall, pl.BlockSpec((1, hidden, tile), lambda e, n: (first + e, 0, n))],
        out_shape=[
            jax.ShapeDtypeStruct((experts, width, hidden), F32),
            jax.ShapeDtypeStruct((experts, width, hidden), F32),
            jax.ShapeDtypeStruct((experts, hidden, width), F32),
        ],
        input_output_aliases={5 * count + i: i for i in range(len(given))},
        compiler_params=pltpu.CompilerParams(vmem_limit_bytes=VMEM_GRANT),
        cost_estimate=pl.CostEstimate(
            flops=6 * (last - first) * slots * width * hidden,
            bytes_accessed=(last - first) * (4 * slots * width + 12 * width * hidden),
            transcendentals=0,
        ),
    )(*rows, *cots, *scaled, *d_gate, *d_up, *given)


def qkv_kernel(*refs):
    blocks, (q_w, k_w, v_w, q_out, k_out, v_out, q_sq, k_sq) = refs[:-8], refs[-8:]
    lanes = q_sq.shape[1]
    rows = blocks[0].shape[0]
    for b, block in enumerate(blocks):
        here = pl.ds(b * rows, rows)
        for weight, out, squares in ((q_w, q_out, q_sq), (k_w, k_out, k_sq)):
            value = nn(block[...], weight[...])
            out[here, :] = value
            value = value * value
            total = value[:, :lanes]
            for low in range(lanes, value.shape[1], lanes):
                total = total + value[:, low : low + lanes]

            @pl.when(pl.program_id(0) == 0)
            def _(squares=squares, total=total):
                squares[here, :] = total

            @pl.when(pl.program_id(0) > 0)
            def _(squares=squares, total=total):
                squares[here, :] += total

        v_out[here, :] = nn(block[...], v_w[...]).astype(BF16)


def qkv(blocks, w_query, w_key, w_value, tile=256):
    rows, depth = blocks[0].shape
    width = w_query.shape[1]
    count = len(blocks) * rows
    weight = pl.BlockSpec((depth, tile), lambda n: (0, n))
    out = pl.BlockSpec((count, tile), lambda n: (0, n))
    return pl.pallas_call(
        qkv_kernel,
        grid=(width // tile,),
        in_specs=[resident(rows, depth)] * len(blocks) + [weight] * 3,
        out_specs=[out] * 3 + [resident(count, HDIM)] * 2,
        out_shape=[
            jax.ShapeDtypeStruct((count, width), F32),
            jax.ShapeDtypeStruct((count, width), F32),
            jax.ShapeDtypeStruct((count, width), BF16),
            jax.ShapeDtypeStruct((count, HDIM), F32),
            jax.ShapeDtypeStruct((count, HDIM), F32),
        ],
        compiler_params=pltpu.CompilerParams(vmem_limit_bytes=VMEM_GRANT),
        cost_estimate=pl.CostEstimate(
            flops=6 * count * depth * width,
            bytes_accessed=2 * count * depth + 6 * depth * width + 10 * count * width,
            transcendentals=0,
        ),
    )(*blocks, w_query, w_key, w_value)


def pair_kernel(near_ref, far_ref, *outs):
    for b, out in enumerate(outs):
        out[...] = (near_ref[b].astype(F32) + far_ref[b].astype(F32)).astype(BF16)


def pair_sum(near, far, tile=64):
    count, rows, width = near.shape
    stack = pl.BlockSpec((count, tile, width), lambda i: (0, i, 0))
    return pl.pallas_call(
        pair_kernel,
        grid=(rows // tile,),
        in_specs=[stack, stack],
        out_specs=[pl.BlockSpec((tile, width), lambda i: (i, 0))] * count,
        out_shape=[jax.ShapeDtypeStruct((rows, width), BF16)] * count,
        compiler_params=pltpu.CompilerParams(vmem_limit_bytes=VMEM_GRANT),
        cost_estimate=pl.CostEstimate(
            flops=count * rows * width, bytes_accessed=6 * count * rows * width, transcendentals=0
        ),
    )(near, far)


def turn(values, cosine, sine):
    return values * cosine + pltpu.roll(values, values.shape[1] // 2, 1) * sine


def attend_kernel(
    row_block, scale, q_ref, k_ref, v_ref, cols_ref, qg_ref, kg_ref, cos_ref, sin_ref, kpos_ref,
    out_ref, lse_ref, qrot_ref, krot_ref,
):
    cosine, sine = cos_ref[...], sin_ref[...]
    qrot_ref[...] = turn(q_ref[...] * cols_ref[:, 0:1] * qg_ref[...], cosine, sine).astype(BF16)
    krot_ref[...] = turn(k_ref[...] * cols_ref[:, 1:2] * kg_ref[...], cosine, sine).astype(BF16)
    for low in range(0, q_ref.shape[0], row_block):
        rows = pl.ds(low, row_block)
        scores = nt(qrot_ref[rows, :], krot_ref[...]) * scale
        scores = jnp.where(kpos_ref[...] <= cols_ref[rows, 2:3], scores, -1e30)
        top = jnp.max(scores, axis=1, keepdims=True)
        powers = jnp.exp(scores - top)
        total = jnp.sum(powers, axis=1, keepdims=True)
        soft = (powers * (1.0 / total)).astype(BF16)
        out_ref[rows, :] = nn(soft, v_ref[...]).astype(BF16)
        lse_ref[rows, :] = jnp.broadcast_to(top + jnp.log(total), (row_block, HDIM))


def attend_back_kernel(
    row_block, scale, q_ref, k_ref, v_ref, qrot_ref, krot_ref, do_ref, lse_ref, cols_ref, qg_ref, kg_ref,
    cos_ref, sin_ref, kpos_ref,
    dq_ref, dk_ref, dv_ref, qgain_ref, kgain_ref, qin_ref, kin_ref, dq_acc, dk_acc, dv_acc,
):
    for low in range(0, q_ref.shape[0], row_block):
        rows = pl.ds(low, row_block)
        query, d_out = qrot_ref[rows, :], do_ref[rows, :]
        scores = nt(query, krot_ref[...]) * scale
        soft = jnp.where(kpos_ref[...] <= cols_ref[rows, 2:3], jnp.exp(scores - lse_ref[rows, 0:1]), 0.0)
        d_weights = nt(d_out, v_ref[...])
        spread = soft * d_weights
        mean = jnp.sum(spread, axis=1, keepdims=True)
        d_scores = (spread - soft * mean).astype(BF16)
        dq_acc[rows, :] = nn(d_scores, krot_ref[...]) * scale
        d_keys = contract_rows(d_scores, query)
        d_values = contract_rows(soft.astype(BF16), d_out)
        if low:
            dk_acc[...] += d_keys
            dv_acc[...] += d_values
        else:
            dk_acc[...] = d_keys
            dv_acc[...] = d_values
    dv_ref[...] = dv_acc[...].astype(BF16)
    cosine, sine = cos_ref[...], -sin_ref[...]
    for lane, raw_ref, gain_ref, grad, hat_ref, gain_out, inner_out in (
        (0, q_ref, qg_ref, dq_acc[...], dq_ref, qgain_ref, qin_ref),
        (1, k_ref, kg_ref, dk_acc[...] * scale, dk_ref, kgain_ref, kin_ref),
    ):
        hat = raw_ref[...] * cols_ref[:, lane : lane + 1]
        turned = turn(grad, cosine, sine)
        gain_out[...] = jnp.sum(turned * hat, axis=0, keepdims=True)
        d_hat = turned * gain_ref[...]
        hat_ref[...] = d_hat
        inner = d_hat * hat

        @pl.when(pl.program_id(0) == 0)
        def _(inner=inner, inner_out=inner_out):
            inner_out[...] = inner

        @pl.when(pl.program_id(0) > 0)
        def _(inner=inner, inner_out=inner_out):
            inner_out[...] += inner


def head_columns(rows):
    return pl.BlockSpec((rows, HDIM), lambda h: (0, h))


def whole(*shape):
    return pl.BlockSpec(shape, lambda h: (0,) * len(shape))


def attend_forward(q_raw, k_raw, v_low, cols, q_gain, k_gain, cosine, sine, kpos):
    seq_len, width = q_raw.shape
    heads = width // HDIM
    part, one = head_columns(seq_len), head_columns(1)
    return pl.pallas_call(
        functools.partial(attend_kernel, min(256, seq_len), HDIM ** (-0.5)),
        grid=(heads,),
        in_specs=[part, part, part, whole(seq_len, HDIM), one, one]
        + [whole(seq_len, HDIM), whole(seq_len, HDIM), whole(1, seq_len)],
        out_specs=[part, part, part, part],
        out_shape=[
            jax.ShapeDtypeStruct((seq_len, width), BF16),
            jax.ShapeDtypeStruct((seq_len, width), F32),
            jax.ShapeDtypeStruct((seq_len, width), BF16),
            jax.ShapeDtypeStruct((seq_len, width), BF16),
        ],
        compiler_params=pltpu.CompilerParams(vmem_limit_bytes=VMEM_GRANT),
        cost_estimate=pl.CostEstimate(
            flops=4 * seq_len * seq_len * width,
            bytes_accessed=20 * seq_len * width,
            transcendentals=heads * seq_len * seq_len,
        ),
    )(q_raw, k_raw, v_low, cols, q_gain, k_gain, cosine, sine, kpos)


def attend_backward(
    q_raw, k_raw, v_low, q_rot, k_rot, d_out, lse, cols, q_gain, k_gain, cosine, sine, kpos
):
    seq_len, width = q_raw.shape
    heads = width // HDIM
    part, one = head_columns(seq_len), head_columns(1)
    return pl.pallas_call(
        functools.partial(attend_back_kernel, min(256, seq_len), HDIM ** (-0.5)),
        grid=(heads,),
        in_specs=[part, part, part, part, part, part, part, whole(seq_len, HDIM), one, one]
        + [whole(seq_len, HDIM), whole(seq_len, HDIM), whole(1, seq_len)],
        out_specs=[part, part, part, one, one, whole(seq_len, HDIM), whole(seq_len, HDIM)],
        out_shape=[
            jax.ShapeDtypeStruct((seq_len, width), F32),
            jax.ShapeDtypeStruct((seq_len, width), F32),
            jax.ShapeDtypeStruct((seq_len, width), BF16),
            jax.ShapeDtypeStruct((1, width), F32),
            jax.ShapeDtypeStruct((1, width), F32),
            jax.ShapeDtypeStruct((seq_len, HDIM), F32),
            jax.ShapeDtypeStruct((seq_len, HDIM), F32),
        ],
        scratch_shapes=[pltpu.VMEM((seq_len, HDIM), F32)] * 3,
        compiler_params=pltpu.CompilerParams(vmem_limit_bytes=VMEM_GRANT),
        cost_estimate=pl.CostEstimate(
            flops=10 * seq_len * seq_len * width,
            bytes_accessed=32 * seq_len * width,
            transcendentals=heads * seq_len * seq_len,
        ),
    )(q_raw, k_raw, v_low, q_rot, k_rot, d_out, lse, cols, q_gain, k_gain, cosine, sine, kpos)


def local_gathered(
    hidden_in,
    cotangent,
    seq_lengths,
    expert_ids,
    attn_gain,
    w_query,
    w_key,
    w_value,
    query_gain,
    key_gain,
    w_out,
    ffn_gain,
    w_router,
    w_gate,
    w_up,
    w_down,
):
    tensor_count = lax.axis_size("tensor")
    group_count = lax.axis_size("dp")
    tok_rows, model_width = hidden_in.shape
    topk = expert_ids.shape[1]
    expert_total = w_router.shape[1]
    experts = w_gate.shape[0]
    slot_count = tok_rows * topk // expert_total
    devices = len(PLACES)
    seq_len = tok_rows * tensor_count
    local_width = w_query.shape[1]
    half_width = HDIM // 2
    live_length = seq_lengths[0]
    absolute, position = place_indices()

    member = lax.axis_index("tensor")
    blocks_at = member ^ jnp.arange(tensor_count)
    cosine, sine = (
        table.reshape(tensor_count, tok_rows, half_width)[blocks_at].reshape(seq_len, half_width)
        for table in rope_tables(seq_len, HDIM)
    )
    cosine = jnp.concatenate([cosine, cosine], axis=1)
    sine = jnp.concatenate([-sine, sine], axis=1)
    positions = (blocks_at[:, None] * tok_rows + jnp.arange(tok_rows)[None, :]).reshape(-1)
    never = 2 * seq_len
    key_pos = jnp.where(positions < live_length, positions, never).astype(F32)[None, :]

    def token_sums(*values):
        stacked = jnp.stack([value.reshape(tensor_count, tok_rows) for value in values])
        summed = lax.psum(stacked[:, blocks_at], "tensor")
        return summed[:, blocks_at].reshape(len(values), seq_len)

    def to_groups(by_expert):
        copies = jnp.broadcast_to(
            by_expert.reshape(group_count, 1, experts, tok_rows),
            (group_count, tensor_count, experts, tok_rows),
        ).reshape(devices, experts, tok_rows)
        return lax.all_to_all(copies, BOTH, split_axis=0, concat_axis=0, tiled=True)[absolute]

    resid = hidden_in.astype(F32)
    scale_one = rms_scale(resid)
    normed = resid * scale_one
    attn_in = (normed * attn_gain.astype(F32)).astype(BF16)
    q_gain = query_gain.astype(F32)[None, :]
    k_gain = key_gain.astype(F32)[None, :]

    hot = jnp.any(expert_ids.T[None, :, :] == jnp.arange(expert_total)[:, None, None], axis=1)
    earlier = jnp.triu(jnp.ones((tok_rows, tok_rows), F32), 1).astype(BF16)
    rank = jnp.dot(hot.astype(BF16), earlier, preferred_element_type=F32)
    slot_of = to_groups(jnp.where(hot, rank, -1.0))
    slots = jnp.arange(slot_count, dtype=F32)
    picks_wide = (slot_of[:, :, None, :] == slots[None, None, :, None]).astype(BF16)
    picks = [
        picks_wide[low : low + len(chunk)].reshape(len(chunk), experts * slot_count, tok_rows)
        for chunk, low in zip(CHUNKS, STARTS)
    ]

    stages = Stages(attn_in)
    cot, ffn = Gather(cotangent), Gather(None)
    d_sum, out_sum = Scatter(), Scatter()
    order = range(len(CHUNKS))
    cot_rows, cot_acts, kept = {}, {}, {}

    def advance(works=(), extra=(), **hops):
        tables = {"cot": cot, "ffn": ffn, "d": d_sum, "out": out_sum}
        sends = list(extra)
        spans = []
        for name, moves in hops.items():
            spans.append((tables[name], moves, len(sends)))
            sends += tables[name].sends(moves)
        got, made = stages.run(sends, works)
        for table, moves, low in spans:
            table.take(moves, got[low : low + len(moves)])
        return got[: len(extra)], made

    def cot_work(i):
        values, crossing, late = cot.chunk(i)

        def work(picks_i, w_down_i, values, crossing):
            return cot_chunk(picks_i, w_down_i, Gather.complete(i, values, crossing, late), slot_count)

        return work, (picks[i], w_down, values, crossing)

    def cot_done(i, made):
        cot_rows[i], cot_acts[i] = made

    def main_work(i):
        values, crossing, late = ffn.chunk(i)

        def work(picks_i, gates_i, acts_i, gate_w, up_w, values, crossing):
            blocks = Gather.complete(i, values, crossing, late)
            return main_chunk(picks_i, gates_i, acts_i, gate_w, up_w, blocks, slot_count)

        gates_i = token_gates[STARTS[i] : STARTS[i] + len(CHUNKS[i])]
        return work, (picks[i], gates_i, cot_acts[i], w_gate, w_up, values, crossing)

    def out_work(i):
        def work(picks_i, scaled_i, w_down_i):
            return out_chunk(picks_i, scaled_i, w_down_i, slot_count)

        return work, (picks[i], kept[i][1], w_down)

    (across, mate), _ = advance(
        extra=[(attn_in, "y"), (attn_in, "c")], cot=[("z", (0, 0, 0)), ("x", (0, 0, 0))]
    )

    def project(block, mate, across, w_query, w_key, w_value):
        blocks = [block, mate, across, send(across, "c")]
        q_raw, k_raw, v_low, q_square, k_square = qkv(blocks, w_query, w_key, w_value)
        squares = token_sums(jnp.sum(q_square, axis=1), jnp.sum(k_square, axis=1))
        return jnp.concatenate(blocks, axis=0), q_raw, k_raw, v_low, squares

    _, (made,) = advance(
        [(project, (attn_in, mate, across, w_query, w_key, w_value))],
        cot=[("z", (1, 0, 0)), ("x", (1, 0, 0)), ("y", (0, 0, 0)), ("c", (0, 0, 0)), ("c", (1, 0, 0))],
    )
    gathered, q_raw, k_raw, v_low, squares = made

    def columns_of(squares):
        scales = lax.rsqrt(squares / model_width + EPS)
        columns = jnp.stack([scales[0], scales[1], positions.astype(F32)], axis=1)
        return jnp.pad(columns, ((0, 0), (0, HDIM - columns.shape[1])))

    cols = columns_of(squares)
    _, (made,) = advance(
        [(attend_forward, (q_raw, k_raw, v_low, cols, q_gain, k_gain, cosine, sine, key_pos))],
        cot=[("z", (2, 0, 0)), ("x", (2, 0, 0)), ("y", (1, 0, 0)), ("c", (0, 1, 0)), ("c", (0, 0, 1))],
    )
    o_low, lse, q_rot, k_rot = made

    def project_back(o_low, w_out):
        parts = [
            jnp.dot(o_low[r * tok_rows : (r + 1) * tok_rows], w_out, preferred_element_type=F32).astype(BF16)
            for r in range(tensor_count)
        ]
        across = add_low(parts[2], send(parts[3], "c"))
        return add_wide(parts[0], send(parts[1], "c")) + send(across, "y").astype(F32)

    _, (attn_rows, made) = advance(
        [(project_back, (o_low, w_out)), cot_work(0)],
        cot=[("x", (3, 0, 0)), ("c", (2, 0, 0)), ("c", (1, 1, 0))],
    )
    cot_done(0, made)
    mixed = resid + attn_rows
    scale_two = rms_scale(mixed)
    mixed_norm = mixed * scale_two
    ffn_in = (mixed_norm * ffn_gain.astype(F32)).astype(BF16)
    ffn.held[0, 0, 0, 0] = ffn_in

    def route(ffn_in, w_router):
        logits = jnp.dot(ffn_in, w_router, preferred_element_type=F32)
        router_probs = jax.nn.softmax(logits, axis=-1)
        return router_probs, to_groups(router_probs.T)

    _, ((router_probs, token_gates),) = advance(
        [(route, (ffn_in, w_router))],
        ffn=[("z", (0, 0, 0)), ("x", (0, 0, 0)), ("y", (0, 0, 0))],
        cot=[("c", (1, 0, 1)), ("c", (2, 1, 0))],
    )
    _, (made,) = advance(
        [cot_work(1)],
        ffn=[("z", (1, 0, 0)), ("x", (1, 0, 0)), ("y", (1, 0, 0))]
        + [("c", (0, 0, 0)), ("c", (0, 1, 0)), ("c", (1, 0, 0)), ("c", (0, 0, 1))],
    )
    cot_done(1, made)
    _, (made,) = advance(
        [main_work(0)],
        ffn=[("z", (2, 0, 0)), ("x", (2, 0, 0)), ("c", (2, 0, 0))],
        cot=[("y", (2, 0, 0)), ("c", (3, 0, 0))],
    )
    kept[0], near, far = made[0], *made[1]
    _, (made,) = advance(
        [(core_sum, (near, far))],
        ffn=[("x", (3, 0, 0)), ("c", (1, 1, 0)), ("c", (1, 0, 1)), ("c", (2, 1, 0))],
        cot=[("y", (3, 0, 0))],
    )
    d_sum.put(0, made)
    _, (made,) = advance(
        [main_work(1)],
        ffn=[("y", (2, 0, 0))],
        cot=[("x", (0, 0, 1)), ("c", (3, 1, 0)), ("c", (2, 0, 1))],
    )
    kept[1], near, far = made[0], *made[1]
    _, (made, other) = advance(
        [(core_sum, (near, far)), cot_work(2)],
        ffn=[("y", (3, 0, 0)), ("c", (3, 0, 0)), ("c", (3, 1, 0))],
        cot=[("x", (1, 0, 1))],
    )
    d_sum.put(1, made)
    cot_done(2, other)
    _, (made,) = advance(
        [main_work(2)],
        cot=[("x", (2, 0, 1)), ("y", (3, 1, 0)), ("c", (0, 1, 1))],
    )
    kept[2], near, far = made[0], *made[1]
    _, (made, other, third) = advance(
        [(core_sum, (near, far)), cot_work(3), cot_work(4)],
        ffn=[("x", (2, 0, 1)), ("y", (1, 1, 0))],
    )
    d_sum.put(2, made)
    cot_done(3, other)
    cot_done(4, third)
    _, (made,) = advance([main_work(3)], ffn=[("x", (3, 0, 1)), ("y", (0, 1, 0))])
    kept[3], near, far = made[0], *made[1]
    _, (made,) = advance([(core_sum, (near, far))], ffn=[("c", (0, 1, 1)), ("c", (3, 1, 1))])
    d_sum.put(3, made)

    def last_main(*args):
        saved, (near, far) = main_work_four[0](*args)
        return saved, core_sum(near, far)

    main_work_four = main_work(4)
    _, (made,) = advance([(last_main, main_work_four[1])], d=[("x", (1, 1, 1)), ("y", (2, 1, 1))])
    kept[4] = made[0]
    d_sum.put(4, made[1])

    def return_probs(*d_probs):
        d_probs = jnp.concatenate(d_probs, axis=0)[position]
        arrived = lax.all_to_all(d_probs, BOTH, split_axis=0, concat_axis=0, tiled=True)
        arrived = arrived.reshape(group_count, tensor_count, experts, tok_rows)
        return jnp.sum(arrived, axis=1).reshape(expert_total, tok_rows).T

    outs = {}
    _, (outs[0], d_probs) = advance(
        [out_work(0), (return_probs, tuple(kept[i][4] for i in order))],
        d=[("x", (3, 1, 1)), ("y", (0, 1, 1))],
    )
    _, (outs[1], made) = advance(
        [out_work(1), (core_sum, tuple(outs[0]))], d=[("x", (1, 1, 0)), ("y", (1, 0, 1))]
    )
    out_sum.put(0, made)
    _, (outs[2], made) = advance(
        [out_work(2), (core_sum, tuple(outs[1]))],
        d=[("x", (2, 1, 0)), ("y", (2, 0, 1)), ("z", (1, 0, 0))],
    )
    out_sum.put(1, made)
    _, (outs[3], outs[4], made) = advance(
        [out_work(3), out_work(4), (core_sum, tuple(outs[2]))],
        d=[("x", (3, 1, 0)), ("y", (3, 0, 1)), ("z", (2, 0, 0))],
    )
    out_sum.put(2, made)
    _, (made, other) = advance(
        [(core_sum, tuple(outs[3])), (core_sum, tuple(outs[4]))],
        d=[("x", (0, 1, 0)), ("y", (0, 0, 1)), ("z", (3, 0, 0))],
    )
    out_sum.put(3, made)
    out_sum.put(4, other)
    d_ffn = d_sum.total()

    d_result = cotangent.astype(F32)
    d_logits = (
        router_probs * (d_probs - jnp.sum(router_probs * d_probs, axis=-1, keepdims=True))
    ).astype(BF16)
    router_part = contract_rows(d_logits, ffn_in)
    d_ffn = d_ffn + times_transpose(d_logits, w_router)
    ffn_gain_part = jnp.sum(d_ffn * mixed_norm, axis=0)
    d_norm_two = d_ffn * ffn_gain.astype(F32)
    d_mixed = d_result + scale_two * (
        d_norm_two - mixed_norm * jnp.mean(d_norm_two * mixed_norm, axis=-1, keepdims=True)
    )
    d_attn = d_mixed.astype(BF16)
    router_sums = jnp.concatenate(
        [router_part, jnp.broadcast_to(ffn_gain_part[None, :], (8, model_width))], axis=0
    )

    (across, mate, other), _ = advance(
        extra=[(d_attn, "y"), (d_attn, "c"), (router_sums, "z1")], out=[("x", (1, 1, 1))]
    )
    router_sums = router_sums + other

    def attend_back(d_attn, mate, across, o_low, w_out, gathered, *rest):
        d_attn_all = jnp.concatenate([d_attn, mate, across, send(across, "c")], axis=0)
        d_attended = times_transpose(d_attn_all, w_out).astype(BF16)
        q_raw, k_raw, v_low, q_rot, k_rot, lse, cols = rest
        made = attend_backward(
            q_raw, k_raw, v_low, q_rot, k_rot, d_attended, lse, cols, q_gain, k_gain, cosine, sine, key_pos
        )
        return made, contract_rows(o_low, d_attn_all).astype(BF16), contract_rows(gathered, made[2]).astype(BF16)

    _, (made,) = advance(
        [
            (
                attend_back,
                (d_attn, mate, across, o_low, w_out, gathered, q_raw, k_raw, v_low, q_rot, k_rot, lse, cols),
            )
        ],
        out=[("x", (3, 1, 1)), ("x", (1, 1, 0)), ("y", (2, 1, 1)), ("y", (0, 1, 1))],
    )
    (dq_hat, dk_hat, dv_raw, query_gain_part, key_gain_part, q_inner, k_inner), grad_w_out, grad_value = made
    grad_w_out, grad_value = lax.psum((grad_w_out, grad_value), "dp")

    def norm_back(q_raw, k_raw, cols, dq_hat, dk_hat, q_inner, k_inner):
        inner = token_sums(jnp.sum(q_inner, axis=1), jnp.sum(k_inner, axis=1)) / model_width
        raws = []
        for n, (raw, d_hat) in enumerate(((q_raw, dq_hat), (k_raw, dk_hat))):
            scale = cols[:, n : n + 1]
            raws.append((scale * (d_hat - raw * scale * inner[n][:, None])).astype(BF16))
        return raws

    (other,), ((dq_raw, dk_raw),) = advance(
        [(norm_back, (q_raw, k_raw, cols, dq_hat, dk_hat, q_inner, k_inner))],
        extra=[(router_sums, "z2")],
        out=[("x", (3, 1, 0)), ("y", (1, 0, 1))],
    )
    router_sums = router_sums + other

    def projections_back(gathered, dq_raw, dk_raw, dv_raw, w_query, w_key, w_value):
        grads = [contract_rows(gathered, part).astype(BF16) for part in (dk_raw, dq_raw)]
        total_term = times_transpose(dq_raw, w_query)
        total_term = total_term + times_transpose(dk_raw, w_key)
        total_term = (total_term + times_transpose(dv_raw, w_value)).astype(BF16)
        return grads, total_term

    (other,), (((grad_key, grad_query), total_term),) = advance(
        [(projections_back, (gathered, dq_raw, dk_raw, dv_raw, w_query, w_key, w_value))],
        extra=[(router_sums, "c")],
        out=[("x", (2, 1, 0)), ("y", (2, 0, 1)), ("z", (1, 0, 0))],
    )
    router_sums = router_sums + other

    key_sum, query_sum = DpSum(grad_key), DpSum(grad_query)

    def saved(n):
        return [kept[i][n] for i in order]

    def grads_of(first, last, earlier=None):
        all_cots = [cot_rows[i] for i in order]

        def work(*args):
            return expert_grads(*args[:5], first, last, args[5] if len(args) > 5 else None)

        args = (saved(0), all_cots, saved(1), saved(2), saved(3))
        return work, args if earlier is None else args + (earlier,)

    thirds = [experts * n // 3 for n in range(4)]
    parts = jnp.split(total_term, tensor_count, axis=0)
    (d_far, d_near, *got), _ = advance(
        extra=[(parts[3], "c"), (parts[1], "c")] + key_sum.split_x(), out=[("y", (3, 0, 1))]
    )
    key_sum.add_x(got)
    (d_across, *got), (made,) = advance(
        [grads_of(thirds[0], thirds[1])],
        extra=[(add_low(parts[2], d_far), "y")] + query_sum.split_x() + key_sum.split_z(),
    )
    query_sum.add_x(got[:1])
    key_sum.add_z(got[1:])
    d_attn_in = add_wide(parts[0], d_near, d_across)
    attn_gain_part = jnp.sum(d_attn_in * normed, axis=0)
    d_norm_one = d_attn_in * attn_gain.astype(F32)
    d_input = d_mixed + scale_one * (
        d_norm_one - normed * jnp.mean(d_norm_one * normed, axis=-1, keepdims=True)
    )
    got, (made,) = advance(
        [grads_of(thirds[1], thirds[2], made)], extra=key_sum.join_z(), out=[("x", (0, 1, 0)), ("y", (0, 0, 1))]
    )
    key_sum.took_z(got)
    (other, *got), ((grad_w_gate, grad_w_up, grad_w_down),) = advance(
        [grads_of(thirds[2], thirds[3], made)],
        extra=[(router_sums, "y")] + key_sum.join_x() + query_sum.split_z(),
    )
    router_sums = router_sums + other
    key_sum.took_x(got[:1])
    query_sum.add_z(got[1:])
    (other, *got), _ = advance(
        extra=[(attn_gain_part, "c")] + query_sum.join_z(), out=[("z", (2, 0, 0))]
    )
    attn_gain_part = attn_gain_part + other
    query_sum.took_z(got)
    (other, third, *got), _ = advance(
        extra=[(attn_gain_part, "y"), (router_sums, "x")] + query_sum.join_x(), out=[("z", (3, 0, 0))]
    )
    query_sum.took_x(got)
    router_sums = router_sums + third
    gain_sums = small_sum(
        jnp.concatenate([attn_gain_part + other, query_gain_part[0], key_gain_part[0]]), ("x", "z1", "z2")
    )
    result = mixed + out_sum.total()
    return (
        result.astype(BF16),
        d_input.astype(BF16),
        query_sum.result,
        key_sum.result,
        grad_value.astype(F32),
        gain_sums[model_width : model_width + local_width],
        gain_sums[model_width + local_width :],
        grad_w_out.astype(F32),
        gain_sums[:model_width],
        router_sums[expert_total],
        router_sums[:expert_total].T,
        grad_w_gate,
        grad_w_up,
        grad_w_down,
    )


def local_sent(
    hidden_in,
    cotangent,
    seq_lengths,
    expert_ids,
    attn_gain,
    w_query,
    w_key,
    w_value,
    query_gain,
    key_gain,
    w_out,
    ffn_gain,
    w_router,
    w_gate,
    w_up,
    w_down,
):
    tensor_count = lax.axis_size("tensor")
    group_count = lax.axis_size("dp")
    device_total = tensor_count * group_count
    tok_rows, model_width = hidden_in.shape
    topk_count = expert_ids.shape[1]
    local_experts = w_gate.shape[0]
    expert_total = w_router.shape[1]
    slot_count = tok_rows * topk_count // expert_total
    per_group = local_experts * slot_count
    seq_len = tok_rows * tensor_count
    local_width = w_query.shape[1]
    head_width = HDIM
    local_heads = local_width // head_width
    block_rows = min(512, seq_len)
    block_count = seq_len // block_rows
    score_scale = head_width ** (-0.5)
    live_length = seq_lengths[0]
    cosine, sine_table = (table[:, None, :] for table in rope_tables(seq_len, head_width))
    key_pos = jnp.arange(seq_len)
    key_live = key_pos < live_length

    def send_out(rows_low):
        grouped_rows = rows_low.reshape(group_count, 1, per_group, model_width)
        copies = jnp.broadcast_to(
            grouped_rows, (group_count, tensor_count, per_group, model_width)
        ).reshape(device_total, per_group, model_width)
        arrived = lax.all_to_all(copies, ("dp", "tensor"), split_axis=0, concat_axis=0, tiled=True)
        return arrived.reshape(device_total, local_experts, slot_count, model_width)

    def send_back(parts_low):
        returned = lax.all_to_all(
            parts_low.reshape(device_total, per_group, model_width),
            ("dp", "tensor"),
            split_axis=0,
            concat_axis=0,
            tiled=True,
        )
        return jnp.sum(
            returned.reshape(group_count, tensor_count, per_group, model_width).astype(F32),
            axis=1,
        ).reshape(-1, model_width)

    resid = hidden_in.astype(F32)
    scale_one = rms_scale(resid)
    normed = resid * scale_one
    attn_in = (normed * attn_gain.astype(F32)).astype(BF16)
    gathered = lax.all_gather(attn_in, "tensor", axis=0, tiled=True)
    q_raw = jnp.dot(gathered, w_query, preferred_element_type=F32)
    k_raw = jnp.dot(gathered, w_key, preferred_element_type=F32)
    v_raw = jnp.dot(gathered, w_value, preferred_element_type=F32)
    q_square, k_square = lax.psum(
        (jnp.sum(q_raw * q_raw, axis=1), jnp.sum(k_raw * k_raw, axis=1)), "tensor"
    )
    q_rscale = lax.rsqrt(q_square / model_width + EPS)[:, None]
    k_rscale = lax.rsqrt(k_square / model_width + EPS)[:, None]
    query_hat = q_raw * q_rscale
    key_hat = k_raw * k_rscale
    q_gain = query_gain.astype(F32)
    k_gain = key_gain.astype(F32)
    q_rot = rotate(
        (query_hat * q_gain).reshape(seq_len, local_heads, head_width), cosine, sine_table
    ).astype(BF16)
    k_rot = rotate(
        (key_hat * k_gain).reshape(seq_len, local_heads, head_width), cosine, sine_table
    ).astype(BF16)
    v_low = v_raw.astype(BF16).reshape(seq_len, local_heads, head_width)
    starts = jnp.arange(block_count) * block_rows
    q_blocks = q_rot.reshape(block_count, block_rows, local_heads, head_width)

    def allowed_mask(row_start):
        q_pos = row_start + jnp.arange(block_rows)
        return ((key_pos[None, :] <= q_pos[:, None]) & key_live[None, :])[None]

    def attend(inputs):
        q_block, row_start = inputs
        scores = (
            jnp.einsum("qhd,khd->hqk", q_block, k_rot, preferred_element_type=F32)
            * score_scale
        )
        scores = jnp.where(allowed_mask(row_start), scores, -1e30)
        row_max = jnp.max(scores, axis=-1, keepdims=True)
        exp_scores = jnp.exp(scores - row_max)
        row_total = jnp.sum(exp_scores, axis=-1, keepdims=True)
        soft_low = (exp_scores / row_total).astype(BF16)
        attended = jnp.einsum("hqk,khd->qhd", soft_low, v_low, preferred_element_type=F32)
        return (attended, (row_max + jnp.log(row_total))[..., 0])

    o_blocks, lse_blocks = lax.map(attend, (q_blocks, starts))
    o_low = o_blocks.reshape(seq_len, local_width).astype(BF16)
    attn_rows = lax.psum_scatter(
        jnp.dot(o_low, w_out, preferred_element_type=F32),
        "tensor",
        scatter_dimension=0,
        tiled=True,
    )
    mixed = resid + attn_rows
    scale_two = rms_scale(mixed)
    mixed_norm = mixed * scale_two
    ffn_in = (mixed_norm * ffn_gain.astype(F32)).astype(BF16)
    logits = jnp.dot(ffn_in, w_router, preferred_element_type=F32)
    router_probs = jax.nn.softmax(logits, axis=-1)
    expert_hot = (expert_ids[:, :, None] == jnp.arange(expert_total)[None, None, :]).astype(
        F32
    )
    gate_values = jnp.einsum("tke,te->tk", expert_hot, router_probs)
    flat_ids = expert_ids.reshape(-1)
    sort_order = jnp.argsort(flat_ids, stable=True)
    inverse = jnp.argsort(sort_order)
    expert_in = send_out(ffn_in[sort_order // topk_count])
    gate_pre = jnp.einsum("secd,edf->secf", expert_in, w_gate, preferred_element_type=F32)
    up_pre = jnp.einsum("secd,edf->secf", expert_in, w_up, preferred_element_type=F32)
    silu_gate = jax.nn.silu(gate_pre)
    acts = (silu_gate * up_pre).astype(BF16)
    partial_value = jnp.einsum(
        "secf,efd->secd", acts, w_down, preferred_element_type=F32
    ).astype(BF16)
    out_sorted = send_back(partial_value)
    out_assign = out_sorted[inverse].reshape(tok_rows, topk_count, model_width)
    expert_mix = jnp.einsum("tk,tkd->td", gate_values, out_assign)
    result = mixed + expert_mix
    d_result = cotangent.astype(F32)
    d_gates = jnp.einsum("tkd,td->tk", out_assign, d_result)
    d_out = (
        (gate_values[:, :, None] * d_result[:, None, :])
        .astype(BF16)
        .reshape(-1, model_width)[sort_order]
    )
    d_arrived = send_out(d_out)
    d_acts = jnp.einsum("secd,efd->secf", d_arrived, w_down, preferred_element_type=F32)
    sigmoid_gate = jax.nn.sigmoid(gate_pre)
    d_gate_pre = (d_acts * up_pre * sigmoid_gate * (1.0 + gate_pre * (1.0 - sigmoid_gate))).astype(
        BF16
    )
    d_up_pre = (d_acts * silu_gate).astype(BF16)
    grad_w_down = jnp.einsum("secf,secd->efd", acts, d_arrived, preferred_element_type=F32)
    grad_w_gate = jnp.einsum(
        "secd,secf->edf", expert_in, d_gate_pre, preferred_element_type=F32
    )
    grad_w_up = jnp.einsum(
        "secd,secf->edf", expert_in, d_up_pre, preferred_element_type=F32
    )
    d_rows = (
        jnp.einsum("secf,edf->secd", d_gate_pre, w_gate, preferred_element_type=F32)
        + jnp.einsum("secf,edf->secd", d_up_pre, w_up, preferred_element_type=F32)
    ).astype(BF16)
    d_sorted = send_back(d_rows)
    d_ffn = jnp.sum(d_sorted[inverse].reshape(tok_rows, topk_count, model_width), axis=1)
    d_probs = jnp.einsum("tk,tke->te", d_gates, expert_hot)
    d_logits = (
        router_probs * (d_probs - jnp.sum(router_probs * d_probs, axis=-1, keepdims=True))
    ).astype(BF16)
    router_part = contract_rows(ffn_in, d_logits)
    d_ffn = d_ffn + times_transpose(d_logits, w_router)
    ffn_gain_part = jnp.sum(d_ffn * mixed_norm, axis=0)
    d_norm_two = d_ffn * ffn_gain.astype(F32)
    d_mixed = d_result + scale_two * (
        d_norm_two - mixed_norm * jnp.mean(d_norm_two * mixed_norm, axis=-1, keepdims=True)
    )
    d_attn = d_mixed.astype(BF16)
    d_attn_all = lax.all_gather(d_attn, "tensor", axis=0, tiled=True)
    grad_w_out = contract_rows(o_low, d_attn_all)
    d_attended = (
        times_transpose(d_attn_all, w_out)
        .astype(BF16)
        .reshape(block_count, block_rows, local_heads, head_width)
    )

    def attend_back(carry, inputs):
        dk_total, dv_total = carry
        q_block, do_block, lse_block, row_start = inputs
        scores = (
            jnp.einsum("qhd,khd->hqk", q_block, k_rot, preferred_element_type=F32)
            * score_scale
        )
        allowed = allowed_mask(row_start)
        scores = jnp.where(allowed, scores, -1e30)
        soft = jnp.where(allowed, jnp.exp(scores - lse_block[..., None]), 0.0)
        d_weights = jnp.einsum("qhd,khd->hqk", do_block, v_low, preferred_element_type=F32)
        d_scores = (soft * (d_weights - jnp.sum(soft * d_weights, axis=-1, keepdims=True))).astype(
            BF16
        )
        dq_block = (
            jnp.einsum("hqk,khd->qhd", d_scores, k_rot, preferred_element_type=F32)
            * score_scale
        )
        dk_total = (
            dk_total
            + jnp.einsum("hqk,qhd->khd", d_scores, q_block, preferred_element_type=F32)
            * score_scale
        )
        dv_total = dv_total + jnp.einsum(
            "hqk,qhd->khd", soft.astype(BF16), do_block, preferred_element_type=F32
        )
        return ((dk_total, dv_total), dq_block)

    zero_field = jnp.zeros((seq_len, local_heads, head_width), F32)
    (dk_rot, dv_full), dq_blocks = lax.scan(
        attend_back, (zero_field, zero_field), (q_blocks, d_attended, lse_blocks, starts)
    )
    dq_gain = unrotate(
        dq_blocks.reshape(seq_len, local_heads, head_width), cosine, sine_table
    ).reshape(seq_len, local_width)
    dk_gain = unrotate(dk_rot, cosine, sine_table).reshape(seq_len, local_width)
    query_gain_part = jnp.sum(dq_gain * query_hat, axis=0)
    key_gain_part = jnp.sum(dk_gain * key_hat, axis=0)
    dq_hat = dq_gain * q_gain
    dk_hat = dk_gain * k_gain
    q_inner, k_inner = lax.psum(
        (jnp.sum(dq_hat * query_hat, axis=1), jnp.sum(dk_hat * key_hat, axis=1)), "tensor"
    )
    dq_raw = (q_rscale * (dq_hat - query_hat * (q_inner / model_width)[:, None])).astype(
        BF16
    )
    dk_raw = (k_rscale * (dk_hat - key_hat * (k_inner / model_width)[:, None])).astype(BF16)
    dv_raw = dv_full.reshape(seq_len, local_width).astype(BF16)
    grad_query = contract_rows(gathered, dq_raw)
    grad_key = contract_rows(gathered, dk_raw)
    grad_value = contract_rows(gathered, dv_raw)
    total_term = times_transpose(dq_raw, w_query)
    total_term = total_term + times_transpose(dk_raw, w_key)
    d_attn_in = lax.psum_scatter(
        (total_term + times_transpose(dv_raw, w_value)).astype(BF16),
        "tensor",
        scatter_dimension=0,
        tiled=True,
    ).astype(F32)
    attn_gain_part = jnp.sum(d_attn_in * normed, axis=0)
    d_norm_one = d_attn_in * attn_gain.astype(F32)
    d_input = d_mixed + scale_one * (
        d_norm_one - normed * jnp.mean(d_norm_one * normed, axis=-1, keepdims=True)
    )
    dp_sums = (
        lax.psum(grad_query.astype(BF16), "dp").astype(F32),
        lax.psum(grad_key.astype(BF16), "dp").astype(F32),
        lax.psum(grad_value.astype(BF16), "dp").astype(F32),
        lax.psum(query_gain_part.astype(BF16), "dp").astype(F32),
        lax.psum(key_gain_part.astype(BF16), "dp").astype(F32),
        lax.psum(grad_w_out.astype(BF16), "dp").astype(F32),
    )
    shared = lax.psum((attn_gain_part, ffn_gain_part, router_part), ("dp", "tensor"))
    return (
        result.astype(BF16),
        d_input.astype(BF16),
        dp_sums[0],
        dp_sums[1],
        dp_sums[2],
        dp_sums[3],
        dp_sums[4],
        dp_sums[5],
        shared[0],
        shared[1],
        shared[2],
        grad_w_gate,
        grad_w_up,
        grad_w_down,
    )


def solution(mesh):
    rows, columns = P(BOTH, None), P(None, "tensor")
    gathered_plan = (mesh.shape["dp"], mesh.shape["tensor"]) == (2 * RING, 4)
    return jax.shard_map(
        local_gathered if gathered_plan else local_sent,
        mesh=mesh,
        in_specs=(
            rows,
            rows,
            P("dp"),
            rows,
            P(),
            columns,
            columns,
            columns,
            P("tensor"),
            P("tensor"),
            P("tensor", None),
            P(),
            P(),
            P("dp", None, "tensor"),
            P("dp", None, "tensor"),
            P("dp", "tensor", None),
        ),
        out_specs=(
            rows,
            rows,
            columns,
            columns,
            columns,
            P("tensor"),
            P("tensor"),
            P("tensor", None),
            P(),
            P(),
            P(),
            P("dp", None, "tensor"),
            P("dp", None, "tensor"),
            P("dp", "tensor", None),
        ),
        check_vma=False,
    )
```

time: 4010 us -> 1150 us (0.29)
  waiting for transfers between devices: 3140 us -> 306 us
  Pallas kernels: 0 us -> 426 us
  matrix products: 322 us -> 49.9 us
  local copies, waits for them, and re-layouts: 202 us -> 48.5 us
  blocking collectives: 74.4 us -> 12.9 us
  starting transfers between devices: 102 us -> 162 us
    all_to_all x4 -> x3, waiting for transfers between devices: 2700 us -> 22.8 us  [the longest x2 22.8 us: to_groups(): lax.all_to_all(copies, BOTH, split_axis=0, concat_axis=0, tiled=True)]
    pallas_call x0 -> x31, Pallas kernels: none -> 426 us  [the longest x5 123 us: main_chunk(): pl.pallas_call(functools.partial(main_kernel, count, slot_count), grid=(e...]
    ppermute x0 -> x140, waiting for transfers between devices: none -> 283 us  [send(): return lax.ppermute(value, BOTH, device_pairs(MOVES[axis]))]
    psum x2 -> x1, waiting for transfers between devices: 282 us -> 0.01 us  [local_gathered(): grad_w_out, grad_value = lax.psum((grad_w_out, grad_value), 'dp')]
    dot_general x31 -> x6, matrix products: 284 us -> 8.2 us  [the longest x4 7.59 us: project_back(): jnp.dot(o_low[r * tok_rows:(r + 1) * tok_rows], w_out, preferred_element_...]
    ppermute x0 -> x140, starting transfers between devices: none -> 151 us  [send(): return lax.ppermute(value, BOTH, device_pairs(MOVES[axis]))]
    all_gather x2 -> x0, waiting for transfers between devices: 96.3 us -> none  [the longest x1 62 us: local(): d_attn_all = lax.all_gather(d_attn, 'tensor', axis=0, tiled=True)]
    all_to_all x4 -> x3, starting transfers between devices: 101 us -> 11 us  [the longest x2 8.37 us: to_groups(): lax.all_to_all(copies, BOTH, split_axis=0, concat_axis=0, tiled=True)]
  transfers between devices with their start and end apart: 10 -> 144, of which waited for: 9 -> 46; matrix products, arithmetic and copies ran while one was open for 8% -> 14% of each run, Pallas kernels for 0% -> 36%
where the time goes in v2:
time: 1150 us; the launch traced here: 1140 us
  Pallas kernels  426 us (37%)
  waiting for transfers between devices  306 us (27%)
  starting transfers between devices  162 us (14%)
  other arithmetic  113 us (10%)
  matrix products  49.9 us (4%)
  local copies, waits for them, and re-layouts  48.5 us (4%)
  between operations  17.1 us (1%)
  blocking collectives  12.9 us (1%)
    ppermute x140, waiting for transfers between devices, send(): return lax.ppermute(value, BOTH, device_pairs(MOVES[axis]))  283 us
    ppermute x140, starting transfers between devices, send(): return lax.ppermute(value, BOTH, device_pairs(MOVES[axis]))  151 us
    pallas_call x5, Pallas kernels, main_chunk(): pl.pallas_call(functools.partial(main_kernel, count, slot_count), grid=(e...  123 us
    pallas_call x5, Pallas kernels, cot_chunk(): pl.pallas_call(functools.partial(cot_kernel, count, slot_count), grid=(ex...  69.3 us
    pallas_call x5, Pallas kernels, out_chunk(): pl.pallas_call(functools.partial(out_kernel, count, slot_count), grid=(ex...  62.1 us
    pallas_call x3, Pallas kernels, expert_grads(): pl.pallas_call(functools.partial(grad_kernel, count), grid=(last - first,...  61.8 us
    pallas_call x10, Pallas kernels, pair_sum(): pl.pallas_call(pair_kernel, grid=(rows // tile,), in_specs=[stack, stack]...  53 us
    convert_element_type x19, other arithmetic, add_low(): return total.astype(BF16)  51.2 us
  transfers between devices with their start and end apart: 144, of which 46 were waited for; matrix products, arithmetic and copies ran while one was open for 14% of the time, Pallas kernels for 36%

profile of v2, /device:TPU:0, one launch (start us, length us, event | category | flops | bytes accessed | tf_op | source)
XLA Modules:
  0.0 1135.3 jit_solution(8076427683498212889)
XLA Ops:
  25.7 13.1 %collective-permute-done.refs_2_ = bf16[256,2048]{1,0:T(8,128)(2,1)} collective-permute-done((bf16[256,2048]{1,0:T(8,128)(2,1)}, bf16[256,2048]{1,0:T(8,128)(2,1)}, u32[]{:S(2)}, u32[]{:S(2)}) %collective-permute-start) | collective-permute-done | bytes 1048608 | tf_op jit(solution)/shard_map/ppermute | solution.py:109
  64.1 17.2 %shard_map.272 = (f32[1024,512]{1,0:T(8,128)}, f32[1024,512]{1,0:T(8,128)}, bf16[1024,512]{1,0:T(8,128)(2,1)}, f32[1024,128]{1,0:T(8,128)}, f32[1024,128]{1,0:T(8,128)}) custom-call(bf16[256,2048]{1,0:T(8,128)(2,1)} %fusion.7.refs_0_, bf16[256,2048]{1,0:T(8,128)(2,1)} %collective-permute-done.1.refs_1_, bf16[256,2048]{1,0:T(8,128)(2,1)} %collective-permute-done.refs_2_, ...), custom_call_target="tpu_custom_call" | custom-call | flops 6442450944 | bytes 15728640 | tf_op jit(solution)/shard_map/pallas_call | solution.py:516
  84.4 7.0 psum.28
  105.9 16.8 %shard_map.273 = (bf16[1024,512]{1,0:T(8,128)(2,1)}, f32[1024,512]{1,0:T(8,128)}, bf16[1024,512]{1,0:T(8,128)(2,1)}, bf16[1024,512]{1,0:T(8,128)(2,1)}) custom-call(f32[1024,512]{1,0:T(8,128)} %get-tuple-element.1251.q_ref, f32[1024,512]{1,0:T(8,128)} %get-tuple-element.1255.k_ref, bf16[1024,512]{1,0:T(8,128)(2,1)} %get-tuple-element.1223.v_ref, ...), custom_call_target="tpu_custom_call" | custom-call | flops 2147483648 | bytes 10485760 | tf_op jit(solution)/shard_map/pallas_call | solution.py:638
  134.8 15.6 %shard_map.274 = (bf16[8,256,2048]{2,1,0:T(8,128)(2,1)}, f32[8,256,256]{2,1,0:T(8,128)}) custom-call(bf16[8,256,256]{2,1,0:T(8,128)(2,1)} %bitcast.157, bf16[8,256,2048]{2,1,0:T(8,128)(2,1)} %down_ref.9, bf16[256,2048]{1,0:T(8,128)(2,1)} %refs_0_, bf16[256,2048]{1,0:T(8,128)(2,1)} %collective-permute-done.2.refs_1_, ...), custom_call_target="tpu_custom_call" | custom-call | flops 4294967296 | bytes 25165824 | tf_op jit(solution)/shard_map/pallas_call | solution.py:360
  150.5 4.4 collective-permute-done.20
  163.7 4.9 all-to-all-start.1
  168.7 22.8 %all-to-all-done.1 = f32[32,8,256]{2,1,0:T(8,128)} async-done(((f32[32,8,256]{2,1,0:T(8,128)}), f32[32,8,256]{2,1,0:T(8,128)}, u32[]{:S(2)}, u32[]{:S(2)}) %all-to-all-start.1) | async-done | bytes 262176 | tf_op jit(solution)/shard_map/all_to_all | solution.py:744
  199.1 15.6 %shard_map.275 = (bf16[8,256,2048]{2,1,0:T(8,128)(2,1)}, f32[8,256,256]{2,1,0:T(8,128)}) custom-call(bf16[8,256,256]{2,1,0:T(8,128)(2,1)} %bitcast.154, bf16[8,256,2048]{2,1,0:T(8,128)(2,1)} %down_ref.9, bf16[256,2048]{1,0:T(8,128)(2,1)} %collective-permute-done.4.refs_0_, bf16[256,2048]{1,0:T(8,128)(2,1)} %collective-permute-done.5.refs_1_, ...), custom_call_target="tpu_custom_call" | custom-call | flops 4294967296 | bytes 25165824 | tf_op jit(solution)/shard_map/pallas_call | solution.py:360
  214.7 4.4 collective-permute-done.26.refs_0_
  223.8 27.6 %shard_map.276 = (bf16[8,256,2048]{2,1,0:T(8,128)(2,1)}, bf16[8,256,256]{2,1,0:T(8,128)(2,1)}, bf16[8,256,256]{2,1,0:T(8,128)(2,1)}, bf16[8,256,256]{2,1,0:T(8,1...) custom-call(bf16[8,256,256]{2,1,0:T(8,128)(2,1)} %bitcast.158, ...), custom_call_target="tpu_custom_call" | custom-call | flops 12884901888 | bytes 41943040 | tf_op jit(solution)/shard_map/pallas_call | solution.py:383
  255.0 6.4 collective-permute-done.39.refs_5_
  261.7 5.9 shard_map.277
  267.6 10.9 collective-permute-done.38.refs_1_
  282.4 27.8 %shard_map.278 = (bf16[8,256,2048]{2,1,0:T(8,128)(2,1)}, bf16[8,256,256]{2,1,0:T(8,128)(2,1)}, bf16[8,256,256]{2,1,0:T(8,128)(2,1)}, bf16[8,256,256]{2,1,0:T(8,1...) custom-call(bf16[8,256,256]{2,1,0:T(8,128)(2,1)} %bitcast.155, ...), custom_call_target="tpu_custom_call" | custom-call | flops 12884901888 | bytes 41943040 | tf_op jit(solution)/shard_map/pallas_call | solution.py:383
  312.2 7.0 collective-permute-done.53.refs_7_
  320.3 15.7 %shard_map.280 = (bf16[8,256,2048]{2,1,0:T(8,128)(2,1)}, f32[8,256,256]{2,1,0:T(8,128)}) custom-call(bf16[8,256,256]{2,1,0:T(8,128)(2,1)} %bitcast.151, bf16[8,256,2048]{2,1,0:T(8,128)(2,1)} %down_ref.9, bf16[256,2048]{1,0:T(8,128)(2,1)} %copy-done.41, bf16[256,2048]{1,0:T(8,128)(2,1)} %copy-done.38, bf16[256,2048]{1,0:T(8,128)(2,1)} %collective-permute-done.36.refs_2_, ...), custom_call_target="tpu_custom_call" | custom-call | flops 4294967296 | bytes 25165824 | tf_op jit(solution)/shard_map/pallas_call | solution.py:360
  336.0 5.9 shard_map.279
  349.8 28.0 %shard_map.281 = (bf16[8,256,2048]{2,1,0:T(8,128)(2,1)}, bf16[8,256,256]{2,1,0:T(8,128)(2,1)}, bf16[8,256,256]{2,1,0:T(8,128)(2,1)}, bf16[8,256,256]{2,1,0:T(8,1...) custom-call(bf16[8,256,256]{2,1,0:T(8,128)(2,1)} %bitcast.152, ...), custom_call_target="tpu_custom_call" | custom-call | flops 12884901888 | bytes 41943040 | tf_op jit(solution)/shard_map/pallas_call | solution.py:383
  380.0 8.6 collective-permute-done.64.refs_3_
  390.3 11.2 shard_map.284
  402.5 11.2 shard_map.283
  413.7 5.9 shard_map.282
  424.1 20.2 %shard_map.285 = (bf16[8,128,2048]{2,1,0:T(8,128)(2,1)}, bf16[8,128,256]{2,1,0:T(8,128)(2,1)}, bf16[8,128,256]{2,1,0:T(8,128)(2,1)}, bf16[8,128,256]{2,1,0:T(8,1...) custom-call(bf16[4,256,256]{2,1,0:T(8,128)(2,1)} %bitcast.143, ...), custom_call_target="tpu_custom_call" | custom-call | flops 6442450944 | bytes 29360128 | tf_op jit(solution)/shard_map/pallas_call | solution.py:383
  455.0 20.0 %shard_map.287 = (bf16[8,128,2048]{2,1,0:T(8,128)(2,1)}, bf16[8,128,256]{2,1,0:T(8,128)(2,1)}, bf16[8,128,256]{2,1,0:T(8,128)(2,1)}, bf16[8,128,256]{2,1,0:T(8,1...) custom-call(bf16[4,256,256]{2,1,0:T(8,128)(2,1)} %bitcast.146, ...), custom_call_target="tpu_custom_call" | custom-call | flops 6442450944 | bytes 29360128 | tf_op jit(solution)/shard_map/pallas_call | solution.py:383
  483.8 17.1 %collective-permute-done.72 = bf16[256,2048]{1,0:T(8,128)(2,1)} collective-permute-done((bf16[256,2048]{1,0:T(8,128)(2,1)}, bf16[256,2048]{1,0:T(8,128)(2,1)}, u32[]{:S(2)}, u32[]{:S(2)}) %collective-permute-start.72) | collective-permute-done | bytes 1048608 | tf_op jit(solution)/shard_map/ppermute | solution.py:109
  509.0 13.9 %shard_map.289 = (bf16[4,256,2048]{2,1,0:T(8,128)(2,1)}, bf16[4,256,2048]{2,1,0:T(8,128)(2,1)}) custom-call(bf16[8,256,256]{2,1,0:T(8,128)(2,1)} %bitcast.159, bf16[8,256,256]{2,1,0:T(8,128)(2,1)} %get-tuple-element.1412.scaled_ref.refs_10_, bf16[8,256,2048]{2,1,0:T(8,128)(2,1)} %down_ref.9), custom_call_target="tpu_custom_call" | custom-call | flops 4294967296 | bytes 25165824 | tf_op jit(solution)/shard_map/pallas_call | solution.py:425
  525.9 8.0 collective-permute-done.75
  539.1 13.7 %shard_map.290 = (bf16[4,256,2048]{2,1,0:T(8,128)(2,1)}, bf16[4,256,2048]{2,1,0:T(8,128)(2,1)}) custom-call(bf16[8,256,256]{2,1,0:T(8,128)(2,1)} %bitcast.156, bf16[8,256,256]{2,1,0:T(8,128)(2,1)} %get-tuple-element.1413.scaled_ref.refs_11_, bf16[8,256,2048]{2,1,0:T(8,128)(2,1)} %down_ref.9), custom_call_target="tpu_custom_call" | custom-call | flops 4294967296 | bytes 25165824 | tf_op jit(solution)/shard_map/pallas_call | solution.py:425
  552.9 6.0 shard_map.291
  572.2 13.9 %shard_map.292 = (bf16[4,256,2048]{2,1,0:T(8,128)(2,1)}, bf16[4,256,2048]{2,1,0:T(8,128)(2,1)}) custom-call(bf16[8,256,256]{2,1,0:T(8,128)(2,1)} %bitcast.153, bf16[8,256,256]{2,1,0:T(8,128)(2,1)} %get-tuple-element.1414.scaled_ref.refs_12_, bf16[8,256,2048]{2,1,0:T(8,128)(2,1)} %down_ref.9), custom_call_target="tpu_custom_call" | custom-call | flops 4294967296 | bytes 25165824 | tf_op jit(solution)/shard_map/pallas_call | solution.py:425
  586.1 6.0 shard_map.293
  605.1 10.3 shard_map.295
  615.4 10.4 shard_map.294
  625.8 6.0 shard_map.296
  638.4 4.4 collective-permute-done.92.far_ref
  642.8 4.7 shard_map.298
  647.5 4.3 shard_map.297
  651.8 9.7 collective-permute-done.88
  671.7 15.7 %collective-permute-done.95 = f32[72,2048]{1,0:T(8,128)S(1)} collective-permute-done((f32[72,2048]{1,0:T(8,128)}, f32[72,2048]{1,0:T(8,128)S(1)}, u32[]{:S(2)}, u32[]{:S(2)}) %collective-permute-start.95) | collective-permute-done | bytes 589856 | tf_op jit(solution)/shard_map/ppermute | solution.py:109
  687.4 6.1 collective-permute-done.93
  716.0 22.6 %shard_map.299 = (f32[1024,512]{1,0:T(8,128)}, f32[1024,512]{1,0:T(8,128)}, bf16[1024,512]{1,0:T(8,128)(2,1)}, f32[1,512]{1,0:T(1,128)}, f32[1,512]{1,0:T(1,128)...) custom-call(f32[1024,512]{1,0:T(8,128)} %get-tuple-element.1251.q_ref, f32[1024,512]{1,0:T(8,128)} %get-tuple-element.1255.k_ref, ...), custom_call_target="tpu_custom_call" | custom-call | flops 5368709120 | bytes 16777216 | tf_op jit(solution)/shard_map/pallas_call | solution.py:665
  738.6 6.3 convolution_convert_fusion.2
  744.9 4.9 collective-permute-done.98
  751.0 6.0 psum.29
  769.9 17.8 %collective-permute-done.102 = f32[72,2048]{1,0:T(8,128)S(1)} collective-permute-done((f32[72,2048]{1,0:T(8,128)S(1)}, f32[72,2048]{1,0:T(8,128)S(1)}, u32[]{:S(2)}, u32[]{:S(2)}) %collective-permute-start.102) | collective-permute-done | bytes 589856 | tf_op jit(solution)/shard_map/ppermute | solution.py:109
  797.2 5.8 fusion.63
  802.9 7.3 add_convert_fusion
  810.3 5.9 convolution_convert_fusion
  831.8 31.8 %collective-permute-done.111 = bf16[1024,512]{1,0:T(8,128)(2,1)} collective-permute-done((bf16[1024,512]{1,0:T(8,128)(2,1)}, bf16[1024,512]{1,0:T(8,128)(2,1)}, u32[]{:S(2)}, u32[]{:S(2)}) %collective-permute-start.111) | collective-permute-done | bytes 1048608 | tf_op jit(solution)/shard_map/ppermute | solution.py:109
  877.2 15.4 %shard_map.300 = (f32[8,2048,256]{2,1,0:T(8,128)}, f32[8,2048,256]{2,1,0:T(8,128)}, f32[8,256,2048]{2,1,0:T(8,128)}) custom-call(bf16[8,256,2048]{2,1,0:T(8,128)(2,1)} %get-tuple-element.1402.refs_0_, bf16[8,256,2048]{2,1,0:T(8,128)(2,1)} %get-tuple-element.1403.refs_1_, bf16[8,256,2048]{2,1,0:T(8,128)(2,1)} %get-tuple-element.1404.refs_2_, ...), custom_call_target="tpu_custom_call" | custom-call | flops 6442450944 | bytes 29360128 | tf_op jit(solution)/shard_map/pallas_call | solution.py:465
  892.7 7.1 collective-permute-done.116
  903.2 10.2 collective-permute-start.118
  917.0 23.0 %shard_map.301 = (f32[8,2048,256]{2,1,0:T(8,128)}, f32[8,2048,256]{2,1,0:T(8,128)}, f32[8,256,2048]{2,1,0:T(8,128)}) custom-call(bf16[8,256,2048]{2,1,0:T(8,128)(2,1)} %get-tuple-element.1402.refs_0_, bf16[8,256,2048]{2,1,0:T(8,128)(2,1)} %get-tuple-element.1403.refs_1_, ...), custom_call_target="tpu_custom_call", output_to_operand_aliasing={{0}: (25, {}), {1}: (26, {}), {2}: (27, {})} | custom-call | flops 9663676416 | bytes 44040192 | tf_op jit(solution)/shard_map/pallas_call | solution.py:465
  957.6 23.4 %shard_map.302 = (f32[8,2048,256]{2,1,0:T(8,128)}, f32[8,2048,256]{2,1,0:T(8,128)}, f32[8,256,2048]{2,1,0:T(8,128)}) custom-call(bf16[8,256,2048]{2,1,0:T(8,128)(2,1)} %get-tuple-element.1402.refs_0_, bf16[8,256,2048]{2,1,0:T(8,128)(2,1)} %get-tuple-element.1403.refs_1_, ...), custom_call_target="tpu_custom_call", output_to_operand_aliasing={{0}: (25, {}), {1}: (26, {}), {2}: (27, {})} | custom-call | flops 9663676416 | bytes 44040192 | tf_op jit(solution)/shard_map/pallas_call | solution.py:465
  981.0 4.5 collective-permute-done.126
  986.7 18.0 %collective-permute-start.132 = (bf16[256,2048]{1,0:T(8,128)(2,1)}, bf16[256,2048]{1,0:T(8,128)(2,1)}, u32[]{:S(2)}, u32[]{:S(2)}) collective-permute-start(bf16[256,2048]{1,0:T(8,128)(2,1)} %add_convert_fusion.3), channel_id=1, source_target_pairs={{0,24},{1,25},{2,26},{3,27},{4,28},{5,29},{6,30},{7,31},{8,0},{9,1... | collective-permute-start | bytes 3145736 | tf_op jit(solution)/shard_map/ppermute | solution.py:109
  1013.8 35.4 %collective-permute-done.129 = bf16[256,512]{1,0:T(8,128)(2,1)S(1)} collective-permute-done((bf16[256,512]{1,0:T(8,128)(2,1)S(1)}, bf16[256,512]{1,0:T(8,128)(2,1)S(1)}, u32[]{:S(2)}, u32[]{:S(2)}) %collective-permute-start.129) | collective-permute-done | bytes 262176 | tf_op jit(solution)/shard_map/ppermute | solution.py:109
  1049.2 15.6 %collective-permute-done.130 = bf16[256,512]{1,0:T(8,128)(2,1)S(1)} collective-permute-done((bf16[256,512]{1,0:T(8,128)(2,1)S(1)}, bf16[256,512]{1,0:T(8,128)(2,1)S(1)}, u32[]{:S(2)}, u32[]{:S(2)}) %collective-permute-start.130) | collective-permute-done | bytes 262176 | tf_op jit(solution)/shard_map/ppermute | solution.py:109
  1071.7 4.3 collective-permute-start.136
  1076.0 4.3 convert_element_type.527
  1090.6 16.3 %collective-permute-done.134 = f32[72,2048]{1,0:T(8,128)S(1)} collective-permute-done((f32[72,2048]{1,0:T(8,128)S(1)}, f32[72,2048]{1,0:T(8,128)S(1)}, u32[]{:S(2)}, u32[]{:S(2)}) %collective-permute-start.134) | collective-permute-done | bytes 589856 | tf_op jit(solution)/shard_map/ppermute | solution.py:109
  1108.5 4.9 fusion.13
  1114.3 6.2 collective-permute-start.138
  (612 shorter events, 337.0 us)
Async XLA Ops:
  21.3 77.9 %all-to-all-start = ((f32[32,8,256]{2,1,0:T(8,128)}), f32[32,8,256]{2,1,0:T(8,128)}, u32[]{:S(2)}, u32[]{:S(2)}) async-start(f32[32,8,256]{2,1,0:T(8,128)} %bitcast.15), calls=%async_computation | async-start | bytes 524288 | tf_op jit(solution)/shard_map/all_to_all | solution.py:744
  60.8 34.9 %collective-permute-start.4 = (bf16[256,2048]{1,0:T(8,128)(2,1)}, bf16[256,2048]{1,0:T(8,128)(2,1)}, u32[]{:S(2)}, u32[]{:S(2)}) collective-permute-start(bf16[256,2048]{1,0:T(8,128)(2,1)} %collective-permute-done.2.refs_1_), channel_id=1, source_target_pairs={{0,24},{1,25},{2,26},{3,27},{4,28},{5,29},{6,30},{7,31},{8,0},{9,1... | collective-permute-start | bytes 3145736 | tf_op jit(solution)/shard_map/ppermute | solution.py:109
  61.5 34.2 %collective-permute-start.5 = (bf16[256,2048]{1,0:T(8,128)(2,1)}, bf16[256,2048]{1,0:T(8,128)(2,1)}, u32[]{:S(2)}, u32[]{:S(2)}) collective-permute-start(bf16[256,2048]{1,0:T(8,128)(2,1)} %collective-permute-done.2.refs_1_), channel_id=1, source_target_pairs={{0,4},{1,5},{2,6},{3,7},{4,0},{5,1},{6,2},{7,3},{8,12},{9,13},{10,... | collective-permute-start | bytes 3145736 | tf_op jit(solution)/shard_map/ppermute | solution.py:109
  63.0 32.7 %collective-permute-start.6 = (bf16[256,2048]{1,0:T(8,128)(2,1)S(1)}, bf16[256,2048]{1,0:T(8,128)(2,1)}, u32[]{:S(2)}, u32[]{:S(2)}) collective-permute-start(bf16[256,2048]{1,0:T(8,128)(2,1)S(1)} %copy-done.12), channel_id=1, source_target_pairs={{0,2},{1,3},{2,0},{3,1},{4,6},{5,7},{6,4},{7,5},{8,10},{9,11},{10,... | collective-permute-start | bytes 3145736 | tf_op jit(solution)/shard_map/ppermute | solution.py:109
  63.6 32.2 %collective-permute-start.7 = (bf16[256,2048]{1,0:T(8,128)(2,1)S(1)}, bf16[256,2048]{1,0:T(8,128)(2,1)}, u32[]{:S(2)}, u32[]{:S(2)}) collective-permute-start(bf16[256,2048]{1,0:T(8,128)(2,1)S(1)} %copy-done.12), channel_id=1, source_target_pairs={{0,1},{1,0},{2,3},{3,2},{4,5},{5,4},{6,7},{7,6},{8,9},{9,8},{10,11... | collective-permute-start | bytes 3145736 | tf_op jit(solution)/shard_map/ppermute | solution.py:109
  63.6 32.2 %collective-permute-start.8 = (bf16[256,2048]{1,0:T(8,128)(2,1)}, bf16[256,2048]{1,0:T(8,128)(2,1)}, u32[]{:S(2)}, u32[]{:S(2)}) collective-permute-start(bf16[256,2048]{1,0:T(8,128)(2,1)} %collective-permute-done.2.refs_1_), channel_id=1, source_target_pairs={{0,1},{1,0},{2,3},{3,2},{4,5},{5,4},{6,7},{7,6},{8,9},{9,8},{10,11... | collective-permute-start | bytes 3145736 | tf_op jit(solution)/shard_map/ppermute | solution.py:109
  158.8 34.1 %collective-permute-start.21 = (bf16[256,2048]{1,0:T(8,128)(2,1)S(1)}, bf16[256,2048]{1,0:T(8,128)(2,1)}, u32[]{:S(2)}, u32[]{:S(2)}) collective-permute-start(bf16[256,2048]{1,0:T(8,128)(2,1)S(1)} %multiply_convert_fusion.2.refs_0_), channel_id=1, source_target_pairs={{0,24},{1,25},{2,26},{3,27},{4,28},{5,29},{6,30},{7,31},{8,0},{9,1... | collective-permute-start | bytes 3145736 | tf_op jit(solution)/shard_map/ppermute | solution.py:109
  159.4 33.6 %collective-permute-start.22 = (bf16[256,2048]{1,0:T(8,128)(2,1)S(1)}, bf16[256,2048]{1,0:T(8,128)(2,1)}, u32[]{:S(2)}, u32[]{:S(2)}) collective-permute-start(bf16[256,2048]{1,0:T(8,128)(2,1)S(1)} %multiply_convert_fusion.2.refs_0_), channel_id=1, source_target_pairs={{0,4},{1,5},{2,6},{3,7},{4,0},{5,1},{6,2},{7,3},{8,12},{9,13},{10,... | collective-permute-start | bytes 3145736 | tf_op jit(solution)/shard_map/ppermute | solution.py:109
  160.7 32.3 %collective-permute-start.23 = (bf16[256,2048]{1,0:T(8,128)(2,1)S(1)}, bf16[256,2048]{1,0:T(8,128)(2,1)}, u32[]{:S(2)}, u32[]{:S(2)}) collective-permute-start(bf16[256,2048]{1,0:T(8,128)(2,1)S(1)} %multiply_convert_fusion.2.refs_0_), channel_id=1, source_target_pairs={{0,2},{1,3},{2,0},{3,1},{4,6},{5,7},{6,4},{7,5},{8,10},{9,11},{10,... | collective-permute-start | bytes 3145736 | tf_op jit(solution)/shard_map/ppermute | solution.py:109
  161.9 31.1 %collective-permute-start.24 = (bf16[256,2048]{1,0:T(8,128)(2,1)}, bf16[256,2048]{1,0:T(8,128)(2,1)}, u32[]{:S(2)}, u32[]{:S(2)}) collective-permute-start(bf16[256,2048]{1,0:T(8,128)(2,1)} %collective-permute-done.12.refs_2_), channel_id=1, source_target_pairs={{0,1},{1,0},{2,3},{3,2},{4,5},{5,4},{6,7},{7,6},{8,9},{9,8},{10,11... | collective-permute-start | bytes 3145736 | tf_op jit(solution)/shard_map/ppermute | solution.py:109
  161.9 31.1 %collective-permute-start.25 = (bf16[256,2048]{1,0:T(8,128)(2,1)}, bf16[256,2048]{1,0:T(8,128)(2,1)}, u32[]{:S(2)}, u32[]{:S(2)}) collective-permute-start(bf16[256,2048]{1,0:T(8,128)(2,1)} %collective-permute-done.11.refs_3_), channel_id=1, source_target_pairs={{0,1},{1,0},{2,3},{3,2},{4,5},{5,4},{6,7},{7,6},{8,9},{9,8},{10,11... | collective-permute-start | bytes 3145736 | tf_op jit(solution)/shard_map/ppermute | solution.py:109
  163.7 27.7 %all-to-all-start.1 = ((f32[32,8,256]{2,1,0:T(8,128)}), f32[32,8,256]{2,1,0:T(8,128)}, u32[]{:S(2)}, u32[]{:S(2)}) async-start(f32[32,8,256]{2,1,0:T(8,128)} %bitcast.52), calls=%async_computation.1 | async-start | bytes 524288 | tf_op jit(solution)/shard_map/all_to_all | solution.py:744
  220.1 31.2 %collective-permute-start.33 = (bf16[256,2048]{1,0:T(8,128)(2,1)}, bf16[256,2048]{1,0:T(8,128)(2,1)}, u32[]{:S(2)}, u32[]{:S(2)}) collective-permute-start(bf16[256,2048]{1,0:T(8,128)(2,1)} %collective-permute-done.26.refs_0_), channel_id=1, source_target_pairs={{0,24},{1,25},{2,26},{3,27},{4,28},{5,29},{6,30},{7,31},{8,0},{9,1... | collective-permute-start | bytes 3145736 | tf_op jit(solution)/shard_map/ppermute | solution.py:109
  221.6 29.8 %collective-permute-start.34 = (bf16[256,2048]{1,0:T(8,128)(2,1)}, bf16[256,2048]{1,0:T(8,128)(2,1)}, u32[]{:S(2)}, u32[]{:S(2)}) collective-permute-start(bf16[256,2048]{1,0:T(8,128)(2,1)} %collective-permute-done.26.refs_0_), channel_id=1, source_target_pairs={{0,4},{1,5},{2,6},{3,7},{4,0},{5,1},{6,2},{7,3},{8,12},{9,13},{10,... | collective-permute-start | bytes 3145736 | tf_op jit(solution)/shard_map/ppermute | solution.py:109
  222.6 28.8 %collective-permute-start.35 = (bf16[256,2048]{1,0:T(8,128)(2,1)}, bf16[256,2048]{1,0:T(8,128)(2,1)}, u32[]{:S(2)}, u32[]{:S(2)}) collective-permute-start(bf16[256,2048]{1,0:T(8,128)(2,1)} %collective-permute-done.26.refs_0_), channel_id=1, source_target_pairs={{0,1},{1,0},{2,3},{3,2},{4,5},{5,4},{6,7},{7,6},{8,9},{9,8},{10,11... | collective-permute-start | bytes 3145736 | tf_op jit(solution)/shard_map/ppermute | solution.py:109
  222.6 28.8 %collective-permute-start.36 = (bf16[256,2048]{1,0:T(8,128)(2,1)}, bf16[256,2048]{1,0:T(8,128)(2,1)}, u32[]{:S(2)}, u32[]{:S(2)}) collective-permute-start(bf16[256,2048]{1,0:T(8,128)(2,1)} %collective-permute-done.4.refs_0_), channel_id=1, source_target_pairs={{0,2},{1,3},{2,0},{3,1},{4,6},{5,7},{6,4},{7,5},{8,10},{9,11},{10,... | collective-permute-start | bytes 3145736 | tf_op jit(solution)/shard_map/ppermute | solution.py:109
  223.6 27.8 %collective-permute-start.37 = (bf16[256,2048]{1,0:T(8,128)(2,1)}, bf16[256,2048]{1,0:T(8,128)(2,1)S(1)}, u32[]{:S(2)}, u32[]{:S(2)}) collective-permute-start(bf16[256,2048]{1,0:T(8,128)(2,1)} %copy-done.41), channel_id=1, source_target_pairs={{0,1},{1,0},{2,3},{3,2},{4,5},{5,4},{6,7},{7,6},{8,9},{9,8},{10,11... | collective-permute-start | bytes 3145736 | tf_op jit(solution)/shard_map/ppermute | solution.py:109
  279.8 30.3 %collective-permute-start.44 = (bf16[256,2048]{1,0:T(8,128)(2,1)}, bf16[256,2048]{1,0:T(8,128)(2,1)}, u32[]{:S(2)}, u32[]{:S(2)}) collective-permute-start(bf16[256,2048]{1,0:T(8,128)(2,1)} %collective-permute-done.26.refs_0_), channel_id=1, source_target_pairs={{0,2},{1,3},{2,0},{3,1},{4,6},{5,7},{6,4},{7,5},{8,10},{9,11},{10,... | collective-permute-start | bytes 3145736 | tf_op jit(solution)/shard_map/ppermute | solution.py:109
  280.9 29.3 %collective-permute-start.45 = (bf16[256,2048]{1,0:T(8,128)(2,1)}, bf16[256,2048]{1,0:T(8,128)(2,1)}, u32[]{:S(2)}, u32[]{:S(2)}) collective-permute-start(bf16[256,2048]{1,0:T(8,128)(2,1)} %collective-permute-done.6.refs_3_), channel_id=1, source_target_pairs={{0,4},{1,5},{2,6},{3,7},{4,0},{5,1},{6,2},{7,3},{8,12},{9,13},{10,... | collective-permute-start | bytes 3145736 | tf_op jit(solution)/shard_map/ppermute | solution.py:109
  281.9 28.3 %collective-permute-start.46 = (bf16[256,2048]{1,0:T(8,128)(2,1)S(1)}, bf16[256,2048]{1,0:T(8,128)(2,1)}, u32[]{:S(2)}, u32[]{:S(2)}) collective-permute-start(bf16[256,2048]{1,0:T(8,128)(2,1)S(1)} %copy-done.39), channel_id=1, source_target_pairs={{0,1},{1,0},{2,3},{3,2},{4,5},{5,4},{6,7},{7,6},{8,9},{9,8},{10,11... | collective-permute-start | bytes 3145736 | tf_op jit(solution)/shard_map/ppermute | solution.py:109
  281.9 28.3 %collective-permute-start.47 = (bf16[256,2048]{1,0:T(8,128)(2,1)}, bf16[256,2048]{1,0:T(8,128)(2,1)}, u32[]{:S(2)}, u32[]{:S(2)}) collective-permute-start(bf16[256,2048]{1,0:T(8,128)(2,1)} %collective-permute-done.36.refs_2_), channel_id=1, source_target_pairs={{0,1},{1,0},{2,3},{3,2},{4,5},{5,4},{6,7},{7,6},{8,9},{9,8},{10,11... | collective-permute-start | bytes 3145736 | tf_op jit(solution)/shard_map/ppermute | solution.py:109
  310.7 31.2 %collective-permute-start.48 = (bf16[256,2048]{1,0:T(8,128)(2,1)}, bf16[256,2048]{1,0:T(8,128)(2,1)}, u32[]{:S(2)}, u32[]{:S(2)}) collective-permute-start(bf16[256,2048]{1,0:T(8,128)(2,1)} %collective-permute-done.33.refs_0_), channel_id=1, source_target_pairs={{0,2},{1,3},{2,0},{3,1},{4,6},{5,7},{6,4},{7,5},{8,10},{9,11},{10,... | collective-permute-start | bytes 3145736 | tf_op jit(solution)/shard_map/ppermute | solution.py:109
  311.7 30.2 %collective-permute-start.49 = (bf16[256,2048]{1,0:T(8,128)(2,1)}, bf16[256,2048]{1,0:T(8,128)(2,1)}, u32[]{:S(2)}, u32[]{:S(2)}) collective-permute-start(bf16[256,2048]{1,0:T(8,128)(2,1)} %collective-permute-done.33.refs_0_), channel_id=1, source_target_pairs={{0,1},{1,0},{2,3},{3,2},{4,5},{5,4},{6,7},{7,6},{8,9},{9,8},{10,11... | collective-permute-start | bytes 3145736 | tf_op jit(solution)/shard_map/ppermute | solution.py:109
  311.7 30.2 %collective-permute-start.50 = (bf16[256,2048]{1,0:T(8,128)(2,1)}, bf16[256,2048]{1,0:T(8,128)(2,1)}, u32[]{:S(2)}, u32[]{:S(2)}) collective-permute-start(bf16[256,2048]{1,0:T(8,128)(2,1)} %collective-permute-done.38.refs_1_), channel_id=1, source_target_pairs={{0,1},{1,0},{2,3},{3,2},{4,5},{5,4},{6,7},{7,6},{8,9},{9,8},{10,11... | collective-permute-start | bytes 3145736 | tf_op jit(solution)/shard_map/ppermute | solution.py:109
  347.8 30.0 %collective-permute-start.54 = (bf16[256,2048]{1,0:T(8,128)(2,1)}, bf16[256,2048]{1,0:T(8,128)(2,1)}, u32[]{:S(2)}, u32[]{:S(2)}) collective-permute-start(bf16[256,2048]{1,0:T(8,128)(2,1)} %collective-permute-done.36.refs_2_), channel_id=1, source_target_pairs={{0,4},{1,5},{2,6},{3,7},{4,0},{5,1},{6,2},{7,3},{8,12},{9,13},{10,... | collective-permute-start | bytes 3145736 | tf_op jit(solution)/shard_map/ppermute | solution.py:109
  348.9 28.9 %collective-permute-start.55 = (bf16[256,2048]{1,0:T(8,128)(2,1)S(1)}, bf16[256,2048]{1,0:T(8,128)(2,1)}, u32[]{:S(2)}, u32[]{:S(2)}) collective-permute-start(bf16[256,2048]{1,0:T(8,128)(2,1)S(1)} %copy-done.40), channel_id=1, source_target_pairs={{0,2},{1,3},{2,0},{3,1},{4,6},{5,7},{6,4},{7,5},{8,10},{9,11},{10,... | collective-permute-start | bytes 3145736 | tf_op jit(solution)/shard_map/ppermute | solution.py:109
  349.8 28.0 %collective-permute-start.56 = (bf16[256,2048]{1,0:T(8,128)(2,1)}, bf16[256,2048]{1,0:T(8,128)(2,1)}, u32[]{:S(2)}, u32[]{:S(2)}) collective-permute-start(bf16[256,2048]{1,0:T(8,128)(2,1)} %collective-permute-done.45.refs_0_), channel_id=1, source_target_pairs={{0,1},{1,0},{2,3},{3,2},{4,5},{5,4},{6,7},{7,6},{8,9},{9,8},{10,11... | collective-permute-start | bytes 3145736 | tf_op jit(solution)/shard_map/ppermute | solution.py:109
  377.9 35.8 %collective-permute-start.61 = (bf16[4,256,2048]{2,1,0:T(8,128)(2,1)}, bf16[4,256,2048]{2,1,0:T(8,128)(2,1)}, u32[]{:S(2)}, u32[]{:S(2)}) collective-permute-start(bf16[4,256,2048]{2,1,0:T(8,128)(2,1)} %get-tuple-element.1002), channel_id=1, source_target_pairs={{0,1},{1,0},{2,3},{3,2},{4,5},{5,4},{6,7},{7,6},{8,9},{9,8},{10,11... | collective-permute-start | bytes 12582920 | tf_op jit(solution)/shard_map/ppermute | solution.py:109
  379.0 40.5 %collective-permute-start.59 = (bf16[256,2048]{1,0:T(8,128)(2,1)}, bf16[256,2048]{1,0:T(8,128)(2,1)}, u32[]{:S(2)}, u32[]{:S(2)}) collective-permute-start(bf16[256,2048]{1,0:T(8,128)(2,1)} %collective-permute-done.44.refs_2_), channel_id=1, source_target_pairs={{0,4},{1,5},{2,6},{3,7},{4,0},{5,1},{6,2},{7,3},{8,12},{9,13},{10,... | collective-permute-start | bytes 3145736 | tf_op jit(solution)/shard_map/ppermute | solution.py:109
  388.5 31.0 %collective-permute-start.60 = (bf16[256,2048]{1,0:T(8,128)(2,1)}, bf16[256,2048]{1,0:T(8,128)(2,1)}, u32[]{:S(2)}, u32[]{:S(2)}) collective-permute-start(bf16[256,2048]{1,0:T(8,128)(2,1)} %collective-permute-done.27.refs_1_), channel_id=1, source_target_pairs={{0,2},{1,3},{2,0},{3,1},{4,6},{5,7},{6,4},{7,5},{8,10},{9,11},{10,... | collective-permute-start | bytes 3145736 | tf_op jit(solution)/shard_map/ppermute | solution.py:109
  505.7 570.4 %all-reduce.4.cloned.1.call-start = ((), (), s32[]{:S(2)}) async-start(), calls=%async_computation.3 | async-start | bytes 8388608 | tf_op jit(solution)/shard_map/psum | solution.py:996
  505.7 28.2 %collective-permute-start.75 = (bf16[256,2048]{1,0:T(8,128)(2,1)}, bf16[256,2048]{1,0:T(8,128)(2,1)}, u32[]{:S(2)}, u32[]{:S(2)}) collective-permute-start(bf16[256,2048]{1,0:T(8,128)(2,1)} %get-tuple-element.1089), channel_id=1, source_target_pairs={{0,4},{1,5},{2,6},{3,7},{4,0},{5,1},{6,2},{7,3},{8,12},{9,13},{10,... | collective-permute-start | bytes 3145736 | tf_op jit(solution)/shard_map/ppermute | solution.py:109
  507.6 27.4 %collective-permute-start.76 = (bf16[256,2048]{1,0:T(8,128)(2,1)}, bf16[256,2048]{1,0:T(8,128)(2,1)}, u32[]{:S(2)}, u32[]{:S(2)}) collective-permute-start(bf16[256,2048]{1,0:T(8,128)(2,1)} %get-tuple-element.1090), channel_id=1, source_target_pairs={{0,2},{1,3},{2,0},{3,1},{4,6},{5,7},{6,4},{7,5},{8,10},{9,11},{10,... | collective-permute-start | bytes 3145736 | tf_op jit(solution)/shard_map/ppermute | solution.py:109
  564.4 27.7 %collective-permute-start.80 = (bf16[256,2048]{1,0:T(8,128)(2,1)}, bf16[256,2048]{1,0:T(8,128)(2,1)}, u32[]{:S(2)}, u32[]{:S(2)}) collective-permute-start(bf16[256,2048]{1,0:T(8,128)(2,1)} %add_convert_fusion.15), channel_id=1, source_target_pairs={{0,4},{1,5},{2,6},{3,7},{4,0},{5,1},{6,2},{7,3},{8,12},{9,13},{10,... | collective-permute-start | bytes 3145736 | tf_op jit(solution)/shard_map/ppermute | solution.py:109
  596.1 29.7 %collective-permute-start.87 = (bf16[4,256,2048]{2,1,0:T(8,128)(2,1)}, bf16[4,256,2048]{2,1,0:T(8,128)(2,1)}, u32[]{:S(2)}, u32[]{:S(2)}) collective-permute-start(bf16[4,256,2048]{2,1,0:T(8,128)(2,1)} %get-tuple-element.1172), channel_id=1, source_target_pairs={{0,1},{1,0},{2,3},{3,2},{4,5},{5,4},{6,7},{7,6},{8,9},{9,8},{10,11... | collective-permute-start | bytes 12582920 | tf_op jit(solution)/shard_map/ppermute | solution.py:109
  596.1 35.6 %collective-permute-start.84 = (bf16[256,2048]{1,0:T(8,128)(2,1)}, bf16[256,2048]{1,0:T(8,128)(2,1)}, u32[]{:S(2)}, u32[]{:S(2)}) collective-permute-start(bf16[256,2048]{1,0:T(8,128)(2,1)} %get-tuple-element.1158), channel_id=1, source_target_pairs={{0,4},{1,5},{2,6},{3,7},{4,0},{5,1},{6,2},{7,3},{8,12},{9,13},{10,... | collective-permute-start | bytes 3145736 | tf_op jit(solution)/shard_map/ppermute | solution.py:109
  596.7 35.1 %collective-permute-start.85 = (bf16[256,2048]{1,0:T(8,128)(2,1)}, bf16[256,2048]{1,0:T(8,128)(2,1)}, u32[]{:S(2)}, u32[]{:S(2)}) collective-permute-start(bf16[256,2048]{1,0:T(8,128)(2,1)} %add_convert_fusion.16), channel_id=1, source_target_pairs={{0,2},{1,3},{2,0},{3,1},{4,6},{5,7},{6,4},{7,5},{8,10},{9,11},{10,... | collective-permute-start | bytes 3145736 | tf_op jit(solution)/shard_map/ppermute | solution.py:109
  598.2 33.6 %collective-permute-start.86 = (bf16[256,2048]{1,0:T(8,128)(2,1)}, bf16[256,2048]{1,0:T(8,128)(2,1)}, u32[]{:S(2)}, u32[]{:S(2)}) collective-permute-start(bf16[256,2048]{1,0:T(8,128)(2,1)} %add_convert_fusion.13), channel_id=1, source_target_pairs={{0,24},{1,25},{2,26},{3,27},{4,28},{5,29},{6,30},{7,31},{8,0},{9,1... | collective-permute-start | bytes 3145736 | tf_op jit(solution)/shard_map/ppermute | solution.py:109
  700.9 44.0 %collective-permute-start.100 = (bf16[256,2048]{1,0:T(8,128)(2,1)}, bf16[256,2048]{1,0:T(8,128)(2,1)}, u32[]{:S(2)}, u32[]{:S(2)}) collective-permute-start(bf16[256,2048]{1,0:T(8,128)(2,1)} %get-tuple-element.1220), channel_id=1, source_target_pairs={{0,2},{1,3},{2,0},{3,1},{4,6},{5,7},{6,4},{7,5},{8,10},{9,11},{10,... | collective-permute-start | bytes 3145736 | tf_op jit(solution)/shard_map/ppermute | solution.py:109
  701.8 43.2 %collective-permute-start.97 = (bf16[256,2048]{1,0:T(8,128)(2,1)}, bf16[256,2048]{1,0:T(8,128)(2,1)}, u32[]{:S(2)}, u32[]{:S(2)}) collective-permute-start(bf16[256,2048]{1,0:T(8,128)(2,1)} %get-tuple-element.1217), channel_id=1, source_target_pairs={{0,4},{1,5},{2,6},{3,7},{4,0},{5,1},{6,2},{7,3},{8,12},{9,13},{10,... | collective-permute-start | bytes 3145736 | tf_op jit(solution)/shard_map/ppermute | solution.py:109
  702.4 47.5 %collective-permute-start.98 = (bf16[256,2048]{1,0:T(8,128)(2,1)}, bf16[256,2048]{1,0:T(8,128)(2,1)}, u32[]{:S(2)}, u32[]{:S(2)}) collective-permute-start(bf16[256,2048]{1,0:T(8,128)(2,1)} %get-tuple-element.1218), channel_id=1, source_target_pairs={{0,4},{1,5},{2,6},{3,7},{4,0},{5,1},{6,2},{7,3},{8,12},{9,13},{10,... | collective-permute-start | bytes 3145736 | tf_op jit(solution)/shard_map/ppermute | solution.py:109
  703.8 46.0 %collective-permute-start.99 = (bf16[256,2048]{1,0:T(8,128)(2,1)}, bf16[256,2048]{1,0:T(8,128)(2,1)}, u32[]{:S(2)}, u32[]{:S(2)}) collective-permute-start(bf16[256,2048]{1,0:T(8,128)(2,1)} %get-tuple-element.1219), channel_id=1, source_target_pairs={{0,2},{1,3},{2,0},{3,1},{4,6},{5,7},{6,4},{7,5},{8,10},{9,11},{10,... | collective-permute-start | bytes 3145736 | tf_op jit(solution)/shard_map/ppermute | solution.py:109
  758.2 29.4 %collective-permute-start.103 = (bf16[256,2048]{1,0:T(8,128)(2,1)}, bf16[256,2048]{1,0:T(8,128)(2,1)S(1)}, u32[]{:S(2)}, u32[]{:S(2)}) collective-permute-start(bf16[256,2048]{1,0:T(8,128)(2,1)} %get-tuple-element.1247), channel_id=1, source_target_pairs={{0,4},{1,5},{2,6},{3,7},{4,0},{5,1},{6,2},{7,3},{8,12},{9,13},{10,... | collective-permute-start | bytes 3145736 | tf_op jit(solution)/shard_map/ppermute | solution.py:109
  759.2 28.5 %collective-permute-start.104 = (bf16[256,2048]{1,0:T(8,128)(2,1)}, bf16[256,2048]{1,0:T(8,128)(2,1)S(1)}, u32[]{:S(2)}, u32[]{:S(2)}) collective-permute-start(bf16[256,2048]{1,0:T(8,128)(2,1)} %add_convert_fusion.11), channel_id=1, source_target_pairs={{0,2},{1,3},{2,0},{3,1},{4,6},{5,7},{6,4},{7,5},{8,10},{9,11},{10,... | collective-permute-start | bytes 3145736 | tf_op jit(solution)/shard_map/ppermute | solution.py:109
  790.9 27.8 %collective-permute-start.106 = (bf16[256,2048]{1,0:T(8,128)(2,1)}, bf16[256,2048]{1,0:T(8,128)(2,1)S(1)}, u32[]{:S(2)}, u32[]{:S(2)}) collective-permute-start(bf16[256,2048]{1,0:T(8,128)(2,1)} %add_convert_fusion.10), channel_id=1, source_target_pairs={{0,4},{1,5},{2,6},{3,7},{4,0},{5,1},{6,2},{7,3},{8,12},{9,13},{10,... | collective-permute-start | bytes 3145736 | tf_op jit(solution)/shard_map/ppermute | solution.py:109
  822.5 41.1 %collective-permute-start.111 = (bf16[1024,512]{1,0:T(8,128)(2,1)}, bf16[1024,512]{1,0:T(8,128)(2,1)}, u32[]{:S(2)}, u32[]{:S(2)}) collective-permute-start(bf16[1024,512]{1,0:T(8,128)(2,1)} %constant_dynamic-slice_fusion.7), channel_id=1, source_target_pairs={{0,4},{1,5},{2,6},{3,7},{4,0},{5,1},{6,2},{7,3},{8,12},{9,13},{10,... | collective-permute-start | bytes 3145736 | tf_op jit(solution)/shard_map/ppermute | solution.py:109
  823.1 40.5 %collective-permute-start.112 = (bf16[256,2048]{1,0:T(8,128)(2,1)}, bf16[256,2048]{1,0:T(8,128)(2,1)}, u32[]{:S(2)}, u32[]{:S(2)}) collective-permute-start(bf16[256,2048]{1,0:T(8,128)(2,1)} %add_convert_fusion.8), channel_id=1, source_target_pairs={{0,2},{1,3},{2,0},{3,1},{4,6},{5,7},{6,4},{7,5},{8,10},{9,11},{10,... | collective-permute-start | bytes 3145736 | tf_op jit(solution)/shard_map/ppermute | solution.py:109
  868.1 31.7 %collective-permute-start.113 = (bf16[256,2048]{1,0:T(8,128)(2,1)S(1)}, bf16[256,2048]{1,0:T(8,128)(2,1)S(1)}, u32[]{:S(2)}, u32[]{:S(2)}) collective-permute-start(bf16[256,2048]{1,0:T(8,128)(2,1)S(1)} %add_convert_fusion.6), channel_id=1, source_target_pairs={{0,2},{1,3},{2,0},{3,1},{4,6},{5,7},{6,4},{7,5},{8,10},{9,11},{10,... | collective-permute-start | bytes 3145736 | tf_op jit(solution)/shard_map/ppermute | solution.py:109
  869.4 30.4 %collective-permute-start.114 = (bf16[1024,512]{1,0:T(8,128)(2,1)}, bf16[1024,512]{1,0:T(8,128)(2,1)}, u32[]{:S(2)}, u32[]{:S(2)}) collective-permute-start(bf16[1024,512]{1,0:T(8,128)(2,1)} %constant_dynamic-slice_fusion.6), channel_id=1, source_target_pairs={{0,4},{1,5},{2,6},{3,7},{4,0},{5,1},{6,2},{7,3},{8,12},{9,13},{10,... | collective-permute-start | bytes 3145736 | tf_op jit(solution)/shard_map/ppermute | solution.py:109
  901.4 41.3 %collective-permute-start.121 = (bf16[256,2048]{1,0:T(8,128)(2,1)}, bf16[256,2048]{1,0:T(8,128)(2,1)S(1)}, u32[]{:S(2)}, u32[]{:S(2)}) collective-permute-start(bf16[256,2048]{1,0:T(8,128)(2,1)} %add_convert_fusion.5), channel_id=1, source_target_pairs={{0,4},{1,5},{2,6},{3,7},{4,0},{5,1},{6,2},{7,3},{8,12},{9,13},{10,... | collective-permute-start | bytes 3145736 | tf_op jit(solution)/shard_map/ppermute | solution.py:109
  901.7 41.0 %collective-permute-start.122 = (bf16[256,2048]{1,0:T(8,128)(2,1)}, bf16[256,2048]{1,0:T(8,128)(2,1)}, u32[]{:S(2)}, u32[]{:S(2)}) collective-permute-start(bf16[256,2048]{1,0:T(8,128)(2,1)} %get-tuple-element.1355), channel_id=1, source_target_pairs={{0,2},{1,3},{2,0},{3,1},{4,6},{5,7},{6,4},{7,5},{8,10},{9,11},{10,... | collective-permute-start | bytes 3145736 | tf_op jit(solution)/shard_map/ppermute | solution.py:109
  903.2 39.4 %collective-permute-start.118 = (bf16[256,512]{1,0:T(8,128)(2,1)S(1)}, bf16[256,512]{1,0:T(8,128)(2,1)S(1)}, u32[]{:S(2)}, u32[]{:S(2)}) collective-permute-start(bf16[256,512]{1,0:T(8,128)(2,1)S(1)} %add_convert_fusion.21), channel_id=1, source_target_pairs={{0,8},{1,9},{2,10},{3,11},{4,12},{5,13},{6,14},{7,15},{8,16},{9,17... | collective-permute-start | bytes 786440 | tf_op jit(solution)/shard_map/ppermute | solution.py:109
  913.4 29.3 %collective-permute-start.119 = (bf16[256,512]{1,0:T(8,128)(2,1)S(1)}, bf16[256,512]{1,0:T(8,128)(2,1)}, u32[]{:S(2)}, u32[]{:S(2)}) collective-permute-start(bf16[256,512]{1,0:T(8,128)(2,1)S(1)} %add_convert_fusion.21), channel_id=1, source_target_pairs={{0,16},{1,17},{2,18},{3,19},{4,20},{5,21},{6,22},{7,23},{8,24},{9,... | collective-permute-start | bytes 786440 | tf_op jit(solution)/shard_map/ppermute | solution.py:109
  947.8 37.7 %collective-permute-start.124 = (bf16[1024,512]{1,0:T(8,128)(2,1)S(1)}, bf16[1024,512]{1,0:T(8,128)(2,1)}, u32[]{:S(2)}, u32[]{:S(2)}) collective-permute-start(bf16[1024,512]{1,0:T(8,128)(2,1)S(1)} %bitcast.149), channel_id=1, source_target_pairs={{0,4},{1,5},{2,6},{3,7},{4,0},{5,1},{6,2},{7,3},{8,12},{9,13},{10,... | collective-permute-start | bytes 3145736 | tf_op jit(solution)/shard_map/ppermute | solution.py:109
  952.4 33.0 %collective-permute-start.123 = (f32[72,2048]{1,0:T(8,128)}, f32[72,2048]{1,0:T(8,128)}, u32[]{:S(2)}, u32[]{:S(2)}) collective-permute-start(f32[72,2048]{1,0:T(8,128)} %add.880), channel_id=1, source_target_pairs={{0,2},{1,3},{2,0},{3,1},{4,6},{5,7},{6,4},{7,5},{8,10},{9,11},{10,... | collective-permute-start | bytes 1769480 | tf_op jit(solution)/shard_map/ppermute | solution.py:109
  953.3 27.7 %collective-permute-start.125 = (bf16[256,512]{1,0:T(8,128)(2,1)S(1)}, bf16[256,512]{1,0:T(8,128)(2,1)}, u32[]{:S(2)}, u32[]{:S(2)}) collective-permute-start(bf16[256,512]{1,0:T(8,128)(2,1)S(1)} %copy-done.70), channel_id=1, source_target_pairs={{0,8},{1,9},{2,10},{3,11},{4,12},{5,13},{6,14},{7,15},{8,16},{9,17... | collective-permute-start | bytes 786440 | tf_op jit(solution)/shard_map/ppermute | solution.py:109
  955.2 30.3 %collective-permute-start.126 = (bf16[256,512]{1,0:T(8,128)(2,1)S(1)}, bf16[256,512]{1,0:T(8,128)(2,1)}, u32[]{:S(2)}, u32[]{:S(2)}) collective-permute-start(bf16[256,512]{1,0:T(8,128)(2,1)S(1)} %copy-done.69), channel_id=1, source_target_pairs={{0,16},{1,17},{2,18},{3,19},{4,20},{5,21},{6,22},{7,23},{8,24},{9,... | collective-permute-start | bytes 786440 | tf_op jit(solution)/shard_map/ppermute | solution.py:109
  955.2 30.3 %collective-permute-start.127 = (bf16[256,512]{1,0:T(8,128)(2,1)S(1)}, bf16[256,512]{1,0:T(8,128)(2,1)}, u32[]{:S(2)}, u32[]{:S(2)}) collective-permute-start(bf16[256,512]{1,0:T(8,128)(2,1)S(1)} %get-tuple-element.1401), channel_id=1, source_target_pairs={{0,24},{1,25},{2,26},{3,27},{4,28},{5,29},{6,30},{7,31},{8,0},{9,1... | collective-permute-start | bytes 786440 | tf_op jit(solution)/shard_map/ppermute | solution.py:109
  986.7 78.1 %collective-permute-start.132 = (bf16[256,2048]{1,0:T(8,128)(2,1)}, bf16[256,2048]{1,0:T(8,128)(2,1)}, u32[]{:S(2)}, u32[]{:S(2)}) collective-permute-start(bf16[256,2048]{1,0:T(8,128)(2,1)} %add_convert_fusion.3), channel_id=1, source_target_pairs={{0,24},{1,25},{2,26},{3,27},{4,28},{5,29},{6,30},{7,31},{8,0},{9,1... | collective-permute-start | bytes 3145736 | tf_op jit(solution)/shard_map/ppermute | solution.py:109
  1004.8 44.4 %collective-permute-start.129 = (bf16[256,512]{1,0:T(8,128)(2,1)S(1)}, bf16[256,512]{1,0:T(8,128)(2,1)S(1)}, u32[]{:S(2)}, u32[]{:S(2)}) collective-permute-start(bf16[256,512]{1,0:T(8,128)(2,1)S(1)} %add_convert_fusion.20), channel_id=1, source_target_pairs={{0,8},{1,9},{2,10},{3,11},{4,12},{5,13},{6,14},{7,15},{8,16},{9,17... | collective-permute-start | bytes 786440 | tf_op jit(solution)/shard_map/ppermute | solution.py:109
  1007.4 57.5 %collective-permute-start.130 = (bf16[256,512]{1,0:T(8,128)(2,1)S(1)}, bf16[256,512]{1,0:T(8,128)(2,1)S(1)}, u32[]{:S(2)}, u32[]{:S(2)}) collective-permute-start(bf16[256,512]{1,0:T(8,128)(2,1)S(1)} %add_convert_fusion.20), channel_id=1, source_target_pairs={{0,16},{1,17},{2,18},{3,19},{4,20},{5,21},{6,22},{7,23},{8,24},{9,... | collective-permute-start | bytes 786440 | tf_op jit(solution)/shard_map/ppermute | solution.py:109
  1008.7 56.1 %collective-permute-start.131 = (bf16[256,512]{1,0:T(8,128)(2,1)S(1)}, bf16[256,512]{1,0:T(8,128)(2,1)S(1)}, u32[]{:S(2)}, u32[]{:S(2)}) collective-permute-start(bf16[256,512]{1,0:T(8,128)(2,1)S(1)} %add_convert_fusion.20), channel_id=1, source_target_pairs={{0,24},{1,25},{2,26},{3,27},{4,28},{5,29},{6,30},{7,31},{8,0},{9,1... | collective-permute-start | bytes 786440 | tf_op jit(solution)/shard_map/ppermute | solution.py:109
  1071.7 35.2 %collective-permute-start.135 = (bf16[1024,512]{1,0:T(8,128)(2,1)S(1)}, bf16[1024,512]{1,0:T(8,128)(2,1)}, u32[]{:S(2)}, u32[]{:S(2)}) collective-permute-start(bf16[1024,512]{1,0:T(8,128)(2,1)S(1)} %bitcast.150), channel_id=1, source_target_pairs={{0,4},{1,5},{2,6},{3,7},{4,0},{5,1},{6,2},{7,3},{8,12},{9,13},{10,... | collective-permute-start | bytes 3145736 | tf_op jit(solution)/shard_map/ppermute | solution.py:109
  1071.7 35.2 %collective-permute-start.136 = (bf16[256,2048]{1,0:T(8,128)(2,1)}, bf16[256,2048]{1,0:T(8,128)(2,1)}, u32[]{:S(2)}, u32[]{:S(2)}) collective-permute-start(bf16[256,2048]{1,0:T(8,128)(2,1)} %add_convert_fusion.2), channel_id=1, source_target_pairs={{0,24},{1,25},{2,26},{3,27},{4,28},{5,29},{6,30},{7,31},{8,0},{9,1... | collective-permute-start | bytes 3145736 | tf_op jit(solution)/shard_map/ppermute | solution.py:109
  (180 other events, 3856.4 us)
Sparse Core Ops, SparseCore 0:
  824.8 210.0 all-reduce.3

commit v3 on v2

--- a/solution.py
+++ b/solution.py
@@ -176,7 +176,10 @@
             self.held.setdefault(chip, []).append(value)
 
     def sends(self, hops):
-        return [(add_low(*self.held[chip]), axis) for axis, chip in hops]
+        groups = [self.held[chip] for _, chip in hops]
+        added = [group for group in groups if len(group) > 1]
+        sums = iter(block_sums(added) if added else ())
+        return [(next(sums) if len(group) > 1 else group[0], axis) for group, (axis, _) in zip(groups, hops)]
 
     def take(self, hops, got):
         for (axis, chip), value in zip(hops, got):
@@ -266,13 +269,14 @@
                 ]
 
 
-def give_rows(picks_ref, rows_ref, blocks, slot_count, width):
+def give_rows(picks_ref, rows_ref, blocks, slot_count, width, first=0):
     experts = rows_ref.shape[0]
     for b, block in enumerate(blocks):
         for low in range(0, block.shape[1], width):
             columns = pl.ds(low, width)
             slots = jnp.concatenate(
-                [rows_ref[e, pl.ds(b * slot_count, slot_count), columns] for e in range(experts)], axis=0
+                [rows_ref[e, pl.ds(first + b * slot_count, slot_count), columns] for e in range(experts)],
+                axis=0,
             )
             block[:, columns] = contract_rows(picks_ref[b], slots).astype(BF16)
 
@@ -334,15 +338,22 @@
         give_rows(picks_ref, rows_ref, results, slot_count, 512)
 
 
-def out_kernel(count, slot_count, picks_ref, scaled_ref, down_ref, *refs):
-    near_out, far_out, rows_ref = refs
-    results = [out.at[b] for out in (near_out, far_out) for b in range(count // 2)]
+def out_kernel(parts, slot_count, *refs):
+    picks, scaled, down_ref = refs[:parts], refs[parts : 2 * parts], refs[2 * parts]
+    near_out, far_out, rows_ref = refs[2 * parts + 1 :]
     e = pl.program_id(0)
-    rows_ref[e] = nn(scaled_ref[0], down_ref[0]).astype(BF16)
+    rows = scaled[0][0] if parts == 1 else jnp.concatenate([part[0] for part in scaled], axis=0)
+    rows_ref[e] = nn(rows, down_ref[0]).astype(BF16)
 
     @pl.when(e == pl.num_programs(0) - 1)
     def _():
-        give_rows(picks_ref, rows_ref, results, slot_count, 512)
+        low, done = 0, 0
+        for part in picks:
+            count = part.shape[0]
+            half = count // 2
+            results = [out.at[done + b] for out in (near_out, far_out) for b in range(half)]
+            give_rows(part, rows_ref, results, slot_count, 512, low)
+            low, done = low + count * slot_count, done + half
 
 
 def per_expert(*shape):
@@ -376,7 +387,7 @@
     )(picks, w_down, *blocks)
 
 
-def main_chunk(picks, gates, cot_acts, w_gate, w_up, blocks, slot_count):
+def main_chunk(picks, gates, cot_acts, acts_at, w_gate, w_up, blocks, slot_count):
     experts, width, hidden = w_gate.shape
     count, tokens = len(blocks), blocks[0].shape[0]
     rows = count * slot_count
@@ -386,7 +397,7 @@
         in_specs=[
             resident(*picks.shape),
             resident(*gates.shape),
-            per_expert(rows, hidden),
+            pl.BlockSpec((1, rows, hidden), lambda e: (e, acts_at, 0)),
             per_expert(width, hidden),
             per_expert(width, hidden),
         ]
@@ -420,12 +431,15 @@
 
 def out_chunk(picks, scaled, w_down, slot_count):
     experts, hidden, width = w_down.shape
-    count, _, tokens = picks.shape
+    tokens = picks[0].shape[2]
+    count = sum(part.shape[0] for part in picks)
     rows = count * slot_count
     return pl.pallas_call(
-        functools.partial(out_kernel, count, slot_count),
+        functools.partial(out_kernel, len(picks), slot_count),
         grid=(experts,),
-        in_specs=[resident(*picks.shape), per_expert(rows, hidden), per_expert(hidden, width)],
+        in_specs=[resident(*part.shape) for part in picks]
+        + [per_expert(*part.shape[1:]) for part in scaled]
+        + [per_expert(hidden, width)],
         out_specs=[resident(count // 2, tokens, width)] * 2,
         out_shape=[jax.ShapeDtypeStruct((count // 2, tokens, width), BF16)] * 2,
         scratch_shapes=[pltpu.VMEM((experts, rows, width), BF16)],
@@ -435,7 +449,7 @@
             bytes_accessed=2 * (count * tokens * width + experts * (rows + hidden) * width),
             transcendentals=0,
         ),
-    )(picks, scaled, w_down)
+    )(*picks, *scaled, w_down)
 
 
 def grad_kernel(count, *refs):
@@ -454,18 +468,22 @@
     down_out[0] = total(scaled, cots)
 
 
-def expert_grads(rows, cots, scaled, d_gate, d_up, first, last, earlier=None, tile=512):
+def expert_grads(rows, cots, scaled, d_gate, d_up, cots_at, first, last, earlier=None, tile=512):
     count, experts, width = len(rows), rows[0].shape[0], rows[0].shape[2]
     hidden = scaled[0].shape[2]
     slots = sum(part.shape[1] for part in rows)
     wide = [pl.BlockSpec((1, part.shape[1], tile), lambda e, n: (first + e, 0, n)) for part in rows]
+    wide_cots = [
+        pl.BlockSpec((1, part.shape[1], tile), lambda e, n, at=at: (first + e, at, n))
+        for part, at in zip(rows, cots_at)
+    ]
     narrow = [pl.BlockSpec((1, part.shape[1], hidden), lambda e, n: (first + e, 0, 0)) for part in rows]
     tall = pl.BlockSpec((1, tile, hidden), lambda e, n: (first + e, n, 0))
     given = [] if earlier is None else list(earlier)
     return pl.pallas_call(
         functools.partial(grad_kernel, count),
         grid=(last - first, width // tile),
-        in_specs=wide * 2 + narrow * 3 + [pl.BlockSpec(memory_space=pl.ANY)] * len(given),
+        in_specs=wide + wide_cots + narrow * 3 + [pl.BlockSpec(memory_space=pl.ANY)] * len(given),
         out_specs=[tall, tall, pl.BlockSpec((1, hidden, tile), lambda e, n: (first + e, 0, n))],
         out_shape=[
             jax.ShapeDtypeStruct((experts, width, hidden), F32),
@@ -480,6 +498,35 @@
             transcendentals=0,
         ),
     )(*rows, *cots, *scaled, *d_gate, *d_up, *given)
+
+
+def sums_kernel(counts, *refs):
+    terms, outs = refs[: sum(counts)], refs[sum(counts) :]
+    for count, out in zip(counts, outs):
+        value = terms[0][...].astype(F32)
+        for term in terms[1:count]:
+            value = value + term[...].astype(F32)
+        out[...] = value.astype(BF16)
+        terms = terms[count:]
+
+
+def block_sums(groups, tile=64):
+    rows, width = groups[0][0].shape
+    counts = [len(group) for group in groups]
+    block = pl.BlockSpec((tile, width), lambda i: (i, 0))
+    return pl.pallas_call(
+        functools.partial(sums_kernel, counts),
+        grid=(rows // tile,),
+        in_specs=[block] * sum(counts),
+        out_specs=[block] * len(groups),
+        out_shape=[jax.ShapeDtypeStruct((rows, width), BF16)] * len(groups),
+        compiler_params=pltpu.CompilerParams(vmem_limit_bytes=VMEM_GRANT),
+        cost_estimate=pl.CostEstimate(
+            flops=sum(counts) * rows * width,
+            bytes_accessed=2 * (sum(counts) + len(groups)) * rows * width,
+            transcendentals=0,
+        ),
+    )(*[term for group in groups for term in group])
 
 
 def qkv_kernel(*refs):
@@ -721,12 +768,14 @@
 
     member = lax.axis_index("tensor")
     blocks_at = member ^ jnp.arange(tensor_count)
-    cosine, sine = (
-        table.reshape(tensor_count, tok_rows, half_width)[blocks_at].reshape(seq_len, half_width)
-        for table in rope_tables(seq_len, HDIM)
-    )
-    cosine = jnp.concatenate([cosine, cosine], axis=1)
-    sine = jnp.concatenate([-sine, sine], axis=1)
+
+    def turn_tables(blocks_at):
+        cosine, sine = (
+            table.reshape(tensor_count, tok_rows, half_width)[blocks_at].reshape(seq_len, half_width)
+            for table in rope_tables(seq_len, HDIM)
+        )
+        return jnp.concatenate([cosine, cosine], axis=1), jnp.concatenate([-sine, sine], axis=1)
+
     positions = (blocks_at[:, None] * tok_rows + jnp.arange(tok_rows)[None, :]).reshape(-1)
     never = 2 * seq_len
     key_pos = jnp.where(positions < live_length, positions, never).astype(F32)[None, :]
@@ -753,13 +802,16 @@
     hot = jnp.any(expert_ids.T[None, :, :] == jnp.arange(expert_total)[:, None, None], axis=1)
     earlier = jnp.triu(jnp.ones((tok_rows, tok_rows), F32), 1).astype(BF16)
     rank = jnp.dot(hot.astype(BF16), earlier, preferred_element_type=F32)
-    slot_of = to_groups(jnp.where(hot, rank, -1.0))
-    slots = jnp.arange(slot_count, dtype=F32)
-    picks_wide = (slot_of[:, :, None, :] == slots[None, None, :, None]).astype(BF16)
-    picks = [
-        picks_wide[low : low + len(chunk)].reshape(len(chunk), experts * slot_count, tok_rows)
-        for chunk, low in zip(CHUNKS, STARTS)
-    ]
+    slot_of = jnp.where(hot, rank, -1.0)
+
+    def all_picks(slot_of):
+        slots = jnp.arange(slot_count, dtype=F32)
+        wide = (slot_of[:, :, None, :] == slots[None, None, :, None]).astype(BF16)
+        return [
+            wide[low : low + len(chunk)].reshape(len(chunk), experts * slot_count, tok_rows)
+            for chunk, low in zip(CHUNKS, STARTS)
+        ]
+
 
     stages = Stages(attn_in)
     cot, ffn = Gather(cotangent), Gather(None)
@@ -779,48 +831,55 @@
             table.take(moves, got[low : low + len(moves)])
         return got[: len(extra)], made
 
-    def cot_work(i):
-        values, crossing, late = cot.chunk(i)
-
-        def work(picks_i, w_down_i, values, crossing):
-            return cot_chunk(picks_i, w_down_i, Gather.complete(i, values, crossing, late), slot_count)
-
-        return work, (picks[i], w_down, values, crossing)
-
-    def cot_done(i, made):
-        cot_rows[i], cot_acts[i] = made
+    def cot_work(*chunks):
+        made = [cot.chunk(i) for i in chunks]
+
+        def work(picks_i, w_down_i, *args):
+            blocks = []
+            for i, (_, _, late), (values, crossing) in zip(chunks, made, args):
+                blocks += Gather.complete(i, values, crossing, late)
+            return cot_chunk(picks_i, w_down_i, blocks, slot_count)
+
+        picks_i = picks[chunks[0]] if len(chunks) == 1 else jnp.concatenate([picks[i] for i in chunks], axis=0)
+        return work, (picks_i, w_down) + tuple((values, crossing) for values, crossing, _ in made)
+
+    def cot_done(chunks, made):
+        for n, i in enumerate(chunks):
+            cot_rows[i], cot_acts[i] = (made[0], n), (made[1], n)
 
     def main_work(i):
         values, crossing, late = ffn.chunk(i)
 
         def work(picks_i, gates_i, acts_i, gate_w, up_w, values, crossing):
             blocks = Gather.complete(i, values, crossing, late)
-            return main_chunk(picks_i, gates_i, acts_i, gate_w, up_w, blocks, slot_count)
+            return main_chunk(picks_i, gates_i, acts_i, cot_acts[i][1], gate_w, up_w, blocks, slot_count)
 
         gates_i = token_gates[STARTS[i] : STARTS[i] + len(CHUNKS[i])]
-        return work, (picks[i], gates_i, cot_acts[i], w_gate, w_up, values, crossing)
-
-    def out_work(i):
+        return work, (picks[i], gates_i, cot_acts[i][0], w_gate, w_up, values, crossing)
+
+    def out_work(*chunks):
         def work(picks_i, scaled_i, w_down_i):
             return out_chunk(picks_i, scaled_i, w_down_i, slot_count)
 
-        return work, (picks[i], kept[i][1], w_down)
-
-    (across, mate), _ = advance(
-        extra=[(attn_in, "y"), (attn_in, "c")], cot=[("z", (0, 0, 0)), ("x", (0, 0, 0))]
+        return work, ([picks[i] for i in chunks], [kept[i][1] for i in chunks], w_down)
+
+    (across, mate), ((cosine, sine), slot_of) = advance(
+        [(turn_tables, (blocks_at,)), (to_groups, (slot_of,))],
+        extra=[(attn_in, "y"), (attn_in, "c")],
+        cot=[("z", (0, 0, 0)), ("x", (0, 0, 0))],
     )
 
     def project(block, mate, across, w_query, w_key, w_value):
         blocks = [block, mate, across, send(across, "c")]
         q_raw, k_raw, v_low, q_square, k_square = qkv(blocks, w_query, w_key, w_value)
         squares = token_sums(jnp.sum(q_square, axis=1), jnp.sum(k_square, axis=1))
-        return jnp.concatenate(blocks, axis=0), q_raw, k_raw, v_low, squares
+        return blocks, q_raw, k_raw, v_low, squares
 
     _, (made,) = advance(
         [(project, (attn_in, mate, across, w_query, w_key, w_value))],
         cot=[("z", (1, 0, 0)), ("x", (1, 0, 0)), ("y", (0, 0, 0)), ("c", (0, 0, 0)), ("c", (1, 0, 0))],
     )
-    gathered, q_raw, k_raw, v_low, squares = made
+    seq_blocks, q_raw, k_raw, v_low, squares = made
 
     def columns_of(squares):
         scales = lax.rsqrt(squares / model_width + EPS)
@@ -842,11 +901,10 @@
         across = add_low(parts[2], send(parts[3], "c"))
         return add_wide(parts[0], send(parts[1], "c")) + send(across, "y").astype(F32)
 
-    _, (attn_rows, made) = advance(
-        [(project_back, (o_low, w_out)), cot_work(0)],
+    _, (attn_rows, picks) = advance(
+        [(project_back, (o_low, w_out)), (all_picks, (slot_of,))],
         cot=[("x", (3, 0, 0)), ("c", (2, 0, 0)), ("c", (1, 1, 0))],
     )
-    cot_done(0, made)
     mixed = resid + attn_rows
     scale_two = rms_scale(mixed)
     mixed_norm = mixed * scale_two
@@ -855,20 +913,23 @@
 
     def route(ffn_in, w_router):
         logits = jnp.dot(ffn_in, w_router, preferred_element_type=F32)
-        router_probs = jax.nn.softmax(logits, axis=-1)
-        return router_probs, to_groups(router_probs.T)
-
-    _, ((router_probs, token_gates),) = advance(
-        [(route, (ffn_in, w_router))],
+        return jax.nn.softmax(logits, axis=-1)
+
+    def join(*blocks):
+        return jnp.concatenate(blocks, axis=0)
+
+    _, (router_probs, made, gathered) = advance(
+        [(route, (ffn_in, w_router)), cot_work(0), (join, tuple(seq_blocks))],
         ffn=[("z", (0, 0, 0)), ("x", (0, 0, 0)), ("y", (0, 0, 0))],
         cot=[("c", (1, 0, 1)), ("c", (2, 1, 0))],
     )
-    _, (made,) = advance(
-        [cot_work(1)],
+    cot_done((0,), made)
+    _, (made, token_gates) = advance(
+        [cot_work(1), (to_groups, (router_probs.T,))],
         ffn=[("z", (1, 0, 0)), ("x", (1, 0, 0)), ("y", (1, 0, 0))]
         + [("c", (0, 0, 0)), ("c", (0, 1, 0)), ("c", (1, 0, 0)), ("c", (0, 0, 1))],
     )
-    cot_done(1, made)
+    cot_done((1,), made)
     _, (made,) = advance(
         [main_work(0)],
         ffn=[("z", (2, 0, 0)), ("x", (2, 0, 0)), ("c", (2, 0, 0))],
@@ -893,32 +954,25 @@
         cot=[("x", (1, 0, 1))],
     )
     d_sum.put(1, made)
-    cot_done(2, other)
+    cot_done((2,), other)
     _, (made,) = advance(
         [main_work(2)],
-        cot=[("x", (2, 0, 1)), ("y", (3, 1, 0)), ("c", (0, 1, 1))],
+        cot=[("x", (2, 0, 1)), ("y", (3, 1, 0)), ("c", (0, 1, 1)), ("c", (1, 1, 1))],
     )
     kept[2], near, far = made[0], *made[1]
-    _, (made, other, third) = advance(
-        [(core_sum, (near, far)), cot_work(3), cot_work(4)],
+    _, (made, other) = advance(
+        [(core_sum, (near, far)), cot_work(3, 4)],
         ffn=[("x", (2, 0, 1)), ("y", (1, 1, 0))],
     )
     d_sum.put(2, made)
-    cot_done(3, other)
-    cot_done(4, third)
+    cot_done((3, 4), other)
     _, (made,) = advance([main_work(3)], ffn=[("x", (3, 0, 1)), ("y", (0, 1, 0))])
     kept[3], near, far = made[0], *made[1]
     _, (made,) = advance([(core_sum, (near, far))], ffn=[("c", (0, 1, 1)), ("c", (3, 1, 1))])
     d_sum.put(3, made)
 
-    def last_main(*args):
-        saved, (near, far) = main_work_four[0](*args)
-        return saved, core_sum(near, far)
-
-    main_work_four = main_work(4)
-    _, (made,) = advance([(last_main, main_work_four[1])], d=[("x", (1, 1, 1)), ("y", (2, 1, 1))])
-    kept[4] = made[0]
-    d_sum.put(4, made[1])
+    _, (made,) = advance([main_work(4)], d=[("x", (1, 1, 1)), ("y", (2, 1, 1))])
+    kept[4], near, far = made[0], *made[1]
 
     def return_probs(*d_probs):
         d_probs = jnp.concatenate(d_probs, axis=0)[position]
@@ -927,12 +981,13 @@
         return jnp.sum(arrived, axis=1).reshape(expert_total, tok_rows).T
 
     outs = {}
-    _, (outs[0], d_probs) = advance(
-        [out_work(0), (return_probs, tuple(kept[i][4] for i in order))],
-        d=[("x", (3, 1, 1)), ("y", (0, 1, 1))],
-    )
+    _, (made, outs[0], d_probs) = advance(
+        [(core_sum, (near, far)), out_work(0), (return_probs, tuple(kept[i][4] for i in order))],
+        d=[("x", (1, 1, 0)), ("y", (1, 0, 1))],
+    )
+    d_sum.put(4, made)
     _, (outs[1], made) = advance(
-        [out_work(1), (core_sum, tuple(outs[0]))], d=[("x", (1, 1, 0)), ("y", (1, 0, 1))]
+        [out_work(1), (core_sum, tuple(outs[0]))], d=[("x", (3, 1, 1)), ("y", (0, 1, 1))]
     )
     out_sum.put(0, made)
     _, (outs[2], made) = advance(
@@ -940,17 +995,17 @@
         d=[("x", (2, 1, 0)), ("y", (2, 0, 1)), ("z", (1, 0, 0))],
     )
     out_sum.put(1, made)
-    _, (outs[3], outs[4], made) = advance(
-        [out_work(3), out_work(4), (core_sum, tuple(outs[2]))],
+    _, (last_outs, made) = advance(
+        [out_work(3, 4), (core_sum, tuple(outs[2]))],
         d=[("x", (3, 1, 0)), ("y", (3, 0, 1)), ("z", (2, 0, 0))],
     )
     out_sum.put(2, made)
-    _, (made, other) = advance(
-        [(core_sum, tuple(outs[3])), (core_sum, tuple(outs[4]))],
+    _, (made,) = advance(
+        [(core_sum, tuple(last_outs))],
         d=[("x", (0, 1, 0)), ("y", (0, 0, 1)), ("z", (3, 0, 0))],
     )
-    out_sum.put(3, made)
-    out_sum.put(4, other)
+    out_sum.put(3, made[:2])
+    out_sum.put(4, made[2:])
     d_ffn = d_sum.total()
 
     d_result = cotangent.astype(F32)
@@ -974,26 +1029,32 @@
     )
     router_sums = router_sums + other
 
-    def attend_back(d_attn, mate, across, o_low, w_out, gathered, *rest):
-        d_attn_all = jnp.concatenate([d_attn, mate, across, send(across, "c")], axis=0)
-        d_attended = times_transpose(d_attn_all, w_out).astype(BF16)
+    def attend_back(d_attn, mate, across, w_out, *rest):
+        d_blocks = [d_attn, mate, across, send(across, "c")]
+        d_attended = join(*[times_transpose(block, w_out).astype(BF16) for block in d_blocks])
         q_raw, k_raw, v_low, q_rot, k_rot, lse, cols = rest
         made = attend_backward(
             q_raw, k_raw, v_low, q_rot, k_rot, d_attended, lse, cols, q_gain, k_gain, cosine, sine, key_pos
         )
-        return made, contract_rows(o_low, d_attn_all).astype(BF16), contract_rows(gathered, made[2]).astype(BF16)
+        return made, d_blocks
 
     _, (made,) = advance(
         [
             (
                 attend_back,
-                (d_attn, mate, across, o_low, w_out, gathered, q_raw, k_raw, v_low, q_rot, k_rot, lse, cols),
+                (d_attn, mate, across, w_out, q_raw, k_raw, v_low, q_rot, k_rot, lse, cols),
             )
         ],
         out=[("x", (3, 1, 1)), ("x", (1, 1, 0)), ("y", (2, 1, 1)), ("y", (0, 1, 1))],
     )
-    (dq_hat, dk_hat, dv_raw, query_gain_part, key_gain_part, q_inner, k_inner), grad_w_out, grad_value = made
-    grad_w_out, grad_value = lax.psum((grad_w_out, grad_value), "dp")
+    (dq_hat, dk_hat, dv_raw, query_gain_part, key_gain_part, q_inner, k_inner), d_blocks = made
+
+    def early_grads(o_low, gathered, dv_raw, *d_blocks):
+        return (
+            contract_rows(o_low, join(*d_blocks)).astype(BF16),
+            contract_rows(gathered, dv_raw).astype(BF16),
+        )
+
 
     def norm_back(q_raw, k_raw, cols, dq_hat, dk_hat, q_inner, k_inner):
         inner = token_sums(jnp.sum(q_inner, axis=1), jnp.sum(k_inner, axis=1)) / model_width
@@ -1003,12 +1064,17 @@
             raws.append((scale * (d_hat - raw * scale * inner[n][:, None])).astype(BF16))
         return raws
 
-    (other,), ((dq_raw, dk_raw),) = advance(
-        [(norm_back, (q_raw, k_raw, cols, dq_hat, dk_hat, q_inner, k_inner))],
+    (other,), ((dq_raw, dk_raw), made) = advance(
+        [
+            (norm_back, (q_raw, k_raw, cols, dq_hat, dk_hat, q_inner, k_inner)),
+            (early_grads, (o_low, gathered, dv_raw) + tuple(d_blocks)),
+        ],
         extra=[(router_sums, "z2")],
         out=[("x", (3, 1, 0)), ("y", (1, 0, 1))],
     )
     router_sums = router_sums + other
+
+    grad_w_out, grad_value = lax.psum(made, "dp")
 
     def projections_back(gathered, dq_raw, dk_raw, dv_raw, w_query, w_key, w_value):
         grads = [contract_rows(gathered, part).astype(BF16) for part in (dk_raw, dq_raw)]
@@ -1030,10 +1096,12 @@
         return [kept[i][n] for i in order]
 
     def grads_of(first, last, earlier=None):
-        all_cots = [cot_rows[i] for i in order]
+        all_cots = [cot_rows[i][0] for i in order]
+
+        places = [cot_rows[i][1] for i in order]
 
         def work(*args):
-            return expert_grads(*args[:5], first, last, args[5] if len(args) > 5 else None)
+            return expert_grads(*args[:5], places, first, last, args[5] if len(args) > 5 else None)
 
         args = (saved(0), all_cots, saved(1), saved(2), saved(3))
         return work, args if earlier is None else args + (earlier,)
@@ -1041,7 +1109,8 @@
     thirds = [experts * n // 3 for n in range(4)]
     parts = jnp.split(total_term, tensor_count, axis=0)
     (d_far, d_near, *got), _ = advance(
-        extra=[(parts[3], "c"), (parts[1], "c")] + key_sum.split_x(), out=[("y", (3, 0, 1))]
+        extra=[(parts[3], "c"), (parts[1], "c")] + key_sum.split_x(),
+        out=[("y", (3, 0, 1)), ("z", (2, 0, 0))],
     )
     key_sum.add_x(got)
     (d_across, *got), (made,) = advance(
@@ -1062,30 +1131,39 @@
     key_sum.took_z(got)
     (other, *got), ((grad_w_gate, grad_w_up, grad_w_down),) = advance(
         [grads_of(thirds[2], thirds[3], made)],
-        extra=[(router_sums, "y")] + key_sum.join_x() + query_sum.split_z(),
-    )
-    router_sums = router_sums + other
+        extra=[(attn_gain_part, "c")] + key_sum.join_x() + query_sum.split_z(),
+    )
+    attn_gain_part = attn_gain_part + other
     key_sum.took_x(got[:1])
     query_sum.add_z(got[1:])
-    (other, *got), _ = advance(
-        extra=[(attn_gain_part, "c")] + query_sum.join_z(), out=[("z", (2, 0, 0))]
-    )
-    attn_gain_part = attn_gain_part + other
+    (other, third, *got), _ = advance(
+        extra=[(attn_gain_part, "y"), (router_sums, "x")] + query_sum.join_z(),
+    )
+    gain_parts = jnp.concatenate([attn_gain_part + other, query_gain_part[0], key_gain_part[0]])
+    router_sums = router_sums + third
     query_sum.took_z(got)
     (other, third, *got), _ = advance(
-        extra=[(attn_gain_part, "y"), (router_sums, "x")] + query_sum.join_x(), out=[("z", (3, 0, 0))]
+        extra=[(gain_parts, "x"), (router_sums, "y")] + query_sum.join_x(), out=[("z", (3, 0, 0))]
     )
     query_sum.took_x(got)
     router_sums = router_sums + third
-    gain_sums = small_sum(
-        jnp.concatenate([attn_gain_part + other, query_gain_part[0], key_gain_part[0]]), ("x", "z1", "z2")
-    )
-    result = mixed + out_sum.total()
+    gain_parts = gain_parts + other
+    result = (mixed + out_sum.total()).astype(BF16)
+    (next_z, far_z, last_z), ((result, d_input, grad_query, grad_key),) = advance(
+        [
+            (
+                lambda *values: values,
+                (result, d_input.astype(BF16), query_sum.result, key_sum.result),
+            )
+        ],
+        extra=[(gain_parts, "u1"), (gain_parts, "u2"), (gain_parts, "u3")],
+    )
+    gain_sums = (gain_parts + far_z) + (next_z + last_z)
     return (
-        result.astype(BF16),
-        d_input.astype(BF16),
-        query_sum.result,
-        key_sum.result,
+        result,
+        d_input,
+        grad_query,
+        grad_key,
         grad_value.astype(F32),
         gain_sums[model_width : model_width + local_width],
         gain_sums[model_width + local_width :],

time: 1150 us -> 1130 us (0.983)
  other arithmetic: 113 us -> 75.3 us
  Pallas kernels: 426 us -> 448 us
    psum x1, waiting for transfers between devices: 0.01 us -> 66.9 us  [local_gathered(): grad_w_out, grad_value = lax.psum(made, 'dp')]
    ppermute x140, waiting for transfers between devices: 283 us -> 225 us  [send(): return lax.ppermute(value, BOTH, device_pairs(MOVES[axis]))]
    convert_element_type x19 -> x5, other arithmetic: 51.2 us -> 8.68 us  [add_low(): return total.astype(BF16)]
    pallas_call x5 -> x13, Pallas kernels: 62.1 us -> 94 us  [the longest x4 55.2 us: out_chunk(): pl.pallas_call(functools.partial(out_kernel, len(picks), slot_count), gri...]
    all_to_all x2, waiting for transfers between devices: 22.8 us -> 6.9 us  [to_groups(): lax.all_to_all(copies, BOTH, split_axis=0, concat_axis=0, tiled=True)]
    pallas_call x5 -> x4, Pallas kernels: 69.3 us -> 62.7 us  [cot_chunk(): pl.pallas_call(functools.partial(cot_kernel, count, slot_count), grid=(ex...]
    dot_general x5 -> x8, matrix products: 22.9 us -> 28.4 us  [times_transpose(): lax.dot_general(left, right, (((1,), (1,)), ((), ())), preferred_element_...]
    pallas_call x10 -> x9, Pallas kernels: 53 us -> 50.1 us  [pair_sum(): pl.pallas_call(pair_kernel, grid=(rows // tile,), in_specs=[stack, stack]...]
  transfers between devices with their start and end apart: 144 -> 144, of which waited for: 46 -> 58; matrix products, arithmetic and copies ran while one was open for 14% -> 11% of each run, Pallas kernels for 36% -> 38%
where the time goes in v3:
time: 1130 us; the launch traced here: 1120 us
  Pallas kernels  448 us (40%)
  waiting for transfers between devices  304 us (27%)
  starting transfers between devices  168 us (15%)
  other arithmetic  75.3 us (7%)
  matrix products  51.5 us (5%)
  local copies, waits for them, and re-layouts  45.9 us (4%)
  between operations  16.8 us (1%)
  blocking collectives  12.4 us (1%)
    ppermute x140, waiting for transfers between devices, send(): return lax.ppermute(value, BOTH, device_pairs(MOVES[axis]))  225 us
    ppermute x140, starting transfers between devices, send(): return lax.ppermute(value, BOTH, device_pairs(MOVES[axis]))  156 us
    pallas_call x5, Pallas kernels, main_chunk(): pl.pallas_call(functools.partial(main_kernel, count, slot_count), grid=(e...  124 us
    psum x1, waiting for transfers between devices, local_gathered(): grad_w_out, grad_value = lax.psum(made, 'dp')  66.9 us
    pallas_call x4, Pallas kernels, cot_chunk(): pl.pallas_call(functools.partial(cot_kernel, count, slot_count), grid=(ex...  62.7 us
    pallas_call x3, Pallas kernels, expert_grads(): pl.pallas_call(functools.partial(grad_kernel, count), grid=(last - first,...  61.4 us
    pallas_call x4, Pallas kernels, out_chunk(): pl.pallas_call(functools.partial(out_kernel, len(picks), slot_count), gri...  55.2 us
    pallas_call x9, Pallas kernels, pair_sum(): pl.pallas_call(pair_kernel, grid=(rows // tile,), in_specs=[stack, stack]...  50.1 us
  transfers between devices with their start and end apart: 144, of which 58 were waited for; matrix products, arithmetic and copies ran while one was open for 11% of the time, Pallas kernels for 38%

profile of v3, /device:TPU:0, one launch (start us, length us, event | category | flops | bytes accessed | tf_op | source)
XLA Modules:
  0.0 1122.2 jit_solution(6370731703307828133)
XLA Ops:
  13.9 7.4 all-to-all-start
  42.0 7.6 collective-permute-done.refs_2_
  54.8 5.0 collective-permute-start.4
  62.8 17.2 %shard_map.272 = (f32[1024,512]{1,0:T(8,128)}, f32[1024,512]{1,0:T(8,128)}, bf16[1024,512]{1,0:T(8,128)(2,1)}, f32[1024,128]{1,0:T(8,128)}, f32[1024,128]{1,0:T(8,128)}) custom-call(bf16[256,2048]{1,0:T(8,128)(2,1)} %fusion.18.refs_0_, bf16[256,2048]{1,0:T(8,128)(2,1)} %collective-permute-done.1.refs_1_, bf16[256,2048]{1,0:T(8,128)(2,1)} %collective-permute-done.refs_2_, ...), custom_call_target="tpu_custom_call" | custom-call | flops 6442450944 | bytes 15728640 | tf_op jit(solution)/shard_map/pallas_call | solution.py:563
  83.1 6.4 psum.28
  95.0 16.9 %shard_map.273 = (bf16[1024,512]{1,0:T(8,128)(2,1)}, f32[1024,512]{1,0:T(8,128)}, bf16[1024,512]{1,0:T(8,128)(2,1)}, bf16[1024,512]{1,0:T(8,128)(2,1)}) custom-call(f32[1024,512]{1,0:T(8,128)} %get-tuple-element.1321.q_ref, f32[1024,512]{1,0:T(8,128)} %get-tuple-element.1325.k_ref, bf16[1024,512]{1,0:T(8,128)(2,1)} %get-tuple-element.1289.v_ref, ...), custom_call_target="tpu_custom_call" | custom-call | flops 2147483648 | bytes 10485760 | tf_op jit(solution)/shard_map/pallas_call | solution.py:685
  111.9 4.3 collective-permute-done.10.refs_0_
  129.7 18.1 %collective-permute-done.20 = bf16[256,2048]{1,0:T(8,128)(2,1)S(1)} collective-permute-done((bf16[256,2048]{1,0:T(8,128)(2,1)S(1)}, bf16[256,2048]{1,0:T(8,128)(2,1)S(1)}, u32[]{:S(2)}, u32[]{:S(2)}) %collective-permute-start.20) | collective-permute-done | bytes 1048608 | tf_op jit(solution)/shard_map/ppermute | solution.py:109
  159.9 15.7 %shard_map.274 = (bf16[8,256,2048]{2,1,0:T(8,128)(2,1)}, f32[8,256,256]{2,1,0:T(8,128)}) custom-call(bf16[8,256,256]{2,1,0:T(8,128)(2,1)} %bitcast.153, bf16[8,256,2048]{2,1,0:T(8,128)(2,1)} %refs_4_.1, bf16[256,2048]{1,0:T(8,128)(2,1)} %refs_0_, bf16[256,2048]{1,0:T(8,128)(2,1)} %collective-permute-done.2.refs_1_, ...), custom_call_target="tpu_custom_call" | custom-call | flops 4294967296 | bytes 25165824 | tf_op jit(solution)/shard_map/pallas_call | solution.py:371
  187.3 15.7 %shard_map.275 = (bf16[8,256,2048]{2,1,0:T(8,128)(2,1)}, f32[8,256,256]{2,1,0:T(8,128)}) custom-call(bf16[8,256,256]{2,1,0:T(8,128)(2,1)} %bitcast.150, bf16[8,256,2048]{2,1,0:T(8,128)(2,1)} %refs_4_.1, bf16[256,2048]{1,0:T(8,128)(2,1)} %collective-permute-done.4.refs_0_, bf16[256,2048]{1,0:T(8,128)(2,1)} %collective-permute-done.5.refs_1_, ...), custom_call_target="tpu_custom_call" | custom-call | flops 4294967296 | bytes 25165824 | tf_op jit(solution)/shard_map/pallas_call | solution.py:371
  202.9 6.9 all-to-all-done.1
  217.0 27.6 %shard_map.276 = (bf16[8,256,2048]{2,1,0:T(8,128)(2,1)}, bf16[8,256,256]{2,1,0:T(8,128)(2,1)}, bf16[8,256,256]{2,1,0:T(8,128)(2,1)}, bf16[8,256,256]{2,1,0:T(8,1...) custom-call(bf16[8,256,256]{2,1,0:T(8,128)(2,1)} %bitcast.154, ...), custom_call_target="tpu_custom_call" | custom-call | flops 12884901888 | bytes 41943040 | tf_op jit(solution)/shard_map/pallas_call | solution.py:394
  246.8 6.9 collective-permute-done.39.refs_5_
  254.1 5.9 shard_map.277
  260.0 11.0 collective-permute-done.38.refs_1_
  274.5 27.8 %shard_map.278 = (bf16[8,256,2048]{2,1,0:T(8,128)(2,1)}, bf16[8,256,256]{2,1,0:T(8,128)(2,1)}, bf16[8,256,256]{2,1,0:T(8,128)(2,1)}, bf16[8,256,256]{2,1,0:T(8,1...) custom-call(bf16[8,256,256]{2,1,0:T(8,128)(2,1)} %bitcast.151, ...), custom_call_target="tpu_custom_call" | custom-call | flops 12884901888 | bytes 41943040 | tf_op jit(solution)/shard_map/pallas_call | solution.py:394
  304.5 6.9 collective-permute-done.53.refs_7_
  312.0 15.7 %shard_map.280 = (bf16[8,256,2048]{2,1,0:T(8,128)(2,1)}, f32[8,256,256]{2,1,0:T(8,128)}) custom-call(bf16[8,256,256]{2,1,0:T(8,128)(2,1)} %bitcast.147, bf16[8,256,2048]{2,1,0:T(8,128)(2,1)} %refs_4_.1, bf16[256,2048]{1,0:T(8,128)(2,1)} %copy-done.41, bf16[256,2048]{1,0:T(8,128)(2,1)} %collective-permute-done.15.refs_1_, ...), custom_call_target="tpu_custom_call" | custom-call | flops 4294967296 | bytes 25165824 | tf_op jit(solution)/shard_map/pallas_call | solution.py:371
  327.7 6.0 shard_map.279
  341.4 28.0 %shard_map.281 = (bf16[8,256,2048]{2,1,0:T(8,128)(2,1)}, bf16[8,256,256]{2,1,0:T(8,128)(2,1)}, bf16[8,256,256]{2,1,0:T(8,128)(2,1)}, bf16[8,256,256]{2,1,0:T(8,1...) custom-call(bf16[8,256,256]{2,1,0:T(8,128)(2,1)} %bitcast.148, ...), custom_call_target="tpu_custom_call" | custom-call | flops 12884901888 | bytes 41943040 | tf_op jit(solution)/shard_map/pallas_call | solution.py:394
  380.1 15.7 %shard_map.283 = (bf16[8,256,2048]{2,1,0:T(8,128)(2,1)}, f32[8,256,256]{2,1,0:T(8,128)}) custom-call(bf16[8,256,256]{2,1,0:T(8,128)(2,1)} %pad_maximum_fusion.1.picks_ref, bf16[8,256,2048]{2,1,0:T(8,128)(2,1)} %refs_4_.1, bf16[256,2048]{1,0:T(8,128)(2,1)} %collective-permute-done.51.refs_0_, bf16[256,2048]{1,0:T(8,128)(2,1)} %copy-done.50, ...), custom_call_target="tpu_custom_call" | custom-call | flops 4294967296 | bytes 25165824 | tf_op jit(solution)/shard_map/pallas_call | solution.py:371
  395.7 5.9 shard_map.282
  406.2 20.2 %shard_map.284 = (bf16[8,128,2048]{2,1,0:T(8,128)(2,1)}, bf16[8,128,256]{2,1,0:T(8,128)(2,1)}, bf16[8,128,256]{2,1,0:T(8,128)(2,1)}, bf16[8,128,256]{2,1,0:T(8,1...) custom-call(bf16[4,256,256]{2,1,0:T(8,128)(2,1)} %bitcast.160, ...), custom_call_target="tpu_custom_call" | custom-call | flops 6442450944 | bytes 29360128 | tf_op jit(solution)/shard_map/pallas_call | solution.py:394
  439.3 20.0 %shard_map.286 = (bf16[8,128,2048]{2,1,0:T(8,128)(2,1)}, bf16[8,128,256]{2,1,0:T(8,128)(2,1)}, bf16[8,128,256]{2,1,0:T(8,128)(2,1)}, bf16[8,128,256]{2,1,0:T(8,1...) custom-call(bf16[4,256,256]{2,1,0:T(8,128)(2,1)} %bitcast.158, ...), custom_call_target="tpu_custom_call" | custom-call | flops 6442450944 | bytes 29360128 | tf_op jit(solution)/shard_map/pallas_call | solution.py:394
  478.6 14.0 %shard_map.289 = (bf16[4,256,2048]{2,1,0:T(8,128)(2,1)}, bf16[4,256,2048]{2,1,0:T(8,128)(2,1)}) custom-call(bf16[8,256,256]{2,1,0:T(8,128)(2,1)} %bitcast.155, bf16[8,256,256]{2,1,0:T(8,128)(2,1)} %get-tuple-element.1494.refs_1_.refs_10_, bf16[8,256,2048]{2,1,0:T(8,128)(2,1)} %refs_4_.1), custom_call_target="tpu_custom_call" | custom-call | flops 4294967296 | bytes 25165824 | tf_op jit(solution)/shard_map/pallas_call | solution.py:437
  492.5 4.8 all-to-all-done.2
  497.4 4.2 shard_map.288
  504.0 4.4 shard_map.292
  508.4 13.7 %shard_map.290 = (bf16[4,256,2048]{2,1,0:T(8,128)(2,1)}, bf16[4,256,2048]{2,1,0:T(8,128)(2,1)}) custom-call(bf16[8,256,256]{2,1,0:T(8,128)(2,1)} %bitcast.152, bf16[8,256,256]{2,1,0:T(8,128)(2,1)} %get-tuple-element.1495.refs_1_.refs_11_, bf16[8,256,2048]{2,1,0:T(8,128)(2,1)} %refs_4_.1), custom_call_target="tpu_custom_call" | custom-call | flops 4294967296 | bytes 25165824 | tf_op jit(solution)/shard_map/pallas_call | solution.py:437
  522.1 5.9 shard_map.291
  531.0 13.7 %shard_map.293 = (bf16[4,256,2048]{2,1,0:T(8,128)(2,1)}, bf16[4,256,2048]{2,1,0:T(8,128)(2,1)}) custom-call(bf16[8,256,256]{2,1,0:T(8,128)(2,1)} %bitcast.149, bf16[8,256,256]{2,1,0:T(8,128)(2,1)} %get-tuple-element.1496.refs_1_.refs_12_, bf16[8,256,2048]{2,1,0:T(8,128)(2,1)} %refs_4_.1), custom_call_target="tpu_custom_call" | custom-call | flops 4294967296 | bytes 25165824 | tf_op jit(solution)/shard_map/pallas_call | solution.py:437
  544.7 5.9 shard_map.294
  556.0 4.7 shard_map.295
  564.7 13.8 %shard_map.296 = (bf16[4,256,2048]{2,1,0:T(8,128)(2,1)}, bf16[4,256,2048]{2,1,0:T(8,128)(2,1)}) custom-call(bf16[4,256,256]{2,1,0:T(8,128)(2,1)} %bitcast.161, bf16[4,256,256]{2,1,0:T(8,128)(2,1)} %bitcast.159, bf16[8,128,256]{2,1,0:T(8,128)(2,1)} %get-tuple-element.1497.refs_2_.refs_13_, bf16[8,128,256]{2,1,0:T(8,128)(2,1)} %get-tuple-element.1498.refs_3_.refs_14_, ...), custom_call_target="tpu_custom_call" | custom-call | flops 4294967296 | bytes 25165824 | tf_op jit(solution)/shard_map/pallas_call | solution.py:437
  578.5 5.9 shard_map.297
  587.8 4.8 shard_map.298
  600.0 6.3 shard_map.299
  606.3 12.1 %collective-permute-done.88 = bf16[256,2048]{1,0:T(8,128)(2,1)} collective-permute-done((bf16[256,2048]{1,0:T(8,128)(2,1)}, bf16[256,2048]{1,0:T(8,128)(2,1)}, u32[]{:S(2)}, u32[]{:S(2)}) %collective-permute-start.88) | collective-permute-done | bytes 1048608 | tf_op jit(solution)/shard_map/ppermute | solution.py:109
  630.0 15.8 %collective-permute-done.94 = f32[72,2048]{1,0:T(8,128)} collective-permute-done((f32[72,2048]{1,0:T(8,128)}, f32[72,2048]{1,0:T(8,128)}, u32[]{:S(2)}, u32[]{:S(2)}) %collective-permute-start.94) | collective-permute-done | bytes 589856 | tf_op jit(solution)/shard_map/ppermute | solution.py:109
  645.7 6.7 collective-permute-done.92
  673.9 22.5 %shard_map.301 = (f32[1024,512]{1,0:T(8,128)}, f32[1024,512]{1,0:T(8,128)}, bf16[1024,512]{1,0:T(8,128)(2,1)}, f32[1,512]{1,0:T(1,128)}, f32[1,512]{1,0:T(1,128)...) custom-call(f32[1024,512]{1,0:T(8,128)} %get-tuple-element.1321.q_ref, f32[1024,512]{1,0:T(8,128)} %get-tuple-element.1325.k_ref, ...), custom_call_target="tpu_custom_call" | custom-call | flops 5368709120 | bytes 16777216 | tf_op jit(solution)/shard_map/pallas_call | solution.py:712
  696.3 9.2 collective-permute-done.97.refs_3_
  710.2 5.9 psum.29
  720.5 6.2 fusion.13
  735.9 11.3 %collective-permute-done.101 = f32[72,2048]{1,0:T(8,128)S(1)} collective-permute-done((f32[72,2048]{1,0:T(8,128)S(1)}, f32[72,2048]{1,0:T(8,128)S(1)}, u32[]{:S(2)}, u32[]{:S(2)}) %collective-permute-start.101) | collective-permute-done | bytes 589856 | tf_op jit(solution)/shard_map/ppermute | solution.py:109
  747.3 4.9 shard_map.302
  761.1 5.8 fusion.74
  766.9 7.0 add_convert_fusion
  773.9 5.9 convolution_convert_fusion
  785.3 4.7 shard_map.303
  795.3 21.0 %collective-permute-done.110 = bf16[1024,512]{1,0:T(8,128)(2,1)} collective-permute-done((bf16[1024,512]{1,0:T(8,128)(2,1)}, bf16[1024,512]{1,0:T(8,128)(2,1)}, u32[]{:S(2)}, u32[]{:S(2)}) %collective-permute-start.110) | collective-permute-done | bytes 1048608 | tf_op jit(solution)/shard_map/ppermute | solution.py:109
  833.2 15.7 %shard_map.304 = (f32[8,2048,256]{2,1,0:T(8,128)}, f32[8,2048,256]{2,1,0:T(8,128)}, f32[8,256,2048]{2,1,0:T(8,128)}) custom-call(bf16[8,256,2048]{2,1,0:T(8,128)(2,1)} %get-tuple-element.1484.refs_0_, bf16[8,256,2048]{2,1,0:T(8,128)(2,1)} %get-tuple-element.1485.refs_1_, bf16[8,256,2048]{2,1,0:T(8,128)(2,1)} %get-tuple-element.1486.refs_2_, ...), custom_call_target="tpu_custom_call" | custom-call | flops 6442450944 | bytes 29360128 | tf_op jit(solution)/shard_map/pallas_call | solution.py:483
  848.9 13.8 %collective-permute-done.116 = bf16[256,512]{1,0:T(8,128)(2,1)S(1)} collective-permute-done((bf16[256,512]{1,0:T(8,128)(2,1)}, bf16[256,512]{1,0:T(8,128)(2,1)S(1)}, u32[]{:S(2)}, u32[]{:S(2)}) %collective-permute-start.116) | collective-permute-done | bytes 262176 | tf_op jit(solution)/shard_map/ppermute | solution.py:109
  868.3 26.0 %collective-permute-start.118 = (bf16[256,512]{1,0:T(8,128)(2,1)S(1)}, bf16[256,512]{1,0:T(8,128)(2,1)S(1)}, u32[]{:S(2)}, u32[]{:S(2)}) collective-permute-start(bf16[256,512]{1,0:T(8,128)(2,1)S(1)} %add_convert_fusion.7), channel_id=1, source_target_pairs={{0,8},{1,9},{2,10},{3,11},{4,12},{5,13},{6,14},{7,15},{8,16},{9,17... | collective-permute-start | bytes 786440 | tf_op jit(solution)/shard_map/ppermute | solution.py:109
  897.5 22.9 %shard_map.306 = (f32[8,2048,256]{2,1,0:T(8,128)}, f32[8,2048,256]{2,1,0:T(8,128)}, f32[8,256,2048]{2,1,0:T(8,128)}) custom-call(bf16[8,256,2048]{2,1,0:T(8,128)(2,1)} %get-tuple-element.1484.refs_0_, bf16[8,256,2048]{2,1,0:T(8,128)(2,1)} %get-tuple-element.1485.refs_1_, ...), custom_call_target="tpu_custom_call", output_to_operand_aliasing={{0}: (25, {}), {1}: (26, {}), {2}: (27, {})} | custom-call | flops 9663676416 | bytes 44040192 | tf_op jit(solution)/shard_map/pallas_call | solution.py:483
  934.8 22.9 %shard_map.307 = (f32[8,2048,256]{2,1,0:T(8,128)}, f32[8,2048,256]{2,1,0:T(8,128)}, f32[8,256,2048]{2,1,0:T(8,128)}) custom-call(bf16[8,256,2048]{2,1,0:T(8,128)(2,1)} %get-tuple-element.1484.refs_0_, bf16[8,256,2048]{2,1,0:T(8,128)(2,1)} %get-tuple-element.1485.refs_1_, ...), custom_call_target="tpu_custom_call", output_to_operand_aliasing={{0}: (25, {}), {1}: (26, {}), {2}: (27, {})} | custom-call | flops 9663676416 | bytes 44040192 | tf_op jit(solution)/shard_map/pallas_call | solution.py:483
  959.7 4.9 collective-permute-start.130
  972.1 5.5 collective-permute-done.130
  977.6 15.3 %collective-permute-done.131 = bf16[256,512]{1,0:T(8,128)(2,1)S(1)} collective-permute-done((bf16[256,512]{1,0:T(8,128)(2,1)S(1)}, bf16[256,512]{1,0:T(8,128)(2,1)S(1)}, u32[]{:S(2)}, u32[]{:S(2)}) %collective-permute-start.131) | collective-permute-done | bytes 262176 | tf_op jit(solution)/shard_map/ppermute | solution.py:109
  1000.7 6.8 collective-permute-start.136
  1007.5 66.9 %all-reduce.4.cloned.1.call-done = (bf16[2048,512]{1,0:T(8,128)(2,1)}, bf16[512,2048]{1,0:T(8,128)(2,1)}) async-done(((bf16[2048,512]{1,0:T(8,128)(2,1)}, bf16[512,2048]{1,0:T(8,128)(2,1)}), (bf16[2048,512]{1,0:T(8,128)(2,1)}, bf16[512,2048]{1,0:T(8,128)(2,1)})) %all-reduce.4.cloned.1.call-update) | async-done | bytes 4194320 | tf_op jit(solution)/shard_map/psum | solution.py:1077
  1074.3 4.3 convert_element_type.299
  1088.2 8.2 collective-permute-done.134
  1102.4 5.2 fusion.24
  (585 shorter events, 327.5 us)
Async XLA Ops:
  13.9 26.5 %all-to-all-start = ((f32[32,8,256]{2,1,0:T(8,128)}), f32[32,8,256]{2,1,0:T(8,128)}, u32[]{:S(2)}, u32[]{:S(2)}) async-start(f32[32,8,256]{2,1,0:T(8,128)} %bitcast.4), calls=%async_computation | async-start | bytes 524288 | tf_op jit(solution)/shard_map/all_to_all | solution.py:793
  21.4 28.3 %collective-permute-start = (bf16[256,2048]{1,0:T(8,128)(2,1)}, bf16[256,2048]{1,0:T(8,128)(2,1)}, u32[]{:S(2)}, u32[]{:S(2)}) collective-permute-start(bf16[256,2048]{1,0:T(8,128)(2,1)} %fusion.18.refs_0_), channel_id=1, source_target_pairs={{0,2},{1,3},{2,0},{3,1},{4,6},{5,7},{6,4},{7,5},{8,10},{9,11},{10,... | collective-permute-start | bytes 3145736 | tf_op jit(solution)/shard_map/ppermute | solution.py:109
  23.1 26.5 %collective-permute-start.1 = (bf16[256,2048]{1,0:T(8,128)(2,1)}, bf16[256,2048]{1,0:T(8,128)(2,1)}, u32[]{:S(2)}, u32[]{:S(2)}) collective-permute-start(bf16[256,2048]{1,0:T(8,128)(2,1)} %fusion.18.refs_0_), channel_id=1, source_target_pairs={{0,1},{1,0},{2,3},{3,2},{4,5},{5,4},{6,7},{7,6},{8,9},{9,8},{10,11... | collective-permute-start | bytes 3145736 | tf_op jit(solution)/shard_map/ppermute | solution.py:109
  23.1 27.9 %collective-permute-start.2 = (bf16[256,2048]{1,0:T(8,128)(2,1)S(1)}, bf16[256,2048]{1,0:T(8,128)(2,1)}, u32[]{:S(2)}, u32[]{:S(2)}) collective-permute-start(bf16[256,2048]{1,0:T(8,128)(2,1)S(1)} %copy-done.11), channel_id=1, source_target_pairs={{0,24},{1,25},{2,26},{3,27},{4,28},{5,29},{6,30},{7,31},{8,0},{9,1... | collective-permute-start | bytes 3145736 | tf_op jit(solution)/shard_map/ppermute | solution.py:109
  54.8 35.3 %collective-permute-start.4 = (bf16[256,2048]{1,0:T(8,128)(2,1)}, bf16[256,2048]{1,0:T(8,128)(2,1)}, u32[]{:S(2)}, u32[]{:S(2)}) collective-permute-start(bf16[256,2048]{1,0:T(8,128)(2,1)} %collective-permute-done.2.refs_1_), channel_id=1, source_target_pairs={{0,24},{1,25},{2,26},{3,27},{4,28},{5,29},{6,30},{7,31},{8,0},{9,1... | collective-permute-start | bytes 3145736 | tf_op jit(solution)/shard_map/ppermute | solution.py:109
  59.8 30.3 %collective-permute-start.5 = (bf16[256,2048]{1,0:T(8,128)(2,1)}, bf16[256,2048]{1,0:T(8,128)(2,1)}, u32[]{:S(2)}, u32[]{:S(2)}) collective-permute-start(bf16[256,2048]{1,0:T(8,128)(2,1)} %collective-permute-done.2.refs_1_), channel_id=1, source_target_pairs={{0,4},{1,5},{2,6},{3,7},{4,0},{5,1},{6,2},{7,3},{8,12},{9,13},{10,... | collective-permute-start | bytes 3145736 | tf_op jit(solution)/shard_map/ppermute | solution.py:109
  60.6 29.6 %collective-permute-start.6 = (bf16[256,2048]{1,0:T(8,128)(2,1)S(1)}, bf16[256,2048]{1,0:T(8,128)(2,1)}, u32[]{:S(2)}, u32[]{:S(2)}) collective-permute-start(bf16[256,2048]{1,0:T(8,128)(2,1)S(1)} %copy-done.11), channel_id=1, source_target_pairs={{0,2},{1,3},{2,0},{3,1},{4,6},{5,7},{6,4},{7,5},{8,10},{9,11},{10,... | collective-permute-start | bytes 3145736 | tf_op jit(solution)/shard_map/ppermute | solution.py:109
  61.7 28.5 %collective-permute-start.7 = (bf16[256,2048]{1,0:T(8,128)(2,1)S(1)}, bf16[256,2048]{1,0:T(8,128)(2,1)}, u32[]{:S(2)}, u32[]{:S(2)}) collective-permute-start(bf16[256,2048]{1,0:T(8,128)(2,1)S(1)} %copy-done.11), channel_id=1, source_target_pairs={{0,1},{1,0},{2,3},{3,2},{4,5},{5,4},{6,7},{7,6},{8,9},{9,8},{10,11... | collective-permute-start | bytes 3145736 | tf_op jit(solution)/shard_map/ppermute | solution.py:109
  61.7 28.5 %collective-permute-start.8 = (bf16[256,2048]{1,0:T(8,128)(2,1)}, bf16[256,2048]{1,0:T(8,128)(2,1)}, u32[]{:S(2)}, u32[]{:S(2)}) collective-permute-start(bf16[256,2048]{1,0:T(8,128)(2,1)} %collective-permute-done.2.refs_1_), channel_id=1, source_target_pairs={{0,1},{1,0},{2,3},{3,2},{4,5},{5,4},{6,7},{7,6},{8,9},{9,8},{10,11... | collective-permute-start | bytes 3145736 | tf_op jit(solution)/shard_map/ppermute | solution.py:109
  178.9 31.5 %collective-permute-start.26 = (bf16[256,2048]{1,0:T(8,128)(2,1)}, bf16[256,2048]{1,0:T(8,128)(2,1)}, u32[]{:S(2)}, u32[]{:S(2)}) collective-permute-start(bf16[256,2048]{1,0:T(8,128)(2,1)} %collective-permute-done.21.refs_1_), channel_id=1, source_target_pairs={{0,24},{1,25},{2,26},{3,27},{4,28},{5,29},{6,30},{7,31},{8,0},{9,1... | collective-permute-start | bytes 3145736 | tf_op jit(solution)/shard_map/ppermute | solution.py:109
  179.8 30.6 %collective-permute-start.27 = (bf16[256,2048]{1,0:T(8,128)(2,1)}, bf16[256,2048]{1,0:T(8,128)(2,1)}, u32[]{:S(2)}, u32[]{:S(2)}) collective-permute-start(bf16[256,2048]{1,0:T(8,128)(2,1)} %collective-permute-done.21.refs_1_), channel_id=1, source_target_pairs={{0,4},{1,5},{2,6},{3,7},{4,0},{5,1},{6,2},{7,3},{8,12},{9,13},{10,... | collective-permute-start | bytes 3145736 | tf_op jit(solution)/shard_map/ppermute | solution.py:109
  181.4 29.1 %collective-permute-start.28 = (bf16[256,2048]{1,0:T(8,128)(2,1)}, bf16[256,2048]{1,0:T(8,128)(2,1)}, u32[]{:S(2)}, u32[]{:S(2)}) collective-permute-start(bf16[256,2048]{1,0:T(8,128)(2,1)} %collective-permute-done.21.refs_1_), channel_id=1, source_target_pairs={{0,2},{1,3},{2,0},{3,1},{4,6},{5,7},{6,4},{7,5},{8,10},{9,11},{10,... | collective-permute-start | bytes 3145736 | tf_op jit(solution)/shard_map/ppermute | solution.py:109
  182.0 28.5 %collective-permute-start.32 = (bf16[256,2048]{1,0:T(8,128)(2,1)}, bf16[256,2048]{1,0:T(8,128)(2,1)}, u32[]{:S(2)}, u32[]{:S(2)}) collective-permute-start(bf16[256,2048]{1,0:T(8,128)(2,1)} %collective-permute-done.23.refs_3_), channel_id=1, source_target_pairs={{0,1},{1,0},{2,3},{3,2},{4,5},{5,4},{6,7},{7,6},{8,9},{9,8},{10,11... | collective-permute-start | bytes 3145736 | tf_op jit(solution)/shard_map/ppermute | solution.py:109
  183.0 27.5 %collective-permute-start.31 = (bf16[256,2048]{1,0:T(8,128)(2,1)}, bf16[256,2048]{1,0:T(8,128)(2,1)}, u32[]{:S(2)}, u32[]{:S(2)}) collective-permute-start(bf16[256,2048]{1,0:T(8,128)(2,1)} %collective-permute-done.21.refs_1_), channel_id=1, source_target_pairs={{0,1},{1,0},{2,3},{3,2},{4,5},{5,4},{6,7},{7,6},{8,9},{9,8},{10,11... | collective-permute-start | bytes 3145736 | tf_op jit(solution)/shard_map/ppermute | solution.py:109
  211.2 33.5 %collective-permute-start.33 = (bf16[256,2048]{1,0:T(8,128)(2,1)}, bf16[256,2048]{1,0:T(8,128)(2,1)}, u32[]{:S(2)}, u32[]{:S(2)}) collective-permute-start(bf16[256,2048]{1,0:T(8,128)(2,1)} %collective-permute-done.26.refs_0_), channel_id=1, source_target_pairs={{0,24},{1,25},{2,26},{3,27},{4,28},{5,29},{6,30},{7,31},{8,0},{9,1... | collective-permute-start | bytes 3145736 | tf_op jit(solution)/shard_map/ppermute | solution.py:109
  214.3 30.4 %collective-permute-start.34 = (bf16[256,2048]{1,0:T(8,128)(2,1)}, bf16[256,2048]{1,0:T(8,128)(2,1)}, u32[]{:S(2)}, u32[]{:S(2)}) collective-permute-start(bf16[256,2048]{1,0:T(8,128)(2,1)} %collective-permute-done.26.refs_0_), channel_id=1, source_target_pairs={{0,4},{1,5},{2,6},{3,7},{4,0},{5,1},{6,2},{7,3},{8,12},{9,13},{10,... | collective-permute-start | bytes 3145736 | tf_op jit(solution)/shard_map/ppermute | solution.py:109
  215.7 29.0 %collective-permute-start.35 = (bf16[256,2048]{1,0:T(8,128)(2,1)}, bf16[256,2048]{1,0:T(8,128)(2,1)}, u32[]{:S(2)}, u32[]{:S(2)}) collective-permute-start(bf16[256,2048]{1,0:T(8,128)(2,1)} %collective-permute-done.26.refs_0_), channel_id=1, source_target_pairs={{0,1},{1,0},{2,3},{3,2},{4,5},{5,4},{6,7},{7,6},{8,9},{9,8},{10,11... | collective-permute-start | bytes 3145736 | tf_op jit(solution)/shard_map/ppermute | solution.py:109
  215.7 29.0 %collective-permute-start.36 = (bf16[256,2048]{1,0:T(8,128)(2,1)}, bf16[256,2048]{1,0:T(8,128)(2,1)}, u32[]{:S(2)}, u32[]{:S(2)}) collective-permute-start(bf16[256,2048]{1,0:T(8,128)(2,1)} %collective-permute-done.4.refs_0_), channel_id=1, source_target_pairs={{0,2},{1,3},{2,0},{3,1},{4,6},{5,7},{6,4},{7,5},{8,10},{9,11},{10,... | collective-permute-start | bytes 3145736 | tf_op jit(solution)/shard_map/ppermute | solution.py:109
  216.8 27.9 %collective-permute-start.37 = (bf16[256,2048]{1,0:T(8,128)(2,1)}, bf16[256,2048]{1,0:T(8,128)(2,1)}, u32[]{:S(2)}, u32[]{:S(2)}) collective-permute-start(bf16[256,2048]{1,0:T(8,128)(2,1)} %copy-done.41), channel_id=1, source_target_pairs={{0,1},{1,0},{2,3},{3,2},{4,5},{5,4},{6,7},{7,6},{8,9},{9,8},{10,11... | collective-permute-start | bytes 3145736 | tf_op jit(solution)/shard_map/ppermute | solution.py:109
  272.2 30.0 %collective-permute-start.44 = (bf16[256,2048]{1,0:T(8,128)(2,1)}, bf16[256,2048]{1,0:T(8,128)(2,1)}, u32[]{:S(2)}, u32[]{:S(2)}) collective-permute-start(bf16[256,2048]{1,0:T(8,128)(2,1)} %collective-permute-done.26.refs_0_), channel_id=1, source_target_pairs={{0,2},{1,3},{2,0},{3,1},{4,6},{5,7},{6,4},{7,5},{8,10},{9,11},{10,... | collective-permute-start | bytes 3145736 | tf_op jit(solution)/shard_map/ppermute | solution.py:109
  272.5 29.7 %collective-permute-start.45 = (bf16[256,2048]{1,0:T(8,128)(2,1)}, bf16[256,2048]{1,0:T(8,128)(2,1)}, u32[]{:S(2)}, u32[]{:S(2)}) collective-permute-start(bf16[256,2048]{1,0:T(8,128)(2,1)} %collective-permute-done.6.refs_3_), channel_id=1, source_target_pairs={{0,4},{1,5},{2,6},{3,7},{4,0},{5,1},{6,2},{7,3},{8,12},{9,13},{10,... | collective-permute-start | bytes 3145736 | tf_op jit(solution)/shard_map/ppermute | solution.py:109
  273.9 28.3 %collective-permute-start.46 = (bf16[256,2048]{1,0:T(8,128)(2,1)}, bf16[256,2048]{1,0:T(8,128)(2,1)S(1)}, u32[]{:S(2)}, u32[]{:S(2)}) collective-permute-start(bf16[256,2048]{1,0:T(8,128)(2,1)} %collective-permute-done.15.refs_1_), channel_id=1, source_target_pairs={{0,1},{1,0},{2,3},{3,2},{4,5},{5,4},{6,7},{7,6},{8,9},{9,8},{10,11... | collective-permute-start | bytes 3145736 | tf_op jit(solution)/shard_map/ppermute | solution.py:109
  273.9 28.4 %collective-permute-start.47 = (bf16[256,2048]{1,0:T(8,128)(2,1)}, bf16[256,2048]{1,0:T(8,128)(2,1)}, u32[]{:S(2)}, u32[]{:S(2)}) collective-permute-start(bf16[256,2048]{1,0:T(8,128)(2,1)} %collective-permute-done.36.refs_2_), channel_id=1, source_target_pairs={{0,1},{1,0},{2,3},{3,2},{4,5},{5,4},{6,7},{7,6},{8,9},{9,8},{10,11... | collective-permute-start | bytes 3145736 | tf_op jit(solution)/shard_map/ppermute | solution.py:109
  302.9 30.8 %collective-permute-start.48 = (bf16[256,2048]{1,0:T(8,128)(2,1)}, bf16[256,2048]{1,0:T(8,128)(2,1)}, u32[]{:S(2)}, u32[]{:S(2)}) collective-permute-start(bf16[256,2048]{1,0:T(8,128)(2,1)} %collective-permute-done.33.refs_0_), channel_id=1, source_target_pairs={{0,2},{1,3},{2,0},{3,1},{4,6},{5,7},{6,4},{7,5},{8,10},{9,11},{10,... | collective-permute-start | bytes 3145736 | tf_op jit(solution)/shard_map/ppermute | solution.py:109
  304.0 29.7 %collective-permute-start.49 = (bf16[256,2048]{1,0:T(8,128)(2,1)}, bf16[256,2048]{1,0:T(8,128)(2,1)}, u32[]{:S(2)}, u32[]{:S(2)}) collective-permute-start(bf16[256,2048]{1,0:T(8,128)(2,1)} %collective-permute-done.33.refs_0_), channel_id=1, source_target_pairs={{0,1},{1,0},{2,3},{3,2},{4,5},{5,4},{6,7},{7,6},{8,9},{9,8},{10,11... | collective-permute-start | bytes 3145736 | tf_op jit(solution)/shard_map/ppermute | solution.py:109
  304.0 29.7 %collective-permute-start.50 = (bf16[256,2048]{1,0:T(8,128)(2,1)}, bf16[256,2048]{1,0:T(8,128)(2,1)}, u32[]{:S(2)}, u32[]{:S(2)}) collective-permute-start(bf16[256,2048]{1,0:T(8,128)(2,1)} %collective-permute-done.38.refs_1_), channel_id=1, source_target_pairs={{0,1},{1,0},{2,3},{3,2},{4,5},{5,4},{6,7},{7,6},{8,9},{9,8},{10,11... | collective-permute-start | bytes 3145736 | tf_op jit(solution)/shard_map/ppermute | solution.py:109
  338.5 31.0 %collective-permute-start.54 = (bf16[256,2048]{1,0:T(8,128)(2,1)}, bf16[256,2048]{1,0:T(8,128)(2,1)S(1)}, u32[]{:S(2)}, u32[]{:S(2)}) collective-permute-start(bf16[256,2048]{1,0:T(8,128)(2,1)} %collective-permute-done.36.refs_2_), channel_id=1, source_target_pairs={{0,4},{1,5},{2,6},{3,7},{4,0},{5,1},{6,2},{7,3},{8,12},{9,13},{10,... | collective-permute-start | bytes 3145736 | tf_op jit(solution)/shard_map/ppermute | solution.py:109
  339.1 30.4 %collective-permute-start.55 = (bf16[256,2048]{1,0:T(8,128)(2,1)}, bf16[256,2048]{1,0:T(8,128)(2,1)}, u32[]{:S(2)}, u32[]{:S(2)}) collective-permute-start(bf16[256,2048]{1,0:T(8,128)(2,1)} %collective-permute-done.15.refs_1_), channel_id=1, source_target_pairs={{0,2},{1,3},{2,0},{3,1},{4,6},{5,7},{6,4},{7,5},{8,10},{9,11},{10,... | collective-permute-start | bytes 3145736 | tf_op jit(solution)/shard_map/ppermute | solution.py:109
  340.8 28.6 %collective-permute-start.56 = (bf16[256,2048]{1,0:T(8,128)(2,1)}, bf16[256,2048]{1,0:T(8,128)(2,1)}, u32[]{:S(2)}, u32[]{:S(2)}) collective-permute-start(bf16[256,2048]{1,0:T(8,128)(2,1)} %collective-permute-done.45.refs_4_), channel_id=1, source_target_pairs={{0,1},{1,0},{2,3},{3,2},{4,5},{5,4},{6,7},{7,6},{8,9},{9,8},{10,11... | collective-permute-start | bytes 3145736 | tf_op jit(solution)/shard_map/ppermute | solution.py:109
  340.8 28.6 %collective-permute-start.57 = (bf16[256,2048]{1,0:T(8,128)(2,1)}, bf16[256,2048]{1,0:T(8,128)(2,1)}, u32[]{:S(2)}, u32[]{:S(2)}) collective-permute-start(bf16[256,2048]{1,0:T(8,128)(2,1)} %collective-permute-done.51.refs_0_), channel_id=1, source_target_pairs={{0,1},{1,0},{2,3},{3,2},{4,5},{5,4},{6,7},{7,6},{8,9},{9,8},{10,11... | collective-permute-start | bytes 3145736 | tf_op jit(solution)/shard_map/ppermute | solution.py:109
  370.2 31.4 %collective-permute-start.60 = (bf16[256,2048]{1,0:T(8,128)(2,1)}, bf16[256,2048]{1,0:T(8,128)(2,1)}, u32[]{:S(2)}, u32[]{:S(2)}) collective-permute-start(bf16[256,2048]{1,0:T(8,128)(2,1)} %collective-permute-done.44.refs_2_), channel_id=1, source_target_pairs={{0,4},{1,5},{2,6},{3,7},{4,0},{5,1},{6,2},{7,3},{8,12},{9,13},{10,... | collective-permute-start | bytes 3145736 | tf_op jit(solution)/shard_map/ppermute | solution.py:109
  370.8 30.8 %collective-permute-start.61 = (bf16[256,2048]{1,0:T(8,128)(2,1)}, bf16[256,2048]{1,0:T(8,128)(2,1)}, u32[]{:S(2)}, u32[]{:S(2)}) collective-permute-start(bf16[256,2048]{1,0:T(8,128)(2,1)} %collective-permute-done.27.refs_1_), channel_id=1, source_target_pairs={{0,2},{1,3},{2,0},{3,1},{4,6},{5,7},{6,4},{7,5},{8,10},{9,11},{10,... | collective-permute-start | bytes 3145736 | tf_op jit(solution)/shard_map/ppermute | solution.py:109
  467.4 30.0 %collective-permute-start.76 = (bf16[2,256,2048]{2,1,0:T(8,128)(2,1)}, bf16[2,256,2048]{2,1,0:T(8,128)(2,1)}, u32[]{:S(2)}, u32[]{:S(2)}) collective-permute-start(bf16[2,256,2048]{2,1,0:T(8,128)(2,1)} %get-tuple-element.1155), channel_id=1, source_target_pairs={{0,1},{1,0},{2,3},{3,2},{4,5},{5,4},{6,7},{7,6},{8,9},{9,8},{10,11... | collective-permute-start | bytes 6291464 | tf_op jit(solution)/shard_map/ppermute | solution.py:109
  468.2 33.4 %collective-permute-start.74 = (bf16[256,2048]{1,0:T(8,128)(2,1)}, bf16[256,2048]{1,0:T(8,128)(2,1)}, u32[]{:S(2)}, u32[]{:S(2)}) collective-permute-start(bf16[256,2048]{1,0:T(8,128)(2,1)} %get-tuple-element.1152), channel_id=1, source_target_pairs={{0,4},{1,5},{2,6},{3,7},{4,0},{5,1},{6,2},{7,3},{8,12},{9,13},{10,... | collective-permute-start | bytes 3145736 | tf_op jit(solution)/shard_map/ppermute | solution.py:109
  468.9 32.7 %collective-permute-start.75 = (bf16[256,2048]{1,0:T(8,128)(2,1)}, bf16[256,2048]{1,0:T(8,128)(2,1)}, u32[]{:S(2)}, u32[]{:S(2)}) collective-permute-start(bf16[256,2048]{1,0:T(8,128)(2,1)} %shard_map.287), channel_id=1, source_target_pairs={{0,2},{1,3},{2,0},{3,1},{4,6},{5,7},{6,4},{7,5},{8,10},{9,11},{10,... | collective-permute-start | bytes 3145736 | tf_op jit(solution)/shard_map/ppermute | solution.py:109
  478.5 595.8 %all-reduce.4.cloned.1.call-start = ((), (), s32[]{:S(2)}) async-start(), calls=%async_computation.3 | async-start | bytes 8388608 | tf_op jit(solution)/shard_map/psum | solution.py:1077
  594.9 26.7 %collective-permute-start.90 = (bf16[256,2048]{1,0:T(8,128)(2,1)}, bf16[256,2048]{1,0:T(8,128)(2,1)}, u32[]{:S(2)}, u32[]{:S(2)}) collective-permute-start(bf16[256,2048]{1,0:T(8,128)(2,1)} %get-tuple-element.1255), channel_id=1, source_target_pairs={{0,24},{1,25},{2,26},{3,27},{4,28},{5,29},{6,30},{7,31},{8,0},{9,1... | collective-permute-start | bytes 3145736 | tf_op jit(solution)/shard_map/ppermute | solution.py:109
  657.1 39.2 %collective-permute-start.96 = (bf16[256,2048]{1,0:T(8,128)(2,1)}, bf16[256,2048]{1,0:T(8,128)(2,1)}, u32[]{:S(2)}, u32[]{:S(2)}) collective-permute-start(bf16[256,2048]{1,0:T(8,128)(2,1)} %get-tuple-element.1283), channel_id=1, source_target_pairs={{0,4},{1,5},{2,6},{3,7},{4,0},{5,1},{6,2},{7,3},{8,12},{9,13},{10,... | collective-permute-start | bytes 3145736 | tf_op jit(solution)/shard_map/ppermute | solution.py:109
  657.9 47.7 %collective-permute-start.97 = (bf16[256,2048]{1,0:T(8,128)(2,1)}, bf16[256,2048]{1,0:T(8,128)(2,1)}, u32[]{:S(2)}, u32[]{:S(2)}) collective-permute-start(bf16[256,2048]{1,0:T(8,128)(2,1)} %get-tuple-element.1284), channel_id=1, source_target_pairs={{0,4},{1,5},{2,6},{3,7},{4,0},{5,1},{6,2},{7,3},{8,12},{9,13},{10,... | collective-permute-start | bytes 3145736 | tf_op jit(solution)/shard_map/ppermute | solution.py:109
  659.2 46.3 %collective-permute-start.98 = (bf16[256,2048]{1,0:T(8,128)(2,1)}, bf16[256,2048]{1,0:T(8,128)(2,1)}, u32[]{:S(2)}, u32[]{:S(2)}) collective-permute-start(bf16[256,2048]{1,0:T(8,128)(2,1)} %get-tuple-element.1285), channel_id=1, source_target_pairs={{0,2},{1,3},{2,0},{3,1},{4,6},{5,7},{6,4},{7,5},{8,10},{9,11},{10,... | collective-permute-start | bytes 3145736 | tf_op jit(solution)/shard_map/ppermute | solution.py:109
  660.1 47.0 %collective-permute-start.99 = (bf16[256,2048]{1,0:T(8,128)(2,1)}, bf16[256,2048]{1,0:T(8,128)(2,1)}, u32[]{:S(2)}, u32[]{:S(2)}) collective-permute-start(bf16[256,2048]{1,0:T(8,128)(2,1)} %get-tuple-element.1286), channel_id=1, source_target_pairs={{0,2},{1,3},{2,0},{3,1},{4,6},{5,7},{6,4},{7,5},{8,10},{9,11},{10,... | collective-permute-start | bytes 3145736 | tf_op jit(solution)/shard_map/ppermute | solution.py:109
  717.4 29.8 %collective-permute-start.102 = (bf16[256,2048]{1,0:T(8,128)(2,1)}, bf16[256,2048]{1,0:T(8,128)(2,1)S(1)}, u32[]{:S(2)}, u32[]{:S(2)}) collective-permute-start(bf16[256,2048]{1,0:T(8,128)(2,1)} %get-tuple-element.1317), channel_id=1, source_target_pairs={{0,4},{1,5},{2,6},{3,7},{4,0},{5,1},{6,2},{7,3},{8,12},{9,13},{10,... | collective-permute-start | bytes 3145736 | tf_op jit(solution)/shard_map/ppermute | solution.py:109
  718.2 29.0 %collective-permute-start.103 = (bf16[256,2048]{1,0:T(8,128)(2,1)}, bf16[256,2048]{1,0:T(8,128)(2,1)}, u32[]{:S(2)}, u32[]{:S(2)}) collective-permute-start(bf16[256,2048]{1,0:T(8,128)(2,1)} %shard_map.300), channel_id=1, source_target_pairs={{0,2},{1,3},{2,0},{3,1},{4,6},{5,7},{6,4},{7,5},{8,10},{9,11},{10,... | collective-permute-start | bytes 3145736 | tf_op jit(solution)/shard_map/ppermute | solution.py:109
  719.2 28.0 %collective-permute-start.101 = (f32[72,2048]{1,0:T(8,128)S(1)}, f32[72,2048]{1,0:T(8,128)S(1)}, u32[]{:S(2)}, u32[]{:S(2)}) collective-permute-start(f32[72,2048]{1,0:T(8,128)S(1)} %copy-done.27), channel_id=1, source_target_pairs={{0,16},{1,17},{2,18},{3,19},{4,20},{5,21},{6,22},{7,23},{8,24},{9,... | collective-permute-start | bytes 1769480 | tf_op jit(solution)/shard_map/ppermute | solution.py:109
  752.2 30.0 %collective-permute-start.105 = (bf16[256,2048]{1,0:T(8,128)(2,1)}, bf16[256,2048]{1,0:T(8,128)(2,1)}, u32[]{:S(2)}, u32[]{:S(2)}) collective-permute-start(bf16[256,2048]{1,0:T(8,128)(2,1)} %get-tuple-element.1345), channel_id=1, source_target_pairs={{0,4},{1,5},{2,6},{3,7},{4,0},{5,1},{6,2},{7,3},{8,12},{9,13},{10,... | collective-permute-start | bytes 3145736 | tf_op jit(solution)/shard_map/ppermute | solution.py:109
  753.5 28.8 %collective-permute-start.106 = (bf16[256,2048]{1,0:T(8,128)(2,1)}, bf16[256,2048]{1,0:T(8,128)(2,1)}, u32[]{:S(2)}, u32[]{:S(2)}) collective-permute-start(bf16[256,2048]{1,0:T(8,128)(2,1)} %get-tuple-element.1346), channel_id=1, source_target_pairs={{0,2},{1,3},{2,0},{3,1},{4,6},{5,7},{6,4},{7,5},{8,10},{9,11},{10,... | collective-permute-start | bytes 3145736 | tf_op jit(solution)/shard_map/ppermute | solution.py:109
  754.7 27.6 %collective-permute-start.107 = (bf16[256,2048]{1,0:T(8,128)(2,1)}, bf16[256,2048]{1,0:T(8,128)(2,1)}, u32[]{:S(2)}, u32[]{:S(2)}) collective-permute-start(bf16[256,2048]{1,0:T(8,128)(2,1)} %get-tuple-element.1347), channel_id=1, source_target_pairs={{0,24},{1,25},{2,26},{3,27},{4,28},{5,29},{6,30},{7,31},{8,0},{9,1... | collective-permute-start | bytes 3145736 | tf_op jit(solution)/shard_map/ppermute | solution.py:109
  823.0 39.7 %collective-permute-start.113 = (bf16[256,2048]{1,0:T(8,128)(2,1)}, bf16[256,2048]{1,0:T(8,128)(2,1)S(1)}, u32[]{:S(2)}, u32[]{:S(2)}) collective-permute-start(bf16[256,2048]{1,0:T(8,128)(2,1)} %add_convert_fusion.4), channel_id=1, source_target_pairs={{0,2},{1,3},{2,0},{3,1},{4,6},{5,7},{6,4},{7,5},{8,10},{9,11},{10,... | collective-permute-start | bytes 3145736 | tf_op jit(solution)/shard_map/ppermute | solution.py:109
  824.1 39.0 %collective-permute-start.114 = (bf16[1024,512]{1,0:T(8,128)(2,1)}, bf16[1024,512]{1,0:T(8,128)(2,1)S(1)}, u32[]{:S(2)}, u32[]{:S(2)}) collective-permute-start(bf16[1024,512]{1,0:T(8,128)(2,1)} %constant_dynamic-slice_fusion.6), channel_id=1, source_target_pairs={{0,4},{1,5},{2,6},{3,7},{4,0},{5,1},{6,2},{7,3},{8,12},{9,13},{10,... | collective-permute-start | bytes 3145736 | tf_op jit(solution)/shard_map/ppermute | solution.py:109
  829.4 33.3 %collective-permute-start.116 = (bf16[256,512]{1,0:T(8,128)(2,1)}, bf16[256,512]{1,0:T(8,128)(2,1)S(1)}, u32[]{:S(2)}, u32[]{:S(2)}) collective-permute-start(bf16[256,512]{1,0:T(8,128)(2,1)} %get-tuple-element.1396), channel_id=1, source_target_pairs={{0,16},{1,17},{2,18},{3,19},{4,20},{5,21},{6,22},{7,23},{8,24},{9,... | collective-permute-start | bytes 786440 | tf_op jit(solution)/shard_map/ppermute | solution.py:109
  832.3 30.4 %collective-permute-start.117 = (bf16[256,512]{1,0:T(8,128)(2,1)S(1)}, bf16[256,512]{1,0:T(8,128)(2,1)}, u32[]{:S(2)}, u32[]{:S(2)}) collective-permute-start(bf16[256,512]{1,0:T(8,128)(2,1)S(1)} %get-tuple-element.1397), channel_id=1, source_target_pairs={{0,24},{1,25},{2,26},{3,27},{4,28},{5,29},{6,30},{7,31},{8,0},{9,1... | collective-permute-start | bytes 786440 | tf_op jit(solution)/shard_map/ppermute | solution.py:109
  866.5 56.4 %collective-permute-start.121 = (bf16[256,2048]{1,0:T(8,128)(2,1)}, bf16[256,2048]{1,0:T(8,128)(2,1)}, u32[]{:S(2)}, u32[]{:S(2)}) collective-permute-start(bf16[256,2048]{1,0:T(8,128)(2,1)} %shard_map.305), channel_id=1, source_target_pairs={{0,4},{1,5},{2,6},{3,7},{4,0},{5,1},{6,2},{7,3},{8,12},{9,13},{10,... | collective-permute-start | bytes 3145736 | tf_op jit(solution)/shard_map/ppermute | solution.py:109
  867.2 55.7 %collective-permute-start.122 = (bf16[256,2048]{1,0:T(8,128)(2,1)}, bf16[256,2048]{1,0:T(8,128)(2,1)}, u32[]{:S(2)}, u32[]{:S(2)}) collective-permute-start(bf16[256,2048]{1,0:T(8,128)(2,1)} %get-tuple-element.1440), channel_id=1, source_target_pairs={{0,2},{1,3},{2,0},{3,1},{4,6},{5,7},{6,4},{7,5},{8,10},{9,11},{10,... | collective-permute-start | bytes 3145736 | tf_op jit(solution)/shard_map/ppermute | solution.py:109
  868.3 54.6 %collective-permute-start.118 = (bf16[256,512]{1,0:T(8,128)(2,1)S(1)}, bf16[256,512]{1,0:T(8,128)(2,1)S(1)}, u32[]{:S(2)}, u32[]{:S(2)}) collective-permute-start(bf16[256,512]{1,0:T(8,128)(2,1)S(1)} %add_convert_fusion.7), channel_id=1, source_target_pairs={{0,8},{1,9},{2,10},{3,11},{4,12},{5,13},{6,14},{7,15},{8,16},{9,17... | collective-permute-start | bytes 786440 | tf_op jit(solution)/shard_map/ppermute | solution.py:109
  894.2 28.6 %collective-permute-start.119 = (bf16[256,512]{1,0:T(8,128)(2,1)S(1)}, bf16[256,512]{1,0:T(8,128)(2,1)}, u32[]{:S(2)}, u32[]{:S(2)}) collective-permute-start(bf16[256,512]{1,0:T(8,128)(2,1)S(1)} %add_convert_fusion.7), channel_id=1, source_target_pairs={{0,16},{1,17},{2,18},{3,19},{4,20},{5,21},{6,22},{7,23},{8,24},{9,... | collective-permute-start | bytes 786440 | tf_op jit(solution)/shard_map/ppermute | solution.py:109
  894.2 28.6 %collective-permute-start.120 = (bf16[256,512]{1,0:T(8,128)(2,1)S(1)}, bf16[256,512]{1,0:T(8,128)(2,1)}, u32[]{:S(2)}, u32[]{:S(2)}) collective-permute-start(bf16[256,512]{1,0:T(8,128)(2,1)S(1)} %add_convert_fusion.7), channel_id=1, source_target_pairs={{0,24},{1,25},{2,26},{3,27},{4,28},{5,29},{6,30},{7,31},{8,0},{9,1... | collective-permute-start | bytes 786440 | tf_op jit(solution)/shard_map/ppermute | solution.py:109
  926.9 30.9 %collective-permute-start.124 = (bf16[1024,512]{1,0:T(8,128)(2,1)S(1)}, bf16[1024,512]{1,0:T(8,128)(2,1)}, u32[]{:S(2)}, u32[]{:S(2)}) collective-permute-start(bf16[1024,512]{1,0:T(8,128)(2,1)S(1)} %bitcast.145), channel_id=1, source_target_pairs={{0,4},{1,5},{2,6},{3,7},{4,0},{5,1},{6,2},{7,3},{8,12},{9,13},{10,... | collective-permute-start | bytes 3145736 | tf_op jit(solution)/shard_map/ppermute | solution.py:109
  931.0 26.7 %collective-permute-start.125 = (bf16[256,512]{1,0:T(8,128)(2,1)}, bf16[256,512]{1,0:T(8,128)(2,1)S(1)}, u32[]{:S(2)}, u32[]{:S(2)}) collective-permute-start(bf16[256,512]{1,0:T(8,128)(2,1)} %get-tuple-element.1481), channel_id=1, source_target_pairs={{0,8},{1,9},{2,10},{3,11},{4,12},{5,13},{6,14},{7,15},{8,16},{9,17... | collective-permute-start | bytes 786440 | tf_op jit(solution)/shard_map/ppermute | solution.py:109
  931.0 26.7 %collective-permute-start.126 = (bf16[256,512]{1,0:T(8,128)(2,1)}, bf16[256,512]{1,0:T(8,128)(2,1)S(1)}, u32[]{:S(2)}, u32[]{:S(2)}) collective-permute-start(bf16[256,512]{1,0:T(8,128)(2,1)} %get-tuple-element.1482), channel_id=1, source_target_pairs={{0,16},{1,17},{2,18},{3,19},{4,20},{5,21},{6,22},{7,23},{8,24},{9,... | collective-permute-start | bytes 786440 | tf_op jit(solution)/shard_map/ppermute | solution.py:109
  959.6 33.3 %collective-permute-start.129 = (f32[72,2048]{1,0:T(8,128)}, f32[72,2048]{1,0:T(8,128)S(1)}, u32[]{:S(2)}, u32[]{:S(2)}) collective-permute-start(f32[72,2048]{1,0:T(8,128)} %add.797), channel_id=1, source_target_pairs={{0,4},{1,5},{2,6},{3,7},{4,0},{5,1},{6,2},{7,3},{8,12},{9,13},{10,... | collective-permute-start | bytes 1769480 | tf_op jit(solution)/shard_map/ppermute | solution.py:109
  964.6 28.3 %collective-permute-start.131 = (bf16[256,512]{1,0:T(8,128)(2,1)S(1)}, bf16[256,512]{1,0:T(8,128)(2,1)S(1)}, u32[]{:S(2)}, u32[]{:S(2)}) collective-permute-start(bf16[256,512]{1,0:T(8,128)(2,1)S(1)} %add_convert_fusion.6), channel_id=1, source_target_pairs={{0,16},{1,17},{2,18},{3,19},{4,20},{5,21},{6,22},{7,23},{8,24},{9,... | collective-permute-start | bytes 786440 | tf_op jit(solution)/shard_map/ppermute | solution.py:109
  966.4 26.5 %collective-permute-start.132 = (bf16[256,512]{1,0:T(8,128)(2,1)S(1)}, bf16[256,512]{1,0:T(8,128)(2,1)S(1)}, u32[]{:S(2)}, u32[]{:S(2)}) collective-permute-start(bf16[256,512]{1,0:T(8,128)(2,1)S(1)} %add_convert_fusion.6), channel_id=1, source_target_pairs={{0,24},{1,25},{2,26},{3,27},{4,28},{5,29},{6,30},{7,31},{8,0},{9,1... | collective-permute-start | bytes 786440 | tf_op jit(solution)/shard_map/ppermute | solution.py:109
  998.8 97.5 %collective-permute-start.135 = (bf16[1024,512]{1,0:T(8,128)(2,1)S(1)}, bf16[1024,512]{1,0:T(8,128)(2,1)}, u32[]{:S(2)}, u32[]{:S(2)}) collective-permute-start(bf16[1024,512]{1,0:T(8,128)(2,1)S(1)} %bitcast.146), channel_id=1, source_target_pairs={{0,4},{1,5},{2,6},{3,7},{4,0},{5,1},{6,2},{7,3},{8,12},{9,13},{10,... | collective-permute-start | bytes 3145736 | tf_op jit(solution)/shard_map/ppermute | solution.py:109
  1000.7 95.7 %collective-permute-start.136 = (bf16[256,2048]{1,0:T(8,128)(2,1)}, bf16[256,2048]{1,0:T(8,128)(2,1)}, u32[]{:S(2)}, u32[]{:S(2)}) collective-permute-start(bf16[256,2048]{1,0:T(8,128)(2,1)} %shard_map.308), channel_id=1, source_target_pairs={{0,24},{1,25},{2,26},{3,27},{4,28},{5,29},{6,30},{7,31},{8,0},{9,1... | collective-permute-start | bytes 3145736 | tf_op jit(solution)/shard_map/ppermute | solution.py:109
  (170 other events, 3562.5 us)
Sparse Core Ops, SparseCore 0:
  829.2 245.0 all-reduce.3

commit v4 on v3

--- a/solution.py
+++ b/solution.py
@@ -210,6 +210,23 @@
 
     def add_z(self, got):
         self.part = add_low(lax.dynamic_slice_in_dim(self.sum, self.z * self.piece, self.piece), *got)
+
+    def reduce_z(self, half):
+        low, high = self.z % 2, self.z // 2
+        pieces = half.reshape((2, 2, self.piece) + half.shape[1:])
+        for bit, axis, name in ((low, 1, "z1"), (high, 0, "z2")):
+            mine = lax.dynamic_index_in_dim(pieces, bit, axis, keepdims=False)
+            other = lax.dynamic_index_in_dim(pieces, 1 - bit, axis, keepdims=False)
+            pieces = add_low(mine, send(other, name))
+        return pieces
+
+    def collect_z(self, part):
+        low, high = self.z % 2, self.z // 2
+        for bit, axis, name in ((high, 0, "z2"), (low, 1, "z1")):
+            other = send(part, name)
+            first, second = jnp.where(bit == 0, part, other), jnp.where(bit == 0, other, part)
+            part = jnp.stack([first, second], axis=axis)
+        return part.reshape((self.half,) + part.shape[3:])
 
     def join_z(self):
         return [(self.part, f"u{d}") for d in (1, 2, 3)]
@@ -1000,8 +1017,23 @@
         d=[("x", (3, 1, 0)), ("y", (3, 0, 1)), ("z", (2, 0, 0))],
     )
     out_sum.put(2, made)
-    _, (made,) = advance(
-        [(core_sum, tuple(last_outs))],
+    def saved(n):
+        return [kept[i][n] for i in order]
+
+    def grads_of(first, last, earlier=None):
+        all_cots = [cot_rows[i][0] for i in order]
+
+        places = [cot_rows[i][1] for i in order]
+
+        def work(*args):
+            return expert_grads(*args[:5], places, first, last, args[5] if len(args) > 5 else None)
+
+        args = (saved(0), all_cots, saved(1), saved(2), saved(3))
+        return work, args if earlier is None else args + (earlier,)
+
+    thirds = [experts * n // 3 for n in range(4)]
+    _, (made, weight_grads) = advance(
+        [(core_sum, tuple(last_outs)), grads_of(thirds[0], thirds[1])],
         d=[("x", (0, 1, 0)), ("y", (0, 0, 1)), ("z", (3, 0, 0))],
     )
     out_sum.put(3, made[:2])
@@ -1021,60 +1053,60 @@
     )
     d_attn = d_mixed.astype(BF16)
     router_sums = jnp.concatenate(
-        [router_part, jnp.broadcast_to(ffn_gain_part[None, :], (8, model_width))], axis=0
-    )
-
-    (across, mate, other), _ = advance(
-        extra=[(d_attn, "y"), (d_attn, "c"), (router_sums, "z1")], out=[("x", (1, 1, 1))]
-    )
-    router_sums = router_sums + other
-
-    def attend_back(d_attn, mate, across, w_out, *rest):
+        [router_part, jnp.broadcast_to(ffn_gain_part[None, :], (16, model_width))], axis=0
+    ).astype(BF16)
+
+    (across, mate, other), (weight_grads,) = advance(
+        [grads_of(thirds[1], thirds[2], weight_grads)],
+        extra=[(d_attn, "y"), (d_attn, "c"), (router_sums, "z1")],
+        out=[("x", (1, 1, 1))],
+    )
+    router_sums = add_low(router_sums, other)
+
+    def attend_back(d_attn, mate, across, w_out, o_low, *rest):
         d_blocks = [d_attn, mate, across, send(across, "c")]
         d_attended = join(*[times_transpose(block, w_out).astype(BF16) for block in d_blocks])
         q_raw, k_raw, v_low, q_rot, k_rot, lse, cols = rest
-        made = attend_backward(
+        *made, q_inner, k_inner = attend_backward(
             q_raw, k_raw, v_low, q_rot, k_rot, d_attended, lse, cols, q_gain, k_gain, cosine, sine, key_pos
         )
-        return made, d_blocks
+        inner = token_sums(jnp.sum(q_inner, axis=1), jnp.sum(k_inner, axis=1)) / model_width
+        return made, inner, contract_rows(o_low, join(*d_blocks)).astype(BF16)
 
     _, (made,) = advance(
         [
             (
                 attend_back,
-                (d_attn, mate, across, w_out, q_raw, k_raw, v_low, q_rot, k_rot, lse, cols),
+                (d_attn, mate, across, w_out, o_low, q_raw, k_raw, v_low, q_rot, k_rot, lse, cols),
             )
         ],
-        out=[("x", (3, 1, 1)), ("x", (1, 1, 0)), ("y", (2, 1, 1)), ("y", (0, 1, 1))],
-    )
-    (dq_hat, dk_hat, dv_raw, query_gain_part, key_gain_part, q_inner, k_inner), d_blocks = made
-
-    def early_grads(o_low, gathered, dv_raw, *d_blocks):
-        return (
-            contract_rows(o_low, join(*d_blocks)).astype(BF16),
-            contract_rows(gathered, dv_raw).astype(BF16),
-        )
-
-
-    def norm_back(q_raw, k_raw, cols, dq_hat, dk_hat, q_inner, k_inner):
-        inner = token_sums(jnp.sum(q_inner, axis=1), jnp.sum(k_inner, axis=1)) / model_width
+        out=[("x", (3, 1, 1)), ("x", (1, 1, 0)), ("y", (2, 1, 1)), ("y", (1, 0, 1))],
+    )
+    (dq_hat, dk_hat, dv_raw, query_gain_part, key_gain_part), inner, grad_w_out = made
+
+    def value_grad(gathered, dv_raw):
+        return contract_rows(gathered, dv_raw).astype(BF16)
+
+    def norm_back(q_raw, k_raw, cols, dq_hat, dk_hat, inner):
         raws = []
         for n, (raw, d_hat) in enumerate(((q_raw, dq_hat), (k_raw, dk_hat))):
             scale = cols[:, n : n + 1]
             raws.append((scale * (d_hat - raw * scale * inner[n][:, None])).astype(BF16))
         return raws
 
-    (other,), ((dq_raw, dk_raw), made) = advance(
+    out_weight = DpSum(grad_w_out)
+    (other, *got), ((dq_raw, dk_raw), grad_value, (grad_w_gate, grad_w_up, grad_w_down)) = advance(
         [
-            (norm_back, (q_raw, k_raw, cols, dq_hat, dk_hat, q_inner, k_inner)),
-            (early_grads, (o_low, gathered, dv_raw) + tuple(d_blocks)),
+            (norm_back, (q_raw, k_raw, cols, dq_hat, dk_hat, inner)),
+            (value_grad, (gathered, dv_raw)),
+            grads_of(thirds[2], thirds[3], weight_grads),
         ],
-        extra=[(router_sums, "z2")],
-        out=[("x", (3, 1, 0)), ("y", (1, 0, 1))],
-    )
-    router_sums = router_sums + other
-
-    grad_w_out, grad_value = lax.psum(made, "dp")
+        extra=[(router_sums, "z2")] + out_weight.split_x(),
+        out=[("x", (2, 1, 0)), ("y", (2, 0, 1)), ("z", (1, 0, 0))],
+    )
+    router_sums = add_low(router_sums, other)
+    out_weight.add_x(got)
+    value_weight = DpSum(grad_value)
 
     def projections_back(gathered, dq_raw, dk_raw, dv_raw, w_query, w_key, w_value):
         grads = [contract_rows(gathered, part).astype(BF16) for part in (dk_raw, dq_raw)]
@@ -1083,91 +1115,87 @@
         total_term = (total_term + times_transpose(dv_raw, w_value)).astype(BF16)
         return grads, total_term
 
-    (other,), (((grad_key, grad_query), total_term),) = advance(
-        [(projections_back, (gathered, dq_raw, dk_raw, dv_raw, w_query, w_key, w_value))],
-        extra=[(router_sums, "c")],
-        out=[("x", (2, 1, 0)), ("y", (2, 0, 1)), ("z", (1, 0, 0))],
-    )
-    router_sums = router_sums + other
-
-    key_sum, query_sum = DpSum(grad_key), DpSum(grad_query)
-
-    def saved(n):
-        return [kept[i][n] for i in order]
-
-    def grads_of(first, last, earlier=None):
-        all_cots = [cot_rows[i][0] for i in order]
-
-        places = [cot_rows[i][1] for i in order]
-
-        def work(*args):
-            return expert_grads(*args[:5], places, first, last, args[5] if len(args) > 5 else None)
-
-        args = (saved(0), all_cots, saved(1), saved(2), saved(3))
-        return work, args if earlier is None else args + (earlier,)
-
-    thirds = [experts * n // 3 for n in range(4)]
+    got, (((grad_key, grad_query), total_term), out_piece) = advance(
+        [
+            (projections_back, (gathered, dq_raw, dk_raw, dv_raw, w_query, w_key, w_value)),
+            (out_weight.reduce_z, (out_weight.sum,)),
+        ],
+        extra=value_weight.split_x(),
+        out=[("x", (3, 1, 0)), ("y", (3, 0, 1)), ("z", (2, 0, 0))],
+    )
+    value_weight.add_x(got)
+    key_weight, query_weight = DpSum(grad_key), DpSum(grad_query)
     parts = jnp.split(total_term, tensor_count, axis=0)
-    (d_far, d_near, *got), _ = advance(
-        extra=[(parts[3], "c"), (parts[1], "c")] + key_sum.split_x(),
-        out=[("y", (3, 0, 1)), ("z", (2, 0, 0))],
-    )
-    key_sum.add_x(got)
-    (d_across, *got), (made,) = advance(
-        [grads_of(thirds[0], thirds[1])],
-        extra=[(add_low(parts[2], d_far), "y")] + query_sum.split_x() + key_sum.split_z(),
-    )
-    query_sum.add_x(got[:1])
-    key_sum.add_z(got[1:])
-    d_attn_in = add_wide(parts[0], d_near, d_across)
+    (d_other, other, *got), (value_piece,) = advance(
+        [(value_weight.reduce_z, (value_weight.sum,))],
+        extra=[(jnp.concatenate([parts[1], parts[3]], axis=0), "c"), (router_sums, "c")] + key_weight.split_x(),
+        out=[("y", (0, 1, 1))],
+    )
+    router_sums = add_low(router_sums, other)
+    key_weight.add_x(got)
+    out_weight.part, value_weight.part = out_piece, value_piece
+    (d_across, *got), _ = advance(
+        extra=[(add_low(parts[2], d_other[tok_rows:]), "y")] + query_weight.split_x() + out_weight.join_z(),
+    )
+    query_weight.add_x(got[:1])
+    out_weight.took_z(got[1:])
+    d_attn_in = add_wide(parts[0], d_other[:tok_rows], d_across)
     attn_gain_part = jnp.sum(d_attn_in * normed, axis=0)
     d_norm_one = d_attn_in * attn_gain.astype(F32)
     d_input = d_mixed + scale_one * (
         d_norm_one - normed * jnp.mean(d_norm_one * normed, axis=-1, keepdims=True)
     )
-    got, (made,) = advance(
-        [grads_of(thirds[1], thirds[2], made)], extra=key_sum.join_z(), out=[("x", (0, 1, 0)), ("y", (0, 0, 1))]
-    )
-    key_sum.took_z(got)
-    (other, *got), ((grad_w_gate, grad_w_up, grad_w_down),) = advance(
-        [grads_of(thirds[2], thirds[3], made)],
-        extra=[(attn_gain_part, "c")] + key_sum.join_x() + query_sum.split_z(),
+    got, (d_input,) = advance(
+        [(lambda value: value, (d_input.astype(BF16),))],
+        extra=out_weight.join_x() + value_weight.join_z(),
+        out=[("y", (0, 0, 1))],
+    )
+    out_weight.took_x(got[:1])
+    value_weight.took_z(got[1:])
+    (other, *got), (grad_w_out,) = advance(
+        [(lambda value: value, (out_weight.result,))],
+        extra=[(attn_gain_part, "c")] + value_weight.join_x() + key_weight.split_z(),
     )
     attn_gain_part = attn_gain_part + other
-    key_sum.took_x(got[:1])
-    query_sum.add_z(got[1:])
+    value_weight.took_x(got[:1])
+    key_weight.add_z(got[1:])
+    (other, *got), (grad_value,) = advance(
+        [(lambda value: value, (value_weight.result,))],
+        extra=[(attn_gain_part, "y")] + query_weight.split_z(),
+        out=[("x", (0, 1, 0))],
+    )
+    query_weight.add_z(got)
+    gain_parts = jnp.concatenate([attn_gain_part + other, query_gain_part[0], key_gain_part[0]])
     (other, third, *got), _ = advance(
-        extra=[(attn_gain_part, "y"), (router_sums, "x")] + query_sum.join_z(),
-    )
-    gain_parts = jnp.concatenate([attn_gain_part + other, query_gain_part[0], key_gain_part[0]])
-    router_sums = router_sums + third
-    query_sum.took_z(got)
-    (other, third, *got), _ = advance(
-        extra=[(gain_parts, "x"), (router_sums, "y")] + query_sum.join_x(), out=[("z", (3, 0, 0))]
-    )
-    query_sum.took_x(got)
-    router_sums = router_sums + third
+        extra=[(gain_parts, "x"), (router_sums, "y")] + key_weight.join_z(),
+    )
     gain_parts = gain_parts + other
+    router_sums = add_low(router_sums, third)
+    key_weight.took_z(got)
+    (other, *got), _ = advance(
+        extra=[(router_sums, "x")] + key_weight.join_x() + query_weight.join_z(),
+    )
+    router_sums = add_wide(router_sums, other)
+    key_weight.took_x(got[:1])
+    query_weight.took_z(got[1:])
+    (next_z, far_z, last_z, *got), (grad_key, router_sums) = advance(
+        [(lambda value: value, (key_weight.result,)), (lambda value: value, (router_sums,))],
+        extra=[(gain_parts, "u1"), (gain_parts, "u2"), (gain_parts, "u3")] + query_weight.join_x(),
+        out=[("z", (3, 0, 0))],
+    )
+    gain_sums = (gain_parts + far_z) + (next_z + last_z)
+    query_weight.took_x(got)
+    grad_query = query_weight.result
     result = (mixed + out_sum.total()).astype(BF16)
-    (next_z, far_z, last_z), ((result, d_input, grad_query, grad_key),) = advance(
-        [
-            (
-                lambda *values: values,
-                (result, d_input.astype(BF16), query_sum.result, key_sum.result),
-            )
-        ],
-        extra=[(gain_parts, "u1"), (gain_parts, "u2"), (gain_parts, "u3")],
-    )
-    gain_sums = (gain_parts + far_z) + (next_z + last_z)
     return (
         result,
         d_input,
         grad_query,
         grad_key,
-        grad_value.astype(F32),
+        grad_value,
         gain_sums[model_width : model_width + local_width],
         gain_sums[model_width + local_width :],
-        grad_w_out.astype(F32),
+        grad_w_out,
         gain_sums[:model_width],
         router_sums[expert_total],
         router_sums[:expert_total].T,

time: 1130 us -> 1120 us (level)
  waiting for transfers between devices: 304 us -> 268 us
  between operations: 16.8 us -> 3.57 us
    psum x1 -> x0, waiting for transfers between devices: 66.9 us -> none  [local_gathered(): grad_w_out, grad_value = lax.psum(made, 'dp')]
    ppermute x140 -> x153, waiting for transfers between devices: 225 us -> 256 us  [send(): return lax.ppermute(value, BOTH, device_pairs(MOVES[axis]))]
    ppermute x140 -> x153, starting transfers between devices: 156 us -> 166 us  [send(): return lax.ppermute(value, BOTH, device_pairs(MOVES[axis]))]
  transfers between devices with their start and end apart: 144 -> 156, of which waited for: 58 -> 68; matrix products, arithmetic and copies ran while one was open for 11% -> 9% of each run, Pallas kernels for 38% -> 38%
where the time goes in v4:
time: 1120 us; the launch traced here: 1100 us
  Pallas kernels  447 us (40%)
  waiting for transfers between devices  268 us (24%)
  starting transfers between devices  179 us (16%)
  other arithmetic  84.5 us (8%)
  local copies, waits for them, and re-layouts  53.2 us (5%)
  matrix products  48.1 us (4%)
  blocking collectives  20.6 us (2%)
    ppermute x153, waiting for transfers between devices, send(): return lax.ppermute(value, BOTH, device_pairs(MOVES[axis]))  256 us
    ppermute x153, starting transfers between devices, send(): return lax.ppermute(value, BOTH, device_pairs(MOVES[axis]))  166 us
    pallas_call x5, Pallas kernels, main_chunk(): pl.pallas_call(functools.partial(main_kernel, count, slot_count), grid=(e...  123 us
    pallas_call x4, Pallas kernels, cot_chunk(): pl.pallas_call(functools.partial(cot_kernel, count, slot_count), grid=(ex...  62.7 us
    pallas_call x3, Pallas kernels, expert_grads(): pl.pallas_call(functools.partial(grad_kernel, count), grid=(last - first,...  61.1 us
    pallas_call x4, Pallas kernels, out_chunk(): pl.pallas_call(functools.partial(out_kernel, len(picks), slot_count), gri...  55 us
    pallas_call x9, Pallas kernels, pair_sum(): pl.pallas_call(pair_kernel, grid=(rows // tile,), in_specs=[stack, stack]...  49.7 us
    pallas_call x9, Pallas kernels, block_sums(): pl.pallas_call(functools.partial(sums_kernel, counts), grid=(rows // tile...  38.1 us
  transfers between devices with their start and end apart: 156, of which 68 were waited for; matrix products, arithmetic and copies ran while one was open for 9% of the time, Pallas kernels for 38%

profile of v4, /device:TPU:0, one launch (start us, length us, event | category | flops | bytes accessed | tf_op | source)
XLA Modules:
  0.0 1103.6 jit_solution(8809148726496216006)
XLA Ops:
  7.4 7.4 all-to-all-start
  35.4 7.7 collective-permute-done.refs_2_
  48.3 5.0 collective-permute-start.4
  56.3 17.2 %shard_map.272 = (f32[1024,512]{1,0:T(8,128)}, f32[1024,512]{1,0:T(8,128)}, bf16[1024,512]{1,0:T(8,128)(2,1)}, f32[1024,128]{1,0:T(8,128)}, f32[1024,128]{1,0:T(8,128)}) custom-call(bf16[256,2048]{1,0:T(8,128)(2,1)} %fusion.18.refs_0_, bf16[256,2048]{1,0:T(8,128)(2,1)} %collective-permute-done.1.refs_1_, bf16[256,2048]{1,0:T(8,128)(2,1)} %collective-permute-done.refs_2_, ...), custom_call_target="tpu_custom_call" | custom-call | flops 6442450944 | bytes 15728640 | tf_op jit(solution)/shard_map/pallas_call | solution.py:580
  76.6 6.4 psum.14
  88.2 16.9 %shard_map.273 = (bf16[1024,512]{1,0:T(8,128)(2,1)}, f32[1024,512]{1,0:T(8,128)}, bf16[1024,512]{1,0:T(8,128)(2,1)}, bf16[1024,512]{1,0:T(8,128)(2,1)}) custom-call(f32[1024,512]{1,0:T(8,128)} %get-tuple-element.1425.q_ref, f32[1024,512]{1,0:T(8,128)} %get-tuple-element.1428.k_ref, bf16[1024,512]{1,0:T(8,128)(2,1)} %get-tuple-element.1383.v_ref, ...), custom_call_target="tpu_custom_call" | custom-call | flops 2147483648 | bytes 10485760 | tf_op jit(solution)/shard_map/pallas_call | solution.py:702
  122.9 18.1 %collective-permute-done.20 = bf16[256,2048]{1,0:T(8,128)(2,1)S(1)} collective-permute-done((bf16[256,2048]{1,0:T(8,128)(2,1)S(1)}, bf16[256,2048]{1,0:T(8,128)(2,1)S(1)}, u32[]{:S(2)}, u32[]{:S(2)}) %collective-permute-start.20) | collective-permute-done | bytes 1048608 | tf_op jit(solution)/shard_map/ppermute | solution.py:109
  153.2 15.7 %shard_map.274 = (bf16[8,256,2048]{2,1,0:T(8,128)(2,1)}, f32[8,256,256]{2,1,0:T(8,128)}) custom-call(bf16[8,256,256]{2,1,0:T(8,128)(2,1)} %bitcast.192, bf16[8,256,2048]{2,1,0:T(8,128)(2,1)} %refs_4_.1, bf16[256,2048]{1,0:T(8,128)(2,1)} %refs_0_, bf16[256,2048]{1,0:T(8,128)(2,1)} %collective-permute-done.2.refs_1_, ...), custom_call_target="tpu_custom_call" | custom-call | flops 4294967296 | bytes 25165824 | tf_op jit(solution)/shard_map/pallas_call | solution.py:388
  180.5 15.7 %shard_map.275 = (bf16[8,256,2048]{2,1,0:T(8,128)(2,1)}, f32[8,256,256]{2,1,0:T(8,128)}) custom-call(bf16[8,256,256]{2,1,0:T(8,128)(2,1)} %bitcast.189, bf16[8,256,2048]{2,1,0:T(8,128)(2,1)} %refs_4_.1, bf16[256,2048]{1,0:T(8,128)(2,1)} %collective-permute-done.4.refs_0_, bf16[256,2048]{1,0:T(8,128)(2,1)} %collective-permute-done.5.refs_1_, ...), custom_call_target="tpu_custom_call" | custom-call | flops 4294967296 | bytes 25165824 | tf_op jit(solution)/shard_map/pallas_call | solution.py:388
  196.2 6.9 all-to-all-done.1
  210.6 27.5 %shard_map.276 = (bf16[8,256,2048]{2,1,0:T(8,128)(2,1)}, bf16[8,256,256]{2,1,0:T(8,128)(2,1)}, bf16[8,256,256]{2,1,0:T(8,128)(2,1)}, bf16[8,256,256]{2,1,0:T(8,1...) custom-call(bf16[8,256,256]{2,1,0:T(8,128)(2,1)} %bitcast.193, ...), custom_call_target="tpu_custom_call" | custom-call | flops 12884901888 | bytes 41943040 | tf_op jit(solution)/shard_map/pallas_call | solution.py:411
  240.3 6.9 collective-permute-done.39.refs_5_
  247.5 5.9 shard_map.277
  253.4 11.0 collective-permute-done.38.refs_1_
  267.9 27.7 %shard_map.278 = (bf16[8,256,2048]{2,1,0:T(8,128)(2,1)}, bf16[8,256,256]{2,1,0:T(8,128)(2,1)}, bf16[8,256,256]{2,1,0:T(8,128)(2,1)}, bf16[8,256,256]{2,1,0:T(8,1...) custom-call(bf16[8,256,256]{2,1,0:T(8,128)(2,1)} %bitcast.190, ...), custom_call_target="tpu_custom_call" | custom-call | flops 12884901888 | bytes 41943040 | tf_op jit(solution)/shard_map/pallas_call | solution.py:411
  297.9 6.9 collective-permute-done.53.refs_7_
  305.4 15.7 %shard_map.280 = (bf16[8,256,2048]{2,1,0:T(8,128)(2,1)}, f32[8,256,256]{2,1,0:T(8,128)}) custom-call(bf16[8,256,256]{2,1,0:T(8,128)(2,1)} %bitcast.186, bf16[8,256,2048]{2,1,0:T(8,128)(2,1)} %refs_4_.1, bf16[256,2048]{1,0:T(8,128)(2,1)} %copy-done.41, bf16[256,2048]{1,0:T(8,128)(2,1)} %collective-permute-done.15.refs_1_, ...), custom_call_target="tpu_custom_call" | custom-call | flops 4294967296 | bytes 25165824 | tf_op jit(solution)/shard_map/pallas_call | solution.py:388
  321.0 6.0 shard_map.279
  334.8 27.8 %shard_map.281 = (bf16[8,256,2048]{2,1,0:T(8,128)(2,1)}, bf16[8,256,256]{2,1,0:T(8,128)(2,1)}, bf16[8,256,256]{2,1,0:T(8,128)(2,1)}, bf16[8,256,256]{2,1,0:T(8,1...) custom-call(bf16[8,256,256]{2,1,0:T(8,128)(2,1)} %bitcast.187, ...), custom_call_target="tpu_custom_call" | custom-call | flops 12884901888 | bytes 41943040 | tf_op jit(solution)/shard_map/pallas_call | solution.py:411
  373.2 15.7 %shard_map.283 = (bf16[8,256,2048]{2,1,0:T(8,128)(2,1)}, f32[8,256,256]{2,1,0:T(8,128)}) custom-call(bf16[8,256,256]{2,1,0:T(8,128)(2,1)} %pad_maximum_fusion.2.picks_ref, bf16[8,256,2048]{2,1,0:T(8,128)(2,1)} %refs_4_.1, bf16[256,2048]{1,0:T(8,128)(2,1)} %collective-permute-done.51.refs_0_, bf16[256,2048]{1,0:T(8,128)(2,1)} %copy-done.50, ...), custom_call_target="tpu_custom_call" | custom-call | flops 4294967296 | bytes 25165824 | tf_op jit(solution)/shard_map/pallas_call | solution.py:388
  388.8 5.9 shard_map.282
  399.3 20.4 %shard_map.284 = (bf16[8,128,2048]{2,1,0:T(8,128)(2,1)}, bf16[8,128,256]{2,1,0:T(8,128)(2,1)}, bf16[8,128,256]{2,1,0:T(8,128)(2,1)}, bf16[8,128,256]{2,1,0:T(8,1...) custom-call(bf16[4,256,256]{2,1,0:T(8,128)(2,1)} %bitcast.203, ...), custom_call_target="tpu_custom_call" | custom-call | flops 6442450944 | bytes 29360128 | tf_op jit(solution)/shard_map/pallas_call | solution.py:411
  432.5 20.0 %shard_map.286 = (bf16[8,128,2048]{2,1,0:T(8,128)(2,1)}, bf16[8,128,256]{2,1,0:T(8,128)(2,1)}, bf16[8,128,256]{2,1,0:T(8,128)(2,1)}, bf16[8,128,256]{2,1,0:T(8,1...) custom-call(bf16[4,256,256]{2,1,0:T(8,128)(2,1)} %bitcast.201, ...), custom_call_target="tpu_custom_call" | custom-call | flops 6442450944 | bytes 29360128 | tf_op jit(solution)/shard_map/pallas_call | solution.py:411
  471.8 13.7 %shard_map.289 = (bf16[4,256,2048]{2,1,0:T(8,128)(2,1)}, bf16[4,256,2048]{2,1,0:T(8,128)(2,1)}) custom-call(bf16[8,256,256]{2,1,0:T(8,128)(2,1)} %bitcast.194, bf16[8,256,256]{2,1,0:T(8,128)(2,1)} %get-tuple-element.1441.refs_1_.refs_10_, bf16[8,256,2048]{2,1,0:T(8,128)(2,1)} %refs_4_.1), custom_call_target="tpu_custom_call" | custom-call | flops 4294967296 | bytes 25165824 | tf_op jit(solution)/shard_map/pallas_call | solution.py:454
  485.6 4.9 all-to-all-done.2
  501.5 13.7 %shard_map.290 = (bf16[4,256,2048]{2,1,0:T(8,128)(2,1)}, bf16[4,256,2048]{2,1,0:T(8,128)(2,1)}) custom-call(bf16[8,256,256]{2,1,0:T(8,128)(2,1)} %bitcast.191, bf16[8,256,256]{2,1,0:T(8,128)(2,1)} %get-tuple-element.1442.refs_1_.refs_11_, bf16[8,256,2048]{2,1,0:T(8,128)(2,1)} %refs_4_.1), custom_call_target="tpu_custom_call" | custom-call | flops 4294967296 | bytes 25165824 | tf_op jit(solution)/shard_map/pallas_call | solution.py:454
  515.2 5.9 shard_map.291
  524.0 13.7 %shard_map.293 = (bf16[4,256,2048]{2,1,0:T(8,128)(2,1)}, bf16[4,256,2048]{2,1,0:T(8,128)(2,1)}) custom-call(bf16[8,256,256]{2,1,0:T(8,128)(2,1)} %bitcast.188, bf16[8,256,256]{2,1,0:T(8,128)(2,1)} %get-tuple-element.1443.refs_1_.refs_12_, bf16[8,256,2048]{2,1,0:T(8,128)(2,1)} %refs_4_.1), custom_call_target="tpu_custom_call" | custom-call | flops 4294967296 | bytes 25165824 | tf_op jit(solution)/shard_map/pallas_call | solution.py:454
  537.7 5.9 shard_map.294
  549.1 4.7 shard_map.295
  557.7 13.8 %shard_map.296 = (bf16[4,256,2048]{2,1,0:T(8,128)(2,1)}, bf16[4,256,2048]{2,1,0:T(8,128)(2,1)}) custom-call(bf16[4,256,256]{2,1,0:T(8,128)(2,1)} %bitcast.204, bf16[4,256,256]{2,1,0:T(8,128)(2,1)} %bitcast.202, bf16[8,128,256]{2,1,0:T(8,128)(2,1)} %get-tuple-element.1444.refs_2_.refs_13_, bf16[8,128,256]{2,1,0:T(8,128)(2,1)} %get-tuple-element.1445.refs_3_.refs_14_, ...), custom_call_target="tpu_custom_call" | custom-call | flops 4294967296 | bytes 25165824 | tf_op jit(solution)/shard_map/pallas_call | solution.py:454
  571.5 5.9 shard_map.297
  580.7 4.7 shard_map.298
  592.2 15.5 %shard_map.300 = (f32[8,2048,256]{2,1,0:T(8,128)}, f32[8,2048,256]{2,1,0:T(8,128)}, f32[8,256,2048]{2,1,0:T(8,128)}) custom-call(bf16[8,256,2048]{2,1,0:T(8,128)(2,1)} %get-tuple-element.1431.refs_0_, bf16[8,256,2048]{2,1,0:T(8,128)(2,1)} %get-tuple-element.1432.refs_1_, bf16[8,256,2048]{2,1,0:T(8,128)(2,1)} %get-tuple-element.1433.refs_2_, ...), custom_call_target="tpu_custom_call" | custom-call | flops 6442450944 | bytes 29360128 | tf_op jit(solution)/shard_map/pallas_call | solution.py:500
  607.7 5.9 shard_map.299
  623.2 22.7 %shard_map.301 = (f32[8,2048,256]{2,1,0:T(8,128)}, f32[8,2048,256]{2,1,0:T(8,128)}, f32[8,256,2048]{2,1,0:T(8,128)}) custom-call(bf16[8,256,2048]{2,1,0:T(8,128)(2,1)} %get-tuple-element.1431.refs_0_, bf16[8,256,2048]{2,1,0:T(8,128)(2,1)} %get-tuple-element.1432.refs_1_, ...), custom_call_target="tpu_custom_call", output_to_operand_aliasing={{0}: (25, {}), {1}: (26, {}), {2}: (27, {})} | custom-call | flops 9663676416 | bytes 44040192 | tf_op jit(solution)/shard_map/pallas_call | solution.py:500
  665.7 22.8 %shard_map.303 = (f32[1024,512]{1,0:T(8,128)}, f32[1024,512]{1,0:T(8,128)}, bf16[1024,512]{1,0:T(8,128)(2,1)}, f32[1,512]{1,0:T(1,128)}, f32[1,512]{1,0:T(1,128)...) custom-call(f32[1024,512]{1,0:T(8,128)} %get-tuple-element.1425.q_ref, f32[1024,512]{1,0:T(8,128)} %get-tuple-element.1428.k_ref, ...), custom_call_target="tpu_custom_call" | custom-call | flops 5368709120 | bytes 16777216 | tf_op jit(solution)/shard_map/pallas_call | solution.py:729
  691.8 14.2 %psum.15 = f32[2,4,256]{2,0,1:T(2,128)S(1)} all-reduce(f32[2,4,256]{2,0,1:T(2,128)S(1)} %bitcast.226), channel_id=1, replica_groups=mesh['dp'=8,'tensor'=4] {'tensor'}, use_global_device_ids=true, to_apply=%region_14.15 | all-reduce | flops 2048 | bytes 16384 | tf_op jit(solution)/shard_map/psum | solution.py:802
  706.6 4.9 fusion.13
  726.4 22.9 %shard_map.305 = (f32[8,2048,256]{2,1,0:T(8,128)}, f32[8,2048,256]{2,1,0:T(8,128)}, f32[8,256,2048]{2,1,0:T(8,128)}) custom-call(bf16[8,256,2048]{2,1,0:T(8,128)(2,1)} %get-tuple-element.1431.refs_0_, bf16[8,256,2048]{2,1,0:T(8,128)(2,1)} %get-tuple-element.1432.refs_1_, ...), custom_call_target="tpu_custom_call", output_to_operand_aliasing={{0}: (25, {}), {1}: (26, {}), {2}: (27, {})} | custom-call | flops 9663676416 | bytes 44040192 | tf_op jit(solution)/shard_map/pallas_call | solution.py:500
  760.1 5.7 collective-permute-done.103.refs_3_
  769.5 4.7 shard_map.306
  776.0 4.4 fusion.76
  787.1 4.5 collective-permute-start.109
  791.5 5.7 fusion.77
  797.2 6.5 add_convert_fusion
  803.8 5.0 convolution_convert_fusion.1
  811.2 12.2 %collective-permute-done.111 = bf16[64,2048]{1,0:T(8,128)(2,1)S(1)} collective-permute-done((bf16[64,2048]{1,0:T(8,128)(2,1)S(1)}, bf16[64,2048]{1,0:T(8,128)(2,1)S(1)}, u32[]{:S(2)}, u32[]{:S(2)}) %collective-permute-start.111) | collective-permute-done | bytes 262176 | tf_op jit(solution)/shard_map/ppermute | solution.py:109
  823.4 6.6 collective-permute-done.107.refs_1_
  837.6 11.2 %collective-permute-done.116 = bf16[2,256,512]{2,1,0:T(8,128)(2,1)S(1)} collective-permute-done((bf16[2,256,512]{2,1,0:T(8,128)(2,1)S(1)}, bf16[2,256,512]{2,1,0:T(8,128)(2,1)S(1)}, u32[]{:S(2)}, u32[]{:S(2)}) %collective-permute-start.116) | collective-permute-done | bytes 524320 | tf_op jit(solution)/shard_map/ppermute | solution.py:109
  849.1 4.5 collective-permute-start.117
  853.7 11.5 %collective-permute-done.117 = bf16[256,512]{1,0:T(8,128)(2,1)S(1)} collective-permute-done((bf16[256,512]{1,0:T(8,128)(2,1)S(1)}, bf16[256,512]{1,0:T(8,128)(2,1)S(1)}, u32[]{:S(2)}, u32[]{:S(2)}) %collective-permute-start.117) | collective-permute-done | bytes 262176 | tf_op jit(solution)/shard_map/ppermute | solution.py:109
  873.7 7.3 collective-permute-done.120
  881.0 9.8 collective-permute-done.121
  913.9 8.5 collective-permute-done.125
  948.5 9.2 collective-permute-done.131
  963.8 6.0 collective-permute-start.134
  980.0 9.4 collective-permute-done.135
  990.4 6.1 collective-permute-start.140
  1004.1 8.8 collective-permute-done.141
  1020.0 5.9 collective-permute-start.145
  1036.3 9.1 collective-permute-done.146
  1063.2 7.9 collective-permute-start.152
  1075.0 18.1 %collective-permute-done.148 = f32[3072]{0:T(1024)S(1)} collective-permute-done((f32[3072]{0:T(1024)S(1)}, f32[3072]{0:T(1024)S(1)}, u32[]{:S(2)}, u32[]{:S(2)}) %collective-permute-start.148) | collective-permute-done | bytes 12320 | tf_op jit(solution)/shard_map/ppermute | solution.py:109
  (634 shorter events, 401.7 us)
Async XLA Ops:
  7.4 26.5 %all-to-all-start = ((f32[32,8,256]{2,1,0:T(8,128)}), f32[32,8,256]{2,1,0:T(8,128)}, u32[]{:S(2)}, u32[]{:S(2)}) async-start(f32[32,8,256]{2,1,0:T(8,128)} %bitcast.4), calls=%async_computation | async-start | bytes 524288 | tf_op jit(solution)/shard_map/all_to_all | solution.py:810
  14.8 28.3 %collective-permute-start = (bf16[256,2048]{1,0:T(8,128)(2,1)}, bf16[256,2048]{1,0:T(8,128)(2,1)}, u32[]{:S(2)}, u32[]{:S(2)}) collective-permute-start(bf16[256,2048]{1,0:T(8,128)(2,1)} %fusion.18.refs_0_), channel_id=1, source_target_pairs={{0,2},{1,3},{2,0},{3,1},{4,6},{5,7},{6,4},{7,5},{8,10},{9,11},{10,... | collective-permute-start | bytes 3145736 | tf_op jit(solution)/shard_map/ppermute | solution.py:109
  16.6 26.5 %collective-permute-start.1 = (bf16[256,2048]{1,0:T(8,128)(2,1)}, bf16[256,2048]{1,0:T(8,128)(2,1)}, u32[]{:S(2)}, u32[]{:S(2)}) collective-permute-start(bf16[256,2048]{1,0:T(8,128)(2,1)} %fusion.18.refs_0_), channel_id=1, source_target_pairs={{0,1},{1,0},{2,3},{3,2},{4,5},{5,4},{6,7},{7,6},{8,9},{9,8},{10,11... | collective-permute-start | bytes 3145736 | tf_op jit(solution)/shard_map/ppermute | solution.py:109
  16.6 27.9 %collective-permute-start.2 = (bf16[256,2048]{1,0:T(8,128)(2,1)S(1)}, bf16[256,2048]{1,0:T(8,128)(2,1)}, u32[]{:S(2)}, u32[]{:S(2)}) collective-permute-start(bf16[256,2048]{1,0:T(8,128)(2,1)S(1)} %copy-done.10), channel_id=1, source_target_pairs={{0,24},{1,25},{2,26},{3,27},{4,28},{5,29},{6,30},{7,31},{8,0},{9,1... | collective-permute-start | bytes 3145736 | tf_op jit(solution)/shard_map/ppermute | solution.py:109
  19.9 25.9 %collective-permute-start.3 = (bf16[256,2048]{1,0:T(8,128)(2,1)S(1)}, bf16[256,2048]{1,0:T(8,128)(2,1)}, u32[]{:S(2)}, u32[]{:S(2)}) collective-permute-start(bf16[256,2048]{1,0:T(8,128)(2,1)S(1)} %copy-done.10), channel_id=1, source_target_pairs={{0,4},{1,5},{2,6},{3,7},{4,0},{5,1},{6,2},{7,3},{8,12},{9,13},{10,... | collective-permute-start | bytes 3145736 | tf_op jit(solution)/shard_map/ppermute | solution.py:109
  48.3 35.3 %collective-permute-start.4 = (bf16[256,2048]{1,0:T(8,128)(2,1)}, bf16[256,2048]{1,0:T(8,128)(2,1)}, u32[]{:S(2)}, u32[]{:S(2)}) collective-permute-start(bf16[256,2048]{1,0:T(8,128)(2,1)} %collective-permute-done.2.refs_1_), channel_id=1, source_target_pairs={{0,24},{1,25},{2,26},{3,27},{4,28},{5,29},{6,30},{7,31},{8,0},{9,1... | collective-permute-start | bytes 3145736 | tf_op jit(solution)/shard_map/ppermute | solution.py:109
  53.3 30.3 %collective-permute-start.5 = (bf16[256,2048]{1,0:T(8,128)(2,1)}, bf16[256,2048]{1,0:T(8,128)(2,1)}, u32[]{:S(2)}, u32[]{:S(2)}) collective-permute-start(bf16[256,2048]{1,0:T(8,128)(2,1)} %collective-permute-done.2.refs_1_), channel_id=1, source_target_pairs={{0,4},{1,5},{2,6},{3,7},{4,0},{5,1},{6,2},{7,3},{8,12},{9,13},{10,... | collective-permute-start | bytes 3145736 | tf_op jit(solution)/shard_map/ppermute | solution.py:109
  54.1 29.6 %collective-permute-start.6 = (bf16[256,2048]{1,0:T(8,128)(2,1)S(1)}, bf16[256,2048]{1,0:T(8,128)(2,1)}, u32[]{:S(2)}, u32[]{:S(2)}) collective-permute-start(bf16[256,2048]{1,0:T(8,128)(2,1)S(1)} %copy-done.10), channel_id=1, source_target_pairs={{0,2},{1,3},{2,0},{3,1},{4,6},{5,7},{6,4},{7,5},{8,10},{9,11},{10,... | collective-permute-start | bytes 3145736 | tf_op jit(solution)/shard_map/ppermute | solution.py:109
  55.2 28.5 %collective-permute-start.7 = (bf16[256,2048]{1,0:T(8,128)(2,1)S(1)}, bf16[256,2048]{1,0:T(8,128)(2,1)}, u32[]{:S(2)}, u32[]{:S(2)}) collective-permute-start(bf16[256,2048]{1,0:T(8,128)(2,1)S(1)} %copy-done.10), channel_id=1, source_target_pairs={{0,1},{1,0},{2,3},{3,2},{4,5},{5,4},{6,7},{7,6},{8,9},{9,8},{10,11... | collective-permute-start | bytes 3145736 | tf_op jit(solution)/shard_map/ppermute | solution.py:109
  55.2 28.5 %collective-permute-start.8 = (bf16[256,2048]{1,0:T(8,128)(2,1)}, bf16[256,2048]{1,0:T(8,128)(2,1)}, u32[]{:S(2)}, u32[]{:S(2)}) collective-permute-start(bf16[256,2048]{1,0:T(8,128)(2,1)} %collective-permute-done.2.refs_1_), channel_id=1, source_target_pairs={{0,1},{1,0},{2,3},{3,2},{4,5},{5,4},{6,7},{7,6},{8,9},{9,8},{10,11... | collective-permute-start | bytes 3145736 | tf_op jit(solution)/shard_map/ppermute | solution.py:109
  172.2 31.5 %collective-permute-start.26 = (bf16[256,2048]{1,0:T(8,128)(2,1)}, bf16[256,2048]{1,0:T(8,128)(2,1)}, u32[]{:S(2)}, u32[]{:S(2)}) collective-permute-start(bf16[256,2048]{1,0:T(8,128)(2,1)} %collective-permute-done.21.refs_1_), channel_id=1, source_target_pairs={{0,24},{1,25},{2,26},{3,27},{4,28},{5,29},{6,30},{7,31},{8,0},{9,1... | collective-permute-start | bytes 3145736 | tf_op jit(solution)/shard_map/ppermute | solution.py:109
  173.1 30.6 %collective-permute-start.27 = (bf16[256,2048]{1,0:T(8,128)(2,1)}, bf16[256,2048]{1,0:T(8,128)(2,1)}, u32[]{:S(2)}, u32[]{:S(2)}) collective-permute-start(bf16[256,2048]{1,0:T(8,128)(2,1)} %collective-permute-done.21.refs_1_), channel_id=1, source_target_pairs={{0,4},{1,5},{2,6},{3,7},{4,0},{5,1},{6,2},{7,3},{8,12},{9,13},{10,... | collective-permute-start | bytes 3145736 | tf_op jit(solution)/shard_map/ppermute | solution.py:109
  174.7 29.1 %collective-permute-start.28 = (bf16[256,2048]{1,0:T(8,128)(2,1)}, bf16[256,2048]{1,0:T(8,128)(2,1)}, u32[]{:S(2)}, u32[]{:S(2)}) collective-permute-start(bf16[256,2048]{1,0:T(8,128)(2,1)} %collective-permute-done.21.refs_1_), channel_id=1, source_target_pairs={{0,2},{1,3},{2,0},{3,1},{4,6},{5,7},{6,4},{7,5},{8,10},{9,11},{10,... | collective-permute-start | bytes 3145736 | tf_op jit(solution)/shard_map/ppermute | solution.py:109
  175.3 28.5 %collective-permute-start.32 = (bf16[256,2048]{1,0:T(8,128)(2,1)}, bf16[256,2048]{1,0:T(8,128)(2,1)}, u32[]{:S(2)}, u32[]{:S(2)}) collective-permute-start(bf16[256,2048]{1,0:T(8,128)(2,1)} %collective-permute-done.23.refs_3_), channel_id=1, source_target_pairs={{0,1},{1,0},{2,3},{3,2},{4,5},{5,4},{6,7},{7,6},{8,9},{9,8},{10,11... | collective-permute-start | bytes 3145736 | tf_op jit(solution)/shard_map/ppermute | solution.py:109
  176.2 27.5 %collective-permute-start.31 = (bf16[256,2048]{1,0:T(8,128)(2,1)}, bf16[256,2048]{1,0:T(8,128)(2,1)}, u32[]{:S(2)}, u32[]{:S(2)}) collective-permute-start(bf16[256,2048]{1,0:T(8,128)(2,1)} %collective-permute-done.21.refs_1_), channel_id=1, source_target_pairs={{0,1},{1,0},{2,3},{3,2},{4,5},{5,4},{6,7},{7,6},{8,9},{9,8},{10,11... | collective-permute-start | bytes 3145736 | tf_op jit(solution)/shard_map/ppermute | solution.py:109
  204.4 33.7 %collective-permute-start.33 = (bf16[256,2048]{1,0:T(8,128)(2,1)}, bf16[256,2048]{1,0:T(8,128)(2,1)}, u32[]{:S(2)}, u32[]{:S(2)}) collective-permute-start(bf16[256,2048]{1,0:T(8,128)(2,1)} %collective-permute-done.26.refs_0_), channel_id=1, source_target_pairs={{0,24},{1,25},{2,26},{3,27},{4,28},{5,29},{6,30},{7,31},{8,0},{9,1... | collective-permute-start | bytes 3145736 | tf_op jit(solution)/shard_map/ppermute | solution.py:109
  207.8 30.3 %collective-permute-start.34 = (bf16[256,2048]{1,0:T(8,128)(2,1)}, bf16[256,2048]{1,0:T(8,128)(2,1)}, u32[]{:S(2)}, u32[]{:S(2)}) collective-permute-start(bf16[256,2048]{1,0:T(8,128)(2,1)} %collective-permute-done.26.refs_0_), channel_id=1, source_target_pairs={{0,4},{1,5},{2,6},{3,7},{4,0},{5,1},{6,2},{7,3},{8,12},{9,13},{10,... | collective-permute-start | bytes 3145736 | tf_op jit(solution)/shard_map/ppermute | solution.py:109
  209.2 28.9 %collective-permute-start.35 = (bf16[256,2048]{1,0:T(8,128)(2,1)}, bf16[256,2048]{1,0:T(8,128)(2,1)}, u32[]{:S(2)}, u32[]{:S(2)}) collective-permute-start(bf16[256,2048]{1,0:T(8,128)(2,1)} %collective-permute-done.26.refs_0_), channel_id=1, source_target_pairs={{0,1},{1,0},{2,3},{3,2},{4,5},{5,4},{6,7},{7,6},{8,9},{9,8},{10,11... | collective-permute-start | bytes 3145736 | tf_op jit(solution)/shard_map/ppermute | solution.py:109
  209.2 28.9 %collective-permute-start.36 = (bf16[256,2048]{1,0:T(8,128)(2,1)}, bf16[256,2048]{1,0:T(8,128)(2,1)}, u32[]{:S(2)}, u32[]{:S(2)}) collective-permute-start(bf16[256,2048]{1,0:T(8,128)(2,1)} %collective-permute-done.4.refs_0_), channel_id=1, source_target_pairs={{0,2},{1,3},{2,0},{3,1},{4,6},{5,7},{6,4},{7,5},{8,10},{9,11},{10,... | collective-permute-start | bytes 3145736 | tf_op jit(solution)/shard_map/ppermute | solution.py:109
  210.3 27.8 %collective-permute-start.37 = (bf16[256,2048]{1,0:T(8,128)(2,1)}, bf16[256,2048]{1,0:T(8,128)(2,1)}, u32[]{:S(2)}, u32[]{:S(2)}) collective-permute-start(bf16[256,2048]{1,0:T(8,128)(2,1)} %copy-done.41), channel_id=1, source_target_pairs={{0,1},{1,0},{2,3},{3,2},{4,5},{5,4},{6,7},{7,6},{8,9},{9,8},{10,11... | collective-permute-start | bytes 3145736 | tf_op jit(solution)/shard_map/ppermute | solution.py:109
  265.7 29.9 %collective-permute-start.44 = (bf16[256,2048]{1,0:T(8,128)(2,1)}, bf16[256,2048]{1,0:T(8,128)(2,1)}, u32[]{:S(2)}, u32[]{:S(2)}) collective-permute-start(bf16[256,2048]{1,0:T(8,128)(2,1)} %collective-permute-done.26.refs_0_), channel_id=1, source_target_pairs={{0,2},{1,3},{2,0},{3,1},{4,6},{5,7},{6,4},{7,5},{8,10},{9,11},{10,... | collective-permute-start | bytes 3145736 | tf_op jit(solution)/shard_map/ppermute | solution.py:109
  266.0 29.7 %collective-permute-start.45 = (bf16[256,2048]{1,0:T(8,128)(2,1)}, bf16[256,2048]{1,0:T(8,128)(2,1)}, u32[]{:S(2)}, u32[]{:S(2)}) collective-permute-start(bf16[256,2048]{1,0:T(8,128)(2,1)} %collective-permute-done.6.refs_3_), channel_id=1, source_target_pairs={{0,4},{1,5},{2,6},{3,7},{4,0},{5,1},{6,2},{7,3},{8,12},{9,13},{10,... | collective-permute-start | bytes 3145736 | tf_op jit(solution)/shard_map/ppermute | solution.py:109
  267.4 28.3 %collective-permute-start.46 = (bf16[256,2048]{1,0:T(8,128)(2,1)}, bf16[256,2048]{1,0:T(8,128)(2,1)S(1)}, u32[]{:S(2)}, u32[]{:S(2)}) collective-permute-start(bf16[256,2048]{1,0:T(8,128)(2,1)} %collective-permute-done.15.refs_1_), channel_id=1, source_target_pairs={{0,1},{1,0},{2,3},{3,2},{4,5},{5,4},{6,7},{7,6},{8,9},{9,8},{10,11... | collective-permute-start | bytes 3145736 | tf_op jit(solution)/shard_map/ppermute | solution.py:109
  267.4 28.3 %collective-permute-start.47 = (bf16[256,2048]{1,0:T(8,128)(2,1)}, bf16[256,2048]{1,0:T(8,128)(2,1)}, u32[]{:S(2)}, u32[]{:S(2)}) collective-permute-start(bf16[256,2048]{1,0:T(8,128)(2,1)} %collective-permute-done.36.refs_2_), channel_id=1, source_target_pairs={{0,1},{1,0},{2,3},{3,2},{4,5},{5,4},{6,7},{7,6},{8,9},{9,8},{10,11... | collective-permute-start | bytes 3145736 | tf_op jit(solution)/shard_map/ppermute | solution.py:109
  296.2 30.8 %collective-permute-start.48 = (bf16[256,2048]{1,0:T(8,128)(2,1)}, bf16[256,2048]{1,0:T(8,128)(2,1)}, u32[]{:S(2)}, u32[]{:S(2)}) collective-permute-start(bf16[256,2048]{1,0:T(8,128)(2,1)} %collective-permute-done.33.refs_0_), channel_id=1, source_target_pairs={{0,2},{1,3},{2,0},{3,1},{4,6},{5,7},{6,4},{7,5},{8,10},{9,11},{10,... | collective-permute-start | bytes 3145736 | tf_op jit(solution)/shard_map/ppermute | solution.py:109
  297.4 29.7 %collective-permute-start.49 = (bf16[256,2048]{1,0:T(8,128)(2,1)}, bf16[256,2048]{1,0:T(8,128)(2,1)}, u32[]{:S(2)}, u32[]{:S(2)}) collective-permute-start(bf16[256,2048]{1,0:T(8,128)(2,1)} %collective-permute-done.33.refs_0_), channel_id=1, source_target_pairs={{0,1},{1,0},{2,3},{3,2},{4,5},{5,4},{6,7},{7,6},{8,9},{9,8},{10,11... | collective-permute-start | bytes 3145736 | tf_op jit(solution)/shard_map/ppermute | solution.py:109
  297.4 29.7 %collective-permute-start.50 = (bf16[256,2048]{1,0:T(8,128)(2,1)}, bf16[256,2048]{1,0:T(8,128)(2,1)}, u32[]{:S(2)}, u32[]{:S(2)}) collective-permute-start(bf16[256,2048]{1,0:T(8,128)(2,1)} %collective-permute-done.38.refs_1_), channel_id=1, source_target_pairs={{0,1},{1,0},{2,3},{3,2},{4,5},{5,4},{6,7},{7,6},{8,9},{9,8},{10,11... | collective-permute-start | bytes 3145736 | tf_op jit(solution)/shard_map/ppermute | solution.py:109
  331.8 30.7 %collective-permute-start.54 = (bf16[256,2048]{1,0:T(8,128)(2,1)}, bf16[256,2048]{1,0:T(8,128)(2,1)S(1)}, u32[]{:S(2)}, u32[]{:S(2)}) collective-permute-start(bf16[256,2048]{1,0:T(8,128)(2,1)} %collective-permute-done.36.refs_2_), channel_id=1, source_target_pairs={{0,4},{1,5},{2,6},{3,7},{4,0},{5,1},{6,2},{7,3},{8,12},{9,13},{10,... | collective-permute-start | bytes 3145736 | tf_op jit(solution)/shard_map/ppermute | solution.py:109
  332.5 30.1 %collective-permute-start.55 = (bf16[256,2048]{1,0:T(8,128)(2,1)}, bf16[256,2048]{1,0:T(8,128)(2,1)}, u32[]{:S(2)}, u32[]{:S(2)}) collective-permute-start(bf16[256,2048]{1,0:T(8,128)(2,1)} %collective-permute-done.15.refs_1_), channel_id=1, source_target_pairs={{0,2},{1,3},{2,0},{3,1},{4,6},{5,7},{6,4},{7,5},{8,10},{9,11},{10,... | collective-permute-start | bytes 3145736 | tf_op jit(solution)/shard_map/ppermute | solution.py:109
  334.2 28.4 %collective-permute-start.56 = (bf16[256,2048]{1,0:T(8,128)(2,1)}, bf16[256,2048]{1,0:T(8,128)(2,1)}, u32[]{:S(2)}, u32[]{:S(2)}) collective-permute-start(bf16[256,2048]{1,0:T(8,128)(2,1)} %collective-permute-done.45.refs_4_), channel_id=1, source_target_pairs={{0,1},{1,0},{2,3},{3,2},{4,5},{5,4},{6,7},{7,6},{8,9},{9,8},{10,11... | collective-permute-start | bytes 3145736 | tf_op jit(solution)/shard_map/ppermute | solution.py:109
  334.2 28.4 %collective-permute-start.57 = (bf16[256,2048]{1,0:T(8,128)(2,1)}, bf16[256,2048]{1,0:T(8,128)(2,1)}, u32[]{:S(2)}, u32[]{:S(2)}) collective-permute-start(bf16[256,2048]{1,0:T(8,128)(2,1)} %collective-permute-done.51.refs_0_), channel_id=1, source_target_pairs={{0,1},{1,0},{2,3},{3,2},{4,5},{5,4},{6,7},{7,6},{8,9},{9,8},{10,11... | collective-permute-start | bytes 3145736 | tf_op jit(solution)/shard_map/ppermute | solution.py:109
  362.6 26.2 %collective-permute-start.62 = (bf16[4,256,2048]{2,1,0:T(8,128)(2,1)}, bf16[4,256,2048]{2,1,0:T(8,128)(2,1)}, u32[]{:S(2)}, u32[]{:S(2)}) collective-permute-start(bf16[4,256,2048]{2,1,0:T(8,128)(2,1)} %get-tuple-element.1087), channel_id=1, source_target_pairs={{0,1},{1,0},{2,3},{3,2},{4,5},{5,4},{6,7},{7,6},{8,9},{9,8},{10,11... | collective-permute-start | bytes 12582920 | tf_op jit(solution)/shard_map/ppermute | solution.py:109
  363.3 31.4 %collective-permute-start.60 = (bf16[256,2048]{1,0:T(8,128)(2,1)}, bf16[256,2048]{1,0:T(8,128)(2,1)}, u32[]{:S(2)}, u32[]{:S(2)}) collective-permute-start(bf16[256,2048]{1,0:T(8,128)(2,1)} %collective-permute-done.44.refs_2_), channel_id=1, source_target_pairs={{0,4},{1,5},{2,6},{3,7},{4,0},{5,1},{6,2},{7,3},{8,12},{9,13},{10,... | collective-permute-start | bytes 3145736 | tf_op jit(solution)/shard_map/ppermute | solution.py:109
  364.0 30.8 %collective-permute-start.61 = (bf16[256,2048]{1,0:T(8,128)(2,1)}, bf16[256,2048]{1,0:T(8,128)(2,1)}, u32[]{:S(2)}, u32[]{:S(2)}) collective-permute-start(bf16[256,2048]{1,0:T(8,128)(2,1)} %collective-permute-done.27.refs_1_), channel_id=1, source_target_pairs={{0,2},{1,3},{2,0},{3,1},{4,6},{5,7},{6,4},{7,5},{8,10},{9,11},{10,... | collective-permute-start | bytes 3145736 | tf_op jit(solution)/shard_map/ppermute | solution.py:109
  460.5 30.0 %collective-permute-start.76 = (bf16[2,256,2048]{2,1,0:T(8,128)(2,1)}, bf16[2,256,2048]{2,1,0:T(8,128)(2,1)}, u32[]{:S(2)}, u32[]{:S(2)}) collective-permute-start(bf16[2,256,2048]{2,1,0:T(8,128)(2,1)} %get-tuple-element.1169), channel_id=1, source_target_pairs={{0,1},{1,0},{2,3},{3,2},{4,5},{5,4},{6,7},{7,6},{8,9},{9,8},{10,11... | collective-permute-start | bytes 6291464 | tf_op jit(solution)/shard_map/ppermute | solution.py:109
  461.2 33.4 %collective-permute-start.74 = (bf16[256,2048]{1,0:T(8,128)(2,1)}, bf16[256,2048]{1,0:T(8,128)(2,1)}, u32[]{:S(2)}, u32[]{:S(2)}) collective-permute-start(bf16[256,2048]{1,0:T(8,128)(2,1)} %get-tuple-element.1166), channel_id=1, source_target_pairs={{0,4},{1,5},{2,6},{3,7},{4,0},{5,1},{6,2},{7,3},{8,12},{9,13},{10,... | collective-permute-start | bytes 3145736 | tf_op jit(solution)/shard_map/ppermute | solution.py:109
  462.0 32.6 %collective-permute-start.75 = (bf16[256,2048]{1,0:T(8,128)(2,1)}, bf16[256,2048]{1,0:T(8,128)(2,1)}, u32[]{:S(2)}, u32[]{:S(2)}) collective-permute-start(bf16[256,2048]{1,0:T(8,128)(2,1)} %shard_map.287), channel_id=1, source_target_pairs={{0,2},{1,3},{2,0},{3,1},{4,6},{5,7},{6,4},{7,5},{8,10},{9,11},{10,... | collective-permute-start | bytes 3145736 | tf_op jit(solution)/shard_map/ppermute | solution.py:109
  494.7 26.4 %collective-permute-start.77 = (bf16[256,2048]{1,0:T(8,128)(2,1)}, bf16[256,2048]{1,0:T(8,128)(2,1)}, u32[]{:S(2)}, u32[]{:S(2)}) collective-permute-start(bf16[256,2048]{1,0:T(8,128)(2,1)} %get-tuple-element.1188), channel_id=1, source_target_pairs={{0,4},{1,5},{2,6},{3,7},{4,0},{5,1},{6,2},{7,3},{8,12},{9,13},{10,... | collective-permute-start | bytes 3145736 | tf_op jit(solution)/shard_map/ppermute | solution.py:109
  585.5 28.1 %collective-permute-start.88 = (bf16[256,2048]{1,0:T(8,128)(2,1)}, bf16[256,2048]{1,0:T(8,128)(2,1)}, u32[]{:S(2)}, u32[]{:S(2)}) collective-permute-start(bf16[256,2048]{1,0:T(8,128)(2,1)} %get-tuple-element.1287), channel_id=1, source_target_pairs={{0,4},{1,5},{2,6},{3,7},{4,0},{5,1},{6,2},{7,3},{8,12},{9,13},{10,... | collective-permute-start | bytes 3145736 | tf_op jit(solution)/shard_map/ppermute | solution.py:109
  586.7 26.9 %collective-permute-start.89 = (bf16[256,2048]{1,0:T(8,128)(2,1)}, bf16[256,2048]{1,0:T(8,128)(2,1)}, u32[]{:S(2)}, u32[]{:S(2)}) collective-permute-start(bf16[256,2048]{1,0:T(8,128)(2,1)} %get-tuple-element.1288), channel_id=1, source_target_pairs={{0,2},{1,3},{2,0},{3,1},{4,6},{5,7},{6,4},{7,5},{8,10},{9,11},{10,... | collective-permute-start | bytes 3145736 | tf_op jit(solution)/shard_map/ppermute | solution.py:109
  588.0 26.7 %collective-permute-start.90 = (bf16[256,2048]{1,0:T(8,128)(2,1)}, bf16[256,2048]{1,0:T(8,128)(2,1)}, u32[]{:S(2)}, u32[]{:S(2)}) collective-permute-start(bf16[256,2048]{1,0:T(8,128)(2,1)} %get-tuple-element.1289), channel_id=1, source_target_pairs={{0,24},{1,25},{2,26},{3,27},{4,28},{5,29},{6,30},{7,31},{8,0},{9,1... | collective-permute-start | bytes 3145736 | tf_op jit(solution)/shard_map/ppermute | solution.py:109
  654.0 57.5 %collective-permute-start.96 = (bf16[256,2048]{1,0:T(8,128)(2,1)}, bf16[256,2048]{1,0:T(8,128)(2,1)}, u32[]{:S(2)}, u32[]{:S(2)}) collective-permute-start(bf16[256,2048]{1,0:T(8,128)(2,1)} %get-tuple-element.1377), channel_id=1, source_target_pairs={{0,4},{1,5},{2,6},{3,7},{4,0},{5,1},{6,2},{7,3},{8,12},{9,13},{10,... | collective-permute-start | bytes 3145736 | tf_op jit(solution)/shard_map/ppermute | solution.py:109
  654.7 56.8 %collective-permute-start.97 = (bf16[256,2048]{1,0:T(8,128)(2,1)}, bf16[256,2048]{1,0:T(8,128)(2,1)}, u32[]{:S(2)}, u32[]{:S(2)}) collective-permute-start(bf16[256,2048]{1,0:T(8,128)(2,1)} %get-tuple-element.1378), channel_id=1, source_target_pairs={{0,4},{1,5},{2,6},{3,7},{4,0},{5,1},{6,2},{7,3},{8,12},{9,13},{10,... | collective-permute-start | bytes 3145736 | tf_op jit(solution)/shard_map/ppermute | solution.py:109
  656.1 55.4 %collective-permute-start.98 = (bf16[256,2048]{1,0:T(8,128)(2,1)}, bf16[256,2048]{1,0:T(8,128)(2,1)}, u32[]{:S(2)}, u32[]{:S(2)}) collective-permute-start(bf16[256,2048]{1,0:T(8,128)(2,1)} %get-tuple-element.1379), channel_id=1, source_target_pairs={{0,2},{1,3},{2,0},{3,1},{4,6},{5,7},{6,4},{7,5},{8,10},{9,11},{10,... | collective-permute-start | bytes 3145736 | tf_op jit(solution)/shard_map/ppermute | solution.py:109
  656.9 54.6 %collective-permute-start.99 = (bf16[256,2048]{1,0:T(8,128)(2,1)}, bf16[256,2048]{1,0:T(8,128)(2,1)}, u32[]{:S(2)}, u32[]{:S(2)}) collective-permute-start(bf16[256,2048]{1,0:T(8,128)(2,1)} %shard_map.302), channel_id=1, source_target_pairs={{0,2},{1,3},{2,0},{3,1},{4,6},{5,7},{6,4},{7,5},{8,10},{9,11},{10,... | collective-permute-start | bytes 3145736 | tf_op jit(solution)/shard_map/ppermute | solution.py:109
  718.9 41.2 %collective-permute-start.102 = (bf16[256,2048]{1,0:T(8,128)(2,1)}, bf16[256,2048]{1,0:T(8,128)(2,1)}, u32[]{:S(2)}, u32[]{:S(2)}) collective-permute-start(bf16[256,2048]{1,0:T(8,128)(2,1)} %constant_dynamic-slice_fusion.9), channel_id=1, source_target_pairs={{0,4},{1,5},{2,6},{3,7},{4,0},{5,1},{6,2},{7,3},{8,12},{9,13},{10,... | collective-permute-start | bytes 3145736 | tf_op jit(solution)/shard_map/ppermute | solution.py:109
  719.7 46.0 %collective-permute-start.103 = (bf16[256,2048]{1,0:T(8,128)(2,1)}, bf16[256,2048]{1,0:T(8,128)(2,1)}, u32[]{:S(2)}, u32[]{:S(2)}) collective-permute-start(bf16[256,2048]{1,0:T(8,128)(2,1)} %get-tuple-element.1420), channel_id=1, source_target_pairs={{0,4},{1,5},{2,6},{3,7},{4,0},{5,1},{6,2},{7,3},{8,12},{9,13},{10,... | collective-permute-start | bytes 3145736 | tf_op jit(solution)/shard_map/ppermute | solution.py:109
  720.9 44.8 %collective-permute-start.104 = (bf16[256,2048]{1,0:T(8,128)(2,1)}, bf16[256,2048]{1,0:T(8,128)(2,1)}, u32[]{:S(2)}, u32[]{:S(2)}) collective-permute-start(bf16[256,2048]{1,0:T(8,128)(2,1)} %get-tuple-element.1421), channel_id=1, source_target_pairs={{0,2},{1,3},{2,0},{3,1},{4,6},{5,7},{6,4},{7,5},{8,10},{9,11},{10,... | collective-permute-start | bytes 3145736 | tf_op jit(solution)/shard_map/ppermute | solution.py:109
  722.1 43.7 %collective-permute-start.105 = (bf16[256,2048]{1,0:T(8,128)(2,1)}, bf16[256,2048]{1,0:T(8,128)(2,1)}, u32[]{:S(2)}, u32[]{:S(2)}) collective-permute-start(bf16[256,2048]{1,0:T(8,128)(2,1)} %get-tuple-element.1422), channel_id=1, source_target_pairs={{0,24},{1,25},{2,26},{3,27},{4,28},{5,29},{6,30},{7,31},{8,0},{9,1... | collective-permute-start | bytes 3145736 | tf_op jit(solution)/shard_map/ppermute | solution.py:109
  726.4 33.6 %collective-permute-start.101 = (bf16[80,2048]{1,0:T(8,128)(2,1)S(1)}, bf16[80,2048]{1,0:T(8,128)(2,1)S(1)}, u32[]{:S(2)}, u32[]{:S(2)}) collective-permute-start(bf16[80,2048]{1,0:T(8,128)(2,1)S(1)} %copy-done.35), channel_id=1, source_target_pairs={{0,16},{1,17},{2,18},{3,19},{4,20},{5,21},{6,22},{7,23},{8,24},{9,... | collective-permute-start | bytes 983048 | tf_op jit(solution)/shard_map/ppermute | solution.py:109
  776.0 32.7 %collective-permute-start.110 = (bf16[2,64,2048]{2,1,0:T(8,128)(2,1)}, bf16[2,64,2048]{2,1,0:T(8,128)(2,1)}, u32[]{:S(2)}, u32[]{:S(2)}) collective-permute-start(bf16[2,64,2048]{2,1,0:T(8,128)(2,1)} %dynamic-slice_bitcast_fusion.1), channel_id=1, source_target_pairs={{0,8},{1,9},{2,10},{3,11},{4,12},{5,13},{6,14},{7,15},{8,0},{9,1},... | collective-permute-start | bytes 1572872 | tf_op jit(solution)/shard_map/ppermute | solution.py:109
  784.2 39.2 %collective-permute-start.106 = (bf16[1024,512]{1,0:T(8,128)(2,1)}, bf16[1024,512]{1,0:T(8,128)(2,1)}, u32[]{:S(2)}, u32[]{:S(2)}) collective-permute-start(bf16[1024,512]{1,0:T(8,128)(2,1)} %constant_dynamic-slice_fusion.8), channel_id=1, source_target_pairs={{0,4},{1,5},{2,6},{3,7},{4,0},{5,1},{6,2},{7,3},{8,12},{9,13},{10,... | collective-permute-start | bytes 3145736 | tf_op jit(solution)/shard_map/ppermute | solution.py:109
  785.1 44.9 %collective-permute-start.107 = (bf16[256,2048]{1,0:T(8,128)(2,1)}, bf16[256,2048]{1,0:T(8,128)(2,1)S(1)}, u32[]{:S(2)}, u32[]{:S(2)}) collective-permute-start(bf16[256,2048]{1,0:T(8,128)(2,1)} %get-tuple-element.1476), channel_id=1, source_target_pairs={{0,4},{1,5},{2,6},{3,7},{4,0},{5,1},{6,2},{7,3},{8,12},{9,13},{10,... | collective-permute-start | bytes 3145736 | tf_op jit(solution)/shard_map/ppermute | solution.py:109
  786.2 43.8 %collective-permute-start.108 = (bf16[256,2048]{1,0:T(8,128)(2,1)}, bf16[256,2048]{1,0:T(8,128)(2,1)}, u32[]{:S(2)}, u32[]{:S(2)}) collective-permute-start(bf16[256,2048]{1,0:T(8,128)(2,1)} %get-tuple-element.1477), channel_id=1, source_target_pairs={{0,2},{1,3},{2,0},{3,1},{4,6},{5,7},{6,4},{7,5},{8,10},{9,11},{10,... | collective-permute-start | bytes 3145736 | tf_op jit(solution)/shard_map/ppermute | solution.py:109
  787.1 43.0 %collective-permute-start.109 = (bf16[256,2048]{1,0:T(8,128)(2,1)}, bf16[256,2048]{1,0:T(8,128)(2,1)}, u32[]{:S(2)}, u32[]{:S(2)}) collective-permute-start(bf16[256,2048]{1,0:T(8,128)(2,1)} %get-tuple-element.1478), channel_id=1, source_target_pairs={{0,24},{1,25},{2,26},{3,27},{4,28},{5,29},{6,30},{7,31},{8,0},{9,1... | collective-permute-start | bytes 3145736 | tf_op jit(solution)/shard_map/ppermute | solution.py:109
  834.4 32.6 %collective-permute-start.112 = (bf16[512,2048]{1,0:T(8,128)(2,1)S(1)}, bf16[512,2048]{1,0:T(8,128)(2,1)S(1)}, u32[]{:S(2)}, u32[]{:S(2)}) collective-permute-start(bf16[512,2048]{1,0:T(8,128)(2,1)S(1)} %pad_maximum_fusion.1), channel_id=1, source_target_pairs={{0,1},{1,0},{2,3},{3,2},{4,5},{5,4},{6,7},{7,6},{8,9},{9,8},{10,11... | collective-permute-start | bytes 6291464 | tf_op jit(solution)/shard_map/ppermute | solution.py:109
  836.2 29.8 %collective-permute-start.114 = (bf16[1024,512]{1,0:T(8,128)(2,1)S(1)}, bf16[1024,512]{1,0:T(8,128)(2,1)S(1)}, u32[]{:S(2)}, u32[]{:S(2)}) collective-permute-start(bf16[1024,512]{1,0:T(8,128)(2,1)S(1)} %constant_dynamic-slice_fusion.7), channel_id=1, source_target_pairs={{0,4},{1,5},{2,6},{3,7},{4,0},{5,1},{6,2},{7,3},{8,12},{9,13},{10,... | collective-permute-start | bytes 3145736 | tf_op jit(solution)/shard_map/ppermute | solution.py:109
  836.9 29.1 %collective-permute-start.115 = (bf16[256,2048]{1,0:T(8,128)(2,1)S(1)}, bf16[256,2048]{1,0:T(8,128)(2,1)S(1)}, u32[]{:S(2)}, u32[]{:S(2)}) collective-permute-start(bf16[256,2048]{1,0:T(8,128)(2,1)S(1)} %copy-done.88), channel_id=1, source_target_pairs={{0,2},{1,3},{2,0},{3,1},{4,6},{5,7},{6,4},{7,5},{8,10},{9,11},{10,... | collective-permute-start | bytes 3145736 | tf_op jit(solution)/shard_map/ppermute | solution.py:109
  933.1 26.1 %collective-permute-start.129 = (bf16[1024,512]{1,0:T(8,128)(2,1)S(1)}, bf16[1024,512]{1,0:T(8,128)(2,1)}, u32[]{:S(2)}, u32[]{:S(2)}) collective-permute-start(bf16[1024,512]{1,0:T(8,128)(2,1)S(1)} %bitcast.183), channel_id=1, source_target_pairs={{0,4},{1,5},{2,6},{3,7},{4,0},{5,1},{6,2},{7,3},{8,12},{9,13},{10,... | collective-permute-start | bytes 3145736 | tf_op jit(solution)/shard_map/ppermute | solution.py:109
  963.2 26.2 %collective-permute-start.137 = (bf16[256,2048]{1,0:T(8,128)(2,1)}, bf16[256,2048]{1,0:T(8,128)(2,1)S(1)}, u32[]{:S(2)}, u32[]{:S(2)}) collective-permute-start(bf16[256,2048]{1,0:T(8,128)(2,1)} %shard_map.307), channel_id=1, source_target_pairs={{0,4},{1,5},{2,6},{3,7},{4,0},{5,1},{6,2},{7,3},{8,12},{9,13},{10,... | collective-permute-start | bytes 3145736 | tf_op jit(solution)/shard_map/ppermute | solution.py:109
  1017.9 31.8 %collective-permute-start.144 = (bf16[1024,512]{1,0:T(8,128)(2,1)S(1)}, bf16[1024,512]{1,0:T(8,128)(2,1)}, u32[]{:S(2)}, u32[]{:S(2)}) collective-permute-start(bf16[1024,512]{1,0:T(8,128)(2,1)S(1)} %bitcast.185), channel_id=1, source_target_pairs={{0,4},{1,5},{2,6},{3,7},{4,0},{5,1},{6,2},{7,3},{8,12},{9,13},{10,... | collective-permute-start | bytes 3145736 | tf_op jit(solution)/shard_map/ppermute | solution.py:109
  1019.2 30.6 %collective-permute-start.143 = (bf16[80,2048]{1,0:T(8,128)(2,1)S(1)}, bf16[80,2048]{1,0:T(8,128)(2,1)S(1)}, u32[]{:S(2)}, u32[]{:S(2)}) collective-permute-start(bf16[80,2048]{1,0:T(8,128)(2,1)S(1)} %add_convert_fusion.8), channel_id=1, source_target_pairs={{0,4},{1,5},{2,6},{3,7},{4,0},{5,1},{6,2},{7,3},{8,12},{9,13},{10,... | collective-permute-start | bytes 983048 | tf_op jit(solution)/shard_map/ppermute | solution.py:109
  1061.8 31.9 %collective-permute-start.151 = (bf16[1024,512]{1,0:T(8,128)(2,1)S(1)}, bf16[1024,512]{1,0:T(8,128)(2,1)S(1)}, u32[]{:S(2)}, u32[]{:S(2)}) collective-permute-start(bf16[1024,512]{1,0:T(8,128)(2,1)S(1)} %bitcast.184), channel_id=1, source_target_pairs={{0,4},{1,5},{2,6},{3,7},{4,0},{5,1},{6,2},{7,3},{8,12},{9,13},{10,... | collective-permute-start | bytes 3145736 | tf_op jit(solution)/shard_map/ppermute | solution.py:109
  1063.2 30.5 %collective-permute-start.152 = (bf16[256,2048]{1,0:T(8,128)(2,1)S(1)}, bf16[256,2048]{1,0:T(8,128)(2,1)S(1)}, u32[]{:S(2)}, u32[]{:S(2)}) collective-permute-start(bf16[256,2048]{1,0:T(8,128)(2,1)S(1)} %copy-done.52), channel_id=1, source_target_pairs={{0,24},{1,25},{2,26},{3,27},{4,28},{5,29},{6,30},{7,31},{8,0},{9,1... | collective-permute-start | bytes 3145736 | tf_op jit(solution)/shard_map/ppermute | solution.py:109
  (185 other events, 2933.9 us)

commit v5 on v4

--- a/solution.py
+++ b/solution.py
@@ -1133,7 +1133,7 @@
     )
     router_sums = add_low(router_sums, other)
     key_weight.add_x(got)
-    out_weight.part, value_weight.part = out_piece, value_piece
+    out_weight.part = out_piece
     (d_across, *got), _ = advance(
         extra=[(add_low(parts[2], d_other[tok_rows:]), "y")] + query_weight.split_x() + out_weight.join_z(),
     )
@@ -1145,45 +1145,55 @@
     d_input = d_mixed + scale_one * (
         d_norm_one - normed * jnp.mean(d_norm_one * normed, axis=-1, keepdims=True)
     )
-    got, (d_input,) = advance(
-        [(lambda value: value, (d_input.astype(BF16),))],
-        extra=out_weight.join_x() + value_weight.join_z(),
+    (other, third, *got), (value_weight.whole_half, d_input) = advance(
+        [
+            (value_weight.collect_z, (value_piece,)),
+            (lambda value: value, (d_input.astype(BF16),)),
+        ],
+        extra=[(attn_gain_part, "c"), (router_sums, "y")] + out_weight.join_x(),
         out=[("y", (0, 0, 1))],
     )
-    out_weight.took_x(got[:1])
-    value_weight.took_z(got[1:])
-    (other, *got), (grad_w_out,) = advance(
-        [(lambda value: value, (out_weight.result,))],
-        extra=[(attn_gain_part, "c")] + value_weight.join_x() + key_weight.split_z(),
-    )
+    router_sums = add_low(router_sums, third)
     attn_gain_part = attn_gain_part + other
-    value_weight.took_x(got[:1])
-    key_weight.add_z(got[1:])
-    (other, *got), (grad_value,) = advance(
-        [(lambda value: value, (value_weight.result,))],
-        extra=[(attn_gain_part, "y")] + query_weight.split_z(),
+    out_weight.took_x(got)
+    (other, *got), (key_piece, grad_w_out) = advance(
+        [
+            (key_weight.reduce_z, (key_weight.sum,)),
+            (lambda value: value, (out_weight.result,)),
+        ],
+        extra=[(attn_gain_part, "y")] + value_weight.join_x(),
+    )
+    value_weight.took_x(got)
+    gain_parts = jnp.concatenate([attn_gain_part + other, query_gain_part[0], key_gain_part[0]])
+    (other, third), (query_piece, grad_value) = advance(
+        [
+            (query_weight.reduce_z, (query_weight.sum,)),
+            (lambda value: value, (value_weight.result,)),
+        ],
+        extra=[(gain_parts, "x"), (router_sums, "x")],
         out=[("x", (0, 1, 0))],
     )
-    query_weight.add_z(got)
-    gain_parts = jnp.concatenate([attn_gain_part + other, query_gain_part[0], key_gain_part[0]])
-    (other, third, *got), _ = advance(
-        extra=[(gain_parts, "x"), (router_sums, "y")] + key_weight.join_z(),
-    )
     gain_parts = gain_parts + other
-    router_sums = add_low(router_sums, third)
-    key_weight.took_z(got)
-    (other, *got), _ = advance(
-        extra=[(router_sums, "x")] + key_weight.join_x() + query_weight.join_z(),
-    )
-    router_sums = add_wide(router_sums, other)
-    key_weight.took_x(got[:1])
-    query_weight.took_z(got[1:])
-    (next_z, far_z, last_z, *got), (grad_key, router_sums) = advance(
-        [(lambda value: value, (key_weight.result,)), (lambda value: value, (router_sums,))],
-        extra=[(gain_parts, "u1"), (gain_parts, "u2"), (gain_parts, "u3")] + query_weight.join_x(),
+    router_sums = add_wide(router_sums, third)
+    (next_z, far_z, last_z), (key_weight.whole_half,) = advance(
+        [(key_weight.collect_z, (key_piece,))],
+        extra=[(gain_parts, "u1"), (gain_parts, "u2"), (gain_parts, "u3")],
+    )
+    gain_sums = (gain_parts + far_z) + (next_z + last_z)
+    got, (query_weight.whole_half, gain_sums, router_sums) = advance(
+        [
+            (query_weight.collect_z, (query_piece,)),
+            (lambda value: value, (gain_sums,)),
+            (lambda value: value, (router_sums,)),
+        ],
+        extra=key_weight.join_x(),
+    )
+    key_weight.took_x(got)
+    got, (grad_key,) = advance(
+        [(lambda value: value, (key_weight.result,))],
+        extra=query_weight.join_x(),
         out=[("z", (3, 0, 0))],
     )
-    gain_sums = (gain_parts + far_z) + (next_z + last_z)
     query_weight.took_x(got)
     grad_query = query_weight.result
     result = (mixed + out_sum.total()).astype(BF16)

time: 1120 us -> 1090 us (0.973)
  starting transfers between devices: 179 us -> 150 us
  waiting for transfers between devices: 268 us -> 286 us
    ppermute x153 -> x148, starting transfers between devices: 166 us -> 138 us  [send(): return lax.ppermute(value, BOTH, device_pairs(MOVES[axis]))]
    ppermute x153 -> x148, waiting for transfers between devices: 256 us -> 273 us  [send(): return lax.ppermute(value, BOTH, device_pairs(MOVES[axis]))]
  transfers between devices with their start and end apart: 156 -> 151, of which waited for: 68 -> 64; matrix products, arithmetic and copies ran while one was open for 9% -> 10% of each run, Pallas kernels for 38% -> 39%
where the time goes in v5:
time: 1090 us; the launch traced here: 1080 us
  Pallas kernels  447 us (41%)
  waiting for transfers between devices  286 us (26%)
  starting transfers between devices  150 us (14%)
  other arithmetic  77.1 us (7%)
  matrix products  48.3 us (4%)
  local copies, waits for them, and re-layouts  43.3 us (4%)
  blocking collectives  20.6 us (2%)
    ppermute x148, waiting for transfers between devices, send(): return lax.ppermute(value, BOTH, device_pairs(MOVES[axis]))  273 us
    ppermute x148, starting transfers between devices, send(): return lax.ppermute(value, BOTH, device_pairs(MOVES[axis]))  138 us
    pallas_call x5, Pallas kernels, main_chunk(): pl.pallas_call(functools.partial(main_kernel, count, slot_count), grid=(e...  123 us
    pallas_call x4, Pallas kernels, cot_chunk(): pl.pallas_call(functools.partial(cot_kernel, count, slot_count), grid=(ex...  62.7 us
    pallas_call x3, Pallas kernels, expert_grads(): pl.pallas_call(functools.partial(grad_kernel, count), grid=(last - first,...  61 us
    pallas_call x4, Pallas kernels, out_chunk(): pl.pallas_call(functools.partial(out_kernel, len(picks), slot_count), gri...  55 us
    pallas_call x9, Pallas kernels, pair_sum(): pl.pallas_call(pair_kernel, grid=(rows // tile,), in_specs=[stack, stack]...  49.7 us
    pallas_call x9, Pallas kernels, block_sums(): pl.pallas_call(functools.partial(sums_kernel, counts), grid=(rows // tile...  37.8 us
  transfers between devices with their start and end apart: 151, of which 64 were waited for; matrix products, arithmetic and copies ran while one was open for 10% of the time, Pallas kernels for 39%

profile of v5, /device:TPU:0, one launch (start us, length us, event | category | flops | bytes accessed | tf_op | source)
XLA Modules:
  0.0 1076.0 jit_solution(15090106348095951992)
XLA Ops:
  7.4 7.4 all-to-all-start
  35.4 7.7 collective-permute-done.refs_2_
  48.4 5.0 collective-permute-start.4
  56.3 17.2 %shard_map.272 = (f32[1024,512]{1,0:T(8,128)}, f32[1024,512]{1,0:T(8,128)}, bf16[1024,512]{1,0:T(8,128)(2,1)}, f32[1024,128]{1,0:T(8,128)}, f32[1024,128]{1,0:T(8,128)}) custom-call(bf16[256,2048]{1,0:T(8,128)(2,1)} %fusion.18.refs_0_, bf16[256,2048]{1,0:T(8,128)(2,1)} %collective-permute-done.1.refs_1_, bf16[256,2048]{1,0:T(8,128)(2,1)} %collective-permute-done.refs_2_, ...), custom_call_target="tpu_custom_call" | custom-call | flops 6442450944 | bytes 15728640 | tf_op jit(solution)/shard_map/pallas_call | solution.py:580
  76.7 6.4 psum.14
  88.3 16.9 %shard_map.273 = (bf16[1024,512]{1,0:T(8,128)(2,1)}, f32[1024,512]{1,0:T(8,128)}, bf16[1024,512]{1,0:T(8,128)(2,1)}, bf16[1024,512]{1,0:T(8,128)(2,1)}) custom-call(f32[1024,512]{1,0:T(8,128)} %get-tuple-element.1407.q_ref, f32[1024,512]{1,0:T(8,128)} %get-tuple-element.1410.k_ref, bf16[1024,512]{1,0:T(8,128)(2,1)} %get-tuple-element.1365.v_ref, ...), custom_call_target="tpu_custom_call" | custom-call | flops 2147483648 | bytes 10485760 | tf_op jit(solution)/shard_map/pallas_call | solution.py:702
  123.4 17.9 %collective-permute-done.20 = bf16[256,2048]{1,0:T(8,128)(2,1)S(1)} collective-permute-done((bf16[256,2048]{1,0:T(8,128)(2,1)S(1)}, bf16[256,2048]{1,0:T(8,128)(2,1)S(1)}, u32[]{:S(2)}, u32[]{:S(2)}) %collective-permute-start.20) | collective-permute-done | bytes 1048608 | tf_op jit(solution)/shard_map/ppermute | solution.py:109
  153.7 15.7 %shard_map.274 = (bf16[8,256,2048]{2,1,0:T(8,128)(2,1)}, f32[8,256,256]{2,1,0:T(8,128)}) custom-call(bf16[8,256,256]{2,1,0:T(8,128)(2,1)} %bitcast.227, bf16[8,256,2048]{2,1,0:T(8,128)(2,1)} %refs_4_.1, bf16[256,2048]{1,0:T(8,128)(2,1)} %refs_0_, bf16[256,2048]{1,0:T(8,128)(2,1)} %collective-permute-done.2.refs_1_, ...), custom_call_target="tpu_custom_call" | custom-call | flops 4294967296 | bytes 25165824 | tf_op jit(solution)/shard_map/pallas_call | solution.py:388
  180.9 15.7 %shard_map.275 = (bf16[8,256,2048]{2,1,0:T(8,128)(2,1)}, f32[8,256,256]{2,1,0:T(8,128)}) custom-call(bf16[8,256,256]{2,1,0:T(8,128)(2,1)} %bitcast.224, bf16[8,256,2048]{2,1,0:T(8,128)(2,1)} %refs_4_.1, bf16[256,2048]{1,0:T(8,128)(2,1)} %collective-permute-done.4.refs_0_, bf16[256,2048]{1,0:T(8,128)(2,1)} %collective-permute-done.5.refs_1_, ...), custom_call_target="tpu_custom_call" | custom-call | flops 4294967296 | bytes 25165824 | tf_op jit(solution)/shard_map/pallas_call | solution.py:388
  196.6 7.0 all-to-all-done.1
  210.9 27.6 %shard_map.276 = (bf16[8,256,2048]{2,1,0:T(8,128)(2,1)}, bf16[8,256,256]{2,1,0:T(8,128)(2,1)}, bf16[8,256,256]{2,1,0:T(8,128)(2,1)}, bf16[8,256,256]{2,1,0:T(8,1...) custom-call(bf16[8,256,256]{2,1,0:T(8,128)(2,1)} %bitcast.228, ...), custom_call_target="tpu_custom_call" | custom-call | flops 12884901888 | bytes 41943040 | tf_op jit(solution)/shard_map/pallas_call | solution.py:411
  240.7 7.0 collective-permute-done.39.refs_5_
  247.9 5.9 shard_map.277
  253.8 11.0 %collective-permute-done.38.refs_1_ = bf16[256,2048]{1,0:T(8,128)(2,1)} collective-permute-done((bf16[256,2048]{1,0:T(8,128)(2,1)}, bf16[256,2048]{1,0:T(8,128)(2,1)}, u32[]{:S(2)}, u32[]{:S(2)}) %collective-permute-start.38) | collective-permute-done | bytes 1048608 | tf_op jit(solution)/shard_map/ppermute | solution.py:109
  268.5 27.7 %shard_map.278 = (bf16[8,256,2048]{2,1,0:T(8,128)(2,1)}, bf16[8,256,256]{2,1,0:T(8,128)(2,1)}, bf16[8,256,256]{2,1,0:T(8,128)(2,1)}, bf16[8,256,256]{2,1,0:T(8,1...) custom-call(bf16[8,256,256]{2,1,0:T(8,128)(2,1)} %bitcast.225, ...), custom_call_target="tpu_custom_call" | custom-call | flops 12884901888 | bytes 41943040 | tf_op jit(solution)/shard_map/pallas_call | solution.py:411
  298.5 6.9 collective-permute-done.53.refs_7_
  305.9 15.7 %shard_map.280 = (bf16[8,256,2048]{2,1,0:T(8,128)(2,1)}, f32[8,256,256]{2,1,0:T(8,128)}) custom-call(bf16[8,256,256]{2,1,0:T(8,128)(2,1)} %bitcast.221, bf16[8,256,2048]{2,1,0:T(8,128)(2,1)} %refs_4_.1, bf16[256,2048]{1,0:T(8,128)(2,1)} %collective-permute-done.10.refs_0_, bf16[256,2048]{1,0:T(8,128)(2,1)} %collective-permute-done.15.refs_1_, ...), custom_call_target="tpu_custom_call" | custom-call | flops 4294967296 | bytes 25165824 | tf_op jit(solution)/shard_map/pallas_call | solution.py:388
  321.6 6.0 shard_map.279
  335.3 27.8 %shard_map.281 = (bf16[8,256,2048]{2,1,0:T(8,128)(2,1)}, bf16[8,256,256]{2,1,0:T(8,128)(2,1)}, bf16[8,256,256]{2,1,0:T(8,128)(2,1)}, bf16[8,256,256]{2,1,0:T(8,1...) custom-call(bf16[8,256,256]{2,1,0:T(8,128)(2,1)} %bitcast.222, ...), custom_call_target="tpu_custom_call" | custom-call | flops 12884901888 | bytes 41943040 | tf_op jit(solution)/shard_map/pallas_call | solution.py:411
  373.7 15.7 %shard_map.283 = (bf16[8,256,2048]{2,1,0:T(8,128)(2,1)}, f32[8,256,256]{2,1,0:T(8,128)}) custom-call(bf16[8,256,256]{2,1,0:T(8,128)(2,1)} %pad_maximum_fusion.2.picks_ref, bf16[8,256,2048]{2,1,0:T(8,128)(2,1)} %refs_4_.1, bf16[256,2048]{1,0:T(8,128)(2,1)} %collective-permute-done.51.refs_0_, bf16[256,2048]{1,0:T(8,128)(2,1)} %copy-done.50, ...), custom_call_target="tpu_custom_call" | custom-call | flops 4294967296 | bytes 25165824 | tf_op jit(solution)/shard_map/pallas_call | solution.py:388
  389.4 5.9 shard_map.282
  399.9 20.4 %shard_map.284 = (bf16[8,128,2048]{2,1,0:T(8,128)(2,1)}, bf16[8,128,256]{2,1,0:T(8,128)(2,1)}, bf16[8,128,256]{2,1,0:T(8,128)(2,1)}, bf16[8,128,256]{2,1,0:T(8,1...) custom-call(bf16[4,256,256]{2,1,0:T(8,128)(2,1)} %bitcast.242, ...), custom_call_target="tpu_custom_call" | custom-call | flops 6442450944 | bytes 29360128 | tf_op jit(solution)/shard_map/pallas_call | solution.py:411
  433.0 20.0 %shard_map.286 = (bf16[8,128,2048]{2,1,0:T(8,128)(2,1)}, bf16[8,128,256]{2,1,0:T(8,128)(2,1)}, bf16[8,128,256]{2,1,0:T(8,128)(2,1)}, bf16[8,128,256]{2,1,0:T(8,1...) custom-call(bf16[4,256,256]{2,1,0:T(8,128)(2,1)} %bitcast.239, ...), custom_call_target="tpu_custom_call" | custom-call | flops 6442450944 | bytes 29360128 | tf_op jit(solution)/shard_map/pallas_call | solution.py:411
  471.2 13.7 %shard_map.289 = (bf16[4,256,2048]{2,1,0:T(8,128)(2,1)}, bf16[4,256,2048]{2,1,0:T(8,128)(2,1)}) custom-call(bf16[8,256,256]{2,1,0:T(8,128)(2,1)} %bitcast.229, bf16[8,256,256]{2,1,0:T(8,128)(2,1)} %get-tuple-element.1423.refs_1_.refs_10_, bf16[8,256,2048]{2,1,0:T(8,128)(2,1)} %refs_4_.1), custom_call_target="tpu_custom_call" | custom-call | flops 4294967296 | bytes 25165824 | tf_op jit(solution)/shard_map/pallas_call | solution.py:454
  485.0 5.7 all-to-all-done.2
  501.8 13.7 %shard_map.290 = (bf16[4,256,2048]{2,1,0:T(8,128)(2,1)}, bf16[4,256,2048]{2,1,0:T(8,128)(2,1)}) custom-call(bf16[8,256,256]{2,1,0:T(8,128)(2,1)} %bitcast.226, bf16[8,256,256]{2,1,0:T(8,128)(2,1)} %get-tuple-element.1424.refs_1_.refs_11_, bf16[8,256,2048]{2,1,0:T(8,128)(2,1)} %refs_4_.1), custom_call_target="tpu_custom_call" | custom-call | flops 4294967296 | bytes 25165824 | tf_op jit(solution)/shard_map/pallas_call | solution.py:454
  515.5 5.9 shard_map.291
  524.4 13.7 %shard_map.293 = (bf16[4,256,2048]{2,1,0:T(8,128)(2,1)}, bf16[4,256,2048]{2,1,0:T(8,128)(2,1)}) custom-call(bf16[8,256,256]{2,1,0:T(8,128)(2,1)} %bitcast.223, bf16[8,256,256]{2,1,0:T(8,128)(2,1)} %get-tuple-element.1425.refs_1_.refs_12_, bf16[8,256,2048]{2,1,0:T(8,128)(2,1)} %refs_4_.1), custom_call_target="tpu_custom_call" | custom-call | flops 4294967296 | bytes 25165824 | tf_op jit(solution)/shard_map/pallas_call | solution.py:454
  538.1 5.9 shard_map.294
  549.5 4.7 shard_map.295
  558.1 13.8 %shard_map.296 = (bf16[4,256,2048]{2,1,0:T(8,128)(2,1)}, bf16[4,256,2048]{2,1,0:T(8,128)(2,1)}) custom-call(bf16[4,256,256]{2,1,0:T(8,128)(2,1)} %bitcast.243, bf16[4,256,256]{2,1,0:T(8,128)(2,1)} %bitcast.240, bf16[8,128,256]{2,1,0:T(8,128)(2,1)} %get-tuple-element.1426.refs_2_.refs_13_, bf16[8,128,256]{2,1,0:T(8,128)(2,1)} %get-tuple-element.1427.refs_3_.refs_14_, ...), custom_call_target="tpu_custom_call" | custom-call | flops 4294967296 | bytes 25165824 | tf_op jit(solution)/shard_map/pallas_call | solution.py:454
  571.9 5.9 shard_map.297
  581.2 4.7 shard_map.298
  592.6 15.4 %shard_map.300 = (f32[8,2048,256]{2,1,0:T(8,128)}, f32[8,2048,256]{2,1,0:T(8,128)}, f32[8,256,2048]{2,1,0:T(8,128)}) custom-call(bf16[8,256,2048]{2,1,0:T(8,128)(2,1)} %get-tuple-element.1413.refs_0_, bf16[8,256,2048]{2,1,0:T(8,128)(2,1)} %get-tuple-element.1414.refs_1_, bf16[8,256,2048]{2,1,0:T(8,128)(2,1)} %get-tuple-element.1415.refs_2_, ...), custom_call_target="tpu_custom_call" | custom-call | flops 6442450944 | bytes 29360128 | tf_op jit(solution)/shard_map/pallas_call | solution.py:500
  608.1 5.9 shard_map.299
  623.6 22.7 %shard_map.301 = (f32[8,2048,256]{2,1,0:T(8,128)}, f32[8,2048,256]{2,1,0:T(8,128)}, f32[8,256,2048]{2,1,0:T(8,128)}) custom-call(bf16[8,256,2048]{2,1,0:T(8,128)(2,1)} %get-tuple-element.1413.refs_0_, bf16[8,256,2048]{2,1,0:T(8,128)(2,1)} %get-tuple-element.1414.refs_1_, ...), custom_call_target="tpu_custom_call", output_to_operand_aliasing={{0}: (25, {}), {1}: (26, {}), {2}: (27, {})} | custom-call | flops 9663676416 | bytes 44040192 | tf_op jit(solution)/shard_map/pallas_call | solution.py:500
  666.1 22.8 %shard_map.303 = (f32[1024,512]{1,0:T(8,128)}, f32[1024,512]{1,0:T(8,128)}, bf16[1024,512]{1,0:T(8,128)(2,1)}, f32[1,512]{1,0:T(1,128)}, f32[1,512]{1,0:T(1,128)...) custom-call(f32[1024,512]{1,0:T(8,128)} %get-tuple-element.1407.q_ref, f32[1024,512]{1,0:T(8,128)} %get-tuple-element.1410.k_ref, ...), custom_call_target="tpu_custom_call" | custom-call | flops 5368709120 | bytes 16777216 | tf_op jit(solution)/shard_map/pallas_call | solution.py:729
  692.2 14.2 %psum.15 = f32[2,4,256]{2,0,1:T(2,128)S(1)} all-reduce(f32[2,4,256]{2,0,1:T(2,128)S(1)} %bitcast.256), channel_id=1, replica_groups=mesh['dp'=8,'tensor'=4] {'tensor'}, use_global_device_ids=true, to_apply=%region_14.15 | all-reduce | flops 2048 | bytes 16384 | tf_op jit(solution)/shard_map/psum | solution.py:802
  707.1 4.9 fusion.13
  726.8 22.9 %shard_map.305 = (f32[8,2048,256]{2,1,0:T(8,128)}, f32[8,2048,256]{2,1,0:T(8,128)}, f32[8,256,2048]{2,1,0:T(8,128)}) custom-call(bf16[8,256,2048]{2,1,0:T(8,128)(2,1)} %get-tuple-element.1413.refs_0_, bf16[8,256,2048]{2,1,0:T(8,128)(2,1)} %get-tuple-element.1414.refs_1_, ...), custom_call_target="tpu_custom_call", output_to_operand_aliasing={{0}: (25, {}), {1}: (26, {}), {2}: (27, {})} | custom-call | flops 9663676416 | bytes 44040192 | tf_op jit(solution)/shard_map/pallas_call | solution.py:500
  760.5 5.7 collective-permute-done.103.refs_3_
  769.9 4.7 shard_map.306
  776.5 4.4 fusion.80
  787.5 4.5 collective-permute-start.109
  792.0 5.6 fusion.81
  797.6 6.5 add_convert_fusion
  804.1 4.9 convolution_convert_fusion.1
  811.5 12.3 %collective-permute-done.111 = bf16[64,2048]{1,0:T(8,128)(2,1)S(1)} collective-permute-done((bf16[64,2048]{1,0:T(8,128)(2,1)S(1)}, bf16[64,2048]{1,0:T(8,128)(2,1)S(1)}, u32[]{:S(2)}, u32[]{:S(2)}) %collective-permute-start.111) | collective-permute-done | bytes 262176 | tf_op jit(solution)/shard_map/ppermute | solution.py:109
  823.9 6.6 collective-permute-done.107.refs_1_
  838.0 11.3 %collective-permute-done.116 = bf16[2,256,512]{2,1,0:T(8,128)(2,1)S(1)} collective-permute-done((bf16[2,256,512]{2,1,0:T(8,128)(2,1)S(1)}, bf16[2,256,512]{2,1,0:T(8,128)(2,1)S(1)}, u32[]{:S(2)}, u32[]{:S(2)}) %collective-permute-start.116) | collective-permute-done | bytes 524320 | tf_op jit(solution)/shard_map/ppermute | solution.py:109
  849.5 4.5 collective-permute-start.117
  854.1 11.6 %collective-permute-done.117 = bf16[256,512]{1,0:T(8,128)(2,1)S(1)} collective-permute-done((bf16[256,512]{1,0:T(8,128)(2,1)S(1)}, bf16[256,512]{1,0:T(8,128)(2,1)S(1)}, u32[]{:S(2)}, u32[]{:S(2)}) %collective-permute-start.117) | collective-permute-done | bytes 262176 | tf_op jit(solution)/shard_map/ppermute | solution.py:109
  872.7 6.3 collective-permute-done.120
  879.0 9.8 collective-permute-done.121
  902.1 9.9 collective-permute-done.127
  918.0 8.8 collective-permute-done.128
  951.2 9.2 collective-permute-done.132
  960.5 6.3 collective-permute-done.130
  971.1 9.7 collective-permute-done.136
  991.0 7.9 collective-permute-done.133
  1001.2 8.3 collective-permute-done.141
  1022.9 8.3 collective-permute-done.144
  1036.3 6.2 collective-permute-done.145
  1053.2 15.0 %collective-permute-done.146 = bf16[1024,512]{1,0:T(8,128)(2,1)S(1)} collective-permute-done((bf16[1024,512]{1,0:T(8,128)(2,1)S(1)}, bf16[1024,512]{1,0:T(8,128)(2,1)S(1)}, u32[]{:S(2)}, u32[]{:S(2)}) %collective-permute-start.146) | collective-permute-done | bytes 1048608 | tf_op jit(solution)/shard_map/ppermute | solution.py:109
  (625 shorter events, 373.2 us)
Async XLA Ops:
  7.4 26.5 %all-to-all-start = ((f32[32,8,256]{2,1,0:T(8,128)}), f32[32,8,256]{2,1,0:T(8,128)}, u32[]{:S(2)}, u32[]{:S(2)}) async-start(f32[32,8,256]{2,1,0:T(8,128)} %bitcast.4), calls=%async_computation | async-start | bytes 524288 | tf_op jit(solution)/shard_map/all_to_all | solution.py:810
  14.8 28.3 %collective-permute-start = (bf16[256,2048]{1,0:T(8,128)(2,1)}, bf16[256,2048]{1,0:T(8,128)(2,1)}, u32[]{:S(2)}, u32[]{:S(2)}) collective-permute-start(bf16[256,2048]{1,0:T(8,128)(2,1)} %fusion.18.refs_0_), channel_id=1, source_target_pairs={{0,2},{1,3},{2,0},{3,1},{4,6},{5,7},{6,4},{7,5},{8,10},{9,11},{10,... | collective-permute-start | bytes 3145736 | tf_op jit(solution)/shard_map/ppermute | solution.py:109
  16.6 26.5 %collective-permute-start.1 = (bf16[256,2048]{1,0:T(8,128)(2,1)}, bf16[256,2048]{1,0:T(8,128)(2,1)}, u32[]{:S(2)}, u32[]{:S(2)}) collective-permute-start(bf16[256,2048]{1,0:T(8,128)(2,1)} %fusion.18.refs_0_), channel_id=1, source_target_pairs={{0,1},{1,0},{2,3},{3,2},{4,5},{5,4},{6,7},{7,6},{8,9},{9,8},{10,11... | collective-permute-start | bytes 3145736 | tf_op jit(solution)/shard_map/ppermute | solution.py:109
  16.6 27.9 %collective-permute-start.2 = (bf16[256,2048]{1,0:T(8,128)(2,1)S(1)}, bf16[256,2048]{1,0:T(8,128)(2,1)}, u32[]{:S(2)}, u32[]{:S(2)}) collective-permute-start(bf16[256,2048]{1,0:T(8,128)(2,1)S(1)} %copy-done.10), channel_id=1, source_target_pairs={{0,24},{1,25},{2,26},{3,27},{4,28},{5,29},{6,30},{7,31},{8,0},{9,1... | collective-permute-start | bytes 3145736 | tf_op jit(solution)/shard_map/ppermute | solution.py:109
  19.9 25.9 %collective-permute-start.3 = (bf16[256,2048]{1,0:T(8,128)(2,1)S(1)}, bf16[256,2048]{1,0:T(8,128)(2,1)}, u32[]{:S(2)}, u32[]{:S(2)}) collective-permute-start(bf16[256,2048]{1,0:T(8,128)(2,1)S(1)} %copy-done.10), channel_id=1, source_target_pairs={{0,4},{1,5},{2,6},{3,7},{4,0},{5,1},{6,2},{7,3},{8,12},{9,13},{10,... | collective-permute-start | bytes 3145736 | tf_op jit(solution)/shard_map/ppermute | solution.py:109
  48.4 35.3 %collective-permute-start.4 = (bf16[256,2048]{1,0:T(8,128)(2,1)}, bf16[256,2048]{1,0:T(8,128)(2,1)}, u32[]{:S(2)}, u32[]{:S(2)}) collective-permute-start(bf16[256,2048]{1,0:T(8,128)(2,1)} %collective-permute-done.2.refs_1_), channel_id=1, source_target_pairs={{0,24},{1,25},{2,26},{3,27},{4,28},{5,29},{6,30},{7,31},{8,0},{9,1... | collective-permute-start | bytes 3145736 | tf_op jit(solution)/shard_map/ppermute | solution.py:109
  53.4 30.3 %collective-permute-start.5 = (bf16[256,2048]{1,0:T(8,128)(2,1)}, bf16[256,2048]{1,0:T(8,128)(2,1)}, u32[]{:S(2)}, u32[]{:S(2)}) collective-permute-start(bf16[256,2048]{1,0:T(8,128)(2,1)} %collective-permute-done.2.refs_1_), channel_id=1, source_target_pairs={{0,4},{1,5},{2,6},{3,7},{4,0},{5,1},{6,2},{7,3},{8,12},{9,13},{10,... | collective-permute-start | bytes 3145736 | tf_op jit(solution)/shard_map/ppermute | solution.py:109
  54.1 29.6 %collective-permute-start.6 = (bf16[256,2048]{1,0:T(8,128)(2,1)S(1)}, bf16[256,2048]{1,0:T(8,128)(2,1)}, u32[]{:S(2)}, u32[]{:S(2)}) collective-permute-start(bf16[256,2048]{1,0:T(8,128)(2,1)S(1)} %copy-done.10), channel_id=1, source_target_pairs={{0,2},{1,3},{2,0},{3,1},{4,6},{5,7},{6,4},{7,5},{8,10},{9,11},{10,... | collective-permute-start | bytes 3145736 | tf_op jit(solution)/shard_map/ppermute | solution.py:109
  55.2 28.5 %collective-permute-start.7 = (bf16[256,2048]{1,0:T(8,128)(2,1)S(1)}, bf16[256,2048]{1,0:T(8,128)(2,1)}, u32[]{:S(2)}, u32[]{:S(2)}) collective-permute-start(bf16[256,2048]{1,0:T(8,128)(2,1)S(1)} %copy-done.10), channel_id=1, source_target_pairs={{0,1},{1,0},{2,3},{3,2},{4,5},{5,4},{6,7},{7,6},{8,9},{9,8},{10,11... | collective-permute-start | bytes 3145736 | tf_op jit(solution)/shard_map/ppermute | solution.py:109
  55.2 28.5 %collective-permute-start.8 = (bf16[256,2048]{1,0:T(8,128)(2,1)}, bf16[256,2048]{1,0:T(8,128)(2,1)}, u32[]{:S(2)}, u32[]{:S(2)}) collective-permute-start(bf16[256,2048]{1,0:T(8,128)(2,1)} %collective-permute-done.2.refs_1_), channel_id=1, source_target_pairs={{0,1},{1,0},{2,3},{3,2},{4,5},{5,4},{6,7},{7,6},{8,9},{9,8},{10,11... | collective-permute-start | bytes 3145736 | tf_op jit(solution)/shard_map/ppermute | solution.py:109
  172.6 31.6 %collective-permute-start.26 = (bf16[256,2048]{1,0:T(8,128)(2,1)}, bf16[256,2048]{1,0:T(8,128)(2,1)}, u32[]{:S(2)}, u32[]{:S(2)}) collective-permute-start(bf16[256,2048]{1,0:T(8,128)(2,1)} %collective-permute-done.21.refs_1_), channel_id=1, source_target_pairs={{0,24},{1,25},{2,26},{3,27},{4,28},{5,29},{6,30},{7,31},{8,0},{9,1... | collective-permute-start | bytes 3145736 | tf_op jit(solution)/shard_map/ppermute | solution.py:109
  173.5 30.7 %collective-permute-start.27 = (bf16[256,2048]{1,0:T(8,128)(2,1)}, bf16[256,2048]{1,0:T(8,128)(2,1)}, u32[]{:S(2)}, u32[]{:S(2)}) collective-permute-start(bf16[256,2048]{1,0:T(8,128)(2,1)} %collective-permute-done.21.refs_1_), channel_id=1, source_target_pairs={{0,4},{1,5},{2,6},{3,7},{4,0},{5,1},{6,2},{7,3},{8,12},{9,13},{10,... | collective-permute-start | bytes 3145736 | tf_op jit(solution)/shard_map/ppermute | solution.py:109
  175.0 29.2 %collective-permute-start.28 = (bf16[256,2048]{1,0:T(8,128)(2,1)}, bf16[256,2048]{1,0:T(8,128)(2,1)}, u32[]{:S(2)}, u32[]{:S(2)}) collective-permute-start(bf16[256,2048]{1,0:T(8,128)(2,1)} %collective-permute-done.21.refs_1_), channel_id=1, source_target_pairs={{0,2},{1,3},{2,0},{3,1},{4,6},{5,7},{6,4},{7,5},{8,10},{9,11},{10,... | collective-permute-start | bytes 3145736 | tf_op jit(solution)/shard_map/ppermute | solution.py:109
  175.6 28.6 %collective-permute-start.32 = (bf16[256,2048]{1,0:T(8,128)(2,1)}, bf16[256,2048]{1,0:T(8,128)(2,1)}, u32[]{:S(2)}, u32[]{:S(2)}) collective-permute-start(bf16[256,2048]{1,0:T(8,128)(2,1)} %collective-permute-done.23.refs_3_), channel_id=1, source_target_pairs={{0,1},{1,0},{2,3},{3,2},{4,5},{5,4},{6,7},{7,6},{8,9},{9,8},{10,11... | collective-permute-start | bytes 3145736 | tf_op jit(solution)/shard_map/ppermute | solution.py:109
  176.6 27.6 %collective-permute-start.31 = (bf16[256,2048]{1,0:T(8,128)(2,1)}, bf16[256,2048]{1,0:T(8,128)(2,1)}, u32[]{:S(2)}, u32[]{:S(2)}) collective-permute-start(bf16[256,2048]{1,0:T(8,128)(2,1)} %collective-permute-done.21.refs_1_), channel_id=1, source_target_pairs={{0,1},{1,0},{2,3},{3,2},{4,5},{5,4},{6,7},{7,6},{8,9},{9,8},{10,11... | collective-permute-start | bytes 3145736 | tf_op jit(solution)/shard_map/ppermute | solution.py:109
  204.9 33.6 %collective-permute-start.33 = (bf16[256,2048]{1,0:T(8,128)(2,1)}, bf16[256,2048]{1,0:T(8,128)(2,1)}, u32[]{:S(2)}, u32[]{:S(2)}) collective-permute-start(bf16[256,2048]{1,0:T(8,128)(2,1)} %collective-permute-done.26.refs_0_), channel_id=1, source_target_pairs={{0,24},{1,25},{2,26},{3,27},{4,28},{5,29},{6,30},{7,31},{8,0},{9,1... | collective-permute-start | bytes 3145736 | tf_op jit(solution)/shard_map/ppermute | solution.py:109
  208.1 30.4 %collective-permute-start.34 = (bf16[256,2048]{1,0:T(8,128)(2,1)}, bf16[256,2048]{1,0:T(8,128)(2,1)}, u32[]{:S(2)}, u32[]{:S(2)}) collective-permute-start(bf16[256,2048]{1,0:T(8,128)(2,1)} %collective-permute-done.26.refs_0_), channel_id=1, source_target_pairs={{0,4},{1,5},{2,6},{3,7},{4,0},{5,1},{6,2},{7,3},{8,12},{9,13},{10,... | collective-permute-start | bytes 3145736 | tf_op jit(solution)/shard_map/ppermute | solution.py:109
  209.6 28.9 %collective-permute-start.35 = (bf16[256,2048]{1,0:T(8,128)(2,1)}, bf16[256,2048]{1,0:T(8,128)(2,1)}, u32[]{:S(2)}, u32[]{:S(2)}) collective-permute-start(bf16[256,2048]{1,0:T(8,128)(2,1)} %collective-permute-done.26.refs_0_), channel_id=1, source_target_pairs={{0,1},{1,0},{2,3},{3,2},{4,5},{5,4},{6,7},{7,6},{8,9},{9,8},{10,11... | collective-permute-start | bytes 3145736 | tf_op jit(solution)/shard_map/ppermute | solution.py:109
  209.6 28.9 %collective-permute-start.36 = (bf16[256,2048]{1,0:T(8,128)(2,1)}, bf16[256,2048]{1,0:T(8,128)(2,1)}, u32[]{:S(2)}, u32[]{:S(2)}) collective-permute-start(bf16[256,2048]{1,0:T(8,128)(2,1)} %collective-permute-done.4.refs_0_), channel_id=1, source_target_pairs={{0,2},{1,3},{2,0},{3,1},{4,6},{5,7},{6,4},{7,5},{8,10},{9,11},{10,... | collective-permute-start | bytes 3145736 | tf_op jit(solution)/shard_map/ppermute | solution.py:109
  210.7 27.8 %collective-permute-start.37 = (bf16[256,2048]{1,0:T(8,128)(2,1)}, bf16[256,2048]{1,0:T(8,128)(2,1)S(1)}, u32[]{:S(2)}, u32[]{:S(2)}) collective-permute-start(bf16[256,2048]{1,0:T(8,128)(2,1)} %collective-permute-done.10.refs_0_), channel_id=1, source_target_pairs={{0,1},{1,0},{2,3},{3,2},{4,5},{5,4},{6,7},{7,6},{8,9},{9,8},{10,11... | collective-permute-start | bytes 3145736 | tf_op jit(solution)/shard_map/ppermute | solution.py:109
  240.4 25.9 %collective-permute-start.42 = (bf16[256,2048]{1,0:T(8,128)(2,1)}, bf16[256,2048]{1,0:T(8,128)(2,1)}, u32[]{:S(2)}, u32[]{:S(2)}) collective-permute-start(bf16[256,2048]{1,0:T(8,128)(2,1)} %collective-permute-done.10.refs_0_), channel_id=1, source_target_pairs={{0,2},{1,3},{2,0},{3,1},{4,6},{5,7},{6,4},{7,5},{8,10},{9,11},{10,... | collective-permute-start | bytes 3145736 | tf_op jit(solution)/shard_map/ppermute | solution.py:109
  266.3 29.9 %collective-permute-start.44 = (bf16[256,2048]{1,0:T(8,128)(2,1)}, bf16[256,2048]{1,0:T(8,128)(2,1)}, u32[]{:S(2)}, u32[]{:S(2)}) collective-permute-start(bf16[256,2048]{1,0:T(8,128)(2,1)} %collective-permute-done.26.refs_0_), channel_id=1, source_target_pairs={{0,2},{1,3},{2,0},{3,1},{4,6},{5,7},{6,4},{7,5},{8,10},{9,11},{10,... | collective-permute-start | bytes 3145736 | tf_op jit(solution)/shard_map/ppermute | solution.py:109
  266.5 29.7 %collective-permute-start.45 = (bf16[256,2048]{1,0:T(8,128)(2,1)}, bf16[256,2048]{1,0:T(8,128)(2,1)}, u32[]{:S(2)}, u32[]{:S(2)}) collective-permute-start(bf16[256,2048]{1,0:T(8,128)(2,1)} %collective-permute-done.6.refs_3_), channel_id=1, source_target_pairs={{0,4},{1,5},{2,6},{3,7},{4,0},{5,1},{6,2},{7,3},{8,12},{9,13},{10,... | collective-permute-start | bytes 3145736 | tf_op jit(solution)/shard_map/ppermute | solution.py:109
  268.0 28.3 %collective-permute-start.46 = (bf16[256,2048]{1,0:T(8,128)(2,1)}, bf16[256,2048]{1,0:T(8,128)(2,1)S(1)}, u32[]{:S(2)}, u32[]{:S(2)}) collective-permute-start(bf16[256,2048]{1,0:T(8,128)(2,1)} %collective-permute-done.15.refs_1_), channel_id=1, source_target_pairs={{0,1},{1,0},{2,3},{3,2},{4,5},{5,4},{6,7},{7,6},{8,9},{9,8},{10,11... | collective-permute-start | bytes 3145736 | tf_op jit(solution)/shard_map/ppermute | solution.py:109
  268.0 28.3 %collective-permute-start.47 = (bf16[256,2048]{1,0:T(8,128)(2,1)}, bf16[256,2048]{1,0:T(8,128)(2,1)}, u32[]{:S(2)}, u32[]{:S(2)}) collective-permute-start(bf16[256,2048]{1,0:T(8,128)(2,1)} %collective-permute-done.36.refs_2_), channel_id=1, source_target_pairs={{0,1},{1,0},{2,3},{3,2},{4,5},{5,4},{6,7},{7,6},{8,9},{9,8},{10,11... | collective-permute-start | bytes 3145736 | tf_op jit(solution)/shard_map/ppermute | solution.py:109
  296.8 30.8 %collective-permute-start.48 = (bf16[256,2048]{1,0:T(8,128)(2,1)}, bf16[256,2048]{1,0:T(8,128)(2,1)}, u32[]{:S(2)}, u32[]{:S(2)}) collective-permute-start(bf16[256,2048]{1,0:T(8,128)(2,1)} %collective-permute-done.33.refs_0_), channel_id=1, source_target_pairs={{0,2},{1,3},{2,0},{3,1},{4,6},{5,7},{6,4},{7,5},{8,10},{9,11},{10,... | collective-permute-start | bytes 3145736 | tf_op jit(solution)/shard_map/ppermute | solution.py:109
  297.9 29.7 %collective-permute-start.49 = (bf16[256,2048]{1,0:T(8,128)(2,1)}, bf16[256,2048]{1,0:T(8,128)(2,1)}, u32[]{:S(2)}, u32[]{:S(2)}) collective-permute-start(bf16[256,2048]{1,0:T(8,128)(2,1)} %collective-permute-done.33.refs_0_), channel_id=1, source_target_pairs={{0,1},{1,0},{2,3},{3,2},{4,5},{5,4},{6,7},{7,6},{8,9},{9,8},{10,11... | collective-permute-start | bytes 3145736 | tf_op jit(solution)/shard_map/ppermute | solution.py:109
  297.9 29.7 %collective-permute-start.50 = (bf16[256,2048]{1,0:T(8,128)(2,1)}, bf16[256,2048]{1,0:T(8,128)(2,1)}, u32[]{:S(2)}, u32[]{:S(2)}) collective-permute-start(bf16[256,2048]{1,0:T(8,128)(2,1)} %collective-permute-done.38.refs_1_), channel_id=1, source_target_pairs={{0,1},{1,0},{2,3},{3,2},{4,5},{5,4},{6,7},{7,6},{8,9},{9,8},{10,11... | collective-permute-start | bytes 3145736 | tf_op jit(solution)/shard_map/ppermute | solution.py:109
  332.4 30.7 %collective-permute-start.54 = (bf16[256,2048]{1,0:T(8,128)(2,1)}, bf16[256,2048]{1,0:T(8,128)(2,1)S(1)}, u32[]{:S(2)}, u32[]{:S(2)}) collective-permute-start(bf16[256,2048]{1,0:T(8,128)(2,1)} %collective-permute-done.36.refs_2_), channel_id=1, source_target_pairs={{0,4},{1,5},{2,6},{3,7},{4,0},{5,1},{6,2},{7,3},{8,12},{9,13},{10,... | collective-permute-start | bytes 3145736 | tf_op jit(solution)/shard_map/ppermute | solution.py:109
  333.0 30.1 %collective-permute-start.55 = (bf16[256,2048]{1,0:T(8,128)(2,1)}, bf16[256,2048]{1,0:T(8,128)(2,1)}, u32[]{:S(2)}, u32[]{:S(2)}) collective-permute-start(bf16[256,2048]{1,0:T(8,128)(2,1)} %collective-permute-done.15.refs_1_), channel_id=1, source_target_pairs={{0,2},{1,3},{2,0},{3,1},{4,6},{5,7},{6,4},{7,5},{8,10},{9,11},{10,... | collective-permute-start | bytes 3145736 | tf_op jit(solution)/shard_map/ppermute | solution.py:109
  334.8 28.4 %collective-permute-start.56 = (bf16[256,2048]{1,0:T(8,128)(2,1)}, bf16[256,2048]{1,0:T(8,128)(2,1)}, u32[]{:S(2)}, u32[]{:S(2)}) collective-permute-start(bf16[256,2048]{1,0:T(8,128)(2,1)} %collective-permute-done.45.refs_4_), channel_id=1, source_target_pairs={{0,1},{1,0},{2,3},{3,2},{4,5},{5,4},{6,7},{7,6},{8,9},{9,8},{10,11... | collective-permute-start | bytes 3145736 | tf_op jit(solution)/shard_map/ppermute | solution.py:109
  334.8 28.4 %collective-permute-start.57 = (bf16[256,2048]{1,0:T(8,128)(2,1)}, bf16[256,2048]{1,0:T(8,128)(2,1)}, u32[]{:S(2)}, u32[]{:S(2)}) collective-permute-start(bf16[256,2048]{1,0:T(8,128)(2,1)} %collective-permute-done.51.refs_0_), channel_id=1, source_target_pairs={{0,1},{1,0},{2,3},{3,2},{4,5},{5,4},{6,7},{7,6},{8,9},{9,8},{10,11... | collective-permute-start | bytes 3145736 | tf_op jit(solution)/shard_map/ppermute | solution.py:109
  363.2 26.2 %collective-permute-start.62 = (bf16[4,256,2048]{2,1,0:T(8,128)(2,1)}, bf16[4,256,2048]{2,1,0:T(8,128)(2,1)}, u32[]{:S(2)}, u32[]{:S(2)}) collective-permute-start(bf16[4,256,2048]{2,1,0:T(8,128)(2,1)} %get-tuple-element.1069), channel_id=1, source_target_pairs={{0,1},{1,0},{2,3},{3,2},{4,5},{5,4},{6,7},{7,6},{8,9},{9,8},{10,11... | collective-permute-start | bytes 12582920 | tf_op jit(solution)/shard_map/ppermute | solution.py:109
  363.9 31.4 %collective-permute-start.60 = (bf16[256,2048]{1,0:T(8,128)(2,1)}, bf16[256,2048]{1,0:T(8,128)(2,1)}, u32[]{:S(2)}, u32[]{:S(2)}) collective-permute-start(bf16[256,2048]{1,0:T(8,128)(2,1)} %collective-permute-done.44.refs_2_), channel_id=1, source_target_pairs={{0,4},{1,5},{2,6},{3,7},{4,0},{5,1},{6,2},{7,3},{8,12},{9,13},{10,... | collective-permute-start | bytes 3145736 | tf_op jit(solution)/shard_map/ppermute | solution.py:109
  364.6 30.8 %collective-permute-start.61 = (bf16[256,2048]{1,0:T(8,128)(2,1)}, bf16[256,2048]{1,0:T(8,128)(2,1)}, u32[]{:S(2)}, u32[]{:S(2)}) collective-permute-start(bf16[256,2048]{1,0:T(8,128)(2,1)} %collective-permute-done.27.refs_1_), channel_id=1, source_target_pairs={{0,2},{1,3},{2,0},{3,1},{4,6},{5,7},{6,4},{7,5},{8,10},{9,11},{10,... | collective-permute-start | bytes 3145736 | tf_op jit(solution)/shard_map/ppermute | solution.py:109
  460.8 30.0 %collective-permute-start.76 = (bf16[2,256,2048]{2,1,0:T(8,128)(2,1)}, bf16[2,256,2048]{2,1,0:T(8,128)(2,1)}, u32[]{:S(2)}, u32[]{:S(2)}) collective-permute-start(bf16[2,256,2048]{2,1,0:T(8,128)(2,1)} %get-tuple-element.1151), channel_id=1, source_target_pairs={{0,1},{1,0},{2,3},{3,2},{4,5},{5,4},{6,7},{7,6},{8,9},{9,8},{10,11... | collective-permute-start | bytes 6291464 | tf_op jit(solution)/shard_map/ppermute | solution.py:109
  461.5 33.4 %collective-permute-start.74 = (bf16[256,2048]{1,0:T(8,128)(2,1)}, bf16[256,2048]{1,0:T(8,128)(2,1)S(1)}, u32[]{:S(2)}, u32[]{:S(2)}) collective-permute-start(bf16[256,2048]{1,0:T(8,128)(2,1)} %get-tuple-element.1148), channel_id=1, source_target_pairs={{0,4},{1,5},{2,6},{3,7},{4,0},{5,1},{6,2},{7,3},{8,12},{9,13},{10,... | collective-permute-start | bytes 3145736 | tf_op jit(solution)/shard_map/ppermute | solution.py:109
  462.3 32.6 %collective-permute-start.75 = (bf16[256,2048]{1,0:T(8,128)(2,1)}, bf16[256,2048]{1,0:T(8,128)(2,1)}, u32[]{:S(2)}, u32[]{:S(2)}) collective-permute-start(bf16[256,2048]{1,0:T(8,128)(2,1)} %shard_map.287), channel_id=1, source_target_pairs={{0,2},{1,3},{2,0},{3,1},{4,6},{5,7},{6,4},{7,5},{8,10},{9,11},{10,... | collective-permute-start | bytes 3145736 | tf_op jit(solution)/shard_map/ppermute | solution.py:109
  495.1 26.4 %collective-permute-start.77 = (bf16[256,2048]{1,0:T(8,128)(2,1)}, bf16[256,2048]{1,0:T(8,128)(2,1)}, u32[]{:S(2)}, u32[]{:S(2)}) collective-permute-start(bf16[256,2048]{1,0:T(8,128)(2,1)} %get-tuple-element.1170), channel_id=1, source_target_pairs={{0,4},{1,5},{2,6},{3,7},{4,0},{5,1},{6,2},{7,3},{8,12},{9,13},{10,... | collective-permute-start | bytes 3145736 | tf_op jit(solution)/shard_map/ppermute | solution.py:109
  521.8 25.8 %collective-permute-start.80 = (bf16[256,2048]{1,0:T(8,128)(2,1)}, bf16[256,2048]{1,0:T(8,128)(2,1)S(1)}, u32[]{:S(2)}, u32[]{:S(2)}) collective-permute-start(bf16[256,2048]{1,0:T(8,128)(2,1)} %get-tuple-element.1203), channel_id=1, source_target_pairs={{0,4},{1,5},{2,6},{3,7},{4,0},{5,1},{6,2},{7,3},{8,12},{9,13},{10,... | collective-permute-start | bytes 3145736 | tf_op jit(solution)/shard_map/ppermute | solution.py:109
  586.0 28.0 %collective-permute-start.88 = (bf16[256,2048]{1,0:T(8,128)(2,1)}, bf16[256,2048]{1,0:T(8,128)(2,1)}, u32[]{:S(2)}, u32[]{:S(2)}) collective-permute-start(bf16[256,2048]{1,0:T(8,128)(2,1)} %get-tuple-element.1269), channel_id=1, source_target_pairs={{0,4},{1,5},{2,6},{3,7},{4,0},{5,1},{6,2},{7,3},{8,12},{9,13},{10,... | collective-permute-start | bytes 3145736 | tf_op jit(solution)/shard_map/ppermute | solution.py:109
  587.1 26.8 %collective-permute-start.89 = (bf16[256,2048]{1,0:T(8,128)(2,1)}, bf16[256,2048]{1,0:T(8,128)(2,1)}, u32[]{:S(2)}, u32[]{:S(2)}) collective-permute-start(bf16[256,2048]{1,0:T(8,128)(2,1)} %get-tuple-element.1270), channel_id=1, source_target_pairs={{0,2},{1,3},{2,0},{3,1},{4,6},{5,7},{6,4},{7,5},{8,10},{9,11},{10,... | collective-permute-start | bytes 3145736 | tf_op jit(solution)/shard_map/ppermute | solution.py:109
  588.4 26.7 %collective-permute-start.90 = (bf16[256,2048]{1,0:T(8,128)(2,1)}, bf16[256,2048]{1,0:T(8,128)(2,1)}, u32[]{:S(2)}, u32[]{:S(2)}) collective-permute-start(bf16[256,2048]{1,0:T(8,128)(2,1)} %get-tuple-element.1271), channel_id=1, source_target_pairs={{0,24},{1,25},{2,26},{3,27},{4,28},{5,29},{6,30},{7,31},{8,0},{9,1... | collective-permute-start | bytes 3145736 | tf_op jit(solution)/shard_map/ppermute | solution.py:109
  623.0 25.9 %collective-permute-start.95 = (bf16[256,2048]{1,0:T(8,128)(2,1)}, bf16[256,2048]{1,0:T(8,128)(2,1)}, u32[]{:S(2)}, u32[]{:S(2)}) collective-permute-start(bf16[256,2048]{1,0:T(8,128)(2,1)} %get-tuple-element.1316), channel_id=1, source_target_pairs={{0,4},{1,5},{2,6},{3,7},{4,0},{5,1},{6,2},{7,3},{8,12},{9,13},{10,... | collective-permute-start | bytes 3145736 | tf_op jit(solution)/shard_map/ppermute | solution.py:109
  654.5 57.5 %collective-permute-start.96 = (bf16[256,2048]{1,0:T(8,128)(2,1)}, bf16[256,2048]{1,0:T(8,128)(2,1)}, u32[]{:S(2)}, u32[]{:S(2)}) collective-permute-start(bf16[256,2048]{1,0:T(8,128)(2,1)} %get-tuple-element.1359), channel_id=1, source_target_pairs={{0,4},{1,5},{2,6},{3,7},{4,0},{5,1},{6,2},{7,3},{8,12},{9,13},{10,... | collective-permute-start | bytes 3145736 | tf_op jit(solution)/shard_map/ppermute | solution.py:109
  655.2 56.8 %collective-permute-start.97 = (bf16[256,2048]{1,0:T(8,128)(2,1)}, bf16[256,2048]{1,0:T(8,128)(2,1)}, u32[]{:S(2)}, u32[]{:S(2)}) collective-permute-start(bf16[256,2048]{1,0:T(8,128)(2,1)} %get-tuple-element.1360), channel_id=1, source_target_pairs={{0,4},{1,5},{2,6},{3,7},{4,0},{5,1},{6,2},{7,3},{8,12},{9,13},{10,... | collective-permute-start | bytes 3145736 | tf_op jit(solution)/shard_map/ppermute | solution.py:109
  656.5 55.4 %collective-permute-start.98 = (bf16[256,2048]{1,0:T(8,128)(2,1)}, bf16[256,2048]{1,0:T(8,128)(2,1)}, u32[]{:S(2)}, u32[]{:S(2)}) collective-permute-start(bf16[256,2048]{1,0:T(8,128)(2,1)} %get-tuple-element.1361), channel_id=1, source_target_pairs={{0,2},{1,3},{2,0},{3,1},{4,6},{5,7},{6,4},{7,5},{8,10},{9,11},{10,... | collective-permute-start | bytes 3145736 | tf_op jit(solution)/shard_map/ppermute | solution.py:109
  657.4 54.6 %collective-permute-start.99 = (bf16[256,2048]{1,0:T(8,128)(2,1)}, bf16[256,2048]{1,0:T(8,128)(2,1)}, u32[]{:S(2)}, u32[]{:S(2)}) collective-permute-start(bf16[256,2048]{1,0:T(8,128)(2,1)} %shard_map.302), channel_id=1, source_target_pairs={{0,2},{1,3},{2,0},{3,1},{4,6},{5,7},{6,4},{7,5},{8,10},{9,11},{10,... | collective-permute-start | bytes 3145736 | tf_op jit(solution)/shard_map/ppermute | solution.py:109
  719.3 41.2 %collective-permute-start.102 = (bf16[256,2048]{1,0:T(8,128)(2,1)}, bf16[256,2048]{1,0:T(8,128)(2,1)}, u32[]{:S(2)}, u32[]{:S(2)}) collective-permute-start(bf16[256,2048]{1,0:T(8,128)(2,1)} %constant_dynamic-slice_fusion.3), channel_id=1, source_target_pairs={{0,4},{1,5},{2,6},{3,7},{4,0},{5,1},{6,2},{7,3},{8,12},{9,13},{10,... | collective-permute-start | bytes 3145736 | tf_op jit(solution)/shard_map/ppermute | solution.py:109
  720.1 46.1 %collective-permute-start.103 = (bf16[256,2048]{1,0:T(8,128)(2,1)}, bf16[256,2048]{1,0:T(8,128)(2,1)}, u32[]{:S(2)}, u32[]{:S(2)}) collective-permute-start(bf16[256,2048]{1,0:T(8,128)(2,1)} %get-tuple-element.1402), channel_id=1, source_target_pairs={{0,4},{1,5},{2,6},{3,7},{4,0},{5,1},{6,2},{7,3},{8,12},{9,13},{10,... | collective-permute-start | bytes 3145736 | tf_op jit(solution)/shard_map/ppermute | solution.py:109
  721.4 44.9 %collective-permute-start.104 = (bf16[256,2048]{1,0:T(8,128)(2,1)}, bf16[256,2048]{1,0:T(8,128)(2,1)}, u32[]{:S(2)}, u32[]{:S(2)}) collective-permute-start(bf16[256,2048]{1,0:T(8,128)(2,1)} %get-tuple-element.1403), channel_id=1, source_target_pairs={{0,2},{1,3},{2,0},{3,1},{4,6},{5,7},{6,4},{7,5},{8,10},{9,11},{10,... | collective-permute-start | bytes 3145736 | tf_op jit(solution)/shard_map/ppermute | solution.py:109
  722.6 43.7 %collective-permute-start.105 = (bf16[256,2048]{1,0:T(8,128)(2,1)}, bf16[256,2048]{1,0:T(8,128)(2,1)}, u32[]{:S(2)}, u32[]{:S(2)}) collective-permute-start(bf16[256,2048]{1,0:T(8,128)(2,1)} %get-tuple-element.1404), channel_id=1, source_target_pairs={{0,24},{1,25},{2,26},{3,27},{4,28},{5,29},{6,30},{7,31},{8,0},{9,1... | collective-permute-start | bytes 3145736 | tf_op jit(solution)/shard_map/ppermute | solution.py:109
  726.8 33.7 %collective-permute-start.101 = (bf16[80,2048]{1,0:T(8,128)(2,1)S(1)}, bf16[80,2048]{1,0:T(8,128)(2,1)S(1)}, u32[]{:S(2)}, u32[]{:S(2)}) collective-permute-start(bf16[80,2048]{1,0:T(8,128)(2,1)S(1)} %copy-done.37), channel_id=1, source_target_pairs={{0,16},{1,17},{2,18},{3,19},{4,20},{5,21},{6,22},{7,23},{8,24},{9,... | collective-permute-start | bytes 983048 | tf_op jit(solution)/shard_map/ppermute | solution.py:109
  776.5 32.6 %collective-permute-start.110 = (bf16[2,64,2048]{2,1,0:T(8,128)(2,1)}, bf16[2,64,2048]{2,1,0:T(8,128)(2,1)}, u32[]{:S(2)}, u32[]{:S(2)}) collective-permute-start(bf16[2,64,2048]{2,1,0:T(8,128)(2,1)} %dynamic-slice_bitcast_fusion.3), channel_id=1, source_target_pairs={{0,8},{1,9},{2,10},{3,11},{4,12},{5,13},{6,14},{7,15},{8,0},{9,1},... | collective-permute-start | bytes 1572872 | tf_op jit(solution)/shard_map/ppermute | solution.py:109
  784.6 39.2 %collective-permute-start.106 = (bf16[1024,512]{1,0:T(8,128)(2,1)}, bf16[1024,512]{1,0:T(8,128)(2,1)}, u32[]{:S(2)}, u32[]{:S(2)}) collective-permute-start(bf16[1024,512]{1,0:T(8,128)(2,1)} %constant_dynamic-slice_fusion.2), channel_id=1, source_target_pairs={{0,4},{1,5},{2,6},{3,7},{4,0},{5,1},{6,2},{7,3},{8,12},{9,13},{10,... | collective-permute-start | bytes 3145736 | tf_op jit(solution)/shard_map/ppermute | solution.py:109
  785.6 44.9 %collective-permute-start.107 = (bf16[256,2048]{1,0:T(8,128)(2,1)}, bf16[256,2048]{1,0:T(8,128)(2,1)S(1)}, u32[]{:S(2)}, u32[]{:S(2)}) collective-permute-start(bf16[256,2048]{1,0:T(8,128)(2,1)} %get-tuple-element.1458), channel_id=1, source_target_pairs={{0,4},{1,5},{2,6},{3,7},{4,0},{5,1},{6,2},{7,3},{8,12},{9,13},{10,... | collective-permute-start | bytes 3145736 | tf_op jit(solution)/shard_map/ppermute | solution.py:109
  786.7 43.8 %collective-permute-start.108 = (bf16[256,2048]{1,0:T(8,128)(2,1)}, bf16[256,2048]{1,0:T(8,128)(2,1)}, u32[]{:S(2)}, u32[]{:S(2)}) collective-permute-start(bf16[256,2048]{1,0:T(8,128)(2,1)} %get-tuple-element.1459), channel_id=1, source_target_pairs={{0,2},{1,3},{2,0},{3,1},{4,6},{5,7},{6,4},{7,5},{8,10},{9,11},{10,... | collective-permute-start | bytes 3145736 | tf_op jit(solution)/shard_map/ppermute | solution.py:109
  787.5 43.0 %collective-permute-start.109 = (bf16[256,2048]{1,0:T(8,128)(2,1)}, bf16[256,2048]{1,0:T(8,128)(2,1)}, u32[]{:S(2)}, u32[]{:S(2)}) collective-permute-start(bf16[256,2048]{1,0:T(8,128)(2,1)} %get-tuple-element.1460), channel_id=1, source_target_pairs={{0,24},{1,25},{2,26},{3,27},{4,28},{5,29},{6,30},{7,31},{8,0},{9,1... | collective-permute-start | bytes 3145736 | tf_op jit(solution)/shard_map/ppermute | solution.py:109
  834.8 31.0 %collective-permute-start.112 = (bf16[512,2048]{1,0:T(8,128)(2,1)S(1)}, bf16[512,2048]{1,0:T(8,128)(2,1)S(1)}, u32[]{:S(2)}, u32[]{:S(2)}) collective-permute-start(bf16[512,2048]{1,0:T(8,128)(2,1)S(1)} %pad_maximum_fusion.1), channel_id=1, source_target_pairs={{0,1},{1,0},{2,3},{3,2},{4,5},{5,4},{6,7},{7,6},{8,9},{9,8},{10,11... | collective-permute-start | bytes 6291464 | tf_op jit(solution)/shard_map/ppermute | solution.py:109
  836.6 29.1 %collective-permute-start.114 = (bf16[1024,512]{1,0:T(8,128)(2,1)S(1)}, bf16[1024,512]{1,0:T(8,128)(2,1)S(1)}, u32[]{:S(2)}, u32[]{:S(2)}) collective-permute-start(bf16[1024,512]{1,0:T(8,128)(2,1)S(1)} %constant_dynamic-slice_fusion.1), channel_id=1, source_target_pairs={{0,4},{1,5},{2,6},{3,7},{4,0},{5,1},{6,2},{7,3},{8,12},{9,13},{10,... | collective-permute-start | bytes 3145736 | tf_op jit(solution)/shard_map/ppermute | solution.py:109
  837.4 28.4 %collective-permute-start.115 = (bf16[256,2048]{1,0:T(8,128)(2,1)S(1)}, bf16[256,2048]{1,0:T(8,128)(2,1)S(1)}, u32[]{:S(2)}, u32[]{:S(2)}) collective-permute-start(bf16[256,2048]{1,0:T(8,128)(2,1)S(1)} %copy-done.82), channel_id=1, source_target_pairs={{0,2},{1,3},{2,0},{3,1},{4,6},{5,7},{6,4},{7,5},{8,10},{9,11},{10,... | collective-permute-start | bytes 3145736 | tf_op jit(solution)/shard_map/ppermute | solution.py:109
  899.6 31.9 %collective-permute-start.125 = (bf16[256,2048]{1,0:T(8,128)(2,1)S(1)}, bf16[256,2048]{1,0:T(8,128)(2,1)}, u32[]{:S(2)}, u32[]{:S(2)}) collective-permute-start(bf16[256,2048]{1,0:T(8,128)(2,1)S(1)} %bitcast.214), channel_id=1, source_target_pairs={{0,4},{1,5},{2,6},{3,7},{4,0},{5,1},{6,2},{7,3},{8,12},{9,13},{10,... | collective-permute-start | bytes 3145736 | tf_op jit(solution)/shard_map/ppermute | solution.py:109
  900.6 30.9 %collective-permute-start.126 = (bf16[256,2048]{1,0:T(8,128)(2,1)}, bf16[256,2048]{1,0:T(8,128)(2,1)}, u32[]{:S(2)}, u32[]{:S(2)}) collective-permute-start(bf16[256,2048]{1,0:T(8,128)(2,1)} %get-tuple-element.1496), channel_id=1, source_target_pairs={{0,2},{1,3},{2,0},{3,1},{4,6},{5,7},{6,4},{7,5},{8,10},{9,11},{10,... | collective-permute-start | bytes 3145736 | tf_op jit(solution)/shard_map/ppermute | solution.py:109
  970.1 28.8 %collective-permute-start.135 = (bf16[256,2048]{1,0:T(8,128)(2,1)S(1)}, bf16[256,2048]{1,0:T(8,128)(2,1)S(1)}, u32[]{:S(2)}, u32[]{:S(2)}) collective-permute-start(bf16[256,2048]{1,0:T(8,128)(2,1)S(1)} %copy-done.49), channel_id=1, source_target_pairs={{0,4},{1,5},{2,6},{3,7},{4,0},{5,1},{6,2},{7,3},{8,12},{9,13},{10,... | collective-permute-start | bytes 3145736 | tf_op jit(solution)/shard_map/ppermute | solution.py:109
  (174 other events, 2360.6 us)

commit v6 on v5

--- a/solution.py
+++ b/solution.py
@@ -274,56 +274,82 @@
     return lax.dot_general(left, right, (((1,), (1,)), ((), ())), preferred_element_type=F32)
 
 
-def pick_rows(picks_ref, blocks, rows_ref, slot_count, width):
+def pick_rows(picks_ref, blocks, buffer, arrived, rows_ref, slot_count, width):
     experts = rows_ref.shape[0]
-    for b, block in enumerate(blocks):
-        for low in range(0, block.shape[1], width):
+    copies = [pltpu.make_async_copy(block, buffer.at[b], arrived.at[b]) for b, block in enumerate(blocks)]
+    for copy in copies:
+        copy.start()
+    for b, copy in enumerate(copies):
+        copy.wait()
+        for low in range(0, buffer.shape[2], width):
             columns = pl.ds(low, width)
-            picked = nn(picks_ref[b], block[:, columns]).astype(BF16)
+            picked = nn(picks_ref[b], buffer[b, :, columns]).astype(BF16)
             for e in range(experts):
                 rows_ref[e, pl.ds(b * slot_count, slot_count), columns] = picked[
                     e * slot_count : (e + 1) * slot_count
                 ]
 
 
-def give_rows(picks_ref, rows_ref, blocks, slot_count, width, first=0):
+def give_rows(groups, rows_ref, buffer, left, slot_count, width):
     experts = rows_ref.shape[0]
-    for b, block in enumerate(blocks):
-        for low in range(0, block.shape[1], width):
-            columns = pl.ds(low, width)
-            slots = jnp.concatenate(
-                [rows_ref[e, pl.ds(first + b * slot_count, slot_count), columns] for e in range(experts)],
-                axis=0,
-            )
-            block[:, columns] = contract_rows(picks_ref[b], slots).astype(BF16)
+    copies, n = [], 0
+    for picks_ref, targets in groups:
+        for b, target in enumerate(targets):
+            for low in range(0, buffer.shape[2], width):
+                columns = pl.ds(low, width)
+                slots = jnp.concatenate(
+                    [rows_ref[e, pl.ds(n * slot_count, slot_count), columns] for e in range(experts)], axis=0
+                )
+                buffer[n, :, columns] = contract_rows(picks_ref[b], slots).astype(BF16)
+            copies.append(pltpu.make_async_copy(buffer.at[n], target, left.at[n]))
+            copies[-1].start()
+            n += 1
+    for copy in copies:
+        copy.wait()
+
+
+def halves_of(outs, first, count):
+    return [out.at[first + b] for out in outs for b in range(count // 2)]
 
 
 def cot_kernel(count, slot_count, picks_ref, down_ref, *refs):
-    blocks, (rows_out, acts_out, rows_ref) = refs[:count], refs[count:]
+    blocks, (rows_out, acts_out, rows_ref, buffer, arrived, left) = refs[:count], refs[count:]
     e = pl.program_id(0)
 
     @pl.when(e == 0)
     def _():
-        pick_rows(picks_ref, blocks, rows_ref, slot_count, 512)
-
-    rows = rows_ref[e]
-    rows_out[0] = rows
-    acts_out[0] = nt(rows, down_ref[0])
+        pick_rows(picks_ref, blocks, buffer, arrived, rows_ref, slot_count, 512)
+
+    out = pltpu.make_async_copy(rows_ref, rows_out, left.at[0])
+
+    @pl.when(e == 0)
+    def _():
+        out.start()
+
+    acts_out[0] = nt(rows_ref[e], down_ref[0])
+
+    @pl.when(e == pl.num_programs(0) - 1)
+    def _():
+        out.wait()
 
 
 def main_kernel(count, slot_count, picks_ref, gates_ref, acts_ref, gate_ref, up_ref, *refs):
     blocks = refs[:count]
     rows_out, scaled_out, d_gate_out, d_up_out, d_probs_out = refs[count : count + 5]
-    near_out, far_out, rows_ref = refs[count + 5 :]
-    results = [out.at[b] for out in (near_out, far_out) for b in range(count // 2)]
+    near_out, far_out, rows_ref, d_rows_ref, buffer, arrived, left, copied = refs[count + 5 :]
     e = pl.program_id(0)
 
     @pl.when(e == 0)
     def _():
-        pick_rows(picks_ref, blocks, rows_ref, slot_count, 512)
+        pick_rows(picks_ref, blocks, buffer, arrived, rows_ref, slot_count, 512)
+
+    out = pltpu.make_async_copy(rows_ref, rows_out, copied.at[0])
+
+    @pl.when(e == 0)
+    def _():
+        out.start()
 
     rows = rows_ref[e]
-    rows_out[0] = rows
     pre, up = nn(rows, gate_ref[0]), nn(rows, up_ref[0])
     cot_acts = acts_ref[0]
     own_slots = pl.ds(pl.multiple_of(e * slot_count, slot_count), slot_count)
@@ -348,33 +374,37 @@
     d_up = (d_acts * silu).astype(BF16)
     d_gate_out[0] = d_pre
     d_up_out[0] = d_up
-    rows_ref[e] = (nt(d_pre, gate_ref[0]) + nt(d_up, up_ref[0])).astype(BF16)
+    d_rows_ref[e] = (nt(d_pre, gate_ref[0]) + nt(d_up, up_ref[0])).astype(BF16)
 
     @pl.when(e == pl.num_programs(0) - 1)
     def _():
-        give_rows(picks_ref, rows_ref, results, slot_count, 512)
+        targets = halves_of((near_out, far_out), 0, count)
+        give_rows([(picks_ref, targets)], d_rows_ref, buffer, left, slot_count, 512)
+        out.wait()
 
 
 def out_kernel(parts, slot_count, *refs):
     picks, scaled, down_ref = refs[:parts], refs[parts : 2 * parts], refs[2 * parts]
-    near_out, far_out, rows_ref = refs[2 * parts + 1 :]
+    near_out, far_out, rows_ref, buffer, left = refs[2 * parts + 1 :]
     e = pl.program_id(0)
     rows = scaled[0][0] if parts == 1 else jnp.concatenate([part[0] for part in scaled], axis=0)
     rows_ref[e] = nn(rows, down_ref[0]).astype(BF16)
 
     @pl.when(e == pl.num_programs(0) - 1)
     def _():
-        low, done = 0, 0
+        groups, done = [], 0
         for part in picks:
-            count = part.shape[0]
-            half = count // 2
-            results = [out.at[done + b] for out in (near_out, far_out) for b in range(half)]
-            give_rows(part, rows_ref, results, slot_count, 512, low)
-            low, done = low + count * slot_count, done + half
+            groups.append((part, halves_of((near_out, far_out), done, part.shape[0])))
+            done += part.shape[0] // 2
+        give_rows(groups, rows_ref, buffer, left, slot_count, 512)
 
 
 def per_expert(*shape):
     return pl.BlockSpec((1,) + shape, lambda e: (e,) + (0,) * len(shape))
+
+
+def in_place(count):
+    return [pl.BlockSpec(memory_space=pl.ANY)] * count
 
 
 def resident(*shape):
@@ -388,13 +418,18 @@
     return pl.pallas_call(
         functools.partial(cot_kernel, count, slot_count),
         grid=(experts,),
-        in_specs=[resident(*picks.shape), per_expert(hidden, width)] + [resident(tokens, width)] * count,
-        out_specs=[per_expert(rows, width), per_expert(rows, hidden)],
+        in_specs=[resident(*picks.shape), per_expert(hidden, width)] + in_place(count),
+        out_specs=in_place(1) + [per_expert(rows, hidden)],
         out_shape=[
             jax.ShapeDtypeStruct((experts, rows, width), BF16),
             jax.ShapeDtypeStruct((experts, rows, hidden), F32),
         ],
-        scratch_shapes=[pltpu.VMEM((experts, rows, width), BF16)],
+        scratch_shapes=[
+            pltpu.VMEM((experts, rows, width), BF16),
+            pltpu.VMEM((count, tokens, width), BF16),
+            pltpu.SemaphoreType.DMA((count,)),
+            pltpu.SemaphoreType.DMA((1,)),
+        ],
         compiler_params=pltpu.CompilerParams(vmem_limit_bytes=VMEM_GRANT),
         cost_estimate=pl.CostEstimate(
             flops=2 * experts * rows * width * (hidden + tokens),
@@ -418,15 +453,15 @@
             per_expert(width, hidden),
             per_expert(width, hidden),
         ]
-        + [resident(tokens, width)] * count,
-        out_specs=[
-            per_expert(rows, width),
+        + in_place(count),
+        out_specs=in_place(1)
+        + [
             per_expert(rows, hidden),
             per_expert(rows, hidden),
             per_expert(rows, hidden),
             resident(*gates.shape),
         ]
-        + [resident(count // 2, tokens, width)] * 2,
+        + in_place(2),
         out_shape=[
             jax.ShapeDtypeStruct((experts, rows, width), BF16),
             jax.ShapeDtypeStruct((experts, rows, hidden), BF16),
@@ -435,7 +470,14 @@
             jax.ShapeDtypeStruct(gates.shape, F32),
         ]
         + [jax.ShapeDtypeStruct((count // 2, tokens, width), BF16)] * 2,
-        scratch_shapes=[pltpu.VMEM((experts, rows, width), BF16)],
+        scratch_shapes=[
+            pltpu.VMEM((experts, rows, width), BF16),
+            pltpu.VMEM((experts, rows, width), BF16),
+            pltpu.VMEM((count, tokens, width), BF16),
+            pltpu.SemaphoreType.DMA((count,)),
+            pltpu.SemaphoreType.DMA((count,)),
+            pltpu.SemaphoreType.DMA((1,)),
+        ],
         compiler_params=pltpu.CompilerParams(vmem_limit_bytes=VMEM_GRANT),
         cost_estimate=pl.CostEstimate(
             flops=2 * experts * rows * width * (4 * hidden + 2 * tokens),
@@ -457,9 +499,13 @@
         in_specs=[resident(*part.shape) for part in picks]
         + [per_expert(*part.shape[1:]) for part in scaled]
         + [per_expert(hidden, width)],
-        out_specs=[resident(count // 2, tokens, width)] * 2,
+        out_specs=in_place(2),
         out_shape=[jax.ShapeDtypeStruct((count // 2, tokens, width), BF16)] * 2,
-        scratch_shapes=[pltpu.VMEM((experts, rows, width), BF16)],
+        scratch_shapes=[
+            pltpu.VMEM((experts, rows, width), BF16),
+            pltpu.VMEM((count, tokens, width), BF16),
+            pltpu.SemaphoreType.DMA((count,)),
+        ],
         compiler_params=pltpu.CompilerParams(vmem_limit_bytes=VMEM_GRANT),
         cost_estimate=pl.CostEstimate(
             flops=2 * experts * rows * width * (hidden + tokens),

time: 1090 us -> 1090 us (level)
  Pallas kernels: 447 us -> 436 us
  transfers between devices with their start and end apart: 151 -> 151, of which waited for: 64 -> 66; matrix products, arithmetic and copies ran while one was open for 10% -> 10% of each run, Pallas kernels for 39% -> 38%
where the time goes in v6:
time: 1090 us; the launch traced here: 1070 us
  Pallas kernels  436 us (40%)
  waiting for transfers between devices  292 us (27%)
  starting transfers between devices  152 us (14%)
  other arithmetic  77.1 us (7%)
  matrix products  48.3 us (4%)
  local copies, waits for them, and re-layouts  43.3 us (4%)
  blocking collectives  20.6 us (2%)
    ppermute x148, waiting for transfers between devices, send(): return lax.ppermute(value, BOTH, device_pairs(MOVES[axis]))  278 us
    ppermute x148, starting transfers between devices, send(): return lax.ppermute(value, BOTH, device_pairs(MOVES[axis]))  139 us
    pallas_call x5, Pallas kernels, main_chunk(): pl.pallas_call(functools.partial(main_kernel, count, slot_count), grid=(e...  119 us
    pallas_call x4, Pallas kernels, cot_chunk(): pl.pallas_call(functools.partial(cot_kernel, count, slot_count), grid=(ex...  64.1 us
    pallas_call x3, Pallas kernels, expert_grads(): pl.pallas_call(functools.partial(grad_kernel, count), grid=(last - first,...  61 us
    pallas_call x9, Pallas kernels, pair_sum(): pl.pallas_call(pair_kernel, grid=(rows // tile,), in_specs=[stack, stack]...  49.8 us
    pallas_call x4, Pallas kernels, out_chunk(): pl.pallas_call(functools.partial(out_kernel, len(picks), slot_count), gri...  47.3 us
    pallas_call x9, Pallas kernels, block_sums(): pl.pallas_call(functools.partial(sums_kernel, counts), grid=(rows // tile...  37.8 us
  transfers between devices with their start and end apart: 151, of which 66 were waited for; matrix products, arithmetic and copies ran while one was open for 10% of the time, Pallas kernels for 38%

profile of v6, /device:TPU:0, one launch (start us, length us, event | category | flops | bytes accessed | tf_op | source)
XLA Modules:
  0.0 1072.8 jit_solution(8916483994345870349)
XLA Ops:
  7.4 7.4 all-to-all-start
  35.4 7.7 collective-permute-done.refs_2_
  48.4 5.0 collective-permute-start.4
  56.3 17.2 %shard_map.272 = (f32[1024,512]{1,0:T(8,128)}, f32[1024,512]{1,0:T(8,128)}, bf16[1024,512]{1,0:T(8,128)(2,1)}, f32[1024,128]{1,0:T(8,128)}, f32[1024,128]{1,0:T(8,128)}) custom-call(bf16[256,2048]{1,0:T(8,128)(2,1)} %fusion.18.refs_0_, bf16[256,2048]{1,0:T(8,128)(2,1)} %collective-permute-done.1.refs_1_, bf16[256,2048]{1,0:T(8,128)(2,1)} %collective-permute-done.refs_2_, ...), custom_call_target="tpu_custom_call" | custom-call | flops 6442450944 | bytes 15728640 | tf_op jit(solution)/shard_map/pallas_call | solution.py:626
  76.7 6.4 psum.14
  88.3 16.9 %shard_map.273 = (bf16[1024,512]{1,0:T(8,128)(2,1)}, f32[1024,512]{1,0:T(8,128)}, bf16[1024,512]{1,0:T(8,128)(2,1)}, bf16[1024,512]{1,0:T(8,128)(2,1)}) custom-call(f32[1024,512]{1,0:T(8,128)} %get-tuple-element.1407.q_ref, f32[1024,512]{1,0:T(8,128)} %get-tuple-element.1410.k_ref, bf16[1024,512]{1,0:T(8,128)(2,1)} %get-tuple-element.1365.v_ref, ...), custom_call_target="tpu_custom_call" | custom-call | flops 2147483648 | bytes 10485760 | tf_op jit(solution)/shard_map/pallas_call | solution.py:748
  123.4 17.9 %collective-permute-done.20 = bf16[256,2048]{1,0:T(8,128)(2,1)S(1)} collective-permute-done((bf16[256,2048]{1,0:T(8,128)(2,1)S(1)}, bf16[256,2048]{1,0:T(8,128)(2,1)S(1)}, u32[]{:S(2)}, u32[]{:S(2)}) %collective-permute-start.20) | collective-permute-done | bytes 1048608 | tf_op jit(solution)/shard_map/ppermute | solution.py:109
  153.7 16.0 %shard_map.274 = (bf16[8,256,2048]{2,1,0:T(8,128)(2,1)}, f32[8,256,256]{2,1,0:T(8,128)}) custom-call(bf16[8,256,256]{2,1,0:T(8,128)(2,1)} %bitcast.227, bf16[8,256,2048]{2,1,0:T(8,128)(2,1)} %refs_4_.1, bf16[256,2048]{1,0:T(8,128)(2,1)} %refs_0_, bf16[256,2048]{1,0:T(8,128)(2,1)} %collective-permute-done.2.refs_1_, ...), custom_call_target="tpu_custom_call" | custom-call | flops 4294967296 | bytes 25165824 | tf_op jit(solution)/shard_map/pallas_call | solution.py:418
  180.9 16.1 %shard_map.275 = (bf16[8,256,2048]{2,1,0:T(8,128)(2,1)}, f32[8,256,256]{2,1,0:T(8,128)}) custom-call(bf16[8,256,256]{2,1,0:T(8,128)(2,1)} %bitcast.224, bf16[8,256,2048]{2,1,0:T(8,128)(2,1)} %refs_4_.1, bf16[256,2048]{1,0:T(8,128)(2,1)} %collective-permute-done.4.refs_0_, bf16[256,2048]{1,0:T(8,128)(2,1)} %collective-permute-done.5.refs_1_, ...), custom_call_target="tpu_custom_call" | custom-call | flops 4294967296 | bytes 25165824 | tf_op jit(solution)/shard_map/pallas_call | solution.py:418
  197.0 6.6 all-to-all-done.1
  210.9 26.4 %shard_map.276 = (bf16[8,256,2048]{2,1,0:T(8,128)(2,1)}, bf16[8,256,256]{2,1,0:T(8,128)(2,1)}, bf16[8,256,256]{2,1,0:T(8,128)(2,1)}, bf16[8,256,256]{2,1,0:T(8,1...) custom-call(bf16[8,256,256]{2,1,0:T(8,128)(2,1)} %bitcast.228, ...), custom_call_target="tpu_custom_call" | custom-call | flops 12884901888 | bytes 41943040 | tf_op jit(solution)/shard_map/pallas_call | solution.py:446
  239.5 6.9 collective-permute-done.39.refs_5_
  246.7 5.9 shard_map.277
  252.6 11.0 %collective-permute-done.38.refs_1_ = bf16[256,2048]{1,0:T(8,128)(2,1)} collective-permute-done((bf16[256,2048]{1,0:T(8,128)(2,1)}, bf16[256,2048]{1,0:T(8,128)(2,1)}, u32[]{:S(2)}, u32[]{:S(2)}) %collective-permute-start.38) | collective-permute-done | bytes 1048608 | tf_op jit(solution)/shard_map/ppermute | solution.py:109
  267.3 26.5 %shard_map.278 = (bf16[8,256,2048]{2,1,0:T(8,128)(2,1)}, bf16[8,256,256]{2,1,0:T(8,128)(2,1)}, bf16[8,256,256]{2,1,0:T(8,128)(2,1)}, bf16[8,256,256]{2,1,0:T(8,1...) custom-call(bf16[8,256,256]{2,1,0:T(8,128)(2,1)} %bitcast.225, ...), custom_call_target="tpu_custom_call" | custom-call | flops 12884901888 | bytes 41943040 | tf_op jit(solution)/shard_map/pallas_call | solution.py:446
  296.0 6.9 collective-permute-done.53.refs_7_
  303.5 16.0 %shard_map.280 = (bf16[8,256,2048]{2,1,0:T(8,128)(2,1)}, f32[8,256,256]{2,1,0:T(8,128)}) custom-call(bf16[8,256,256]{2,1,0:T(8,128)(2,1)} %bitcast.221, bf16[8,256,2048]{2,1,0:T(8,128)(2,1)} %refs_4_.1, bf16[256,2048]{1,0:T(8,128)(2,1)} %collective-permute-done.10.refs_0_, bf16[256,2048]{1,0:T(8,128)(2,1)} %collective-permute-done.15.refs_1_, ...), custom_call_target="tpu_custom_call" | custom-call | flops 4294967296 | bytes 25165824 | tf_op jit(solution)/shard_map/pallas_call | solution.py:418
  319.6 6.0 shard_map.279
  332.9 26.5 %shard_map.281 = (bf16[8,256,2048]{2,1,0:T(8,128)(2,1)}, bf16[8,256,256]{2,1,0:T(8,128)(2,1)}, bf16[8,256,256]{2,1,0:T(8,128)(2,1)}, bf16[8,256,256]{2,1,0:T(8,1...) custom-call(bf16[8,256,256]{2,1,0:T(8,128)(2,1)} %bitcast.222, ...), custom_call_target="tpu_custom_call" | custom-call | flops 12884901888 | bytes 41943040 | tf_op jit(solution)/shard_map/pallas_call | solution.py:446
  370.1 16.0 %shard_map.283 = (bf16[8,256,2048]{2,1,0:T(8,128)(2,1)}, f32[8,256,256]{2,1,0:T(8,128)}) custom-call(bf16[8,256,256]{2,1,0:T(8,128)(2,1)} %pad_maximum_fusion.2.picks_ref, bf16[8,256,2048]{2,1,0:T(8,128)(2,1)} %refs_4_.1, bf16[256,2048]{1,0:T(8,128)(2,1)} %collective-permute-done.51.refs_0_, bf16[256,2048]{1,0:T(8,128)(2,1)} %copy-done.50, ...), custom_call_target="tpu_custom_call" | custom-call | flops 4294967296 | bytes 25165824 | tf_op jit(solution)/shard_map/pallas_call | solution.py:418
  386.1 5.9 shard_map.282
  396.6 20.0 %shard_map.284 = (bf16[8,128,2048]{2,1,0:T(8,128)(2,1)}, bf16[8,128,256]{2,1,0:T(8,128)(2,1)}, bf16[8,128,256]{2,1,0:T(8,128)(2,1)}, bf16[8,128,256]{2,1,0:T(8,1...) custom-call(bf16[4,256,256]{2,1,0:T(8,128)(2,1)} %bitcast.242, ...), custom_call_target="tpu_custom_call" | custom-call | flops 6442450944 | bytes 29360128 | tf_op jit(solution)/shard_map/pallas_call | solution.py:446
  429.7 19.6 %shard_map.286 = (bf16[8,128,2048]{2,1,0:T(8,128)(2,1)}, bf16[8,128,256]{2,1,0:T(8,128)(2,1)}, bf16[8,128,256]{2,1,0:T(8,128)(2,1)}, bf16[8,128,256]{2,1,0:T(8,1...) custom-call(bf16[4,256,256]{2,1,0:T(8,128)(2,1)} %bitcast.239, ...), custom_call_target="tpu_custom_call" | custom-call | flops 6442450944 | bytes 29360128 | tf_op jit(solution)/shard_map/pallas_call | solution.py:446
  467.9 11.8 %shard_map.289 = (bf16[4,256,2048]{2,1,0:T(8,128)(2,1)}, bf16[4,256,2048]{2,1,0:T(8,128)(2,1)}) custom-call(bf16[8,256,256]{2,1,0:T(8,128)(2,1)} %bitcast.229, bf16[8,256,256]{2,1,0:T(8,128)(2,1)} %get-tuple-element.1423.refs_1_.refs_10_, bf16[8,256,2048]{2,1,0:T(8,128)(2,1)} %refs_4_.1), custom_call_target="tpu_custom_call" | custom-call | flops 4294967296 | bytes 25165824 | tf_op jit(solution)/shard_map/pallas_call | solution.py:496
  479.8 7.7 all-to-all-done.2
  498.5 11.8 %shard_map.290 = (bf16[4,256,2048]{2,1,0:T(8,128)(2,1)}, bf16[4,256,2048]{2,1,0:T(8,128)(2,1)}) custom-call(bf16[8,256,256]{2,1,0:T(8,128)(2,1)} %bitcast.226, bf16[8,256,256]{2,1,0:T(8,128)(2,1)} %get-tuple-element.1424.refs_1_.refs_11_, bf16[8,256,2048]{2,1,0:T(8,128)(2,1)} %refs_4_.1), custom_call_target="tpu_custom_call" | custom-call | flops 4294967296 | bytes 25165824 | tf_op jit(solution)/shard_map/pallas_call | solution.py:496
  510.3 5.9 shard_map.291
  521.1 11.8 %shard_map.293 = (bf16[4,256,2048]{2,1,0:T(8,128)(2,1)}, bf16[4,256,2048]{2,1,0:T(8,128)(2,1)}) custom-call(bf16[8,256,256]{2,1,0:T(8,128)(2,1)} %bitcast.223, bf16[8,256,256]{2,1,0:T(8,128)(2,1)} %get-tuple-element.1425.refs_1_.refs_12_, bf16[8,256,2048]{2,1,0:T(8,128)(2,1)} %refs_4_.1), custom_call_target="tpu_custom_call" | custom-call | flops 4294967296 | bytes 25165824 | tf_op jit(solution)/shard_map/pallas_call | solution.py:496
  532.9 5.9 shard_map.294
  538.8 5.5 collective-permute-done.80.refs_3_
  546.2 4.7 shard_map.295
  554.8 11.9 %shard_map.296 = (bf16[4,256,2048]{2,1,0:T(8,128)(2,1)}, bf16[4,256,2048]{2,1,0:T(8,128)(2,1)}) custom-call(bf16[4,256,256]{2,1,0:T(8,128)(2,1)} %bitcast.243, bf16[4,256,256]{2,1,0:T(8,128)(2,1)} %bitcast.240, bf16[8,128,256]{2,1,0:T(8,128)(2,1)} %get-tuple-element.1426.refs_2_.refs_13_, bf16[8,128,256]{2,1,0:T(8,128)(2,1)} %get-tuple-element.1427.refs_3_.refs_14_, ...), custom_call_target="tpu_custom_call" | custom-call | flops 4294967296 | bytes 25165824 | tf_op jit(solution)/shard_map/pallas_call | solution.py:496
  566.8 5.9 shard_map.297
  577.9 4.7 shard_map.298
  589.3 15.4 %shard_map.300 = (f32[8,2048,256]{2,1,0:T(8,128)}, f32[8,2048,256]{2,1,0:T(8,128)}, f32[8,256,2048]{2,1,0:T(8,128)}) custom-call(bf16[8,256,2048]{2,1,0:T(8,128)(2,1)} %get-tuple-element.1413.refs_0_, bf16[8,256,2048]{2,1,0:T(8,128)(2,1)} %get-tuple-element.1414.refs_1_, bf16[8,256,2048]{2,1,0:T(8,128)(2,1)} %get-tuple-element.1415.refs_2_, ...), custom_call_target="tpu_custom_call" | custom-call | flops 6442450944 | bytes 29360128 | tf_op jit(solution)/shard_map/pallas_call | solution.py:546
  604.8 5.9 shard_map.299
  620.3 22.7 %shard_map.301 = (f32[8,2048,256]{2,1,0:T(8,128)}, f32[8,2048,256]{2,1,0:T(8,128)}, f32[8,256,2048]{2,1,0:T(8,128)}) custom-call(bf16[8,256,2048]{2,1,0:T(8,128)(2,1)} %get-tuple-element.1413.refs_0_, bf16[8,256,2048]{2,1,0:T(8,128)(2,1)} %get-tuple-element.1414.refs_1_, ...), custom_call_target="tpu_custom_call", output_to_operand_aliasing={{0}: (25, {}), {1}: (26, {}), {2}: (27, {})} | custom-call | flops 9663676416 | bytes 44040192 | tf_op jit(solution)/shard_map/pallas_call | solution.py:546
  662.9 22.8 %shard_map.303 = (f32[1024,512]{1,0:T(8,128)}, f32[1024,512]{1,0:T(8,128)}, bf16[1024,512]{1,0:T(8,128)(2,1)}, f32[1,512]{1,0:T(1,128)}, f32[1,512]{1,0:T(1,128)...) custom-call(f32[1024,512]{1,0:T(8,128)} %get-tuple-element.1407.q_ref, f32[1024,512]{1,0:T(8,128)} %get-tuple-element.1410.k_ref, ...), custom_call_target="tpu_custom_call" | custom-call | flops 5368709120 | bytes 16777216 | tf_op jit(solution)/shard_map/pallas_call | solution.py:775
  688.9 14.2 %psum.15 = f32[2,4,256]{2,0,1:T(2,128)S(1)} all-reduce(f32[2,4,256]{2,0,1:T(2,128)S(1)} %bitcast.256), channel_id=1, replica_groups=mesh['dp'=8,'tensor'=4] {'tensor'}, use_global_device_ids=true, to_apply=%region_14.15 | all-reduce | flops 2048 | bytes 16384 | tf_op jit(solution)/shard_map/psum | solution.py:848
  703.8 4.9 fusion.13
  723.6 22.9 %shard_map.305 = (f32[8,2048,256]{2,1,0:T(8,128)}, f32[8,2048,256]{2,1,0:T(8,128)}, f32[8,256,2048]{2,1,0:T(8,128)}) custom-call(bf16[8,256,2048]{2,1,0:T(8,128)(2,1)} %get-tuple-element.1413.refs_0_, bf16[8,256,2048]{2,1,0:T(8,128)(2,1)} %get-tuple-element.1414.refs_1_, ...), custom_call_target="tpu_custom_call", output_to_operand_aliasing={{0}: (25, {}), {1}: (26, {}), {2}: (27, {})} | custom-call | flops 9663676416 | bytes 44040192 | tf_op jit(solution)/shard_map/pallas_call | solution.py:546
  757.2 5.7 collective-permute-done.103.refs_3_
  766.6 4.7 shard_map.306
  784.2 4.5 collective-permute-start.109
  788.7 5.6 fusion.81
  794.3 6.5 add_convert_fusion
  800.8 4.9 convolution_convert_fusion.1
  808.2 12.3 %collective-permute-done.111 = bf16[64,2048]{1,0:T(8,128)(2,1)S(1)} collective-permute-done((bf16[64,2048]{1,0:T(8,128)(2,1)S(1)}, bf16[64,2048]{1,0:T(8,128)(2,1)S(1)}, u32[]{:S(2)}, u32[]{:S(2)}) %collective-permute-start.111) | collective-permute-done | bytes 262176 | tf_op jit(solution)/shard_map/ppermute | solution.py:109
  820.5 6.7 collective-permute-done.107.refs_1_
  834.8 11.3 %collective-permute-done.116 = bf16[2,256,512]{2,1,0:T(8,128)(2,1)S(1)} collective-permute-done((bf16[2,256,512]{2,1,0:T(8,128)(2,1)S(1)}, bf16[2,256,512]{2,1,0:T(8,128)(2,1)S(1)}, u32[]{:S(2)}, u32[]{:S(2)}) %collective-permute-start.116) | collective-permute-done | bytes 524320 | tf_op jit(solution)/shard_map/ppermute | solution.py:109
  846.2 4.5 collective-permute-start.117
  850.8 11.6 %collective-permute-done.117 = bf16[256,512]{1,0:T(8,128)(2,1)S(1)} collective-permute-done((bf16[256,512]{1,0:T(8,128)(2,1)S(1)}, bf16[256,512]{1,0:T(8,128)(2,1)S(1)}, u32[]{:S(2)}, u32[]{:S(2)}) %collective-permute-start.117) | collective-permute-done | bytes 262176 | tf_op jit(solution)/shard_map/ppermute | solution.py:109
  869.5 6.3 collective-permute-done.120
  875.7 9.8 collective-permute-done.121
  898.9 9.9 collective-permute-done.127
  914.8 8.9 collective-permute-done.128
  948.0 9.1 collective-permute-done.132
  957.2 6.3 collective-permute-done.130
  967.8 9.6 collective-permute-done.136
  987.7 7.9 collective-permute-done.133
  998.0 8.1 collective-permute-done.141
  1019.8 8.0 collective-permute-done.144
  1032.8 6.2 collective-permute-done.145
  1050.1 14.6 %collective-permute-done.146 = bf16[1024,512]{1,0:T(8,128)(2,1)S(1)} collective-permute-done((bf16[1024,512]{1,0:T(8,128)(2,1)S(1)}, bf16[1024,512]{1,0:T(8,128)(2,1)S(1)}, u32[]{:S(2)}, u32[]{:S(2)}) %collective-permute-start.146) | collective-permute-done | bytes 1048608 | tf_op jit(solution)/shard_map/ppermute | solution.py:109
  (625 shorter events, 379.0 us)
Async XLA Ops:
  7.4 26.5 %all-to-all-start = ((f32[32,8,256]{2,1,0:T(8,128)}), f32[32,8,256]{2,1,0:T(8,128)}, u32[]{:S(2)}, u32[]{:S(2)}) async-start(f32[32,8,256]{2,1,0:T(8,128)} %bitcast.4), calls=%async_computation | async-start | bytes 524288 | tf_op jit(solution)/shard_map/all_to_all | solution.py:856
  14.8 28.3 %collective-permute-start = (bf16[256,2048]{1,0:T(8,128)(2,1)}, bf16[256,2048]{1,0:T(8,128)(2,1)}, u32[]{:S(2)}, u32[]{:S(2)}) collective-permute-start(bf16[256,2048]{1,0:T(8,128)(2,1)} %fusion.18.refs_0_), channel_id=1, source_target_pairs={{0,2},{1,3},{2,0},{3,1},{4,6},{5,7},{6,4},{7,5},{8,10},{9,11},{10,... | collective-permute-start | bytes 3145736 | tf_op jit(solution)/shard_map/ppermute | solution.py:109
  16.6 26.5 %collective-permute-start.1 = (bf16[256,2048]{1,0:T(8,128)(2,1)}, bf16[256,2048]{1,0:T(8,128)(2,1)}, u32[]{:S(2)}, u32[]{:S(2)}) collective-permute-start(bf16[256,2048]{1,0:T(8,128)(2,1)} %fusion.18.refs_0_), channel_id=1, source_target_pairs={{0,1},{1,0},{2,3},{3,2},{4,5},{5,4},{6,7},{7,6},{8,9},{9,8},{10,11... | collective-permute-start | bytes 3145736 | tf_op jit(solution)/shard_map/ppermute | solution.py:109
  16.6 27.9 %collective-permute-start.2 = (bf16[256,2048]{1,0:T(8,128)(2,1)S(1)}, bf16[256,2048]{1,0:T(8,128)(2,1)}, u32[]{:S(2)}, u32[]{:S(2)}) collective-permute-start(bf16[256,2048]{1,0:T(8,128)(2,1)S(1)} %copy-done.10), channel_id=1, source_target_pairs={{0,24},{1,25},{2,26},{3,27},{4,28},{5,29},{6,30},{7,31},{8,0},{9,1... | collective-permute-start | bytes 3145736 | tf_op jit(solution)/shard_map/ppermute | solution.py:109
  19.9 25.9 %collective-permute-start.3 = (bf16[256,2048]{1,0:T(8,128)(2,1)S(1)}, bf16[256,2048]{1,0:T(8,128)(2,1)}, u32[]{:S(2)}, u32[]{:S(2)}) collective-permute-start(bf16[256,2048]{1,0:T(8,128)(2,1)S(1)} %copy-done.10), channel_id=1, source_target_pairs={{0,4},{1,5},{2,6},{3,7},{4,0},{5,1},{6,2},{7,3},{8,12},{9,13},{10,... | collective-permute-start | bytes 3145736 | tf_op jit(solution)/shard_map/ppermute | solution.py:109
  48.4 35.3 %collective-permute-start.4 = (bf16[256,2048]{1,0:T(8,128)(2,1)}, bf16[256,2048]{1,0:T(8,128)(2,1)}, u32[]{:S(2)}, u32[]{:S(2)}) collective-permute-start(bf16[256,2048]{1,0:T(8,128)(2,1)} %collective-permute-done.2.refs_1_), channel_id=1, source_target_pairs={{0,24},{1,25},{2,26},{3,27},{4,28},{5,29},{6,30},{7,31},{8,0},{9,1... | collective-permute-start | bytes 3145736 | tf_op jit(solution)/shard_map/ppermute | solution.py:109
  53.4 30.3 %collective-permute-start.5 = (bf16[256,2048]{1,0:T(8,128)(2,1)}, bf16[256,2048]{1,0:T(8,128)(2,1)}, u32[]{:S(2)}, u32[]{:S(2)}) collective-permute-start(bf16[256,2048]{1,0:T(8,128)(2,1)} %collective-permute-done.2.refs_1_), channel_id=1, source_target_pairs={{0,4},{1,5},{2,6},{3,7},{4,0},{5,1},{6,2},{7,3},{8,12},{9,13},{10,... | collective-permute-start | bytes 3145736 | tf_op jit(solution)/shard_map/ppermute | solution.py:109
  54.1 29.6 %collective-permute-start.6 = (bf16[256,2048]{1,0:T(8,128)(2,1)S(1)}, bf16[256,2048]{1,0:T(8,128)(2,1)}, u32[]{:S(2)}, u32[]{:S(2)}) collective-permute-start(bf16[256,2048]{1,0:T(8,128)(2,1)S(1)} %copy-done.10), channel_id=1, source_target_pairs={{0,2},{1,3},{2,0},{3,1},{4,6},{5,7},{6,4},{7,5},{8,10},{9,11},{10,... | collective-permute-start | bytes 3145736 | tf_op jit(solution)/shard_map/ppermute | solution.py:109
  55.2 28.5 %collective-permute-start.7 = (bf16[256,2048]{1,0:T(8,128)(2,1)S(1)}, bf16[256,2048]{1,0:T(8,128)(2,1)}, u32[]{:S(2)}, u32[]{:S(2)}) collective-permute-start(bf16[256,2048]{1,0:T(8,128)(2,1)S(1)} %copy-done.10), channel_id=1, source_target_pairs={{0,1},{1,0},{2,3},{3,2},{4,5},{5,4},{6,7},{7,6},{8,9},{9,8},{10,11... | collective-permute-start | bytes 3145736 | tf_op jit(solution)/shard_map/ppermute | solution.py:109
  55.2 28.5 %collective-permute-start.8 = (bf16[256,2048]{1,0:T(8,128)(2,1)}, bf16[256,2048]{1,0:T(8,128)(2,1)}, u32[]{:S(2)}, u32[]{:S(2)}) collective-permute-start(bf16[256,2048]{1,0:T(8,128)(2,1)} %collective-permute-done.2.refs_1_), channel_id=1, source_target_pairs={{0,1},{1,0},{2,3},{3,2},{4,5},{5,4},{6,7},{7,6},{8,9},{9,8},{10,11... | collective-permute-start | bytes 3145736 | tf_op jit(solution)/shard_map/ppermute | solution.py:109
  172.6 31.6 %collective-permute-start.26 = (bf16[256,2048]{1,0:T(8,128)(2,1)}, bf16[256,2048]{1,0:T(8,128)(2,1)}, u32[]{:S(2)}, u32[]{:S(2)}) collective-permute-start(bf16[256,2048]{1,0:T(8,128)(2,1)} %collective-permute-done.21.refs_1_), channel_id=1, source_target_pairs={{0,24},{1,25},{2,26},{3,27},{4,28},{5,29},{6,30},{7,31},{8,0},{9,1... | collective-permute-start | bytes 3145736 | tf_op jit(solution)/shard_map/ppermute | solution.py:109
  173.5 30.7 %collective-permute-start.27 = (bf16[256,2048]{1,0:T(8,128)(2,1)}, bf16[256,2048]{1,0:T(8,128)(2,1)}, u32[]{:S(2)}, u32[]{:S(2)}) collective-permute-start(bf16[256,2048]{1,0:T(8,128)(2,1)} %collective-permute-done.21.refs_1_), channel_id=1, source_target_pairs={{0,4},{1,5},{2,6},{3,7},{4,0},{5,1},{6,2},{7,3},{8,12},{9,13},{10,... | collective-permute-start | bytes 3145736 | tf_op jit(solution)/shard_map/ppermute | solution.py:109
  175.0 29.2 %collective-permute-start.28 = (bf16[256,2048]{1,0:T(8,128)(2,1)}, bf16[256,2048]{1,0:T(8,128)(2,1)}, u32[]{:S(2)}, u32[]{:S(2)}) collective-permute-start(bf16[256,2048]{1,0:T(8,128)(2,1)} %collective-permute-done.21.refs_1_), channel_id=1, source_target_pairs={{0,2},{1,3},{2,0},{3,1},{4,6},{5,7},{6,4},{7,5},{8,10},{9,11},{10,... | collective-permute-start | bytes 3145736 | tf_op jit(solution)/shard_map/ppermute | solution.py:109
  175.6 28.6 %collective-permute-start.32 = (bf16[256,2048]{1,0:T(8,128)(2,1)}, bf16[256,2048]{1,0:T(8,128)(2,1)}, u32[]{:S(2)}, u32[]{:S(2)}) collective-permute-start(bf16[256,2048]{1,0:T(8,128)(2,1)} %collective-permute-done.23.refs_3_), channel_id=1, source_target_pairs={{0,1},{1,0},{2,3},{3,2},{4,5},{5,4},{6,7},{7,6},{8,9},{9,8},{10,11... | collective-permute-start | bytes 3145736 | tf_op jit(solution)/shard_map/ppermute | solution.py:109
  176.6 27.6 %collective-permute-start.31 = (bf16[256,2048]{1,0:T(8,128)(2,1)}, bf16[256,2048]{1,0:T(8,128)(2,1)}, u32[]{:S(2)}, u32[]{:S(2)}) collective-permute-start(bf16[256,2048]{1,0:T(8,128)(2,1)} %collective-permute-done.21.refs_1_), channel_id=1, source_target_pairs={{0,1},{1,0},{2,3},{3,2},{4,5},{5,4},{6,7},{7,6},{8,9},{9,8},{10,11... | collective-permute-start | bytes 3145736 | tf_op jit(solution)/shard_map/ppermute | solution.py:109
  204.9 32.4 %collective-permute-start.33 = (bf16[256,2048]{1,0:T(8,128)(2,1)}, bf16[256,2048]{1,0:T(8,128)(2,1)}, u32[]{:S(2)}, u32[]{:S(2)}) collective-permute-start(bf16[256,2048]{1,0:T(8,128)(2,1)} %collective-permute-done.26.refs_0_), channel_id=1, source_target_pairs={{0,24},{1,25},{2,26},{3,27},{4,28},{5,29},{6,30},{7,31},{8,0},{9,1... | collective-permute-start | bytes 3145736 | tf_op jit(solution)/shard_map/ppermute | solution.py:109
  208.1 29.2 %collective-permute-start.34 = (bf16[256,2048]{1,0:T(8,128)(2,1)}, bf16[256,2048]{1,0:T(8,128)(2,1)}, u32[]{:S(2)}, u32[]{:S(2)}) collective-permute-start(bf16[256,2048]{1,0:T(8,128)(2,1)} %collective-permute-done.26.refs_0_), channel_id=1, source_target_pairs={{0,4},{1,5},{2,6},{3,7},{4,0},{5,1},{6,2},{7,3},{8,12},{9,13},{10,... | collective-permute-start | bytes 3145736 | tf_op jit(solution)/shard_map/ppermute | solution.py:109
  209.6 27.7 %collective-permute-start.35 = (bf16[256,2048]{1,0:T(8,128)(2,1)}, bf16[256,2048]{1,0:T(8,128)(2,1)}, u32[]{:S(2)}, u32[]{:S(2)}) collective-permute-start(bf16[256,2048]{1,0:T(8,128)(2,1)} %collective-permute-done.26.refs_0_), channel_id=1, source_target_pairs={{0,1},{1,0},{2,3},{3,2},{4,5},{5,4},{6,7},{7,6},{8,9},{9,8},{10,11... | collective-permute-start | bytes 3145736 | tf_op jit(solution)/shard_map/ppermute | solution.py:109
  209.6 27.7 %collective-permute-start.36 = (bf16[256,2048]{1,0:T(8,128)(2,1)}, bf16[256,2048]{1,0:T(8,128)(2,1)}, u32[]{:S(2)}, u32[]{:S(2)}) collective-permute-start(bf16[256,2048]{1,0:T(8,128)(2,1)} %collective-permute-done.4.refs_0_), channel_id=1, source_target_pairs={{0,2},{1,3},{2,0},{3,1},{4,6},{5,7},{6,4},{7,5},{8,10},{9,11},{10,... | collective-permute-start | bytes 3145736 | tf_op jit(solution)/shard_map/ppermute | solution.py:109
  210.7 26.6 %collective-permute-start.37 = (bf16[256,2048]{1,0:T(8,128)(2,1)}, bf16[256,2048]{1,0:T(8,128)(2,1)S(1)}, u32[]{:S(2)}, u32[]{:S(2)}) collective-permute-start(bf16[256,2048]{1,0:T(8,128)(2,1)} %collective-permute-done.10.refs_0_), channel_id=1, source_target_pairs={{0,1},{1,0},{2,3},{3,2},{4,5},{5,4},{6,7},{7,6},{8,9},{9,8},{10,11... | collective-permute-start | bytes 3145736 | tf_op jit(solution)/shard_map/ppermute | solution.py:109
  239.2 25.9 %collective-permute-start.42 = (bf16[256,2048]{1,0:T(8,128)(2,1)}, bf16[256,2048]{1,0:T(8,128)(2,1)}, u32[]{:S(2)}, u32[]{:S(2)}) collective-permute-start(bf16[256,2048]{1,0:T(8,128)(2,1)} %collective-permute-done.10.refs_0_), channel_id=1, source_target_pairs={{0,2},{1,3},{2,0},{3,1},{4,6},{5,7},{6,4},{7,5},{8,10},{9,11},{10,... | collective-permute-start | bytes 3145736 | tf_op jit(solution)/shard_map/ppermute | solution.py:109
  265.1 28.7 %collective-permute-start.44 = (bf16[256,2048]{1,0:T(8,128)(2,1)}, bf16[256,2048]{1,0:T(8,128)(2,1)}, u32[]{:S(2)}, u32[]{:S(2)}) collective-permute-start(bf16[256,2048]{1,0:T(8,128)(2,1)} %collective-permute-done.26.refs_0_), channel_id=1, source_target_pairs={{0,2},{1,3},{2,0},{3,1},{4,6},{5,7},{6,4},{7,5},{8,10},{9,11},{10,... | collective-permute-start | bytes 3145736 | tf_op jit(solution)/shard_map/ppermute | solution.py:109
  265.4 28.4 %collective-permute-start.45 = (bf16[256,2048]{1,0:T(8,128)(2,1)}, bf16[256,2048]{1,0:T(8,128)(2,1)}, u32[]{:S(2)}, u32[]{:S(2)}) collective-permute-start(bf16[256,2048]{1,0:T(8,128)(2,1)} %collective-permute-done.6.refs_3_), channel_id=1, source_target_pairs={{0,4},{1,5},{2,6},{3,7},{4,0},{5,1},{6,2},{7,3},{8,12},{9,13},{10,... | collective-permute-start | bytes 3145736 | tf_op jit(solution)/shard_map/ppermute | solution.py:109
  266.8 27.0 %collective-permute-start.46 = (bf16[256,2048]{1,0:T(8,128)(2,1)}, bf16[256,2048]{1,0:T(8,128)(2,1)S(1)}, u32[]{:S(2)}, u32[]{:S(2)}) collective-permute-start(bf16[256,2048]{1,0:T(8,128)(2,1)} %collective-permute-done.15.refs_1_), channel_id=1, source_target_pairs={{0,1},{1,0},{2,3},{3,2},{4,5},{5,4},{6,7},{7,6},{8,9},{9,8},{10,11... | collective-permute-start | bytes 3145736 | tf_op jit(solution)/shard_map/ppermute | solution.py:109
  266.8 27.1 %collective-permute-start.47 = (bf16[256,2048]{1,0:T(8,128)(2,1)}, bf16[256,2048]{1,0:T(8,128)(2,1)}, u32[]{:S(2)}, u32[]{:S(2)}) collective-permute-start(bf16[256,2048]{1,0:T(8,128)(2,1)} %collective-permute-done.36.refs_2_), channel_id=1, source_target_pairs={{0,1},{1,0},{2,3},{3,2},{4,5},{5,4},{6,7},{7,6},{8,9},{9,8},{10,11... | collective-permute-start | bytes 3145736 | tf_op jit(solution)/shard_map/ppermute | solution.py:109
  294.4 31.1 %collective-permute-start.48 = (bf16[256,2048]{1,0:T(8,128)(2,1)}, bf16[256,2048]{1,0:T(8,128)(2,1)}, u32[]{:S(2)}, u32[]{:S(2)}) collective-permute-start(bf16[256,2048]{1,0:T(8,128)(2,1)} %collective-permute-done.33.refs_0_), channel_id=1, source_target_pairs={{0,2},{1,3},{2,0},{3,1},{4,6},{5,7},{6,4},{7,5},{8,10},{9,11},{10,... | collective-permute-start | bytes 3145736 | tf_op jit(solution)/shard_map/ppermute | solution.py:109
  295.5 30.1 %collective-permute-start.49 = (bf16[256,2048]{1,0:T(8,128)(2,1)}, bf16[256,2048]{1,0:T(8,128)(2,1)}, u32[]{:S(2)}, u32[]{:S(2)}) collective-permute-start(bf16[256,2048]{1,0:T(8,128)(2,1)} %collective-permute-done.33.refs_0_), channel_id=1, source_target_pairs={{0,1},{1,0},{2,3},{3,2},{4,5},{5,4},{6,7},{7,6},{8,9},{9,8},{10,11... | collective-permute-start | bytes 3145736 | tf_op jit(solution)/shard_map/ppermute | solution.py:109
  295.5 30.1 %collective-permute-start.50 = (bf16[256,2048]{1,0:T(8,128)(2,1)}, bf16[256,2048]{1,0:T(8,128)(2,1)}, u32[]{:S(2)}, u32[]{:S(2)}) collective-permute-start(bf16[256,2048]{1,0:T(8,128)(2,1)} %collective-permute-done.38.refs_1_), channel_id=1, source_target_pairs={{0,1},{1,0},{2,3},{3,2},{4,5},{5,4},{6,7},{7,6},{8,9},{9,8},{10,11... | collective-permute-start | bytes 3145736 | tf_op jit(solution)/shard_map/ppermute | solution.py:109
  330.0 29.5 %collective-permute-start.54 = (bf16[256,2048]{1,0:T(8,128)(2,1)}, bf16[256,2048]{1,0:T(8,128)(2,1)S(1)}, u32[]{:S(2)}, u32[]{:S(2)}) collective-permute-start(bf16[256,2048]{1,0:T(8,128)(2,1)} %collective-permute-done.36.refs_2_), channel_id=1, source_target_pairs={{0,4},{1,5},{2,6},{3,7},{4,0},{5,1},{6,2},{7,3},{8,12},{9,13},{10,... | collective-permute-start | bytes 3145736 | tf_op jit(solution)/shard_map/ppermute | solution.py:109
  330.6 28.9 %collective-permute-start.55 = (bf16[256,2048]{1,0:T(8,128)(2,1)}, bf16[256,2048]{1,0:T(8,128)(2,1)}, u32[]{:S(2)}, u32[]{:S(2)}) collective-permute-start(bf16[256,2048]{1,0:T(8,128)(2,1)} %collective-permute-done.15.refs_1_), channel_id=1, source_target_pairs={{0,2},{1,3},{2,0},{3,1},{4,6},{5,7},{6,4},{7,5},{8,10},{9,11},{10,... | collective-permute-start | bytes 3145736 | tf_op jit(solution)/shard_map/ppermute | solution.py:109
  332.4 27.1 %collective-permute-start.56 = (bf16[256,2048]{1,0:T(8,128)(2,1)}, bf16[256,2048]{1,0:T(8,128)(2,1)}, u32[]{:S(2)}, u32[]{:S(2)}) collective-permute-start(bf16[256,2048]{1,0:T(8,128)(2,1)} %collective-permute-done.45.refs_4_), channel_id=1, source_target_pairs={{0,1},{1,0},{2,3},{3,2},{4,5},{5,4},{6,7},{7,6},{8,9},{9,8},{10,11... | collective-permute-start | bytes 3145736 | tf_op jit(solution)/shard_map/ppermute | solution.py:109
  332.4 27.1 %collective-permute-start.57 = (bf16[256,2048]{1,0:T(8,128)(2,1)}, bf16[256,2048]{1,0:T(8,128)(2,1)}, u32[]{:S(2)}, u32[]{:S(2)}) collective-permute-start(bf16[256,2048]{1,0:T(8,128)(2,1)} %collective-permute-done.51.refs_0_), channel_id=1, source_target_pairs={{0,1},{1,0},{2,3},{3,2},{4,5},{5,4},{6,7},{7,6},{8,9},{9,8},{10,11... | collective-permute-start | bytes 3145736 | tf_op jit(solution)/shard_map/ppermute | solution.py:109
  359.5 26.6 %collective-permute-start.62 = (bf16[4,256,2048]{2,1,0:T(8,128)(2,1)}, bf16[4,256,2048]{2,1,0:T(8,128)(2,1)}, u32[]{:S(2)}, u32[]{:S(2)}) collective-permute-start(bf16[4,256,2048]{2,1,0:T(8,128)(2,1)} %get-tuple-element.1069), channel_id=1, source_target_pairs={{0,1},{1,0},{2,3},{3,2},{4,5},{5,4},{6,7},{7,6},{8,9},{9,8},{10,11... | collective-permute-start | bytes 12582920 | tf_op jit(solution)/shard_map/ppermute | solution.py:109
  360.2 31.8 %collective-permute-start.60 = (bf16[256,2048]{1,0:T(8,128)(2,1)}, bf16[256,2048]{1,0:T(8,128)(2,1)}, u32[]{:S(2)}, u32[]{:S(2)}) collective-permute-start(bf16[256,2048]{1,0:T(8,128)(2,1)} %collective-permute-done.44.refs_2_), channel_id=1, source_target_pairs={{0,4},{1,5},{2,6},{3,7},{4,0},{5,1},{6,2},{7,3},{8,12},{9,13},{10,... | collective-permute-start | bytes 3145736 | tf_op jit(solution)/shard_map/ppermute | solution.py:109
  360.9 31.1 %collective-permute-start.61 = (bf16[256,2048]{1,0:T(8,128)(2,1)}, bf16[256,2048]{1,0:T(8,128)(2,1)}, u32[]{:S(2)}, u32[]{:S(2)}) collective-permute-start(bf16[256,2048]{1,0:T(8,128)(2,1)} %collective-permute-done.27.refs_1_), channel_id=1, source_target_pairs={{0,2},{1,3},{2,0},{3,1},{4,6},{5,7},{6,4},{7,5},{8,10},{9,11},{10,... | collective-permute-start | bytes 3145736 | tf_op jit(solution)/shard_map/ppermute | solution.py:109
  457.5 30.0 %collective-permute-start.76 = (bf16[2,256,2048]{2,1,0:T(8,128)(2,1)}, bf16[2,256,2048]{2,1,0:T(8,128)(2,1)}, u32[]{:S(2)}, u32[]{:S(2)}) collective-permute-start(bf16[2,256,2048]{2,1,0:T(8,128)(2,1)} %get-tuple-element.1151), channel_id=1, source_target_pairs={{0,1},{1,0},{2,3},{3,2},{4,5},{5,4},{6,7},{7,6},{8,9},{9,8},{10,11... | collective-permute-start | bytes 6291464 | tf_op jit(solution)/shard_map/ppermute | solution.py:109
  458.3 33.4 %collective-permute-start.74 = (bf16[256,2048]{1,0:T(8,128)(2,1)}, bf16[256,2048]{1,0:T(8,128)(2,1)S(1)}, u32[]{:S(2)}, u32[]{:S(2)}) collective-permute-start(bf16[256,2048]{1,0:T(8,128)(2,1)} %get-tuple-element.1148), channel_id=1, source_target_pairs={{0,4},{1,5},{2,6},{3,7},{4,0},{5,1},{6,2},{7,3},{8,12},{9,13},{10,... | collective-permute-start | bytes 3145736 | tf_op jit(solution)/shard_map/ppermute | solution.py:109
  459.0 32.6 %collective-permute-start.75 = (bf16[256,2048]{1,0:T(8,128)(2,1)}, bf16[256,2048]{1,0:T(8,128)(2,1)}, u32[]{:S(2)}, u32[]{:S(2)}) collective-permute-start(bf16[256,2048]{1,0:T(8,128)(2,1)} %shard_map.287), channel_id=1, source_target_pairs={{0,2},{1,3},{2,0},{3,1},{4,6},{5,7},{6,4},{7,5},{8,10},{9,11},{10,... | collective-permute-start | bytes 3145736 | tf_op jit(solution)/shard_map/ppermute | solution.py:109
  491.8 25.9 %collective-permute-start.77 = (bf16[256,2048]{1,0:T(8,128)(2,1)}, bf16[256,2048]{1,0:T(8,128)(2,1)}, u32[]{:S(2)}, u32[]{:S(2)}) collective-permute-start(bf16[256,2048]{1,0:T(8,128)(2,1)} %get-tuple-element.1170), channel_id=1, source_target_pairs={{0,4},{1,5},{2,6},{3,7},{4,0},{5,1},{6,2},{7,3},{8,12},{9,13},{10,... | collective-permute-start | bytes 3145736 | tf_op jit(solution)/shard_map/ppermute | solution.py:109
  518.5 25.8 %collective-permute-start.80 = (bf16[256,2048]{1,0:T(8,128)(2,1)}, bf16[256,2048]{1,0:T(8,128)(2,1)S(1)}, u32[]{:S(2)}, u32[]{:S(2)}) collective-permute-start(bf16[256,2048]{1,0:T(8,128)(2,1)} %get-tuple-element.1203), channel_id=1, source_target_pairs={{0,4},{1,5},{2,6},{3,7},{4,0},{5,1},{6,2},{7,3},{8,12},{9,13},{10,... | collective-permute-start | bytes 3145736 | tf_op jit(solution)/shard_map/ppermute | solution.py:109
  582.7 28.0 %collective-permute-start.88 = (bf16[256,2048]{1,0:T(8,128)(2,1)}, bf16[256,2048]{1,0:T(8,128)(2,1)}, u32[]{:S(2)}, u32[]{:S(2)}) collective-permute-start(bf16[256,2048]{1,0:T(8,128)(2,1)} %get-tuple-element.1269), channel_id=1, source_target_pairs={{0,4},{1,5},{2,6},{3,7},{4,0},{5,1},{6,2},{7,3},{8,12},{9,13},{10,... | collective-permute-start | bytes 3145736 | tf_op jit(solution)/shard_map/ppermute | solution.py:109
  583.9 26.8 %collective-permute-start.89 = (bf16[256,2048]{1,0:T(8,128)(2,1)}, bf16[256,2048]{1,0:T(8,128)(2,1)}, u32[]{:S(2)}, u32[]{:S(2)}) collective-permute-start(bf16[256,2048]{1,0:T(8,128)(2,1)} %get-tuple-element.1270), channel_id=1, source_target_pairs={{0,2},{1,3},{2,0},{3,1},{4,6},{5,7},{6,4},{7,5},{8,10},{9,11},{10,... | collective-permute-start | bytes 3145736 | tf_op jit(solution)/shard_map/ppermute | solution.py:109
  585.1 26.7 %collective-permute-start.90 = (bf16[256,2048]{1,0:T(8,128)(2,1)}, bf16[256,2048]{1,0:T(8,128)(2,1)}, u32[]{:S(2)}, u32[]{:S(2)}) collective-permute-start(bf16[256,2048]{1,0:T(8,128)(2,1)} %get-tuple-element.1271), channel_id=1, source_target_pairs={{0,24},{1,25},{2,26},{3,27},{4,28},{5,29},{6,30},{7,31},{8,0},{9,1... | collective-permute-start | bytes 3145736 | tf_op jit(solution)/shard_map/ppermute | solution.py:109
  619.7 25.9 %collective-permute-start.95 = (bf16[256,2048]{1,0:T(8,128)(2,1)}, bf16[256,2048]{1,0:T(8,128)(2,1)}, u32[]{:S(2)}, u32[]{:S(2)}) collective-permute-start(bf16[256,2048]{1,0:T(8,128)(2,1)} %get-tuple-element.1316), channel_id=1, source_target_pairs={{0,4},{1,5},{2,6},{3,7},{4,0},{5,1},{6,2},{7,3},{8,12},{9,13},{10,... | collective-permute-start | bytes 3145736 | tf_op jit(solution)/shard_map/ppermute | solution.py:109
  651.2 57.5 %collective-permute-start.96 = (bf16[256,2048]{1,0:T(8,128)(2,1)}, bf16[256,2048]{1,0:T(8,128)(2,1)}, u32[]{:S(2)}, u32[]{:S(2)}) collective-permute-start(bf16[256,2048]{1,0:T(8,128)(2,1)} %get-tuple-element.1359), channel_id=1, source_target_pairs={{0,4},{1,5},{2,6},{3,7},{4,0},{5,1},{6,2},{7,3},{8,12},{9,13},{10,... | collective-permute-start | bytes 3145736 | tf_op jit(solution)/shard_map/ppermute | solution.py:109
  651.9 56.8 %collective-permute-start.97 = (bf16[256,2048]{1,0:T(8,128)(2,1)}, bf16[256,2048]{1,0:T(8,128)(2,1)}, u32[]{:S(2)}, u32[]{:S(2)}) collective-permute-start(bf16[256,2048]{1,0:T(8,128)(2,1)} %get-tuple-element.1360), channel_id=1, source_target_pairs={{0,4},{1,5},{2,6},{3,7},{4,0},{5,1},{6,2},{7,3},{8,12},{9,13},{10,... | collective-permute-start | bytes 3145736 | tf_op jit(solution)/shard_map/ppermute | solution.py:109
  653.3 55.4 %collective-permute-start.98 = (bf16[256,2048]{1,0:T(8,128)(2,1)}, bf16[256,2048]{1,0:T(8,128)(2,1)}, u32[]{:S(2)}, u32[]{:S(2)}) collective-permute-start(bf16[256,2048]{1,0:T(8,128)(2,1)} %get-tuple-element.1361), channel_id=1, source_target_pairs={{0,2},{1,3},{2,0},{3,1},{4,6},{5,7},{6,4},{7,5},{8,10},{9,11},{10,... | collective-permute-start | bytes 3145736 | tf_op jit(solution)/shard_map/ppermute | solution.py:109
  654.1 54.6 %collective-permute-start.99 = (bf16[256,2048]{1,0:T(8,128)(2,1)}, bf16[256,2048]{1,0:T(8,128)(2,1)}, u32[]{:S(2)}, u32[]{:S(2)}) collective-permute-start(bf16[256,2048]{1,0:T(8,128)(2,1)} %shard_map.302), channel_id=1, source_target_pairs={{0,2},{1,3},{2,0},{3,1},{4,6},{5,7},{6,4},{7,5},{8,10},{9,11},{10,... | collective-permute-start | bytes 3145736 | tf_op jit(solution)/shard_map/ppermute | solution.py:109
  716.0 41.2 %collective-permute-start.102 = (bf16[256,2048]{1,0:T(8,128)(2,1)}, bf16[256,2048]{1,0:T(8,128)(2,1)}, u32[]{:S(2)}, u32[]{:S(2)}) collective-permute-start(bf16[256,2048]{1,0:T(8,128)(2,1)} %constant_dynamic-slice_fusion.3), channel_id=1, source_target_pairs={{0,4},{1,5},{2,6},{3,7},{4,0},{5,1},{6,2},{7,3},{8,12},{9,13},{10,... | collective-permute-start | bytes 3145736 | tf_op jit(solution)/shard_map/ppermute | solution.py:109
  716.9 46.1 %collective-permute-start.103 = (bf16[256,2048]{1,0:T(8,128)(2,1)}, bf16[256,2048]{1,0:T(8,128)(2,1)}, u32[]{:S(2)}, u32[]{:S(2)}) collective-permute-start(bf16[256,2048]{1,0:T(8,128)(2,1)} %get-tuple-element.1402), channel_id=1, source_target_pairs={{0,4},{1,5},{2,6},{3,7},{4,0},{5,1},{6,2},{7,3},{8,12},{9,13},{10,... | collective-permute-start | bytes 3145736 | tf_op jit(solution)/shard_map/ppermute | solution.py:109
  718.1 44.9 %collective-permute-start.104 = (bf16[256,2048]{1,0:T(8,128)(2,1)}, bf16[256,2048]{1,0:T(8,128)(2,1)}, u32[]{:S(2)}, u32[]{:S(2)}) collective-permute-start(bf16[256,2048]{1,0:T(8,128)(2,1)} %get-tuple-element.1403), channel_id=1, source_target_pairs={{0,2},{1,3},{2,0},{3,1},{4,6},{5,7},{6,4},{7,5},{8,10},{9,11},{10,... | collective-permute-start | bytes 3145736 | tf_op jit(solution)/shard_map/ppermute | solution.py:109
  719.3 43.7 %collective-permute-start.105 = (bf16[256,2048]{1,0:T(8,128)(2,1)}, bf16[256,2048]{1,0:T(8,128)(2,1)}, u32[]{:S(2)}, u32[]{:S(2)}) collective-permute-start(bf16[256,2048]{1,0:T(8,128)(2,1)} %get-tuple-element.1404), channel_id=1, source_target_pairs={{0,24},{1,25},{2,26},{3,27},{4,28},{5,29},{6,30},{7,31},{8,0},{9,1... | collective-permute-start | bytes 3145736 | tf_op jit(solution)/shard_map/ppermute | solution.py:109
  723.6 33.7 %collective-permute-start.101 = (bf16[80,2048]{1,0:T(8,128)(2,1)S(1)}, bf16[80,2048]{1,0:T(8,128)(2,1)S(1)}, u32[]{:S(2)}, u32[]{:S(2)}) collective-permute-start(bf16[80,2048]{1,0:T(8,128)(2,1)S(1)} %copy-done.37), channel_id=1, source_target_pairs={{0,16},{1,17},{2,18},{3,19},{4,20},{5,21},{6,22},{7,23},{8,24},{9,... | collective-permute-start | bytes 983048 | tf_op jit(solution)/shard_map/ppermute | solution.py:109
  773.2 32.6 %collective-permute-start.110 = (bf16[2,64,2048]{2,1,0:T(8,128)(2,1)}, bf16[2,64,2048]{2,1,0:T(8,128)(2,1)}, u32[]{:S(2)}, u32[]{:S(2)}) collective-permute-start(bf16[2,64,2048]{2,1,0:T(8,128)(2,1)} %dynamic-slice_bitcast_fusion.3), channel_id=1, source_target_pairs={{0,8},{1,9},{2,10},{3,11},{4,12},{5,13},{6,14},{7,15},{8,0},{9,1},... | collective-permute-start | bytes 1572872 | tf_op jit(solution)/shard_map/ppermute | solution.py:109
  781.3 39.2 %collective-permute-start.106 = (bf16[1024,512]{1,0:T(8,128)(2,1)}, bf16[1024,512]{1,0:T(8,128)(2,1)}, u32[]{:S(2)}, u32[]{:S(2)}) collective-permute-start(bf16[1024,512]{1,0:T(8,128)(2,1)} %constant_dynamic-slice_fusion.2), channel_id=1, source_target_pairs={{0,4},{1,5},{2,6},{3,7},{4,0},{5,1},{6,2},{7,3},{8,12},{9,13},{10,... | collective-permute-start | bytes 3145736 | tf_op jit(solution)/shard_map/ppermute | solution.py:109
  782.3 44.9 %collective-permute-start.107 = (bf16[256,2048]{1,0:T(8,128)(2,1)}, bf16[256,2048]{1,0:T(8,128)(2,1)S(1)}, u32[]{:S(2)}, u32[]{:S(2)}) collective-permute-start(bf16[256,2048]{1,0:T(8,128)(2,1)} %get-tuple-element.1458), channel_id=1, source_target_pairs={{0,4},{1,5},{2,6},{3,7},{4,0},{5,1},{6,2},{7,3},{8,12},{9,13},{10,... | collective-permute-start | bytes 3145736 | tf_op jit(solution)/shard_map/ppermute | solution.py:109
  783.4 43.8 %collective-permute-start.108 = (bf16[256,2048]{1,0:T(8,128)(2,1)}, bf16[256,2048]{1,0:T(8,128)(2,1)}, u32[]{:S(2)}, u32[]{:S(2)}) collective-permute-start(bf16[256,2048]{1,0:T(8,128)(2,1)} %get-tuple-element.1459), channel_id=1, source_target_pairs={{0,2},{1,3},{2,0},{3,1},{4,6},{5,7},{6,4},{7,5},{8,10},{9,11},{10,... | collective-permute-start | bytes 3145736 | tf_op jit(solution)/shard_map/ppermute | solution.py:109
  784.2 43.0 %collective-permute-start.109 = (bf16[256,2048]{1,0:T(8,128)(2,1)}, bf16[256,2048]{1,0:T(8,128)(2,1)}, u32[]{:S(2)}, u32[]{:S(2)}) collective-permute-start(bf16[256,2048]{1,0:T(8,128)(2,1)} %get-tuple-element.1460), channel_id=1, source_target_pairs={{0,24},{1,25},{2,26},{3,27},{4,28},{5,29},{6,30},{7,31},{8,0},{9,1... | collective-permute-start | bytes 3145736 | tf_op jit(solution)/shard_map/ppermute | solution.py:109
  831.6 31.0 %collective-permute-start.112 = (bf16[512,2048]{1,0:T(8,128)(2,1)S(1)}, bf16[512,2048]{1,0:T(8,128)(2,1)S(1)}, u32[]{:S(2)}, u32[]{:S(2)}) collective-permute-start(bf16[512,2048]{1,0:T(8,128)(2,1)S(1)} %pad_maximum_fusion.1), channel_id=1, source_target_pairs={{0,1},{1,0},{2,3},{3,2},{4,5},{5,4},{6,7},{7,6},{8,9},{9,8},{10,11... | collective-permute-start | bytes 6291464 | tf_op jit(solution)/shard_map/ppermute | solution.py:109
  833.4 29.2 %collective-permute-start.114 = (bf16[1024,512]{1,0:T(8,128)(2,1)S(1)}, bf16[1024,512]{1,0:T(8,128)(2,1)S(1)}, u32[]{:S(2)}, u32[]{:S(2)}) collective-permute-start(bf16[1024,512]{1,0:T(8,128)(2,1)S(1)} %constant_dynamic-slice_fusion.1), channel_id=1, source_target_pairs={{0,4},{1,5},{2,6},{3,7},{4,0},{5,1},{6,2},{7,3},{8,12},{9,13},{10,... | collective-permute-start | bytes 3145736 | tf_op jit(solution)/shard_map/ppermute | solution.py:109
  834.1 28.5 %collective-permute-start.115 = (bf16[256,2048]{1,0:T(8,128)(2,1)S(1)}, bf16[256,2048]{1,0:T(8,128)(2,1)S(1)}, u32[]{:S(2)}, u32[]{:S(2)}) collective-permute-start(bf16[256,2048]{1,0:T(8,128)(2,1)S(1)} %copy-done.82), channel_id=1, source_target_pairs={{0,2},{1,3},{2,0},{3,1},{4,6},{5,7},{6,4},{7,5},{8,10},{9,11},{10,... | collective-permute-start | bytes 3145736 | tf_op jit(solution)/shard_map/ppermute | solution.py:109
  896.3 31.8 %collective-permute-start.125 = (bf16[256,2048]{1,0:T(8,128)(2,1)S(1)}, bf16[256,2048]{1,0:T(8,128)(2,1)}, u32[]{:S(2)}, u32[]{:S(2)}) collective-permute-start(bf16[256,2048]{1,0:T(8,128)(2,1)S(1)} %bitcast.214), channel_id=1, source_target_pairs={{0,4},{1,5},{2,6},{3,7},{4,0},{5,1},{6,2},{7,3},{8,12},{9,13},{10,... | collective-permute-start | bytes 3145736 | tf_op jit(solution)/shard_map/ppermute | solution.py:109
  897.3 30.9 %collective-permute-start.126 = (bf16[256,2048]{1,0:T(8,128)(2,1)}, bf16[256,2048]{1,0:T(8,128)(2,1)}, u32[]{:S(2)}, u32[]{:S(2)}) collective-permute-start(bf16[256,2048]{1,0:T(8,128)(2,1)} %get-tuple-element.1496), channel_id=1, source_target_pairs={{0,2},{1,3},{2,0},{3,1},{4,6},{5,7},{6,4},{7,5},{8,10},{9,11},{10,... | collective-permute-start | bytes 3145736 | tf_op jit(solution)/shard_map/ppermute | solution.py:109
  966.8 28.8 %collective-permute-start.135 = (bf16[256,2048]{1,0:T(8,128)(2,1)S(1)}, bf16[256,2048]{1,0:T(8,128)(2,1)S(1)}, u32[]{:S(2)}, u32[]{:S(2)}) collective-permute-start(bf16[256,2048]{1,0:T(8,128)(2,1)S(1)} %copy-done.49), channel_id=1, source_target_pairs={{0,4},{1,5},{2,6},{3,7},{4,0},{5,1},{6,2},{7,3},{8,12},{9,13},{10,... | collective-permute-start | bytes 3145736 | tf_op jit(solution)/shard_map/ppermute | solution.py:109
  (174 other events, 2355.0 us)
